TPU v7x, 32 devices: a whole 2x2x4 slice. The times are simulated.
32 devices in a mesh: cases: 2 (over y), runs: 16 (over z, x, core).
Axes of the slice: x: 2, y: 2, z: 4, core: 2. Of those that a mesh axis runs over, the one named last changes fastest.
Arguments:
- run_inputs: float32 [2048, 24], P(('cases', 'runs')), parts along dimension 0, may hold values from -3 to 3
- term_codes: int32 [4096, 4], replicated, may hold values from 0 to 119
- weight_levels: int32 [4096], replicated, may hold values from 0 to 3
- correlations: bfloat16 [8192, 1024], P(('cases', 'runs')), parts along dimension 0, may hold values from -32 to 32
- slab_modes: bfloat16 [4096, 1024], P('cases'), parts along dimension 0, may hold values from -0.1875 to 0.1875
- cell_map: int32 [2048], replicated, may hold values from 0 to 2047, each once
Outputs:
- coefficients: float32 [8192, 1024], P(('cases', 'runs')), parts along dimension 0
- lifted: bfloat16 [8192, 2048], P(('cases', 'runs')), parts along dimension 0
There are 2 independent parts, one for each index of `cases`. A program takes and returns all parts, laid end to end along the dimension named above; an argument that names none is the same for every part. Nothing has to cross between parts.
All inputs are finite; a program needn't handle non-finite values.
Results may differ from a plain program's by a relative error of at most 0.0067.
Values may be sent and summed in bfloat16 or wider, within the bound.
No kernel may reach another device: no remote copies, remote signals or barrier semaphores. Data moves between devices by JAX's collectives and lax.ppermute only.
A program may use at most 64 MiB of HBM per device.

v0:
```python
import math

import jax
import jax.numpy as jnp
from jax import lax
from jax.sharding import PartitionSpec as P

STEP = 0.5
LAMBDA_FRACTION = 0.05
EPSILON = 1e-06
ROOT_TWO = math.sqrt(2.0)
ROOT_SIX = math.sqrt(6.0)
ROOT_TWENTYFOUR = math.sqrt(24.0)


def hermite_table(points):
    squared = points * points
    columns = [
        jnp.ones_like(points),
        points,
        (squared - 1.0) / ROOT_TWO,
        points * (squared - 3.0) / ROOT_SIX,
        (squared * squared - 6.0 * squared + 3.0) / ROOT_TWENTYFOUR,
    ]
    return jnp.stack(columns, axis=-1).reshape(points.shape[0], -1)


def basis(points, codes):
    hermite = hermite_table(points)
    product = jnp.take(hermite, codes[:, 0], axis=1)
    for column in range(1, codes.shape[1]):
        product = product * jnp.take(hermite, codes[:, column], axis=1)
    return product.astype(jnp.bfloat16)


def shrink(values, limits):
    length = jnp.sqrt(jnp.sum(values * values, axis=1, keepdims=True) + EPSILON)
    return values * jnp.maximum(0.0, 1.0 - limits[:, None] / length)


def transposed_product(left, right):
    return lax.dot_general(
        left, right, (((0,), (0,)), ((), ())), preferred_element_type=jnp.float32
    )


def on_device(run_inputs, term_codes, weight_levels, correlations, slab_modes, cell_map):
    run_count = run_inputs.shape[0]
    term_count = correlations.shape[0]
    devices = lax.axis_size("runs")
    offset = lax.axis_index("runs") * term_count
    total_runs = run_count * devices
    weights_all = jnp.exp2(weight_levels.astype(jnp.float32))
    own_weights = lax.dynamic_slice_in_dim(weights_all, offset, term_count)
    own_corr = correlations.astype(jnp.float32)
    ratio = jnp.max(jnp.sqrt(jnp.sum(own_corr * own_corr, axis=1)) / own_weights)
    penalty = LAMBDA_FRACTION * lax.pmax(ratio, "runs")
    first = shrink(STEP * own_corr, STEP * penalty * own_weights)
    design = basis(run_inputs, term_codes)
    fitted = jnp.dot(
        design,
        lax.all_gather(first.astype(jnp.bfloat16), "runs", axis=0, tiled=True),
        preferred_element_type=jnp.float32,
    )
    fitted_half = fitted.astype(jnp.bfloat16)
    all_points = lax.all_gather(run_inputs, "runs", axis=0, tiled=True)
    own_codes = lax.dynamic_slice_in_dim(term_codes, offset, term_count, 0)
    owned_design = basis(all_points, own_codes)
    summed = transposed_product(
        owned_design, lax.all_gather(fitted_half, "runs", axis=0, tiled=True)
    )
    gradient = summed / total_runs - own_corr
    coefficients = shrink(first - STEP * gradient, STEP * penalty * own_weights)
    modes = jnp.take(slab_modes, cell_map, axis=0)
    lifted = lax.dot_general(
        coefficients.astype(jnp.bfloat16),
        modes,
        (((1,), (1,)), ((), ())),
        preferred_element_type=jnp.float32,
    ).astype(jnp.bfloat16)
    return (coefficients, lifted)


def solution(mesh):
    return jax.shard_map(
        on_device,
        mesh=mesh,
        in_specs=(
            P(("cases", "runs"), None),
            P(),
            P(),
            P(("cases", "runs"), None),
            P("cases", None),
            P(),
        ),
        out_specs=(P(("cases", "runs"), None), P(("cases", "runs"), None)),
        check_vma=False,
    )
```

profile of v0, /device:TPU:0, one launch (start us, length us, event | category | flops | bytes accessed | tf_op | source)
XLA Modules:
  0.0 185.9 jit_solution(7335811870694302214)
XLA Ops:
  7.2 0.0 copy-start.3
  7.2 0.0 copy-start.4
  7.2 0.0 all-gather.4.cloned.1.call-start
  7.2 1.3 fusion.11
  8.6 1.4 fusion.35
  9.9 35.5 %pmax.7 = f32[]{:T(128)} all-reduce(f32[]{:T(128)} %fusion.35), channel_id=1, replica_groups=mesh['cases'=2,'runs'=16] {'runs'}, use_global_device_ids=true, to_apply=%region_2.0 | all-reduce | flops 1 | bytes 8 | tf_op jit(solution)/shard_map/pmax | solution.py:57
  46.1 0.8 maximum_multiply_fusion
  46.9 2.0 %fusion.10 = bf16[256,1024]{1,0:T(8,128)(2,1)} fusion(bf16[256,1024]{1,0:T(8,128)(2,1)} %param.13, f32[256]{0:T(256)S(1)} %maximum_multiply_fusion), kind=kLoop, calls=%fused_computation.25 | loop fusion | flops 786432 | bytes 1049600 | tf_op jit(solution)/shard_map/convert_element_type | solution.py:62
  48.9 0.0 all-gather.4.cloned.1.call-update
  48.9 0.0 all-gather.6.cloned.1.call-start
  49.0 0.0 copy-done.3
  49.1 0.0 copy-done.4
  49.2 10.8 %gather_fusion.5 = f32[4096,64]{1,0:T(8,128)S(1)} fusion(f32[64,120]{0,1:T(8,128)S(1)} %reshape.38, s32[4096]{0:T(1024)S(1)} %get-tuple-element.16), kind=kCustom, calls=%fused_computation.1.clone | custom fusion | bytes 2113536 | tf_op jit(solution)/shard_map/jit(_take)/gather | solution.py:30
  59.9 14.1 %gather_fusion.6 = f32[4096,64]{1,0:T(8,128)} fusion(f32[64,120]{0,1:T(8,128)S(1)} %reshape.38, s32[4096]{0:T(1024)S(1)} %get-tuple-element.17), kind=kCustom, calls=%fused_computation.5.clone | custom fusion | bytes 2113536 | tf_op jit(solution)/shard_map/jit(_take)/gather | solution.py:32
  74.0 14.1 %gather_fusion.7 = f32[4096,64]{1,0:T(8,128)} fusion(f32[64,120]{0,1:T(8,128)S(1)} %reshape.38, s32[4096]{0:T(1024)S(1)} %get-tuple-element.18), kind=kCustom, calls=%fused_computation.6.clone | custom fusion | bytes 2113536 | tf_op jit(solution)/shard_map/jit(_take)/gather | solution.py:32
  88.2 14.1 %gather_fusion.8 = f32[4096,64]{1,0:T(8,128)} fusion(f32[64,120]{0,1:T(8,128)S(1)} %reshape.38, s32[4096]{0:T(1024)S(1)} %get-tuple-element.19), kind=kCustom, calls=%fused_computation.7.clone | custom fusion | bytes 2113536 | tf_op jit(solution)/shard_map/jit(_take)/gather | solution.py:32
  102.3 18.9 %all-gather.4.cloned.1.call-done = bf16[4096,1024]{1,0:T(8,128)(2,1)} async-done(((bf16[256,1024]{1,0:T(8,128)(2,1)}), bf16[4096,1024]{1,0:T(8,128)(2,1)}) %all-gather.4.cloned.1.call-update) | async-done | bytes 8388624 | tf_op jit(solution)/shard_map/all_gather | solution.py:62
  121.2 10.3 %convolution_convert_fusion = bf16[64,1024]{1,0:T(8,128)(2,1)} fusion(bf16[4096,1024]{1,0:T(8,128)(2,1)} %all-gather.4.cloned.1.call-done, f32[4096,64]{1,0:T(8,128)} %gather_fusion.8, f32[4096,64]{1,0:T(8,128)} %gather_fusion.7, f32[4096,64]{1,0:T(8,128)} %gather_fusion.6, f32[4096,64]{1,0:T(8,128)S(1)} %gather_fusion.5, ...), kind=kOutput, calls=%fused_computation.26 | convolution fusion | flops 539033600 | bytes 12730368 | tf_op jit(solution)/shard_map/dot_general | solution.py:60
  131.5 0.0 all-gather.6.cloned.1.call-update
  131.5 19.6 %all-gather = f32[16,64,24]{1,2,0:T(8,128)S(1)} all-gather(f32[1,64,24]{1,2,0:T(8,128)S(1)} %bitcast.77), channel_id=1, replica_groups=mesh['cases'=2,'runs'=16] {'runs'}, dimensions={0}, use_global_device_ids=true | all-gather | bytes 104448 | tf_op jit(solution)/shard_map/all_gather | solution.py:66
  151.1 0.1 reshape.121
  151.3 0.1 stack.30
  151.5 0.3 copy.17
  151.8 0.1 reshape.37
  151.9 0.1 constant_dynamic-slice_fusion
  152.0 1.1 gather_fusion.2
  153.1 1.1 gather_fusion.3
  154.2 2.0 %gather_fusion.4 = f32[256,1024]{1,0:T(8,128)} fusion(f32[1024,120]{0,1:T(8,128)S(1)} %reshape.37, s32[1024]{0:T(1024)S(1)} %get-tuple-element.20), kind=kCustom, calls=%fused_computation.4.clone | custom fusion | bytes 2098176 | tf_op jit(solution)/shard_map/jit(_take)/gather | solution.py:32
  156.2 0.0 copy-start.5
  156.2 2.0 %gather_fusion.1 = f32[256,1024]{1,0:T(8,128)} fusion(f32[1024,120]{0,1:T(8,128)S(1)} %reshape.37, s32[1024]{0:T(1024)S(1)} %get-tuple-element.23), kind=kCustom, calls=%fused_computation.clone | custom fusion | bytes 2098176 | tf_op jit(solution)/shard_map/jit(_take)/gather | solution.py:30
  158.2 0.0 copy-done.5
  158.2 0.0 copy-start
  158.2 13.7 %gather_fusion = bf16[2048,1024]{1,0:T(8,128)(2,1)} fusion(bf16[2048,1024]{1,0:T(8,128)(2,1)} %param.14, s32[2048]{0:T(1024)S(1)} %fusion.32), kind=kCustom, calls=%fused_computation.8 | custom fusion | bytes 8396800 | tf_op jit(solution)/shard_map/jit(_take)/gather | solution.py:74
  172.0 0.0 all-gather.6.cloned.1.call-done
  172.1 0.0 copy-done
  172.1 0.0 copy-start.1
  172.1 3.5 %multiply_reduce_fusion = (f32[256]{0:T(256)S(1)}, f32[256,1024]{1,0:T(8,128)S(1)}) fusion(bf16[1024,1024]{1,0:T(8,128)(2,1)} %all-gather.6.cloned.1.call-done, f32[256,1024]{1,0:T(8,128)} %gather_fusion.4, f32[256,1024]{1,0:T(8,128)S(1)} %gather_fusion.3, f32[256,1024]{1,0:T(8,128)S(1)} %gather_fusion.2, f32[256,1024]{1,0:T(8,128)} %gather_fusion.1, ...), kind=kOutput, calls=%fused_computation.35 | convolution fusion | flops 541064960 | bytes 7867392 | tf_op jit(solution)/shard_map/dot_general | solution.py:42
  175.6 0.8 subtract_maximum_fusion
  176.4 0.1 broadcast_multiply_fusion
  176.5 0.0 copy-done.1
  176.5 0.0 copy-start.2
  176.6 2.5 %fusion.3 = bf16[256,2048]{1,0:T(8,128)(2,1)} fusion(bf16[2048,1024]{1,0:T(8,128)(2,1)S(1)} %copy-done.1, pred[2048]{0:T(1024)(128)(4,1)S(1)} %compare_and_fusion.4, f32[256,1024]{1,0:T(8,128)S(1)} %broadcast_multiply_fusion), kind=kOutput, calls=%fused_computation.12 | convolution fusion | flops 1076625408 | bytes 6293504 | tf_op jit(solution)/shard_map/dot_general | solution.py:75
  179.0 0.0 copy-done.2
  (28 shorter events, 0.3 us)
Async XLA Ops:
  7.2 41.8 %copy-start.3 = (f32[64,24]{0,1:T(8,128)S(1)}, f32[64,24]{0,1:T(8,128)}, u32[]{:S(2)}) copy-start(f32[64,24]{0,1:T(8,128)} %param.10) | copy-start | bytes 18436
  7.2 41.9 %copy-start.4 = (s32[4096,4]{0,1:T(4,128)S(1)}, s32[4096,4]{0,1:T(4,128)}, u32[]{:S(2)}) copy-start(s32[4096,4]{0,1:T(4,128)} %param.11) | copy-start | bytes 196612
  7.2 114.0 %all-gather.4.cloned.1.call-start = ((), (), s32[]{:S(2)}) async-start(), calls=%async_computation | async-start | bytes 8912896 | tf_op jit(solution)/shard_map/all_gather | solution.py:62
  48.9 123.2 %all-gather.6.cloned.1.call-start = ((), (), s32[]{:S(2)}) async-start(), calls=%async_computation.1 | async-start | bytes 2228224 | tf_op jit(solution)/shard_map/all_gather | solution.py:70
  156.2 2.0 %copy-start.5 = (s32[2048]{0:T(1024)S(1)}, s32[2048]{0:T(1024)}, u32[]{:S(2)}) copy-start(s32[2048]{0:T(1024)} %param.15) | copy-start | bytes 24580
  158.2 13.8 %copy-start = (bf16[256,1024]{1,0:T(8,128)(2,1)S(1)}, bf16[256,1024]{1,0:T(8,128)(2,1)}, u32[]{:S(2)}) copy-start(bf16[256,1024]{1,0:T(8,128)(2,1)} %param.13) | copy-start | bytes 1572868
  172.1 4.5 %copy-start.1 = (bf16[2048,1024]{1,0:T(8,128)(2,1)S(1)}, bf16[2048,1024]{1,0:T(8,128)(2,1)}, u32[]{:S(2)}) copy-start(bf16[2048,1024]{1,0:T(8,128)(2,1)} %gather_fusion) | copy-start | bytes 12582916
  176.5 2.5 %copy-start.2 = (f32[256,1024]{1,0:T(8,128)}, f32[256,1024]{1,0:T(8,128)S(1)}, u32[]{:S(2)}) copy-start(f32[256,1024]{1,0:T(8,128)S(1)} %broadcast_multiply_fusion) | copy-start | bytes 3145732
Sparse Core Ops, SparseCore 0:
  49.0 72.1 all-gather.3
  131.7 40.0 all-gather.5
where the time goes:
time: 186 us
  local copies, waits for them, and re-layouts  73.9 us (40%)
  blocking collectives  55.1 us (30%)
  waiting for transfers between devices  19 us (10%)
  matrix products  16.3 us (9%)
  between operations  15 us (8%)
  other arithmetic  6.58 us (4%)
    gather x6, local copies, waits for them, and re-layouts, basis(): product = product * jnp.take(hermite, codes[:, column], axis=1)  46.5 us
    pmax x1, blocking collectives, on_device(): penalty = LAMBDA_FRACTION * lax.pmax(ratio, 'runs')  35.5 us
    all_gather x1, blocking collectives, on_device(): all_points = lax.all_gather(run_inputs, 'runs', axis=0, tiled=True)  19.6 us
    all_gather x1, waiting for transfers between devices, on_device(): lax.all_gather(first.astype(jnp.bfloat16), 'runs', axis=0, tiled=True)  18.9 us
    gather x1, local copies, waits for them, and re-layouts, on_device(): modes = jnp.take(slab_modes, cell_map, axis=0)  13.7 us
    gather x2, local copies, waits for them, and re-layouts, basis(): product = jnp.take(hermite, codes[:, 0], axis=1)  12.8 us
    dot_general x1, matrix products, on_device(): jnp.dot(design, lax.all_gather(first.astype(jnp.bfloat16), 'runs', axis=0...  10.3 us
  transfers between devices with their start and end apart: 2, of which 1 were waited for; matrix products, arithmetic and copies ran while one was open for 40% of the time, Pallas kernels for 0%

commit v1 on v0

--- a/solution.py
+++ b/solution.py
@@ -1,16 +1,274 @@
+import functools
 import math
 
 import jax
 import jax.numpy as jnp
 from jax import lax
+from jax.experimental import pallas as pl
+from jax.experimental.pallas import tpu as pltpu
 from jax.sharding import PartitionSpec as P
 
 STEP = 0.5
 LAMBDA_FRACTION = 0.05
 EPSILON = 1e-06
+DEGREES = 5
+LANES = 128
 ROOT_TWO = math.sqrt(2.0)
 ROOT_SIX = math.sqrt(6.0)
 ROOT_TWENTYFOUR = math.sqrt(24.0)
+MIB = 1 << 20
+
+
+def round_up(value, multiple):
+    return -(-value // multiple) * multiple
+
+
+def prepare_kernel(corr_ref, points_ref, turned_ref, packet_ref):
+    turned = corr_ref[...].astype(jnp.float32).T
+    turned_ref[...] = turned.astype(jnp.bfloat16)
+    squares = jnp.sum(turned * turned, axis=0, keepdims=True)
+    dim, runs = points_ref.shape
+    packet_ref[...] = jnp.zeros_like(packet_ref)
+    packet_ref[0:dim, 0:runs] = points_ref[...]
+    for part in range(squares.shape[1] // LANES):
+        packet_ref[dim + part : dim + part + 1, :] = squares[
+            :, part * LANES : (part + 1) * LANES
+        ]
+
+
+def hermite_columns(points):
+    squared = points * points
+    return jnp.concatenate(
+        [
+            jnp.ones_like(points),
+            points,
+            (squared - 1.0) / ROOT_TWO,
+            points * (squared - 3.0) / ROOT_SIX,
+            (squared * squared - 6.0 * squared + 3.0) / ROOT_TWENTYFOUR,
+        ],
+        axis=0,
+    )
+
+
+def design_kernel(dim, run_count, packets_ref, codes_ref, design_ref, table):
+    devices = packets_ref.shape[0]
+    half = table.shape[1] // 2
+
+    @pl.when(pl.program_id(0) == 0)
+    def _():
+        per = LANES // run_count
+        for group in range(devices // per):
+            points = jnp.concatenate(
+                [
+                    packets_ref[group * per + i, 0:dim, 0:run_count]
+                    for i in range(per)
+                ],
+                axis=1,
+            )
+            columns = hermite_columns(points)
+            columns = jnp.concatenate(
+                [
+                    columns,
+                    jnp.zeros((half - columns.shape[0], LANES), jnp.float32),
+                ],
+                axis=0,
+            ).T
+            high = columns.astype(jnp.bfloat16)
+            low = (columns - high.astype(jnp.float32)).astype(jnp.bfloat16)
+            rows = slice(group * LANES, (group + 1) * LANES)
+            table[rows, 0:half] = high
+            table[rows, half : 2 * half] = low
+
+    codes = codes_ref[...]
+    spots = (codes % DEGREES) * dim + codes // DEGREES
+    terms = codes.shape[1]
+    row = lax.broadcasted_iota(jnp.int32, (half, terms), 0)
+    product = None
+    for slot in range(codes.shape[0]):
+        chosen = jnp.where(row == spots[slot : slot + 1, :], 1.0, 0.0).astype(
+            jnp.bfloat16
+        )
+        chosen = jnp.concatenate([chosen, chosen], axis=0)
+        factor = jnp.dot(table[...], chosen, preferred_element_type=jnp.float32)
+        product = factor if product is None else product * factor
+    design_ref[...] = product.astype(jnp.bfloat16)
+
+
+def penalty_rows(dim, term_count, packets_ref, levels_ref):
+    squares = jnp.concatenate(
+        [
+            packets_ref[i, dim + part : dim + part + 1, :]
+            for i in range(packets_ref.shape[0])
+            for part in range(term_count // LANES)
+        ],
+        axis=1,
+    )
+    weights = jnp.exp2(levels_ref[...].astype(jnp.float32))
+    ratio = jnp.max(jnp.sqrt(squares) / weights, axis=1, keepdims=True)
+    return squares, weights, LAMBDA_FRACTION * ratio
+
+
+def shrink_factor(squares, limits):
+    return jnp.maximum(0.0, 1.0 - limits / jnp.sqrt(squares + EPSILON))
+
+
+def fit_kernel(
+    dim, total_runs, packets_ref, levels_ref, corr_ref, design_ref, summed_ref, scale_ref
+):
+    devices, _, term_count = corr_ref.shape
+    squares, weights, penalty = penalty_rows(dim, term_count, packets_ref, levels_ref)
+    limits = STEP * penalty * weights
+    factor = shrink_factor(STEP * STEP * squares, limits)
+    scale_ref[0:1, :] = factor
+    scale_ref[1:2, :] = limits
+    fitted = None
+    for i in range(devices):
+        terms = slice(i * term_count, (i + 1) * term_count)
+        first = STEP * corr_ref[i].astype(jnp.float32) * factor[:, terms]
+        part = lax.dot_general(
+            first.astype(jnp.bfloat16),
+            design_ref[:, terms],
+            (((1,), (1,)), ((), ())),
+            preferred_element_type=jnp.float32,
+        )
+        fitted = part if fitted is None else fitted + part
+    fitted = fitted.astype(jnp.bfloat16)
+    for i in range(devices):
+        terms = slice(i * term_count, (i + 1) * term_count)
+        summed = jnp.dot(
+            fitted, design_ref[:, terms], preferred_element_type=jnp.float32
+        )
+        summed_ref[i] = (summed / total_runs).astype(jnp.bfloat16)
+
+
+def finish_kernel(summed_ref, corr_ref, scale_ref, out_ref, half_ref):
+    corr = corr_ref[...].astype(jnp.float32)
+    first = STEP * corr * scale_ref[0:1, :]
+    gradient = summed_ref[...].astype(jnp.float32) - corr
+    moved = first - STEP * gradient
+    squares = jnp.sum(moved * moved, axis=0, keepdims=True)
+    values = (moved * shrink_factor(squares, scale_ref[1:2, :])).T
+    out_ref[...] = values
+    half_ref[...] = values.astype(jnp.bfloat16)
+
+
+def reorder_kernel(map_ref, slab_ref, modes_ref):
+    cells = slab_ref.shape[0]
+    block = modes_ref.shape[0]
+    row = lax.broadcasted_iota(jnp.int32, (cells, block), 0)
+    chosen = jnp.where(row == map_ref[...], 1.0, 0.0).astype(jnp.bfloat16)
+    modes_ref[...] = lax.dot_general(
+        chosen,
+        slab_ref[...],
+        (((0,), (0,)), ((), ())),
+        preferred_element_type=jnp.float32,
+    ).astype(jnp.bfloat16)
+
+
+def lift_kernel(half_ref, modes_ref, lifted_ref):
+    lifted_ref[...] = lax.dot_general(
+        half_ref[...],
+        modes_ref[...],
+        (((1,), (1,)), ((), ())),
+        preferred_element_type=jnp.float32,
+    ).astype(jnp.bfloat16)
+
+
+def split_by_modes(
+    run_inputs, term_codes, weight_levels, correlations, slab_modes, cell_map
+):
+    run_count, dim = run_inputs.shape
+    term_count, modes = correlations.shape
+    terms, slots = term_codes.shape
+    cells = slab_modes.shape[0]
+    slab_cells = cell_map.shape[0]
+    devices = lax.axis_size("runs")
+    total_runs = run_count * devices
+    own_modes = modes // devices
+    offset = lax.axis_index("runs") * term_count
+    packet_rows = round_up(dim + term_count // LANES, 8)
+    params = pltpu.CompilerParams(vmem_limit_bytes=48 * MIB)
+
+    turned, packet = pl.pallas_call(
+        prepare_kernel,
+        out_shape=(
+            jax.ShapeDtypeStruct((modes, term_count), jnp.bfloat16),
+            jax.ShapeDtypeStruct((packet_rows, LANES), jnp.float32),
+        ),
+        compiler_params=params,
+        name="prepare",
+    )(correlations, run_inputs.T)
+    packets = lax.all_gather(packet, "runs", axis=0, tiled=False)
+    blocks = lax.all_to_all(
+        turned.reshape(devices, own_modes, term_count), "runs", 0, 0, tiled=False
+    )
+
+    tile = term_count
+    half = round_up(DEGREES * dim, LANES)
+    design = pl.pallas_call(
+        functools.partial(design_kernel, dim, run_count),
+        grid=(terms // tile,),
+        in_specs=[
+            pl.BlockSpec((devices, packet_rows, LANES), lambda i: (0, 0, 0)),
+            pl.BlockSpec((slots, tile), lambda i: (0, i)),
+        ],
+        out_specs=pl.BlockSpec((total_runs, tile), lambda i: (0, i)),
+        out_shape=jax.ShapeDtypeStruct((total_runs, terms), jnp.bfloat16),
+        scratch_shapes=[pltpu.VMEM((total_runs, 2 * half), jnp.bfloat16)],
+        compiler_params=params,
+        name="design",
+    )(packets, term_codes.T)
+
+    summed, scale = pl.pallas_call(
+        functools.partial(fit_kernel, dim, float(total_runs)),
+        out_shape=(
+            jax.ShapeDtypeStruct((devices, own_modes, term_count), jnp.bfloat16),
+            jax.ShapeDtypeStruct((8, terms), jnp.float32),
+        ),
+        compiler_params=params,
+        name="fit",
+    )(packets, weight_levels[None, :], blocks, design)
+    own_scale = lax.dynamic_slice_in_dim(scale, offset, term_count, 1)
+    returned = lax.all_to_all(summed, "runs", 0, 0, tiled=False).reshape(
+        modes, term_count
+    )
+
+    block = min(512, slab_cells)
+    ordered = pl.pallas_call(
+        reorder_kernel,
+        grid=(slab_cells // block,),
+        in_specs=[
+            pl.BlockSpec((1, block), lambda i: (0, i)),
+            pl.BlockSpec((cells, modes), lambda i: (0, 0)),
+        ],
+        out_specs=pl.BlockSpec((block, modes), lambda i: (i, 0)),
+        out_shape=jax.ShapeDtypeStruct((slab_cells, modes), jnp.bfloat16),
+        compiler_params=params,
+        name="reorder",
+    )(cell_map[None, :], slab_modes)
+
+    coefficients, half_width = pl.pallas_call(
+        finish_kernel,
+        out_shape=(
+            jax.ShapeDtypeStruct((term_count, modes), jnp.float32),
+            jax.ShapeDtypeStruct((term_count, modes), jnp.bfloat16),
+        ),
+        compiler_params=params,
+        name="finish",
+    )(returned, turned, own_scale)
+    lifted = pl.pallas_call(
+        lift_kernel,
+        grid=(slab_cells // block,),
+        in_specs=[
+            pl.BlockSpec((term_count, modes), lambda i: (0, 0)),
+            pl.BlockSpec((block, modes), lambda i: (i, 0)),
+        ],
+        out_specs=pl.BlockSpec((term_count, block), lambda i: (0, i)),
+        out_shape=jax.ShapeDtypeStruct((term_count, slab_cells), jnp.bfloat16),
+        compiler_params=params,
+        name="lift",
+    )(half_width, ordered)
+    return (coefficients, lifted)
 
 
 def hermite_table(points):
@@ -44,7 +302,9 @@
     )
 
 
-def on_device(run_inputs, term_codes, weight_levels, correlations, slab_modes, cell_map):
+def split_by_runs(
+    run_inputs, term_codes, weight_levels, correlations, slab_modes, cell_map
+):
     run_count = run_inputs.shape[0]
     term_count = correlations.shape[0]
     devices = lax.axis_size("runs")
@@ -81,6 +341,24 @@
     return (coefficients, lifted)
 
 
+def on_device(
+    run_inputs, term_codes, weight_levels, correlations, slab_modes, cell_map
+):
+    devices = lax.axis_size("runs")
+    run_count = run_inputs.shape[0]
+    term_count, modes = correlations.shape
+    whole_tiles = (
+        modes % (16 * devices) == 0
+        and term_count % LANES == 0
+        and LANES % run_count == 0
+        and devices % (LANES // run_count) == 0
+    )
+    plan = split_by_modes if whole_tiles else split_by_runs
+    return plan(
+        run_inputs, term_codes, weight_levels, correlations, slab_modes, cell_map
+    )
+
+
 def solution(mesh):
     return jax.shard_map(
         on_device,

time: 186 us -> 86.3 us (0.46)
  local copies, waits for them, and re-layouts: 73.9 us -> 6.72 us
  Pallas kernels: 0 us -> 40.7 us
  blocking collectives: 55.1 us -> 25.9 us
  waiting for transfers between devices: 19 us -> 0.77 us
  matrix products: 16.3 us -> 0 us
  between operations: 15 us -> 0.69 us
  starting transfers between devices: 0.08 us -> 10.9 us
  other arithmetic: 6.58 us -> 0 us
    gather x9 -> x0, local copies, waits for them, and re-layouts: 73 us -> none  [the longest x6 46.5 us: basis(): product = product * jnp.take(hermite, codes[:, column], axis=1)]
    pallas_call x0 -> x6, Pallas kernels: none -> 40.7 us  [the longest x1 13.8 us: split_by_modes(): pl.pallas_call(functools.partial(design_kernel, dim, run_count), grid=(te...]
    pmax x1 -> x0, blocking collectives: 35.5 us -> none  [on_device(): penalty = LAMBDA_FRACTION * lax.pmax(ratio, 'runs')]
    all_gather x2 -> x0, waiting for transfers between devices: 18.9 us -> none  [the longest x1 18.9 us: on_device(): lax.all_gather(first.astype(jnp.bfloat16), 'runs', axis=0, tiled=True)]
    dot_general x3 -> x0, matrix products: 16.3 us -> none  [the longest x1 10.3 us: on_device(): jnp.dot(design, lax.all_gather(first.astype(jnp.bfloat16), 'runs', axis=0...]
    all_to_all x0 -> x2, starting transfers between devices: none -> 10.9 us  [the longest x1 7.36 us: split_by_modes(): lax.all_to_all(turned.reshape(devices, own_modes, term_count), 'runs', 0,...]
    unnamed x17 -> x14, local copies, waits for them, and re-layouts: 0.16 us -> 6.71 us
    all_gather x1, blocking collectives: 19.6 us -> 25.9 us  [split_by_modes(): packets = lax.all_gather(packet, 'runs', axis=0, tiled=False)]
  transfers between devices with their start and end apart: 2 -> 2, of which waited for: 1 -> 1; matrix products, arithmetic and copies ran while one was open for 40% -> 0% of each run, Pallas kernels for 0% -> 30%
where the time goes in v1:
time: 86.3 us; the launch traced here: 85.7 us
  Pallas kernels  40.7 us (47%)
  blocking collectives  25.9 us (30%)
  starting transfers between devices  10.9 us (13%)
  local copies, waits for them, and re-layouts  6.72 us (8%)
    all_gather x1, blocking collectives, split_by_modes(): packets = lax.all_gather(packet, 'runs', axis=0, tiled=False)  25.9 us
    pallas_call x1, Pallas kernels, split_by_modes(): pl.pallas_call(functools.partial(design_kernel, dim, run_count), grid=(te...  13.8 us
    pallas_call x1, Pallas kernels, split_by_modes(): pl.pallas_call(reorder_kernel, grid=(slab_cells // block,), in_specs=[pl....  11.7 us
    pallas_call x1, Pallas kernels, split_by_modes(): pl.pallas_call(functools.partial(fit_kernel, dim, float(total_runs)), out...  8.43 us
    all_to_all x1, starting transfers between devices, split_by_modes(): lax.all_to_all(turned.reshape(devices, own_modes, term_count), 'runs', 0,...  7.36 us
    unnamed x14, local copies, waits for them, and re-layouts  6.71 us
    all_to_all x1, starting transfers between devices, split_by_modes(): lax.all_to_all(summed, 'runs', 0, 0, tiled=False).reshape(modes, term_count)  3.57 us
    pallas_call x1, Pallas kernels, split_by_modes(): pl.pallas_call(finish_kernel, out_shape=(jax.ShapeDtypeStruct((term_count...  2.88 us
  transfers between devices with their start and end apart: 2, of which 1 were waited for; matrix products, arithmetic and copies ran while one was open for 0% of the time, Pallas kernels for 30%

profile of v1, /device:TPU:0, one launch (start us, length us, event | category | flops | bytes accessed | tf_op | source)
XLA Modules:
  0.0 85.7 jit_solution(1151592600111403816)
XLA Ops:
  0.6 0.0 copy-start.2
  0.6 1.0 %copy-done.2 = bf16[256,1024]{1,0:T(8,128)(2,1)S(1)} copy-done((bf16[256,1024]{1,0:T(8,128)(2,1)S(1)}, bf16[256,1024]{1,0:T(8,128)(2,1)}, u32[]{:S(2)}) %copy-start.2) | copy-done | bytes 524312
  1.7 0.0 copy-start.5
  1.7 0.7 copy-done.5
  2.4 1.0 %prepare.1 = (bf16[1024,256]{1,0:T(8,128)(2,1)}, f32[32,128]{1,0:T(8,128)S(1)}) custom-call(bf16[256,1024]{1,0:T(8,128)(2,1)S(1)} %copy-done.2, f32[24,64]{1,0:T(8,128)S(1)} %bitcast.12), custom_call_target="tpu_custom_call" | custom-call | tf_op jit(solution)/shard_map/prepare/pallas_call | solution.py:192
  3.4 7.4 %all-to-all-start = ((bf16[16,64,256]{2,1,0:T(8,128)(2,1)}), bf16[16,64,256]{2,1,0:T(8,128)(2,1)S(1)}, u32[]{:S(2)}, u32[]{:S(2)}) async-start(bf16[16,64,256]{2,1,0:T(8,128)(2,1)} %bitcast.3), calls=%async_computation | async-start | bytes 1048576 | tf_op jit(solution)/shard_map/all_to_all | solution.py:202
  10.8 25.9 %all-gather = f32[512,128]{1,0:T(8,128)S(1)} all-gather(f32[32,128]{1,0:T(8,128)S(1)} %get-tuple-element.8), channel_id=2, replica_groups=mesh['cases'=2,'runs'=16] {'runs'}, dimensions={0}, use_global_device_ids=true | all-gather | bytes 278528 | tf_op jit(solution)/shard_map/all_gather | solution.py:201
  36.7 0.0 copy-start.3
  36.7 0.8 copy-done.3
  37.5 0.0 copy-start.4
  37.5 13.8 %design.1.design_ref = bf16[1024,4096]{1,0:T(8,128)(2,1)} custom-call(f32[16,32,128]{2,1,0:T(8,128)S(1)} %bitcast.7, s32[4,4096]{1,0:T(4,128)S(1)} %bitcast.10), custom_call_target="tpu_custom_call" | custom-call | tf_op jit(solution)/shard_map/design/pallas_call | solution.py:208
  51.4 0.0 all-to-all-done.corr_ref
  51.4 0.0 copy-done.4
  51.4 0.0 copy-start.6
  51.4 8.4 %fit.1 = (bf16[16,64,256]{2,1,0:T(8,128)(2,1)}, f32[8,4096]{1,0:T(8,128)S(1)}) custom-call(f32[16,32,128]{2,1,0:T(8,128)S(1)} %bitcast.8, s32[1,4096]{1,0:T(1,128)S(1)} %bitcast.11, bf16[16,64,256]{2,1,0:T(8,128)(2,1)S(1)} %all-to-all-done.corr_ref, bf16[1024,4096]{1,0:T(8,128)(2,1)} %design.1.design_ref), custom_call_target="tpu_custom_call" | custom-call | tf_op jit(solution)/shard_map/fit/pallas_call | solution.py:222
  59.8 3.6 %all-to-all-start.1 = ((bf16[16,64,256]{2,1,0:T(8,128)(2,1)}), bf16[16,64,256]{2,1,0:T(8,128)(2,1)S(1)}, u32[]{:S(2)}, u32[]{:S(2)}) async-start(bf16[16,64,256]{2,1,0:T(8,128)(2,1)} %get-tuple-element.10), calls=%async_computation.1 | async-start | bytes 1048576 | tf_op jit(solution)/shard_map/all_to_all | solution.py:232
  63.4 0.0 copy-done.6
  63.4 11.7 %reorder.1.modes_ref = bf16[2048,1024]{1,0:T(8,128)(2,1)S(1)} custom-call(s32[1,2048]{1,0:T(1,128)S(1)} %bitcast.13, bf16[2048,1024]{1,0:T(8,128)(2,1)} %slab_ref.1), custom_call_target="tpu_custom_call" | custom-call | tf_op jit(solution)/shard_map/reorder/pallas_call | solution.py:237
  75.1 0.0 copy-start
  75.1 1.9 %copy-done = bf16[2048,1024]{1,0:T(8,128)(2,1)} copy-done((bf16[2048,1024]{1,0:T(8,128)(2,1)}, bf16[2048,1024]{1,0:T(8,128)(2,1)S(1)}, u32[]{:S(2)}) %copy-start) | copy-done | bytes 4194328
  77.0 0.8 all-to-all-done.1
  77.8 2.9 %finish.1 = (f32[256,1024]{1,0:T(8,128)}, bf16[256,1024]{1,0:T(8,128)(2,1)S(1)}) custom-call(bf16[1024,256]{1,0:T(8,128)(2,1)S(1)} %bitcast.9, bf16[1024,256]{1,0:T(8,128)(2,1)} %get-tuple-element.9.corr_ref, f32[8,256]{1,0:T(8,128)S(1)} %constant_dynamic-slice_fusion.scale_ref), custom_call_target="tpu_custom_call" | custom-call | tf_op jit(solution)/shard_map/finish/pallas_call | solution.py:250
  80.7 0.0 copy-start.1
  80.7 2.2 %copy-done.1 = bf16[2048,1024]{1,0:T(8,128)(2,1)S(1)} copy-done((bf16[2048,1024]{1,0:T(8,128)(2,1)S(1)}, bf16[2048,1024]{1,0:T(8,128)(2,1)}, u32[]{:S(2)}) %copy-start.1) | copy-done | bytes 4194328
  82.9 2.8 %lift.1 = bf16[256,2048]{1,0:T(8,128)(2,1)} custom-call(bf16[256,1024]{1,0:T(8,128)(2,1)S(1)} %get-tuple-element.13.half_ref, bf16[2048,1024]{1,0:T(8,128)(2,1)S(1)} %copy-done.1), custom_call_target="tpu_custom_call" | custom-call | tf_op jit(solution)/shard_map/lift/pallas_call | solution.py:259
  (1 shorter events, 0.0 us)
Async XLA Ops:
  0.6 1.0 %copy-start.2 = (bf16[256,1024]{1,0:T(8,128)(2,1)S(1)}, bf16[256,1024]{1,0:T(8,128)(2,1)}, u32[]{:S(2)}) copy-start(bf16[256,1024]{1,0:T(8,128)(2,1)} %corr_ref.1) | copy-start | bytes 1572868
  1.7 0.7 copy-start.5
  3.4 48.0 %all-to-all-start = ((bf16[16,64,256]{2,1,0:T(8,128)(2,1)}), bf16[16,64,256]{2,1,0:T(8,128)(2,1)S(1)}, u32[]{:S(2)}, u32[]{:S(2)}) async-start(bf16[16,64,256]{2,1,0:T(8,128)(2,1)} %bitcast.3), calls=%async_computation | async-start | bytes 1048576 | tf_op jit(solution)/shard_map/all_to_all | solution.py:202
  36.7 0.8 copy-start.3
  37.5 13.8 %copy-start.4 = (s32[4096]{0:T(1024)S(1)}, s32[4096]{0:T(1024)}, u32[]{:S(2)}) copy-start(s32[4096]{0:T(1024)} %param.8) | copy-start | bytes 49156
  51.4 12.0 %copy-start.6 = (s32[2048]{0:T(1024)S(1)}, s32[2048]{0:T(1024)}, u32[]{:S(2)}) copy-start(s32[2048]{0:T(1024)} %param.11) | copy-start | bytes 24580
  59.8 18.0 %all-to-all-start.1 = ((bf16[16,64,256]{2,1,0:T(8,128)(2,1)}), bf16[16,64,256]{2,1,0:T(8,128)(2,1)S(1)}, u32[]{:S(2)}, u32[]{:S(2)}) async-start(bf16[16,64,256]{2,1,0:T(8,128)(2,1)} %get-tuple-element.10), calls=%async_computation.1 | async-start | bytes 1048576 | tf_op jit(solution)/shard_map/all_to_all | solution.py:232
  75.1 1.9 %copy-start = (bf16[2048,1024]{1,0:T(8,128)(2,1)}, bf16[2048,1024]{1,0:T(8,128)(2,1)S(1)}, u32[]{:S(2)}) copy-start(bf16[2048,1024]{1,0:T(8,128)(2,1)S(1)} %reorder.1.modes_ref) | copy-start | bytes 12582916
  80.7 2.2 %copy-start.1 = (bf16[2048,1024]{1,0:T(8,128)(2,1)S(1)}, bf16[2048,1024]{1,0:T(8,128)(2,1)}, u32[]{:S(2)}) copy-start(bf16[2048,1024]{1,0:T(8,128)(2,1)} %copy-done) | copy-start | bytes 12582916

commit v2 on v1

--- a/solution.py
+++ b/solution.py
@@ -23,17 +23,27 @@
     return -(-value // multiple) * multiple
 
 
-def prepare_kernel(corr_ref, points_ref, turned_ref, packet_ref):
+def prepare_kernel(parts, corr_ref, points_ref, turned_ref, packets_ref):
     turned = corr_ref[...].astype(jnp.float32).T
     turned_ref[...] = turned.astype(jnp.bfloat16)
     squares = jnp.sum(turned * turned, axis=0, keepdims=True)
-    dim, runs = points_ref.shape
-    packet_ref[...] = jnp.zeros_like(packet_ref)
-    packet_ref[0:dim, 0:runs] = points_ref[...]
-    for part in range(squares.shape[1] // LANES):
-        packet_ref[dim + part : dim + part + 1, :] = squares[
-            :, part * LANES : (part + 1) * LANES
-        ]
+    rows = points_ref.shape[0] // parts
+    pieces = [
+        jnp.concatenate(
+            [points_ref[part * rows : (part + 1) * rows, :] for part in range(parts)],
+            axis=1,
+        )
+    ]
+    pieces += [
+        squares[:, part * LANES : (part + 1) * LANES]
+        for part in range(squares.shape[1] // LANES)
+    ]
+    used = rows + len(pieces) - 1
+    if packets_ref.shape[1] > used:
+        pieces.append(jnp.zeros((packets_ref.shape[1] - used, LANES), jnp.float32))
+    packet = jnp.concatenate(pieces, axis=0)
+    for i in range(packets_ref.shape[0]):
+        packets_ref[i] = packet
 
 
 def hermite_columns(points):
@@ -50,20 +60,31 @@
     )
 
 
-def design_kernel(dim, run_count, packets_ref, codes_ref, design_ref, table):
+def design_kernel(dim, run_count, packets_ref, codes_ref, design_ref, table, chosen):
     devices = packets_ref.shape[0]
     half = table.shape[1] // 2
+    parts = LANES // run_count
+    rows = dim // parts
 
     @pl.when(pl.program_id(0) == 0)
     def _():
-        per = LANES // run_count
-        for group in range(devices // per):
+        for group in range(devices // parts):
             points = jnp.concatenate(
                 [
-                    packets_ref[group * per + i, 0:dim, 0:run_count]
-                    for i in range(per)
+                    jnp.concatenate(
+                        [
+                            packets_ref[
+                                group * parts + i,
+                                0:rows,
+                                part * run_count : (part + 1) * run_count,
+                            ]
+                            for i in range(parts)
+                        ],
+                        axis=1,
+                    )
+                    for part in range(parts)
                 ],
-                axis=1,
+                axis=0,
             )
             columns = hermite_columns(points)
             columns = jnp.concatenate(
@@ -75,29 +96,35 @@
             ).T
             high = columns.astype(jnp.bfloat16)
             low = (columns - high.astype(jnp.float32)).astype(jnp.bfloat16)
-            rows = slice(group * LANES, (group + 1) * LANES)
-            table[rows, 0:half] = high
-            table[rows, half : 2 * half] = low
+            block = slice(group * LANES, (group + 1) * LANES)
+            table[block, 0:half] = high
+            table[block, half : 2 * half] = low
 
     codes = codes_ref[...]
     spots = (codes % DEGREES) * dim + codes // DEGREES
-    terms = codes.shape[1]
+    slots, terms = codes.shape
     row = lax.broadcasted_iota(jnp.int32, (half, terms), 0)
-    product = None
-    for slot in range(codes.shape[0]):
-        chosen = jnp.where(row == spots[slot : slot + 1, :], 1.0, 0.0).astype(
+    for slot in range(slots):
+        picked = jnp.where(row == spots[slot : slot + 1, :], 1.0, 0.0).astype(
             jnp.bfloat16
         )
-        chosen = jnp.concatenate([chosen, chosen], axis=0)
-        factor = jnp.dot(table[...], chosen, preferred_element_type=jnp.float32)
-        product = factor if product is None else product * factor
-    design_ref[...] = product.astype(jnp.bfloat16)
-
-
-def penalty_rows(dim, term_count, packets_ref, levels_ref):
+        chosen[slot, 0:half, :] = picked
+        chosen[slot, half : 2 * half, :] = picked
+    for start in range(0, table.shape[0], LANES):
+        block = slice(start, start + LANES)
+        product = None
+        for slot in range(slots):
+            factor = jnp.dot(
+                table[block, :], chosen[slot], preferred_element_type=jnp.float32
+            )
+            product = factor if product is None else product * factor
+        design_ref[block, :] = product.astype(jnp.bfloat16)
+
+
+def penalty_rows(first_row, term_count, packets_ref, levels_ref):
     squares = jnp.concatenate(
         [
-            packets_ref[i, dim + part : dim + part + 1, :]
+            packets_ref[i, first_row + part : first_row + part + 1, :]
             for i in range(packets_ref.shape[0])
             for part in range(term_count // LANES)
         ],
@@ -113,26 +140,34 @@
 
 
 def fit_kernel(
-    dim, total_runs, packets_ref, levels_ref, corr_ref, design_ref, summed_ref, scale_ref
+    first_row,
+    total_runs,
+    packets_ref,
+    levels_ref,
+    corr_ref,
+    design_ref,
+    summed_ref,
+    scale_ref,
+    first_ref,
 ):
     devices, _, term_count = corr_ref.shape
-    squares, weights, penalty = penalty_rows(dim, term_count, packets_ref, levels_ref)
+    squares, weights, penalty = penalty_rows(
+        first_row, term_count, packets_ref, levels_ref
+    )
     limits = STEP * penalty * weights
     factor = shrink_factor(STEP * STEP * squares, limits)
     scale_ref[0:1, :] = factor
     scale_ref[1:2, :] = limits
-    fitted = None
     for i in range(devices):
         terms = slice(i * term_count, (i + 1) * term_count)
         first = STEP * corr_ref[i].astype(jnp.float32) * factor[:, terms]
-        part = lax.dot_general(
-            first.astype(jnp.bfloat16),
-            design_ref[:, terms],
-            (((1,), (1,)), ((), ())),
-            preferred_element_type=jnp.float32,
-        )
-        fitted = part if fitted is None else fitted + part
-    fitted = fitted.astype(jnp.bfloat16)
+        first_ref[:, terms] = first.astype(jnp.bfloat16)
+    fitted = lax.dot_general(
+        first_ref[...],
+        design_ref[...],
+        (((1,), (1,)), ((), ())),
+        preferred_element_type=jnp.float32,
+    ).astype(jnp.bfloat16)
     for i in range(devices):
         terms = slice(i * term_count, (i + 1) * term_count)
         summed = jnp.dot(
@@ -141,37 +176,72 @@
         summed_ref[i] = (summed / total_runs).astype(jnp.bfloat16)
 
 
-def finish_kernel(summed_ref, corr_ref, scale_ref, out_ref, half_ref):
-    corr = corr_ref[...].astype(jnp.float32)
-    first = STEP * corr * scale_ref[0:1, :]
-    gradient = summed_ref[...].astype(jnp.float32) - corr
-    moved = first - STEP * gradient
-    squares = jnp.sum(moved * moved, axis=0, keepdims=True)
-    values = (moved * shrink_factor(squares, scale_ref[1:2, :])).T
-    out_ref[...] = values
-    half_ref[...] = values.astype(jnp.bfloat16)
-
-
-def reorder_kernel(map_ref, slab_ref, modes_ref):
-    cells = slab_ref.shape[0]
-    block = modes_ref.shape[0]
+def reorder_kernel(map_ref, slab_ref, modes_ref, turned):
+    cells, block = slab_ref.shape[0], modes_ref.shape[1]
+
+    @pl.when(pl.program_id(0) == 0)
+    def _():
+        for start in range(0, cells, LANES):
+            rows = slice(start, start + LANES)
+            turned[:, rows] = slab_ref[rows, :].T
+
     row = lax.broadcasted_iota(jnp.int32, (cells, block), 0)
     chosen = jnp.where(row == map_ref[...], 1.0, 0.0).astype(jnp.bfloat16)
-    modes_ref[...] = lax.dot_general(
-        chosen,
-        slab_ref[...],
-        (((0,), (0,)), ((), ())),
-        preferred_element_type=jnp.float32,
+    modes_ref[...] = jnp.dot(
+        turned[...], chosen, preferred_element_type=jnp.float32
     ).astype(jnp.bfloat16)
 
 
-def lift_kernel(half_ref, modes_ref, lifted_ref):
-    lifted_ref[...] = lax.dot_general(
-        half_ref[...],
-        modes_ref[...],
-        (((1,), (1,)), ((), ())),
-        preferred_element_type=jnp.float32,
-    ).astype(jnp.bfloat16)
+def finish_kernel(
+    summed_ref,
+    corr_ref,
+    scale_ref,
+    modes_ref,
+    out_ref,
+    lifted_ref,
+    moved,
+    values,
+    half,
+    lifted,
+    out_sem,
+    lifted_sem,
+):
+    modes, terms = corr_ref.shape
+    squares = jnp.zeros((1, terms), jnp.float32)
+    for start in range(0, modes, LANES):
+        block = slice(start, start + LANES)
+        corr = corr_ref[block, :].astype(jnp.float32)
+        first = STEP * corr * scale_ref[0:1, :]
+        gradient = summed_ref[block, :].astype(jnp.float32) - corr
+        step = first - STEP * gradient
+        moved[block, :] = step
+        squares = squares + jnp.sum(step * step, axis=0, keepdims=True)
+    factor = shrink_factor(squares, scale_ref[1:2, :])
+    for start in range(0, modes, LANES):
+        block = slice(start, start + LANES)
+        turned = (moved[block, :] * factor).T
+        values[:, block] = turned
+        half[:, block] = turned.astype(jnp.bfloat16)
+    copies = [pltpu.make_async_copy(values, out_ref, out_sem)]
+    copies[0].start()
+    width = lifted.shape[2]
+    for i in range(lifted.shape[0]):
+        block = slice(i * width, (i + 1) * width)
+        lifted[i] = jnp.dot(
+            half[...], modes_ref[:, block], preferred_element_type=jnp.float32
+        ).astype(jnp.bfloat16)
+        copies.append(
+            pltpu.make_async_copy(
+                lifted.at[i], lifted_ref.at[:, block], lifted_sem.at[i]
+            )
+        )
+        copies[-1].start()
+    for copy in copies:
+        copy.wait()
+
+
+def params(limit):
+    return pltpu.CompilerParams(vmem_limit_bytes=limit * MIB)
 
 
 def split_by_modes(
@@ -186,19 +256,20 @@
     total_runs = run_count * devices
     own_modes = modes // devices
     offset = lax.axis_index("runs") * term_count
-    packet_rows = round_up(dim + term_count // LANES, 8)
-    params = pltpu.CompilerParams(vmem_limit_bytes=48 * MIB)
-
-    turned, packet = pl.pallas_call(
-        prepare_kernel,
+    parts = LANES // run_count
+    first_row = dim // parts
+    packet_rows = round_up(first_row + term_count // LANES, 8)
+
+    turned, packets = pl.pallas_call(
+        functools.partial(prepare_kernel, parts),
         out_shape=(
             jax.ShapeDtypeStruct((modes, term_count), jnp.bfloat16),
-            jax.ShapeDtypeStruct((packet_rows, LANES), jnp.float32),
+            jax.ShapeDtypeStruct((devices, packet_rows, LANES), jnp.float32),
         ),
-        compiler_params=params,
+        compiler_params=params(16),
         name="prepare",
     )(correlations, run_inputs.T)
-    packets = lax.all_gather(packet, "runs", axis=0, tiled=False)
+    packets = lax.all_to_all(packets, "runs", 0, 0, tiled=False)
     blocks = lax.all_to_all(
         turned.reshape(devices, own_modes, term_count), "runs", 0, 0, tiled=False
     )
@@ -214,18 +285,22 @@
         ],
         out_specs=pl.BlockSpec((total_runs, tile), lambda i: (0, i)),
         out_shape=jax.ShapeDtypeStruct((total_runs, terms), jnp.bfloat16),
-        scratch_shapes=[pltpu.VMEM((total_runs, 2 * half), jnp.bfloat16)],
-        compiler_params=params,
+        scratch_shapes=[
+            pltpu.VMEM((total_runs, 2 * half), jnp.bfloat16),
+            pltpu.VMEM((slots, 2 * half, tile), jnp.bfloat16),
+        ],
+        compiler_params=params(16),
         name="design",
     )(packets, term_codes.T)
 
     summed, scale = pl.pallas_call(
-        functools.partial(fit_kernel, dim, float(total_runs)),
+        functools.partial(fit_kernel, first_row, float(total_runs)),
         out_shape=(
             jax.ShapeDtypeStruct((devices, own_modes, term_count), jnp.bfloat16),
             jax.ShapeDtypeStruct((8, terms), jnp.float32),
         ),
-        compiler_params=params,
+        scratch_shapes=[pltpu.VMEM((own_modes, terms), jnp.bfloat16)],
+        compiler_params=params(20),
         name="fit",
     )(packets, weight_levels[None, :], blocks, design)
     own_scale = lax.dynamic_slice_in_dim(scale, offset, term_count, 1)
@@ -233,7 +308,7 @@
         modes, term_count
     )
 
-    block = min(512, slab_cells)
+    block = math.gcd(512, slab_cells)
     ordered = pl.pallas_call(
         reorder_kernel,
         grid=(slab_cells // block,),
@@ -241,34 +316,34 @@
             pl.BlockSpec((1, block), lambda i: (0, i)),
             pl.BlockSpec((cells, modes), lambda i: (0, 0)),
         ],
-        out_specs=pl.BlockSpec((block, modes), lambda i: (i, 0)),
-        out_shape=jax.ShapeDtypeStruct((slab_cells, modes), jnp.bfloat16),
-        compiler_params=params,
+        out_specs=pl.BlockSpec((modes, block), lambda i: (0, i)),
+        out_shape=jax.ShapeDtypeStruct((modes, slab_cells), jnp.bfloat16),
+        scratch_shapes=[pltpu.VMEM((modes, cells), jnp.bfloat16)],
+        compiler_params=params(24),
         name="reorder",
     )(cell_map[None, :], slab_modes)
 
-    coefficients, half_width = pl.pallas_call(
+    vmem = pl.BlockSpec(memory_space=pltpu.VMEM)
+    anywhere = pl.BlockSpec(memory_space=pl.ANY)
+    return pl.pallas_call(
         finish_kernel,
+        in_specs=[vmem, vmem, vmem, vmem],
+        out_specs=(anywhere, anywhere),
         out_shape=(
             jax.ShapeDtypeStruct((term_count, modes), jnp.float32),
-            jax.ShapeDtypeStruct((term_count, modes), jnp.bfloat16),
+            jax.ShapeDtypeStruct((term_count, slab_cells), jnp.bfloat16),
         ),
-        compiler_params=params,
+        scratch_shapes=[
+            pltpu.VMEM((modes, term_count), jnp.float32),
+            pltpu.VMEM((term_count, modes), jnp.float32),
+            pltpu.VMEM((term_count, modes), jnp.bfloat16),
+            pltpu.VMEM((slab_cells // block, term_count, block), jnp.bfloat16),
+            pltpu.SemaphoreType.DMA,
+            pltpu.SemaphoreType.DMA((slab_cells // block,)),
+        ],
+        compiler_params=params(20),
         name="finish",
-    )(returned, turned, own_scale)
-    lifted = pl.pallas_call(
-        lift_kernel,
-        grid=(slab_cells // block,),
-        in_specs=[
-            pl.BlockSpec((term_count, modes), lambda i: (0, 0)),
-            pl.BlockSpec((block, modes), lambda i: (i, 0)),
-        ],
-        out_specs=pl.BlockSpec((term_count, block), lambda i: (0, i)),
-        out_shape=jax.ShapeDtypeStruct((term_count, slab_cells), jnp.bfloat16),
-        compiler_params=params,
-        name="lift",
-    )(half_width, ordered)
-    return (coefficients, lifted)
+    )(returned, turned, own_scale, ordered)
 
 
 def hermite_table(points):
@@ -352,6 +427,9 @@
         and term_count % LANES == 0
         and LANES % run_count == 0
         and devices % (LANES // run_count) == 0
+        and run_inputs.shape[1] % (LANES // run_count) == 0
+        and slab_modes.shape[0] % LANES == 0
+        and cell_map.shape[0] % LANES == 0
     )
     plan = split_by_modes if whole_tiles else split_by_runs
     return plan(

time: 86.3 us -> 75.9 us (0.88)
  blocking collectives: 25.9 us -> 15.1 us
  local copies, waits for them, and re-layouts: 6.72 us -> 15.5 us
  Pallas kernels: 40.7 us -> 34.3 us
  starting transfers between devices: 10.9 us -> 9.54 us
    all_gather x1 -> x0, blocking collectives: 25.9 us -> none  [split_by_modes(): packets = lax.all_gather(packet, 'runs', axis=0, tiled=False)]
    all_to_all x0 -> x1, blocking collectives: none -> 15.1 us  [split_by_modes(): packets = lax.all_to_all(packets, 'runs', 0, 0, tiled=False)]
    unnamed x14 -> x20, local copies, waits for them, and re-layouts: 6.71 us -> 15.5 us
    pallas_call x4 -> x3, Pallas kernels: 15.1 us -> 9.66 us  [the longest x1 5.05 us: split_by_modes(): pl.pallas_call(functools.partial(fit_kernel, first_row, float(total_runs)...]
    all_to_all x1, starting transfers between devices: 7.36 us -> 3.57 us  [split_by_modes(): lax.all_to_all(turned.reshape(devices, own_modes, term_count), 'runs', 0,...]
    all_to_all x1, starting transfers between devices: 3.57 us -> 5.97 us  [split_by_modes(): lax.all_to_all(summed, 'runs', 0, 0, tiled=False).reshape(modes, term_count)]
  transfers between devices with their start and end apart: 2 -> 2, of which waited for: 1 -> 0; matrix products, arithmetic and copies ran while one was open for 0% -> 0% of each run, Pallas kernels for 30% -> 33%
where the time goes in v2:
time: 75.9 us; the launch traced here: 75.2 us
  Pallas kernels  34.3 us (45%)
  local copies, waits for them, and re-layouts  15.5 us (20%)
  blocking collectives  15.1 us (20%)
  starting transfers between devices  9.54 us (13%)
    unnamed x20, local copies, waits for them, and re-layouts  15.5 us
    all_to_all x1, blocking collectives, split_by_modes(): packets = lax.all_to_all(packets, 'runs', 0, 0, tiled=False)  15.1 us
    pallas_call x1, Pallas kernels, split_by_modes(): pl.pallas_call(functools.partial(design_kernel, dim, run_count), grid=(te...  13.7 us
    pallas_call x1, Pallas kernels, split_by_modes(): pl.pallas_call(reorder_kernel, grid=(slab_cells // block,), in_specs=[pl....  11 us
    all_to_all x1, starting transfers between devices, split_by_modes(): lax.all_to_all(summed, 'runs', 0, 0, tiled=False).reshape(modes, term_count)  5.97 us
    pallas_call x1, Pallas kernels, split_by_modes(): pl.pallas_call(functools.partial(fit_kernel, first_row, float(total_runs)...  5.05 us
    all_to_all x1, starting transfers between devices, split_by_modes(): lax.all_to_all(turned.reshape(devices, own_modes, term_count), 'runs', 0,...  3.57 us
    pallas_call x1, Pallas kernels, split_by_modes(): pl.pallas_call(finish_kernel, in_specs=[vmem, vmem, vmem, vmem], out_spec...  3.56 us
  transfers between devices with their start and end apart: 2, of which 0 were waited for; matrix products, arithmetic and copies ran while one was open for 0% of the time, Pallas kernels for 33%

profile of v2, /device:TPU:0, one launch (start us, length us, event | category | flops | bytes accessed | tf_op | source)
XLA Modules:
  0.0 75.2 jit_solution(15438114355810744347)
XLA Ops:
  0.6 0.0 copy-start.5
  0.6 1.0 %copy-done.5 = bf16[256,1024]{1,0:T(8,128)(2,1)S(1)} copy-done((bf16[256,1024]{1,0:T(8,128)(2,1)S(1)}, bf16[256,1024]{1,0:T(8,128)(2,1)}, u32[]{:S(2)}) %copy-start.5) | copy-done | bytes 524312
  1.7 0.0 copy-start.8
  1.7 0.7 copy-done.8
  2.4 1.1 %prepare.1 = (bf16[1024,256]{1,0:T(8,128)(2,1)}, f32[16,16,128]{2,1,0:T(8,128)S(1)}) custom-call(bf16[256,1024]{1,0:T(8,128)(2,1)S(1)} %copy-done.5, f32[24,64]{1,0:T(8,128)S(1)} %bitcast.9), custom_call_target="tpu_custom_call" | custom-call | tf_op jit(solution)/shard_map/prepare/pallas_call | solution.py:263
  3.4 15.1 %all_to_all.15.packets_ref = f32[16,16,128]{2,1,0:T(8,128)S(1)} all-to-all(f32[16,16,128]{2,1,0:T(8,128)S(1)} %get-tuple-element.6), channel_id=1, replica_groups=mesh['cases'=2,'runs'=16] {'runs'}, dimensions={0} | all-to-all | bytes 262144 | tf_op jit(solution)/shard_map/all_to_all | solution.py:272
  18.5 3.6 %all-to-all-start.1 = ((bf16[16,64,256]{2,1,0:T(8,128)(2,1)}), bf16[16,64,256]{2,1,0:T(8,128)(2,1)S(1)}, u32[]{:S(2)}, u32[]{:S(2)}) async-start(bf16[16,64,256]{2,1,0:T(8,128)(2,1)} %bitcast.2), calls=%async_computation.1 | async-start | bytes 1048576 | tf_op jit(solution)/shard_map/all_to_all | solution.py:273
  22.1 0.0 copy-start.6
  22.1 0.8 %copy-done.6 = s32[4096,4]{0,1:T(4,128)S(1)} copy-done((s32[4096,4]{0,1:T(4,128)S(1)}, s32[4096,4]{0,1:T(4,128)}, u32[]{:S(2)}) %copy-start.6) | copy-done | bytes 65560
  22.9 0.0 copy-start.7
  22.9 13.7 %design.1.design_ref = bf16[1024,4096]{1,0:T(8,128)(2,1)S(1)} custom-call(f32[16,16,128]{2,1,0:T(8,128)S(1)} %all_to_all.15.packets_ref, s32[4,4096]{1,0:T(4,128)S(1)} %bitcast.7), custom_call_target="tpu_custom_call" | custom-call | tf_op jit(solution)/shard_map/design/pallas_call | solution.py:279
  36.7 0.0 copy-start
  36.7 3.2 %copy-done = bf16[1024,4096]{1,0:T(8,128)(2,1)} copy-done((bf16[1024,4096]{1,0:T(8,128)(2,1)}, bf16[1024,4096]{1,0:T(8,128)(2,1)S(1)}, u32[]{:S(2)}) %copy-start) | copy-done | bytes 8388632
  39.9 0.0 all-to-all-done.1.corr_ref
  39.9 0.0 copy-done.7
  39.9 0.0 copy-start.1
  39.9 3.4 %copy-done.1 = bf16[1024,4096]{1,0:T(8,128)(2,1)S(1)} copy-done((bf16[1024,4096]{1,0:T(8,128)(2,1)S(1)}, bf16[1024,4096]{1,0:T(8,128)(2,1)}, u32[]{:S(2)}) %copy-start.1) | copy-done | bytes 8388632
  43.3 0.0 copy-start.9
  43.3 5.0 %fit.1 = (bf16[16,64,256]{2,1,0:T(8,128)(2,1)}, f32[8,4096]{1,0:T(8,128)S(1)}) custom-call(f32[16,16,128]{2,1,0:T(8,128)S(1)} %all_to_all.15.packets_ref, s32[1,4096]{1,0:T(1,128)S(1)} %bitcast.8, bf16[16,64,256]{2,1,0:T(8,128)(2,1)S(1)} %all-to-all-done.1.corr_ref, bf16[1024,4096]{1,0:T(8,128)(2,1)S(1)} %copy-done.1), custom_call_target="tpu_custom_call" | custom-call | tf_op jit(solution)/shard_map/fit/pallas_call | solution.py:296
  48.3 6.0 %all-to-all-start.2 = ((bf16[16,64,256]{2,1,0:T(8,128)(2,1)}), bf16[16,64,256]{2,1,0:T(8,128)(2,1)S(1)}, u32[]{:S(2)}, u32[]{:S(2)}) async-start(bf16[16,64,256]{2,1,0:T(8,128)(2,1)} %get-tuple-element.8), calls=%async_computation.2 | async-start | bytes 1048576 | tf_op jit(solution)/shard_map/all_to_all | solution.py:307
  54.3 0.0 copy-done.9
  54.3 0.0 copy-start.4
  54.3 2.2 %copy-done.4 = bf16[2048,1024]{1,0:T(8,128)(2,1)S(1)} copy-done((bf16[2048,1024]{1,0:T(8,128)(2,1)S(1)}, bf16[2048,1024]{1,0:T(8,128)(2,1)}, u32[]{:S(2)}) %copy-start.4) | copy-done | bytes 4194328
  56.5 11.0 %reorder.1.modes_ref = bf16[1024,2048]{1,0:T(8,128)(2,1)S(1)} custom-call(s32[1,2048]{1,0:T(1,128)S(1)} %bitcast.10, bf16[2048,1024]{1,0:T(8,128)(2,1)S(1)} %copy-done.4), custom_call_target="tpu_custom_call" | custom-call | tf_op jit(solution)/shard_map/reorder/pallas_call | solution.py:312
  67.5 0.0 copy-start.2
  67.5 1.9 %copy-done.2 = bf16[1024,2048]{1,0:T(8,128)(2,1)} copy-done((bf16[1024,2048]{1,0:T(8,128)(2,1)}, bf16[1024,2048]{1,0:T(8,128)(2,1)S(1)}, u32[]{:S(2)}) %copy-start.2) | copy-done | bytes 4194328
  69.4 0.0 all-to-all-done.2
  69.4 0.0 copy-start.3
  69.4 2.2 %copy-done.3 = bf16[1024,2048]{1,0:T(8,128)(2,1)S(1)} copy-done((bf16[1024,2048]{1,0:T(8,128)(2,1)S(1)}, bf16[1024,2048]{1,0:T(8,128)(2,1)}, u32[]{:S(2)}) %copy-start.3) | copy-done | bytes 4194328
  71.6 3.6 %finish.1 = (f32[256,1024]{1,0:T(8,128)}, bf16[256,2048]{1,0:T(8,128)(2,1)}) custom-call(bf16[1024,256]{1,0:T(8,128)(2,1)S(1)} %bitcast.6, bf16[1024,256]{1,0:T(8,128)(2,1)} %get-tuple-element.7.corr_ref, f32[8,256]{1,0:T(8,128)S(1)} %constant_dynamic-slice_fusion.scale_ref, bf16[1024,2048]{1,0:T(8,128)(2,1)S(1)} %copy-done.3), custom_call_target="tpu_custom_call" | custom-call | tf_op jit(solution)/shard_map/finish/pallas_call | solution.py:328
  (1 shorter events, 0.0 us)
Async XLA Ops:
  0.6 1.0 %copy-start.5 = (bf16[256,1024]{1,0:T(8,128)(2,1)S(1)}, bf16[256,1024]{1,0:T(8,128)(2,1)}, u32[]{:S(2)}) copy-start(bf16[256,1024]{1,0:T(8,128)(2,1)} %corr_ref.1) | copy-start | bytes 1572868
  1.7 0.7 copy-start.8
  18.5 21.4 %all-to-all-start.1 = ((bf16[16,64,256]{2,1,0:T(8,128)(2,1)}), bf16[16,64,256]{2,1,0:T(8,128)(2,1)S(1)}, u32[]{:S(2)}, u32[]{:S(2)}) async-start(bf16[16,64,256]{2,1,0:T(8,128)(2,1)} %bitcast.2), calls=%async_computation.1 | async-start | bytes 1048576 | tf_op jit(solution)/shard_map/all_to_all | solution.py:273
  22.1 0.8 %copy-start.6 = (s32[4096,4]{0,1:T(4,128)S(1)}, s32[4096,4]{0,1:T(4,128)}, u32[]{:S(2)}) copy-start(s32[4096,4]{0,1:T(4,128)} %param.7) | copy-start | bytes 196612
  22.9 17.0 %copy-start.7 = (s32[4096]{0:T(1024)S(1)}, s32[4096]{0:T(1024)}, u32[]{:S(2)}) copy-start(s32[4096]{0:T(1024)} %param.8) | copy-start | bytes 49156
  36.7 3.2 %copy-start = (bf16[1024,4096]{1,0:T(8,128)(2,1)}, bf16[1024,4096]{1,0:T(8,128)(2,1)S(1)}, u32[]{:S(2)}) copy-start(bf16[1024,4096]{1,0:T(8,128)(2,1)S(1)} %design.1.design_ref) | copy-start | bytes 25165828
  39.9 3.4 %copy-start.1 = (bf16[1024,4096]{1,0:T(8,128)(2,1)S(1)}, bf16[1024,4096]{1,0:T(8,128)(2,1)}, u32[]{:S(2)}) copy-start(bf16[1024,4096]{1,0:T(8,128)(2,1)} %copy-done) | copy-start | bytes 25165828
  43.3 11.0 %copy-start.9 = (s32[2048]{0:T(1024)S(1)}, s32[2048]{0:T(1024)}, u32[]{:S(2)}) copy-start(s32[2048]{0:T(1024)} %param.11) | copy-start | bytes 24580
  48.3 21.1 %all-to-all-start.2 = ((bf16[16,64,256]{2,1,0:T(8,128)(2,1)}), bf16[16,64,256]{2,1,0:T(8,128)(2,1)S(1)}, u32[]{:S(2)}, u32[]{:S(2)}) async-start(bf16[16,64,256]{2,1,0:T(8,128)(2,1)} %get-tuple-element.8), calls=%async_computation.2 | async-start | bytes 1048576 | tf_op jit(solution)/shard_map/all_to_all | solution.py:307
  54.3 2.2 %copy-start.4 = (bf16[2048,1024]{1,0:T(8,128)(2,1)S(1)}, bf16[2048,1024]{1,0:T(8,128)(2,1)}, u32[]{:S(2)}) copy-start(bf16[2048,1024]{1,0:T(8,128)(2,1)} %slab_ref.1) | copy-start | bytes 12582916
  67.5 2.0 %copy-start.2 = (bf16[1024,2048]{1,0:T(8,128)(2,1)}, bf16[1024,2048]{1,0:T(8,128)(2,1)S(1)}, u32[]{:S(2)}) copy-start(bf16[1024,2048]{1,0:T(8,128)(2,1)S(1)} %reorder.1.modes_ref) | copy-start | bytes 12582916
  69.4 2.2 %copy-start.3 = (bf16[1024,2048]{1,0:T(8,128)(2,1)S(1)}, bf16[1024,2048]{1,0:T(8,128)(2,1)}, u32[]{:S(2)}) copy-start(bf16[1024,2048]{1,0:T(8,128)(2,1)} %copy-done.2) | copy-start | bytes 12582916

commit v3 on v2

--- a/solution.py
+++ b/solution.py
@@ -60,9 +60,11 @@
     )
 
 
-def design_kernel(dim, run_count, packets_ref, codes_ref, design_ref, table, chosen):
+def design_kernel(
+    dim, run_count, packets_ref, codes_ref, design_ref, exact, table, chosen
+):
     devices = packets_ref.shape[0]
-    half = table.shape[1] // 2
+    half = exact.shape[1]
     parts = LANES // run_count
     rows = dim // parts
 
@@ -97,6 +99,7 @@
             high = columns.astype(jnp.bfloat16)
             low = (columns - high.astype(jnp.float32)).astype(jnp.bfloat16)
             block = slice(group * LANES, (group + 1) * LANES)
+            exact[block, :] = columns
             table[block, 0:half] = high
             table[block, half : 2 * half] = low
 
@@ -104,7 +107,8 @@
     spots = (codes % DEGREES) * dim + codes // DEGREES
     slots, terms = codes.shape
     row = lax.broadcasted_iota(jnp.int32, (half, terms), 0)
-    for slot in range(slots):
+    matmuls = chosen.shape[0]
+    for slot in range(matmuls):
         picked = jnp.where(row == spots[slot : slot + 1, :], 1.0, 0.0).astype(
             jnp.bfloat16
         )
@@ -112,13 +116,20 @@
         chosen[slot, half : 2 * half, :] = picked
     for start in range(0, table.shape[0], LANES):
         block = slice(start, start + LANES)
+        rows = exact[block, :]
         product = None
-        for slot in range(slots):
+        for slot in range(matmuls):
             factor = jnp.dot(
                 table[block, :], chosen[slot], preferred_element_type=jnp.float32
             )
             product = factor if product is None else product * factor
-        design_ref[block, :] = product.astype(jnp.bfloat16)
+        for part in range(0, terms, half):
+            lanes = slice(part, part + half)
+            factor = product[:, lanes]
+            for slot in range(matmuls, slots):
+                spot = jnp.broadcast_to(spots[slot : slot + 1, lanes], rows.shape)
+                factor = factor * jnp.take_along_axis(rows, spot, axis=1)
+            design_ref[block, lanes] = factor.astype(jnp.bfloat16)
 
 
 def penalty_rows(first_row, term_count, packets_ref, levels_ref):
@@ -149,8 +160,18 @@
     summed_ref,
     scale_ref,
     first_ref,
+    held,
+    sems,
 ):
     devices, _, term_count = corr_ref.shape
+    width = held.shape[1] // sems.shape[0]
+    copies = []
+    for i in range(sems.shape[0]):
+        chunk = slice(i * width, (i + 1) * width)
+        copies.append(
+            pltpu.make_async_copy(design_ref.at[:, chunk], held.at[:, chunk], sems.at[i])
+        )
+        copies[-1].start()
     squares, weights, penalty = penalty_rows(
         first_row, term_count, packets_ref, levels_ref
     )
@@ -162,17 +183,21 @@
         terms = slice(i * term_count, (i + 1) * term_count)
         first = STEP * corr_ref[i].astype(jnp.float32) * factor[:, terms]
         first_ref[:, terms] = first.astype(jnp.bfloat16)
-    fitted = lax.dot_general(
-        first_ref[...],
-        design_ref[...],
-        (((1,), (1,)), ((), ())),
-        preferred_element_type=jnp.float32,
-    ).astype(jnp.bfloat16)
+    fitted = None
+    for i in range(sems.shape[0]):
+        chunk = slice(i * width, (i + 1) * width)
+        copies[i].wait()
+        part = lax.dot_general(
+            first_ref[:, chunk],
+            held[:, chunk],
+            (((1,), (1,)), ((), ())),
+            preferred_element_type=jnp.float32,
+        )
+        fitted = part if fitted is None else fitted + part
+    fitted = fitted.astype(jnp.bfloat16)
     for i in range(devices):
         terms = slice(i * term_count, (i + 1) * term_count)
-        summed = jnp.dot(
-            fitted, design_ref[:, terms], preferred_element_type=jnp.float32
-        )
+        summed = jnp.dot(fitted, held[:, terms], preferred_element_type=jnp.float32)
         summed_ref[i] = (summed / total_runs).astype(jnp.bfloat16)
 
 
@@ -203,9 +228,13 @@
     values,
     half,
     lifted,
+    held,
+    held_sem,
     out_sem,
     lifted_sem,
 ):
+    load = pltpu.make_async_copy(modes_ref, held, held_sem)
+    load.start()
     modes, terms = corr_ref.shape
     squares = jnp.zeros((1, terms), jnp.float32)
     for start in range(0, modes, LANES):
@@ -225,10 +254,11 @@
     copies = [pltpu.make_async_copy(values, out_ref, out_sem)]
     copies[0].start()
     width = lifted.shape[2]
+    load.wait()
     for i in range(lifted.shape[0]):
         block = slice(i * width, (i + 1) * width)
         lifted[i] = jnp.dot(
-            half[...], modes_ref[:, block], preferred_element_type=jnp.float32
+            half[...], held[:, block], preferred_element_type=jnp.float32
         ).astype(jnp.bfloat16)
         copies.append(
             pltpu.make_async_copy(
@@ -238,6 +268,10 @@
         copies[-1].start()
     for copy in copies:
         copy.wait()
+
+
+def in_hbm(array):
+    return pltpu.with_memory_space_constraint(array, pltpu.HBM)
 
 
 def params(limit):
@@ -268,7 +302,7 @@
         ),
         compiler_params=params(16),
         name="prepare",
-    )(correlations, run_inputs.T)
+    )(in_hbm(correlations), in_hbm(run_inputs.T))
     packets = lax.all_to_all(packets, "runs", 0, 0, tiled=False)
     blocks = lax.all_to_all(
         turned.reshape(devices, own_modes, term_count), "runs", 0, 0, tiled=False
@@ -284,25 +318,34 @@
             pl.BlockSpec((slots, tile), lambda i: (0, i)),
         ],
         out_specs=pl.BlockSpec((total_runs, tile), lambda i: (0, i)),
-        out_shape=jax.ShapeDtypeStruct((total_runs, terms), jnp.bfloat16),
+        out_shape=pltpu.HBM((total_runs, terms), jnp.bfloat16),
         scratch_shapes=[
+            pltpu.VMEM((total_runs, half), jnp.float32),
             pltpu.VMEM((total_runs, 2 * half), jnp.bfloat16),
-            pltpu.VMEM((slots, 2 * half, tile), jnp.bfloat16),
+            pltpu.VMEM((slots - slots // 2, 2 * half, tile), jnp.bfloat16),
         ],
         compiler_params=params(16),
         name="design",
-    )(packets, term_codes.T)
-
+    )(packets, in_hbm(term_codes.T))
+
+    vmem = pl.BlockSpec(memory_space=pltpu.VMEM)
+    anywhere = pl.BlockSpec(memory_space=pl.ANY)
+    chunks = math.gcd(8, terms // LANES)
     summed, scale = pl.pallas_call(
         functools.partial(fit_kernel, first_row, float(total_runs)),
+        in_specs=[vmem, vmem, vmem, anywhere],
         out_shape=(
             jax.ShapeDtypeStruct((devices, own_modes, term_count), jnp.bfloat16),
             jax.ShapeDtypeStruct((8, terms), jnp.float32),
         ),
-        scratch_shapes=[pltpu.VMEM((own_modes, terms), jnp.bfloat16)],
-        compiler_params=params(20),
+        scratch_shapes=[
+            pltpu.VMEM((own_modes, terms), jnp.bfloat16),
+            pltpu.VMEM((total_runs, terms), jnp.bfloat16),
+            pltpu.SemaphoreType.DMA((chunks,)),
+        ],
+        compiler_params=params(24),
         name="fit",
-    )(packets, weight_levels[None, :], blocks, design)
+    )(packets, weight_levels[None, :], blocks, in_hbm(design))
     own_scale = lax.dynamic_slice_in_dim(scale, offset, term_count, 1)
     returned = lax.all_to_all(summed, "runs", 0, 0, tiled=False).reshape(
         modes, term_count
@@ -317,17 +360,15 @@
             pl.BlockSpec((cells, modes), lambda i: (0, 0)),
         ],
         out_specs=pl.BlockSpec((modes, block), lambda i: (0, i)),
-        out_shape=jax.ShapeDtypeStruct((modes, slab_cells), jnp.bfloat16),
+        out_shape=pltpu.HBM((modes, slab_cells), jnp.bfloat16),
         scratch_shapes=[pltpu.VMEM((modes, cells), jnp.bfloat16)],
         compiler_params=params(24),
         name="reorder",
-    )(cell_map[None, :], slab_modes)
-
-    vmem = pl.BlockSpec(memory_space=pltpu.VMEM)
-    anywhere = pl.BlockSpec(memory_space=pl.ANY)
+    )(cell_map[None, :], in_hbm(slab_modes))
+
     return pl.pallas_call(
         finish_kernel,
-        in_specs=[vmem, vmem, vmem, vmem],
+        in_specs=[vmem, vmem, vmem, anywhere],
         out_specs=(anywhere, anywhere),
         out_shape=(
             jax.ShapeDtypeStruct((term_count, modes), jnp.float32),
@@ -338,12 +379,14 @@
             pltpu.VMEM((term_count, modes), jnp.float32),
             pltpu.VMEM((term_count, modes), jnp.bfloat16),
             pltpu.VMEM((slab_cells // block, term_count, block), jnp.bfloat16),
+            pltpu.VMEM((modes, slab_cells), jnp.bfloat16),
+            pltpu.SemaphoreType.DMA,
             pltpu.SemaphoreType.DMA,
             pltpu.SemaphoreType.DMA((slab_cells // block,)),
         ],
         compiler_params=params(20),
         name="finish",
-    )(returned, turned, own_scale, ordered)
+    )(returned, turned, own_scale, in_hbm(ordered))
 
 
 def hermite_table(points):
@@ -424,6 +467,7 @@
     term_count, modes = correlations.shape
     whole_tiles = (
         modes % (16 * devices) == 0
+        and DEGREES * run_inputs.shape[1] <= LANES
         and term_count % LANES == 0
         and LANES % run_count == 0
         and devices % (LANES // run_count) == 0

time: 75.9 us -> 69.8 us (0.920)
  local copies, waits for them, and re-layouts: 15.5 us -> 0.01 us
  Pallas kernels: 34.3 us -> 43.3 us
    unnamed x20 -> x4, local copies, waits for them, and re-layouts: 15.5 us -> 0.01 us
    pallas_call x1, Pallas kernels: 11 us -> 14 us  [split_by_modes(): pl.pallas_call(reorder_kernel, grid=(slab_cells // block,), in_specs=[pl....]
    pallas_call x1, Pallas kernels: 3.56 us -> 5.97 us  [split_by_modes(): pl.pallas_call(finish_kernel, in_specs=[vmem, vmem, vmem, anywhere], out_...]
    pallas_call x1, Pallas kernels: 5.05 us -> 6.67 us  [split_by_modes(): pl.pallas_call(functools.partial(fit_kernel, first_row, float(total_runs)...]
    pallas_call x1, Pallas kernels: 1.06 us -> 2.1 us  [split_by_modes(): pl.pallas_call(functools.partial(prepare_kernel, parts), out_shape=(jax.S...]
    pallas_call x1, Pallas kernels: 13.7 us -> 14.6 us  [split_by_modes(): pl.pallas_call(functools.partial(design_kernel, dim, run_count), grid=(te...]
  transfers between devices with their start and end apart: 2 -> 2, of which waited for: 0 -> 1; matrix products, arithmetic and copies ran while one was open for 0% -> 0% of each run, Pallas kernels for 33% -> 41%
where the time goes in v3:
time: 69.8 us; the launch traced here: 69.1 us
  Pallas kernels  43.3 us (62%)
  blocking collectives  15.1 us (22%)
  starting transfers between devices  9.55 us (14%)
    all_to_all x1, blocking collectives, split_by_modes(): packets = lax.all_to_all(packets, 'runs', 0, 0, tiled=False)  15.1 us
    pallas_call x1, Pallas kernels, split_by_modes(): pl.pallas_call(functools.partial(design_kernel, dim, run_count), grid=(te...  14.6 us
    pallas_call x1, Pallas kernels, split_by_modes(): pl.pallas_call(reorder_kernel, grid=(slab_cells // block,), in_specs=[pl....  14 us
    pallas_call x1, Pallas kernels, split_by_modes(): pl.pallas_call(functools.partial(fit_kernel, first_row, float(total_runs)...  6.67 us
    all_to_all x1, starting transfers between devices, split_by_modes(): lax.all_to_all(summed, 'runs', 0, 0, tiled=False).reshape(modes, term_count)  5.98 us
    pallas_call x1, Pallas kernels, split_by_modes(): pl.pallas_call(finish_kernel, in_specs=[vmem, vmem, vmem, anywhere], out_...  5.97 us
    all_to_all x1, starting transfers between devices, split_by_modes(): lax.all_to_all(turned.reshape(devices, own_modes, term_count), 'runs', 0,...  3.57 us
    pallas_call x1, Pallas kernels, split_by_modes(): pl.pallas_call(functools.partial(prepare_kernel, parts), out_shape=(jax.S...  2.1 us
  transfers between devices with their start and end apart: 2, of which 1 were waited for; matrix products, arithmetic and copies ran while one was open for 0% of the time, Pallas kernels for 41%

profile of v3, /device:TPU:0, one launch (start us, length us, event | category | flops | bytes accessed | tf_op | source)
XLA Modules:
  0.0 69.1 jit_solution(14673282482620585747)
XLA Ops:
  0.6 2.1 %prepare.1 = (bf16[1024,256]{1,0:T(8,128)(2,1)}, f32[16,16,128]{2,1,0:T(8,128)S(1)}) custom-call(bf16[256,1024]{1,0:T(8,128)(2,1)} %corr_ref.1, f32[24,64]{1,0:T(8,128)} %bitcast.10), custom_call_target="tpu_custom_call" | custom-call | tf_op jit(solution)/shard_map/prepare/pallas_call | solution.py:297
  2.7 15.1 %all_to_all.15.packets_ref = f32[16,16,128]{2,1,0:T(8,128)S(1)} all-to-all(f32[16,16,128]{2,1,0:T(8,128)S(1)} %get-tuple-element.6), channel_id=1, replica_groups=mesh['cases'=2,'runs'=16] {'runs'}, dimensions={0} | all-to-all | bytes 262144 | tf_op jit(solution)/shard_map/all_to_all | solution.py:306
  17.8 3.6 %all-to-all-start.1 = ((bf16[16,64,256]{2,1,0:T(8,128)(2,1)}), bf16[16,64,256]{2,1,0:T(8,128)(2,1)S(1)}, u32[]{:S(2)}, u32[]{:S(2)}) async-start(bf16[16,64,256]{2,1,0:T(8,128)(2,1)} %bitcast.2), calls=%async_computation.1 | async-start | bytes 1048576 | tf_op jit(solution)/shard_map/all_to_all | solution.py:307
  21.4 0.0 copy-start
  21.4 14.6 %design.1.design_ref = bf16[1024,4096]{1,0:T(8,128)(2,1)} custom-call(f32[16,16,128]{2,1,0:T(8,128)S(1)} %all_to_all.15.packets_ref, s32[4,4096]{1,0:T(4,128)} %bitcast.9), custom_call_target="tpu_custom_call" | custom-call | tf_op jit(solution)/shard_map/design/pallas_call | solution.py:313
  36.0 0.0 all-to-all-done.1.corr_ref
  36.0 0.0 copy-done
  36.0 0.0 copy-start.1
  36.0 6.7 %fit.1 = (bf16[16,64,256]{2,1,0:T(8,128)(2,1)}, f32[8,4096]{1,0:T(8,128)S(1)}) custom-call(f32[16,16,128]{2,1,0:T(8,128)S(1)} %all_to_all.15.packets_ref, s32[1,4096]{1,0:T(1,128)S(1)} %bitcast.7, bf16[16,64,256]{2,1,0:T(8,128)(2,1)S(1)} %all-to-all-done.1.corr_ref, bf16[1024,4096]{1,0:T(8,128)(2,1)} %design.1.design_ref), custom_call_target="tpu_custom_call" | custom-call | tf_op jit(solution)/shard_map/fit/pallas_call | solution.py:334
  42.7 6.0 %all-to-all-start.2 = ((bf16[16,64,256]{2,1,0:T(8,128)(2,1)}), bf16[16,64,256]{2,1,0:T(8,128)(2,1)S(1)}, u32[]{:S(2)}, u32[]{:S(2)}) async-start(bf16[16,64,256]{2,1,0:T(8,128)(2,1)} %get-tuple-element.8), calls=%async_computation.2 | async-start | bytes 1048576 | tf_op jit(solution)/shard_map/all_to_all | solution.py:350
  48.7 0.0 copy-done.1
  48.7 14.0 %reorder.1.modes_ref = bf16[1024,2048]{1,0:T(8,128)(2,1)} custom-call(s32[1,2048]{1,0:T(1,128)S(1)} %bitcast.8, bf16[2048,1024]{1,0:T(8,128)(2,1)} %slab_ref.1), custom_call_target="tpu_custom_call" | custom-call | tf_op jit(solution)/shard_map/reorder/pallas_call | solution.py:355
  62.7 0.5 all-to-all-done.2
  63.1 6.0 %finish.1 = (f32[256,1024]{1,0:T(8,128)}, bf16[256,2048]{1,0:T(8,128)(2,1)}) custom-call(bf16[1024,256]{1,0:T(8,128)(2,1)S(1)} %bitcast.6, bf16[1024,256]{1,0:T(8,128)(2,1)} %get-tuple-element.7.corr_ref, f32[8,256]{1,0:T(8,128)S(1)} %constant_dynamic-slice_fusion.scale_ref, bf16[1024,2048]{1,0:T(8,128)(2,1)} %reorder.1.modes_ref), custom_call_target="tpu_custom_call" | custom-call | tf_op jit(solution)/shard_map/finish/pallas_call | solution.py:369
  (1 shorter events, 0.0 us)
Async XLA Ops:
  17.8 18.2 %all-to-all-start.1 = ((bf16[16,64,256]{2,1,0:T(8,128)(2,1)}), bf16[16,64,256]{2,1,0:T(8,128)(2,1)S(1)}, u32[]{:S(2)}, u32[]{:S(2)}) async-start(bf16[16,64,256]{2,1,0:T(8,128)(2,1)} %bitcast.2), calls=%async_computation.1 | async-start | bytes 1048576 | tf_op jit(solution)/shard_map/all_to_all | solution.py:307
  21.4 14.6 %copy-start = (s32[4096]{0:T(1024)S(1)}, s32[4096]{0:T(1024)}, u32[]{:S(2)}) copy-start(s32[4096]{0:T(1024)} %param.8) | copy-start | bytes 49156
  36.0 12.7 %copy-start.1 = (s32[2048]{0:T(1024)S(1)}, s32[2048]{0:T(1024)}, u32[]{:S(2)}) copy-start(s32[2048]{0:T(1024)} %param.11) | copy-start | bytes 24580
  42.7 20.5 %all-to-all-start.2 = ((bf16[16,64,256]{2,1,0:T(8,128)(2,1)}), bf16[16,64,256]{2,1,0:T(8,128)(2,1)S(1)}, u32[]{:S(2)}, u32[]{:S(2)}) async-start(bf16[16,64,256]{2,1,0:T(8,128)(2,1)} %get-tuple-element.8), calls=%async_computation.2 | async-start | bytes 1048576 | tf_op jit(solution)/shard_map/all_to_all | solution.py:350

commit v4 on v2

--- a/solution.py
+++ b/solution.py
@@ -23,7 +23,7 @@
     return -(-value // multiple) * multiple
 
 
-def prepare_kernel(parts, corr_ref, points_ref, turned_ref, packets_ref):
+def prepare_kernel(parts, me_ref, corr_ref, points_ref, turned_ref, packet_ref, *sent):
     turned = corr_ref[...].astype(jnp.float32).T
     turned_ref[...] = turned.astype(jnp.bfloat16)
     squares = jnp.sum(turned * turned, axis=0, keepdims=True)
@@ -39,11 +39,15 @@
         for part in range(squares.shape[1] // LANES)
     ]
     used = rows + len(pieces) - 1
-    if packets_ref.shape[1] > used:
-        pieces.append(jnp.zeros((packets_ref.shape[1] - used, LANES), jnp.float32))
-    packet = jnp.concatenate(pieces, axis=0)
-    for i in range(packets_ref.shape[0]):
-        packets_ref[i] = packet
+    if packet_ref.shape[0] > used:
+        pieces.append(jnp.zeros((packet_ref.shape[0] - used, LANES), jnp.float32))
+    packet_ref[...] = jnp.concatenate(pieces, axis=0)
+    for k, block_ref in enumerate(sent):
+        block_ref[...] = turned_ref[own_rows(me_ref, k, block_ref.shape[0]), :]
+
+
+def own_rows(me_ref, k, count):
+    return pl.ds(pl.multiple_of((me_ref[0] ^ k) * count, count), count)
 
 
 def hermite_columns(points):
@@ -60,23 +64,21 @@
     )
 
 
-def design_kernel(dim, run_count, packets_ref, codes_ref, design_ref, table, chosen):
-    devices = packets_ref.shape[0]
-    half = table.shape[1] // 2
+def design_kernel(dim, run_count, me_ref, codes_ref, *refs):
+    *packet_refs, design_ref, exact, table, chosen = refs
+    half = exact.shape[1]
     parts = LANES // run_count
     rows = dim // parts
 
     @pl.when(pl.program_id(0) == 0)
     def _():
-        for group in range(devices // parts):
+        for group in range(len(packet_refs) // parts):
             points = jnp.concatenate(
                 [
                     jnp.concatenate(
                         [
-                            packets_ref[
-                                group * parts + i,
-                                0:rows,
-                                part * run_count : (part + 1) * run_count,
+                            packet_refs[group * parts + i][
+                                0:rows, part * run_count : (part + 1) * run_count
                             ]
                             for i in range(parts)
                         ],
@@ -97,6 +99,7 @@
             high = columns.astype(jnp.bfloat16)
             low = (columns - high.astype(jnp.float32)).astype(jnp.bfloat16)
             block = slice(group * LANES, (group + 1) * LANES)
+            exact[block, :] = columns
             table[block, 0:half] = high
             table[block, half : 2 * half] = low
 
@@ -104,7 +107,8 @@
     spots = (codes % DEGREES) * dim + codes // DEGREES
     slots, terms = codes.shape
     row = lax.broadcasted_iota(jnp.int32, (half, terms), 0)
-    for slot in range(slots):
+    matmuls = chosen.shape[0]
+    for slot in range(matmuls):
         picked = jnp.where(row == spots[slot : slot + 1, :], 1.0, 0.0).astype(
             jnp.bfloat16
         )
@@ -112,55 +116,53 @@
         chosen[slot, half : 2 * half, :] = picked
     for start in range(0, table.shape[0], LANES):
         block = slice(start, start + LANES)
+        rows = exact[block, :]
         product = None
-        for slot in range(slots):
+        for slot in range(matmuls):
             factor = jnp.dot(
                 table[block, :], chosen[slot], preferred_element_type=jnp.float32
             )
             product = factor if product is None else product * factor
-        design_ref[block, :] = product.astype(jnp.bfloat16)
-
-
-def penalty_rows(first_row, term_count, packets_ref, levels_ref):
+        for part in range(0, terms, half):
+            lanes = slice(part, part + half)
+            factor = product[:, lanes]
+            for slot in range(matmuls, slots):
+                spot = jnp.broadcast_to(spots[slot : slot + 1, lanes], rows.shape)
+                factor = factor * jnp.take_along_axis(rows, spot, axis=1)
+            design_ref[block, lanes] = factor.astype(jnp.bfloat16)
+
+
+def shrink_factor(squares, limits):
+    return jnp.maximum(0.0, 1.0 - limits / jnp.sqrt(squares + EPSILON))
+
+
+def fit_kernel(first_row, total_runs, me_ref, levels_ref, design_ref, *refs):
+    devices = (len(refs) - 2) // 3
+    packet_refs, corr_refs = refs[:devices], refs[devices : 2 * devices]
+    summed_refs = refs[2 * devices : 3 * devices]
+    scale_ref, first_ref = refs[3 * devices :]
+    term_count = corr_refs[0].shape[1]
     squares = jnp.concatenate(
         [
-            packets_ref[i, first_row + part : first_row + part + 1, :]
-            for i in range(packets_ref.shape[0])
+            packet_ref[first_row + part : first_row + part + 1, :]
+            for packet_ref in packet_refs
             for part in range(term_count // LANES)
         ],
         axis=1,
     )
-    weights = jnp.exp2(levels_ref[...].astype(jnp.float32))
+    levels = jnp.concatenate(
+        [levels_ref[:, own_rows(me_ref, k, term_count)] for k in range(devices)],
+        axis=1,
+    )
+    weights = jnp.exp2(levels.astype(jnp.float32))
     ratio = jnp.max(jnp.sqrt(squares) / weights, axis=1, keepdims=True)
-    return squares, weights, LAMBDA_FRACTION * ratio
-
-
-def shrink_factor(squares, limits):
-    return jnp.maximum(0.0, 1.0 - limits / jnp.sqrt(squares + EPSILON))
-
-
-def fit_kernel(
-    first_row,
-    total_runs,
-    packets_ref,
-    levels_ref,
-    corr_ref,
-    design_ref,
-    summed_ref,
-    scale_ref,
-    first_ref,
-):
-    devices, _, term_count = corr_ref.shape
-    squares, weights, penalty = penalty_rows(
-        first_row, term_count, packets_ref, levels_ref
-    )
-    limits = STEP * penalty * weights
+    limits = STEP * (LAMBDA_FRACTION * ratio) * weights
     factor = shrink_factor(STEP * STEP * squares, limits)
-    scale_ref[0:1, :] = factor
-    scale_ref[1:2, :] = limits
-    for i in range(devices):
-        terms = slice(i * term_count, (i + 1) * term_count)
-        first = STEP * corr_ref[i].astype(jnp.float32) * factor[:, terms]
+    scale_ref[0:1, :] = factor[:, 0:term_count]
+    scale_ref[1:2, :] = limits[:, 0:term_count]
+    for k in range(devices):
+        terms = slice(k * term_count, (k + 1) * term_count)
+        first = STEP * corr_refs[k][...].astype(jnp.float32) * factor[:, terms]
         first_ref[:, terms] = first.astype(jnp.bfloat16)
     fitted = lax.dot_general(
         first_ref[...],
@@ -168,12 +170,12 @@
         (((1,), (1,)), ((), ())),
         preferred_element_type=jnp.float32,
     ).astype(jnp.bfloat16)
-    for i in range(devices):
-        terms = slice(i * term_count, (i + 1) * term_count)
+    for k in range(devices):
+        terms = slice(k * term_count, (k + 1) * term_count)
         summed = jnp.dot(
             fitted, design_ref[:, terms], preferred_element_type=jnp.float32
         )
-        summed_ref[i] = (summed / total_runs).astype(jnp.bfloat16)
+        summed_refs[k][...] = (summed / total_runs).astype(jnp.bfloat16)
 
 
 def reorder_kernel(map_ref, slab_ref, modes_ref, turned):
@@ -192,29 +194,18 @@
     ).astype(jnp.bfloat16)
 
 
-def finish_kernel(
-    summed_ref,
-    corr_ref,
-    scale_ref,
-    modes_ref,
-    out_ref,
-    lifted_ref,
-    moved,
-    values,
-    half,
-    lifted,
-    out_sem,
-    lifted_sem,
-):
+def finish_kernel(me_ref, corr_ref, scale_ref, modes_ref, *refs):
+    *summed_refs, out_ref, lifted_ref, moved, values, half, lifted, out_sem, lifted_sem = refs
     modes, terms = corr_ref.shape
+    count = summed_refs[0].shape[0]
     squares = jnp.zeros((1, terms), jnp.float32)
-    for start in range(0, modes, LANES):
-        block = slice(start, start + LANES)
-        corr = corr_ref[block, :].astype(jnp.float32)
+    for k, summed_ref in enumerate(summed_refs):
+        rows = own_rows(me_ref, k, count)
+        corr = corr_ref[rows, :].astype(jnp.float32)
         first = STEP * corr * scale_ref[0:1, :]
-        gradient = summed_ref[block, :].astype(jnp.float32) - corr
+        gradient = summed_ref[...].astype(jnp.float32) - corr
         step = first - STEP * gradient
-        moved[block, :] = step
+        moved[rows, :] = step
         squares = squares + jnp.sum(step * step, axis=0, keepdims=True)
     factor = shrink_factor(squares, scale_ref[1:2, :])
     for start in range(0, modes, LANES):
@@ -240,8 +231,21 @@
         copy.wait()
 
 
+def in_hbm(array):
+    return pltpu.with_memory_space_constraint(array, pltpu.HBM)
+
+
 def params(limit):
     return pltpu.CompilerParams(vmem_limit_bytes=limit * MIB)
+
+
+def cost(flops, moved):
+    return pl.CostEstimate(flops=flops, bytes_accessed=moved, transcendentals=0)
+
+
+def to_partner(array, k):
+    devices = lax.axis_size("runs")
+    return lax.ppermute(array, "runs", [(i, i ^ k) for i in range(devices)])
 
 
 def split_by_modes(
@@ -255,58 +259,66 @@
     devices = lax.axis_size("runs")
     total_runs = run_count * devices
     own_modes = modes // devices
-    offset = lax.axis_index("runs") * term_count
     parts = LANES // run_count
     first_row = dim // parts
     packet_rows = round_up(first_row + term_count // LANES, 8)
-
-    turned, packets = pl.pallas_call(
+    me = lax.axis_index("runs").astype(jnp.int32).reshape(1)
+    smem = pl.BlockSpec(memory_space=pltpu.SMEM)
+    vmem = pl.BlockSpec(memory_space=pltpu.VMEM)
+    anywhere = pl.BlockSpec(memory_space=pl.ANY)
+    block_type = jax.ShapeDtypeStruct((own_modes, term_count), jnp.bfloat16)
+
+    turned, packet, *sent = pl.pallas_call(
         functools.partial(prepare_kernel, parts),
-        out_shape=(
+        in_specs=[smem, vmem, vmem],
+        out_specs=[vmem] * (2 + devices),
+        out_shape=[
             jax.ShapeDtypeStruct((modes, term_count), jnp.bfloat16),
-            jax.ShapeDtypeStruct((devices, packet_rows, LANES), jnp.float32),
-        ),
+            jax.ShapeDtypeStruct((packet_rows, LANES), jnp.float32),
+        ]
+        + [block_type] * devices,
         compiler_params=params(16),
         name="prepare",
-    )(correlations, run_inputs.T)
-    packets = lax.all_to_all(packets, "runs", 0, 0, tiled=False)
-    blocks = lax.all_to_all(
-        turned.reshape(devices, own_modes, term_count), "runs", 0, 0, tiled=False
-    )
+    )(me, in_hbm(correlations), in_hbm(run_inputs.T))
+    packets = [packet] + [to_partner(packet, k) for k in range(1, devices)]
+    blocks = sent[:1] + [to_partner(sent[k], k) for k in range(1, devices)]
 
     tile = term_count
     half = round_up(DEGREES * dim, LANES)
     design = pl.pallas_call(
         functools.partial(design_kernel, dim, run_count),
-        grid=(terms // tile,),
-        in_specs=[
-            pl.BlockSpec((devices, packet_rows, LANES), lambda i: (0, 0, 0)),
-            pl.BlockSpec((slots, tile), lambda i: (0, i)),
-        ],
-        out_specs=pl.BlockSpec((total_runs, tile), lambda i: (0, i)),
+        grid_spec=pltpu.PrefetchScalarGridSpec(
+            num_scalar_prefetch=1,
+            grid=(terms // tile,),
+            in_specs=[pl.BlockSpec((slots, tile), lambda i, me: (0, me[0] ^ i))]
+            + [pl.BlockSpec((packet_rows, LANES), lambda i, me: (0, 0))] * devices,
+            out_specs=pl.BlockSpec((total_runs, tile), lambda i, me: (0, i)),
+            scratch_shapes=[
+                pltpu.VMEM((total_runs, half), jnp.float32),
+                pltpu.VMEM((total_runs, 2 * half), jnp.bfloat16),
+                pltpu.VMEM((slots - slots // 4, 2 * half, tile), jnp.bfloat16),
+            ],
+        ),
         out_shape=jax.ShapeDtypeStruct((total_runs, terms), jnp.bfloat16),
-        scratch_shapes=[
-            pltpu.VMEM((total_runs, 2 * half), jnp.bfloat16),
-            pltpu.VMEM((slots, 2 * half, tile), jnp.bfloat16),
-        ],
         compiler_params=params(16),
+        cost_estimate=cost(
+            4 * total_runs * terms * slots * half, 2 * total_runs * terms
+        ),
         name="design",
-    )(packets, term_codes.T)
-
-    summed, scale = pl.pallas_call(
+    )(me, in_hbm(term_codes.T), *packets)
+
+    *summed, scale = pl.pallas_call(
         functools.partial(fit_kernel, first_row, float(total_runs)),
-        out_shape=(
-            jax.ShapeDtypeStruct((devices, own_modes, term_count), jnp.bfloat16),
-            jax.ShapeDtypeStruct((8, terms), jnp.float32),
-        ),
+        in_specs=[smem] + [vmem] * (2 + 2 * devices),
+        out_specs=[vmem] * (devices + 1),
+        out_shape=[block_type] * devices
+        + [jax.ShapeDtypeStruct((8, term_count), jnp.float32)],
         scratch_shapes=[pltpu.VMEM((own_modes, terms), jnp.bfloat16)],
-        compiler_params=params(20),
+        compiler_params=params(24),
+        cost_estimate=cost(4 * total_runs * terms * own_modes, 2 * total_runs * terms),
         name="fit",
-    )(packets, weight_levels[None, :], blocks, design)
-    own_scale = lax.dynamic_slice_in_dim(scale, offset, term_count, 1)
-    returned = lax.all_to_all(summed, "runs", 0, 0, tiled=False).reshape(
-        modes, term_count
-    )
+    )(me, weight_levels[None, :], design, *packets, *blocks)
+    returned = summed[:1] + [to_partner(summed[k], k) for k in range(1, devices)]
 
     block = math.gcd(512, slab_cells)
     ordered = pl.pallas_call(
@@ -320,14 +332,13 @@
         out_shape=jax.ShapeDtypeStruct((modes, slab_cells), jnp.bfloat16),
         scratch_shapes=[pltpu.VMEM((modes, cells), jnp.bfloat16)],
         compiler_params=params(24),
+        cost_estimate=cost(2 * cells * slab_cells * modes, 4 * cells * modes),
         name="reorder",
-    )(cell_map[None, :], slab_modes)
-
-    vmem = pl.BlockSpec(memory_space=pltpu.VMEM)
-    anywhere = pl.BlockSpec(memory_space=pl.ANY)
+    )(cell_map[None, :], in_hbm(slab_modes))
+
     return pl.pallas_call(
         finish_kernel,
-        in_specs=[vmem, vmem, vmem, vmem],
+        in_specs=[smem] + [vmem] * (3 + devices),
         out_specs=(anywhere, anywhere),
         out_shape=(
             jax.ShapeDtypeStruct((term_count, modes), jnp.float32),
@@ -343,7 +354,7 @@
         ],
         compiler_params=params(20),
         name="finish",
-    )(returned, turned, own_scale, ordered)
+    )(me, turned, scale, ordered, *returned)
 
 
 def hermite_table(points):
@@ -423,7 +434,9 @@
     run_count = run_inputs.shape[0]
     term_count, modes = correlations.shape
     whole_tiles = (
-        modes % (16 * devices) == 0
+        devices & (devices - 1) == 0
+        and modes % (16 * devices) == 0
+        and DEGREES * run_inputs.shape[1] <= LANES
         and term_count % LANES == 0
         and LANES % run_count == 0
         and devices % (LANES // run_count) == 0

time: 75.9 us -> 100 us (1.32)
  starting transfers between devices: 9.54 us -> 61 us
  local copies, waits for them, and re-layouts: 15.5 us -> 0.01 us
  blocking collectives: 15.1 us -> 0 us
  waiting for transfers between devices: 0.01 us -> 4.1 us
  Pallas kernels: 34.3 us -> 33.2 us
    ppermute x0 -> x45, starting transfers between devices: none -> 61 us  [to_partner(): return lax.ppermute(array, 'runs', [(i, i ^ k) for i in range(devices)])]
    unnamed x20 -> x4, local copies, waits for them, and re-layouts: 15.5 us -> 0.01 us
    all_to_all x1 -> x0, blocking collectives: 15.1 us -> none  [split_by_modes(): packets = lax.all_to_all(packets, 'runs', 0, 0, tiled=False)]
    all_to_all x2 -> x0, starting transfers between devices: 9.54 us -> none  [the longest x1 5.97 us: split_by_modes(): lax.all_to_all(summed, 'runs', 0, 0, tiled=False).reshape(modes, term_count)]
    ppermute x0 -> x45, waiting for transfers between devices: none -> 4.1 us  [to_partner(): return lax.ppermute(array, 'runs', [(i, i ^ k) for i in range(devices)])]
    pallas_call x3, Pallas kernels: 18.3 us -> 15.8 us  [the longest x1 11.9 us: split_by_modes(): pl.pallas_call(functools.partial(design_kernel, dim, run_count), grid_spe...]
    pallas_call x1, Pallas kernels: 11 us -> 13.1 us  [split_by_modes(): pl.pallas_call(reorder_kernel, grid=(slab_cells // block,), in_specs=[pl....]
  transfers between devices with their start and end apart: 2 -> 45, of which waited for: 0 -> 2; matrix products, arithmetic and copies ran while one was open for 0% -> 0% of each run, Pallas kernels for 33% -> 25%
where the time goes in v4:
time: 100 us; the launch traced here: 99.2 us
  starting transfers between devices  61 us (61%)
  Pallas kernels  33.2 us (33%)
  waiting for transfers between devices  4.1 us (4%)
    ppermute x45, starting transfers between devices, to_partner(): return lax.ppermute(array, 'runs', [(i, i ^ k) for i in range(devices)])  61 us
    pallas_call x1, Pallas kernels, split_by_modes(): pl.pallas_call(reorder_kernel, grid=(slab_cells // block,), in_specs=[pl....  13.1 us
    pallas_call x1, Pallas kernels, split_by_modes(): pl.pallas_call(functools.partial(design_kernel, dim, run_count), grid_spe...  11.9 us
    pallas_call x1, Pallas kernels, split_by_modes(): pl.pallas_call(functools.partial(fit_kernel, first_row, float(total_runs)...  4.28 us
    ppermute x45, waiting for transfers between devices, to_partner(): return lax.ppermute(array, 'runs', [(i, i ^ k) for i in range(devices)])  4.1 us
    pallas_call x1, Pallas kernels, split_by_modes(): pl.pallas_call(finish_kernel, in_specs=[smem] + [vmem] * (3 + devices), o...  2.57 us
  transfers between devices with their start and end apart: 45, of which 2 were waited for; matrix products, arithmetic and copies ran while one was open for 0% of the time, Pallas kernels for 25%

profile of v4, /device:TPU:0, one launch (start us, length us, event | category | flops | bytes accessed | tf_op | source)
XLA Modules:
  0.0 99.2 jit_solution(8330149940742700649)
XLA Ops:
  0.6 1.4 %prepare.1 = (bf16[1024,256]{1,0:T(8,128)(2,1)S(1)}, f32[16,128]{1,0:T(8,128)S(1)}, bf16[64,256]{1,0:T(8,128)(2,1)S(1)}, bf16[64,256]{1,0:T(8,128)(2,1)S(1)}, bf...) custom-call(s32[1]{0:T(128)} %bitcast.me_ref, ...), custom_call_target="tpu_custom_call" | custom-call | tf_op jit(solution)/shard_map/prepare/pallas_call | solution.py:271
  2.0 0.5 collective-permute-start
  2.5 2.6 %collective-permute-start.1 = (f32[16,128]{1,0:T(8,128)S(1)}, f32[16,128]{1,0:T(8,128)S(1)}, u32[]{:S(2)}, u32[]{:S(2)}) collective-permute-start(f32[16,128]{1,0:T(8,128)S(1)} %get-tuple-element.38.refs_0_), channel_id=1, source_target_pairs={{0,2},{1,3},{2,0},{3,1},{4,6},{5,7},{6,4},{7,5},{8,10},{9,11},{10,... | collective-permute-start | bytes 24584 | tf_op jit(solution)/shard_map/ppermute | solution.py:248
  5.1 0.1 collective-permute-start.2
  5.2 1.8 %collective-permute-start.3 = (f32[16,128]{1,0:T(8,128)S(1)}, f32[16,128]{1,0:T(8,128)S(1)}, u32[]{:S(2)}, u32[]{:S(2)}) collective-permute-start(f32[16,128]{1,0:T(8,128)S(1)} %get-tuple-element.38.refs_0_), channel_id=1, source_target_pairs={{0,4},{1,5},{2,6},{3,7},{4,0},{5,1},{6,2},{7,3},{8,12},{9,13},{10,... | collective-permute-start | bytes 24584 | tf_op jit(solution)/shard_map/ppermute | solution.py:248
  7.0 0.0 collective-permute-start.4
  7.0 2.6 %collective-permute-start.5 = (f32[16,128]{1,0:T(8,128)S(1)}, f32[16,128]{1,0:T(8,128)S(1)}, u32[]{:S(2)}, u32[]{:S(2)}) collective-permute-start(f32[16,128]{1,0:T(8,128)S(1)} %get-tuple-element.38.refs_0_), channel_id=1, source_target_pairs={{0,6},{1,7},{2,4},{3,5},{4,2},{5,3},{6,0},{7,1},{8,14},{9,15},{10,... | collective-permute-start | bytes 24584 | tf_op jit(solution)/shard_map/ppermute | solution.py:248
  9.6 0.1 collective-permute-start.6
  9.7 0.0 collective-permute-done.2.refs_3_
  9.7 2.7 %collective-permute-start.7 = (f32[16,128]{1,0:T(8,128)S(1)}, f32[16,128]{1,0:T(8,128)S(1)}, u32[]{:S(2)}, u32[]{:S(2)}) collective-permute-start(f32[16,128]{1,0:T(8,128)S(1)} %get-tuple-element.38.refs_0_), channel_id=1, source_target_pairs={{0,8},{1,9},{2,10},{3,11},{4,12},{5,13},{6,14},{7,15},{8,0},{9,1},... | collective-permute-start | bytes 24584 | tf_op jit(solution)/shard_map/ppermute | solution.py:248
  12.4 0.0 collective-permute-done.3.refs_4_
  12.4 0.0 collective-permute-start.8
  12.4 3.5 %collective-permute-start.9 = (f32[16,128]{1,0:T(8,128)S(1)}, f32[16,128]{1,0:T(8,128)S(1)}, u32[]{:S(2)}, u32[]{:S(2)}) collective-permute-start(f32[16,128]{1,0:T(8,128)S(1)} %get-tuple-element.38.refs_0_), channel_id=1, source_target_pairs={{0,10},{1,11},{2,8},{3,9},{4,14},{5,15},{6,12},{7,13},{8,2},{9,3},... | collective-permute-start | bytes 24584 | tf_op jit(solution)/shard_map/ppermute | solution.py:248
  15.9 0.0 collective-permute-done.5.refs_6_
  15.9 0.1 collective-permute-start.10
  16.0 3.6 %collective-permute-start.11 = (f32[16,128]{1,0:T(8,128)S(1)}, f32[16,128]{1,0:T(8,128)S(1)}, u32[]{:S(2)}, u32[]{:S(2)}) collective-permute-start(f32[16,128]{1,0:T(8,128)S(1)} %get-tuple-element.38.refs_0_), channel_id=1, source_target_pairs={{0,12},{1,13},{2,14},{3,15},{4,8},{5,9},{6,10},{7,11},{8,4},{9,5},... | collective-permute-start | bytes 24584 | tf_op jit(solution)/shard_map/ppermute | solution.py:248
  19.6 0.0 collective-permute-done.7.refs_8_
  19.6 0.0 collective-permute-start.12
  19.6 0.0 collective-permute-done.8.refs_9_
  19.6 4.4 %collective-permute-start.13 = (f32[16,128]{1,0:T(8,128)S(1)}, f32[16,128]{1,0:T(8,128)S(1)}, u32[]{:S(2)}, u32[]{:S(2)}) collective-permute-start(f32[16,128]{1,0:T(8,128)S(1)} %get-tuple-element.38.refs_0_), channel_id=1, source_target_pairs={{0,14},{1,15},{2,12},{3,13},{4,10},{5,11},{6,8},{7,9},{8,6},{9,7},... | collective-permute-start | bytes 24584 | tf_op jit(solution)/shard_map/ppermute | solution.py:248
  24.0 0.0 collective-permute-done.9.refs_10_
  24.0 0.1 collective-permute-start.14
  24.2 0.4 collective-permute-start.15
  24.5 0.0 collective-permute-done.11.refs_12_
  24.5 1.5 %collective-permute-start.16 = (bf16[64,256]{1,0:T(8,128)(2,1)S(1)}, bf16[64,256]{1,0:T(8,128)(2,1)S(1)}, u32[]{:S(2)}, u32[]{:S(2)}) collective-permute-start(bf16[64,256]{1,0:T(8,128)(2,1)S(1)} %get-tuple-element.41), channel_id=1, source_target_pairs={{0,2},{1,3},{2,0},{3,1},{4,6},{5,7},{6,4},{7,5},{8,10},{9,11},{10,... | collective-permute-start | bytes 98312 | tf_op jit(solution)/shard_map/ppermute | solution.py:248
  26.0 0.0 collective-permute-start.17
  26.1 0.0 collective-permute-start.18
  26.1 3.7 %collective-permute-done.14.refs_15_ = f32[16,128]{1,0:T(8,128)S(1)} collective-permute-done((f32[16,128]{1,0:T(8,128)S(1)}, f32[16,128]{1,0:T(8,128)S(1)}, u32[]{:S(2)}, u32[]{:S(2)}) %collective-permute-start.14) | collective-permute-done | bytes 8224 | tf_op jit(solution)/shard_map/ppermute | solution.py:248
  29.8 1.8 %collective-permute-start.20 = (bf16[64,256]{1,0:T(8,128)(2,1)S(1)}, bf16[64,256]{1,0:T(8,128)(2,1)S(1)}, u32[]{:S(2)}, u32[]{:S(2)}) collective-permute-start(bf16[64,256]{1,0:T(8,128)(2,1)S(1)} %get-tuple-element.45), channel_id=1, source_target_pairs={{0,6},{1,7},{2,4},{3,5},{4,2},{5,3},{6,0},{7,1},{8,14},{9,15},{10,... | collective-permute-start | bytes 98312 | tf_op jit(solution)/shard_map/ppermute | solution.py:248
  31.6 0.6 collective-permute-start.21
  32.2 0.0 collective-permute-done.17.refs_19_
  32.2 0.9 collective-permute-start.22
  33.2 1.9 %collective-permute-start.23 = (bf16[64,256]{1,0:T(8,128)(2,1)S(1)}, bf16[64,256]{1,0:T(8,128)(2,1)S(1)}, u32[]{:S(2)}, u32[]{:S(2)}) collective-permute-start(bf16[64,256]{1,0:T(8,128)(2,1)S(1)} %get-tuple-element.48), channel_id=1, source_target_pairs={{0,9},{1,8},{2,11},{3,10},{4,13},{5,12},{6,15},{7,14},{8,1},{9,0},... | collective-permute-start | bytes 98312 | tf_op jit(solution)/shard_map/ppermute | solution.py:248
  35.1 0.0 collective-permute-done.19.refs_21_
  35.1 1.5 %collective-permute-start.24 = (bf16[64,256]{1,0:T(8,128)(2,1)S(1)}, bf16[64,256]{1,0:T(8,128)(2,1)S(1)}, u32[]{:S(2)}, u32[]{:S(2)}) collective-permute-start(bf16[64,256]{1,0:T(8,128)(2,1)S(1)} %get-tuple-element.49), channel_id=1, source_target_pairs={{0,10},{1,11},{2,8},{3,9},{4,14},{5,15},{6,12},{7,13},{8,2},{9,3},... | collective-permute-start | bytes 98312 | tf_op jit(solution)/shard_map/ppermute | solution.py:248
  36.6 0.0 collective-permute-done.20.refs_22_
  36.6 1.8 %collective-permute-start.25 = (bf16[64,256]{1,0:T(8,128)(2,1)S(1)}, bf16[64,256]{1,0:T(8,128)(2,1)S(1)}, u32[]{:S(2)}, u32[]{:S(2)}) collective-permute-start(bf16[64,256]{1,0:T(8,128)(2,1)S(1)} %get-tuple-element.50), channel_id=1, source_target_pairs={{0,11},{1,10},{2,9},{3,8},{4,15},{5,14},{6,13},{7,12},{8,3},{9,2},... | collective-permute-start | bytes 98312 | tf_op jit(solution)/shard_map/ppermute | solution.py:248
  38.4 1.7 %collective-permute-start.26 = (bf16[64,256]{1,0:T(8,128)(2,1)S(1)}, bf16[64,256]{1,0:T(8,128)(2,1)S(1)}, u32[]{:S(2)}, u32[]{:S(2)}) collective-permute-start(bf16[64,256]{1,0:T(8,128)(2,1)S(1)} %get-tuple-element.51), channel_id=1, source_target_pairs={{0,12},{1,13},{2,14},{3,15},{4,8},{5,9},{6,10},{7,11},{8,4},{9,5},... | collective-permute-start | bytes 98312 | tf_op jit(solution)/shard_map/ppermute | solution.py:248
  40.1 0.0 collective-permute-done.22.refs_24_
  40.1 2.1 %collective-permute-start.27 = (bf16[64,256]{1,0:T(8,128)(2,1)S(1)}, bf16[64,256]{1,0:T(8,128)(2,1)S(1)}, u32[]{:S(2)}, u32[]{:S(2)}) collective-permute-start(bf16[64,256]{1,0:T(8,128)(2,1)S(1)} %get-tuple-element.52), channel_id=1, source_target_pairs={{0,13},{1,12},{2,15},{3,14},{4,9},{5,8},{6,11},{7,10},{8,5},{9,4},... | collective-permute-start | bytes 98312 | tf_op jit(solution)/shard_map/ppermute | solution.py:248
  42.2 2.6 %collective-permute-start.28 = (bf16[64,256]{1,0:T(8,128)(2,1)S(1)}, bf16[64,256]{1,0:T(8,128)(2,1)S(1)}, u32[]{:S(2)}, u32[]{:S(2)}) collective-permute-start(bf16[64,256]{1,0:T(8,128)(2,1)S(1)} %get-tuple-element.53), channel_id=1, source_target_pairs={{0,14},{1,15},{2,12},{3,13},{4,10},{5,11},{6,8},{7,9},{8,6},{9,7},... | collective-permute-start | bytes 98312 | tf_op jit(solution)/shard_map/ppermute | solution.py:248
  44.8 0.0 collective-permute-done.24.refs_26_
  44.8 1.6 %collective-permute-start.29 = (bf16[64,256]{1,0:T(8,128)(2,1)S(1)}, bf16[64,256]{1,0:T(8,128)(2,1)S(1)}, u32[]{:S(2)}, u32[]{:S(2)}) collective-permute-start(bf16[64,256]{1,0:T(8,128)(2,1)S(1)} %get-tuple-element.54), channel_id=1, source_target_pairs={{0,15},{1,14},{2,13},{3,12},{4,11},{5,10},{6,9},{7,8},{8,7},{9,6},... | collective-permute-start | bytes 98312 | tf_op jit(solution)/shard_map/ppermute | solution.py:248
  46.4 11.9 %design.1.design_ref = bf16[1024,4096]{1,0:T(8,128)(2,1)S(1)} custom-call(s32[1]{0:T(128)} %bitcast.me_ref, s32[4,4096]{1,0:T(4,128)} %bitcast.8, f32[16,128]{1,0:T(8,128)S(1)} %get-tuple-element.38.refs_0_, f32[16,128]{1,0:T(8,128)S(1)} %collective-permute-done.refs_1_, f32[16,128]{1,0:T(8,128)S(1)} %collective-permute-done.1.refs_2_, ...), custom_call_target="tpu_custom_call" | custom-call | flops 8589934592 | bytes 8388608 | tf_op jit(solution)/shard_map/design/pallas_call | solution.py:288
  58.3 0.0 collective-permute-done.27.refs_29_
  58.4 0.0 copy-start.1
  58.4 4.3 %fit.1 = (bf16[64,256]{1,0:T(8,128)(2,1)S(1)}, bf16[64,256]{1,0:T(8,128)(2,1)S(1)}, bf16[64,256]{1,0:T(8,128)(2,1)S(1)}, bf16[64,256]{1,0:T(8,128)(2,1)S(1)}, bf...) custom-call(s32[1]{0:T(128)} %bitcast.me_ref, ...), custom_call_target="tpu_custom_call" | custom-call | flops 1073741824 | bytes 8388608 | tf_op jit(solution)/shard_map/fit/pallas_call | solution.py:310
  62.7 0.7 collective-permute-start.30
  63.4 0.6 collective-permute-start.31
  64.0 0.8 collective-permute-start.32
  64.8 2.1 %collective-permute-start.34 = (bf16[64,256]{1,0:T(8,128)(2,1)S(1)}, bf16[64,256]{1,0:T(8,128)(2,1)S(1)}, u32[]{:S(2)}, u32[]{:S(2)}) collective-permute-start(bf16[64,256]{1,0:T(8,128)(2,1)S(1)} %get-tuple-element.61), channel_id=1, source_target_pairs={{0,5},{1,4},{2,7},{3,6},{4,1},{5,0},{6,3},{7,2},{8,13},{9,12},{10,... | collective-permute-start | bytes 98312 | tf_op jit(solution)/shard_map/ppermute | solution.py:248
  66.9 0.4 collective-permute-start.35
  67.2 0.3 collective-permute-done.31.refs_2_
  67.5 1.6 %collective-permute-start.36 = (bf16[64,256]{1,0:T(8,128)(2,1)S(1)}, bf16[64,256]{1,0:T(8,128)(2,1)S(1)}, u32[]{:S(2)}, u32[]{:S(2)}) collective-permute-start(bf16[64,256]{1,0:T(8,128)(2,1)S(1)} %get-tuple-element.63), channel_id=1, source_target_pairs={{0,7},{1,6},{2,5},{3,4},{4,3},{5,2},{6,1},{7,0},{8,15},{9,14},{10,... | collective-permute-start | bytes 98312 | tf_op jit(solution)/shard_map/ppermute | solution.py:248
  69.2 0.9 collective-permute-start.37
  70.1 2.1 %collective-permute-start.38 = (bf16[64,256]{1,0:T(8,128)(2,1)S(1)}, bf16[64,256]{1,0:T(8,128)(2,1)S(1)}, u32[]{:S(2)}, u32[]{:S(2)}) collective-permute-start(bf16[64,256]{1,0:T(8,128)(2,1)S(1)} %get-tuple-element.65), channel_id=1, source_target_pairs={{0,9},{1,8},{2,11},{3,10},{4,13},{5,12},{6,15},{7,14},{8,1},{9,0},... | collective-permute-start | bytes 98312 | tf_op jit(solution)/shard_map/ppermute | solution.py:248
  72.2 1.4 %collective-permute-start.39 = (bf16[64,256]{1,0:T(8,128)(2,1)S(1)}, bf16[64,256]{1,0:T(8,128)(2,1)S(1)}, u32[]{:S(2)}, u32[]{:S(2)}) collective-permute-start(bf16[64,256]{1,0:T(8,128)(2,1)S(1)} %get-tuple-element.66), channel_id=1, source_target_pairs={{0,10},{1,11},{2,8},{3,9},{4,14},{5,15},{6,12},{7,13},{8,2},{9,3},... | collective-permute-start | bytes 98312 | tf_op jit(solution)/shard_map/ppermute | solution.py:248
  73.6 1.8 %collective-permute-start.40 = (bf16[64,256]{1,0:T(8,128)(2,1)S(1)}, bf16[64,256]{1,0:T(8,128)(2,1)S(1)}, u32[]{:S(2)}, u32[]{:S(2)}) collective-permute-start(bf16[64,256]{1,0:T(8,128)(2,1)S(1)} %get-tuple-element.67), channel_id=1, source_target_pairs={{0,11},{1,10},{2,9},{3,8},{4,15},{5,14},{6,13},{7,12},{8,3},{9,2},... | collective-permute-start | bytes 98312 | tf_op jit(solution)/shard_map/ppermute | solution.py:248
  75.4 1.7 %collective-permute-start.41 = (bf16[64,256]{1,0:T(8,128)(2,1)S(1)}, bf16[64,256]{1,0:T(8,128)(2,1)S(1)}, u32[]{:S(2)}, u32[]{:S(2)}) collective-permute-start(bf16[64,256]{1,0:T(8,128)(2,1)S(1)} %get-tuple-element.68), channel_id=1, source_target_pairs={{0,12},{1,13},{2,14},{3,15},{4,8},{5,9},{6,10},{7,11},{8,4},{9,5},... | collective-permute-start | bytes 98312 | tf_op jit(solution)/shard_map/ppermute | solution.py:248
  77.1 2.1 %collective-permute-start.42 = (bf16[64,256]{1,0:T(8,128)(2,1)S(1)}, bf16[64,256]{1,0:T(8,128)(2,1)S(1)}, u32[]{:S(2)}, u32[]{:S(2)}) collective-permute-start(bf16[64,256]{1,0:T(8,128)(2,1)S(1)} %get-tuple-element.69), channel_id=1, source_target_pairs={{0,13},{1,12},{2,15},{3,14},{4,9},{5,8},{6,11},{7,10},{8,5},{9,4},... | collective-permute-start | bytes 98312 | tf_op jit(solution)/shard_map/ppermute | solution.py:248
  79.3 2.6 %collective-permute-start.43 = (bf16[64,256]{1,0:T(8,128)(2,1)S(1)}, bf16[64,256]{1,0:T(8,128)(2,1)S(1)}, u32[]{:S(2)}, u32[]{:S(2)}) collective-permute-start(bf16[64,256]{1,0:T(8,128)(2,1)S(1)} %get-tuple-element.70), channel_id=1, source_target_pairs={{0,14},{1,15},{2,12},{3,13},{4,10},{5,11},{6,8},{7,9},{8,6},{9,7},... | collective-permute-start | bytes 98312 | tf_op jit(solution)/shard_map/ppermute | solution.py:248
  81.9 1.5 %collective-permute-start.44 = (bf16[64,256]{1,0:T(8,128)(2,1)S(1)}, bf16[64,256]{1,0:T(8,128)(2,1)S(1)}, u32[]{:S(2)}, u32[]{:S(2)}) collective-permute-start(bf16[64,256]{1,0:T(8,128)(2,1)S(1)} %get-tuple-element.71), channel_id=1, source_target_pairs={{0,15},{1,14},{2,13},{3,12},{4,11},{5,10},{6,9},{7,8},{8,7},{9,6},... | collective-permute-start | bytes 98312 | tf_op jit(solution)/shard_map/ppermute | solution.py:248
  83.4 13.1 %reorder.1.modes_ref = bf16[1024,2048]{1,0:T(8,128)(2,1)S(1)} custom-call(s32[1,2048]{1,0:T(1,128)S(1)} %bitcast.6, bf16[2048,1024]{1,0:T(8,128)(2,1)} %slab_ref.1), custom_call_target="tpu_custom_call" | custom-call | flops 8589934592 | bytes 8388608 | tf_op jit(solution)/shard_map/reorder/pallas_call | solution.py:324
  96.6 2.6 %finish.1 = (f32[256,1024]{1,0:T(8,128)}, bf16[256,2048]{1,0:T(8,128)(2,1)}) custom-call(s32[1]{0:T(128)} %bitcast.me_ref, bf16[1024,256]{1,0:T(8,128)(2,1)S(1)} %get-tuple-element.37.corr_ref, f32[8,256]{1,0:T(8,128)S(1)} %get-tuple-element.55.scale_ref, bf16[1024,2048]{1,0:T(8,128)(2,1)S(1)} %reorder.1.modes_ref, ...), custom_call_target="tpu_custom_call" | custom-call | tf_op jit(solution)/shard_map/finish/pallas_call | solution.py:339
  (35 shorter events, 0.1 us)
Async XLA Ops:
  2.0 5.0 %collective-permute-start = (f32[16,128]{1,0:T(8,128)S(1)}, f32[16,128]{1,0:T(8,128)S(1)}, u32[]{:S(2)}, u32[]{:S(2)}) collective-permute-start(f32[16,128]{1,0:T(8,128)S(1)} %get-tuple-element.38.refs_0_), channel_id=1, source_target_pairs={{0,1},{1,0},{2,3},{3,2},{4,5},{5,4},{6,7},{7,6},{8,9},{9,8},{10,11... | collective-permute-start | bytes 24584 | tf_op jit(solution)/shard_map/ppermute | solution.py:248
  2.5 7.1 %collective-permute-start.1 = (f32[16,128]{1,0:T(8,128)S(1)}, f32[16,128]{1,0:T(8,128)S(1)}, u32[]{:S(2)}, u32[]{:S(2)}) collective-permute-start(f32[16,128]{1,0:T(8,128)S(1)} %get-tuple-element.38.refs_0_), channel_id=1, source_target_pairs={{0,2},{1,3},{2,0},{3,1},{4,6},{5,7},{6,4},{7,5},{8,10},{9,11},{10,... | collective-permute-start | bytes 24584 | tf_op jit(solution)/shard_map/ppermute | solution.py:248
  5.1 4.6 %collective-permute-start.2 = (f32[16,128]{1,0:T(8,128)S(1)}, f32[16,128]{1,0:T(8,128)S(1)}, u32[]{:S(2)}, u32[]{:S(2)}) collective-permute-start(f32[16,128]{1,0:T(8,128)S(1)} %get-tuple-element.38.refs_0_), channel_id=1, source_target_pairs={{0,3},{1,2},{2,1},{3,0},{4,7},{5,6},{6,5},{7,4},{8,11},{9,10},{10,... | collective-permute-start | bytes 24584 | tf_op jit(solution)/shard_map/ppermute | solution.py:248
  5.2 7.2 %collective-permute-start.3 = (f32[16,128]{1,0:T(8,128)S(1)}, f32[16,128]{1,0:T(8,128)S(1)}, u32[]{:S(2)}, u32[]{:S(2)}) collective-permute-start(f32[16,128]{1,0:T(8,128)S(1)} %get-tuple-element.38.refs_0_), channel_id=1, source_target_pairs={{0,4},{1,5},{2,6},{3,7},{4,0},{5,1},{6,2},{7,3},{8,12},{9,13},{10,... | collective-permute-start | bytes 24584 | tf_op jit(solution)/shard_map/ppermute | solution.py:248
  7.0 5.4 %collective-permute-start.4 = (f32[16,128]{1,0:T(8,128)S(1)}, f32[16,128]{1,0:T(8,128)S(1)}, u32[]{:S(2)}, u32[]{:S(2)}) collective-permute-start(f32[16,128]{1,0:T(8,128)S(1)} %get-tuple-element.38.refs_0_), channel_id=1, source_target_pairs={{0,5},{1,4},{2,7},{3,6},{4,1},{5,0},{6,3},{7,2},{8,13},{9,12},{10,... | collective-permute-start | bytes 24584 | tf_op jit(solution)/shard_map/ppermute | solution.py:248
  7.0 8.9 %collective-permute-start.5 = (f32[16,128]{1,0:T(8,128)S(1)}, f32[16,128]{1,0:T(8,128)S(1)}, u32[]{:S(2)}, u32[]{:S(2)}) collective-permute-start(f32[16,128]{1,0:T(8,128)S(1)} %get-tuple-element.38.refs_0_), channel_id=1, source_target_pairs={{0,6},{1,7},{2,4},{3,5},{4,2},{5,3},{6,0},{7,1},{8,14},{9,15},{10,... | collective-permute-start | bytes 24584 | tf_op jit(solution)/shard_map/ppermute | solution.py:248
  9.6 6.4 %collective-permute-start.6 = (f32[16,128]{1,0:T(8,128)S(1)}, f32[16,128]{1,0:T(8,128)S(1)}, u32[]{:S(2)}, u32[]{:S(2)}) collective-permute-start(f32[16,128]{1,0:T(8,128)S(1)} %get-tuple-element.38.refs_0_), channel_id=1, source_target_pairs={{0,7},{1,6},{2,5},{3,4},{4,3},{5,2},{6,1},{7,0},{8,15},{9,14},{10,... | collective-permute-start | bytes 24584 | tf_op jit(solution)/shard_map/ppermute | solution.py:248
  9.7 9.9 %collective-permute-start.7 = (f32[16,128]{1,0:T(8,128)S(1)}, f32[16,128]{1,0:T(8,128)S(1)}, u32[]{:S(2)}, u32[]{:S(2)}) collective-permute-start(f32[16,128]{1,0:T(8,128)S(1)} %get-tuple-element.38.refs_0_), channel_id=1, source_target_pairs={{0,8},{1,9},{2,10},{3,11},{4,12},{5,13},{6,14},{7,15},{8,0},{9,1},... | collective-permute-start | bytes 24584 | tf_op jit(solution)/shard_map/ppermute | solution.py:248
  12.4 7.3 %collective-permute-start.8 = (f32[16,128]{1,0:T(8,128)S(1)}, f32[16,128]{1,0:T(8,128)S(1)}, u32[]{:S(2)}, u32[]{:S(2)}) collective-permute-start(f32[16,128]{1,0:T(8,128)S(1)} %get-tuple-element.38.refs_0_), channel_id=1, source_target_pairs={{0,9},{1,8},{2,11},{3,10},{4,13},{5,12},{6,15},{7,14},{8,1},{9,0},... | collective-permute-start | bytes 24584 | tf_op jit(solution)/shard_map/ppermute | solution.py:248
  12.4 11.6 %collective-permute-start.9 = (f32[16,128]{1,0:T(8,128)S(1)}, f32[16,128]{1,0:T(8,128)S(1)}, u32[]{:S(2)}, u32[]{:S(2)}) collective-permute-start(f32[16,128]{1,0:T(8,128)S(1)} %get-tuple-element.38.refs_0_), channel_id=1, source_target_pairs={{0,10},{1,11},{2,8},{3,9},{4,14},{5,15},{6,12},{7,13},{8,2},{9,3},... | collective-permute-start | bytes 24584 | tf_op jit(solution)/shard_map/ppermute | solution.py:248
  15.9 8.2 %collective-permute-start.10 = (f32[16,128]{1,0:T(8,128)S(1)}, f32[16,128]{1,0:T(8,128)S(1)}, u32[]{:S(2)}, u32[]{:S(2)}) collective-permute-start(f32[16,128]{1,0:T(8,128)S(1)} %get-tuple-element.38.refs_0_), channel_id=1, source_target_pairs={{0,11},{1,10},{2,9},{3,8},{4,15},{5,14},{6,13},{7,12},{8,3},{9,2},... | collective-permute-start | bytes 24584 | tf_op jit(solution)/shard_map/ppermute | solution.py:248
  16.0 8.5 %collective-permute-start.11 = (f32[16,128]{1,0:T(8,128)S(1)}, f32[16,128]{1,0:T(8,128)S(1)}, u32[]{:S(2)}, u32[]{:S(2)}) collective-permute-start(f32[16,128]{1,0:T(8,128)S(1)} %get-tuple-element.38.refs_0_), channel_id=1, source_target_pairs={{0,12},{1,13},{2,14},{3,15},{4,8},{5,9},{6,10},{7,11},{8,4},{9,5},... | collective-permute-start | bytes 24584 | tf_op jit(solution)/shard_map/ppermute | solution.py:248
  19.6 6.4 %collective-permute-start.12 = (f32[16,128]{1,0:T(8,128)S(1)}, f32[16,128]{1,0:T(8,128)S(1)}, u32[]{:S(2)}, u32[]{:S(2)}) collective-permute-start(f32[16,128]{1,0:T(8,128)S(1)} %get-tuple-element.38.refs_0_), channel_id=1, source_target_pairs={{0,13},{1,12},{2,15},{3,14},{4,9},{5,8},{6,11},{7,10},{8,5},{9,4},... | collective-permute-start | bytes 24584 | tf_op jit(solution)/shard_map/ppermute | solution.py:248
  19.6 6.4 %collective-permute-start.13 = (f32[16,128]{1,0:T(8,128)S(1)}, f32[16,128]{1,0:T(8,128)S(1)}, u32[]{:S(2)}, u32[]{:S(2)}) collective-permute-start(f32[16,128]{1,0:T(8,128)S(1)} %get-tuple-element.38.refs_0_), channel_id=1, source_target_pairs={{0,14},{1,15},{2,12},{3,13},{4,10},{5,11},{6,8},{7,9},{8,6},{9,7},... | collective-permute-start | bytes 24584 | tf_op jit(solution)/shard_map/ppermute | solution.py:248
  24.0 5.8 %collective-permute-start.14 = (f32[16,128]{1,0:T(8,128)S(1)}, f32[16,128]{1,0:T(8,128)S(1)}, u32[]{:S(2)}, u32[]{:S(2)}) collective-permute-start(f32[16,128]{1,0:T(8,128)S(1)} %get-tuple-element.38.refs_0_), channel_id=1, source_target_pairs={{0,15},{1,14},{2,13},{3,12},{4,11},{5,10},{6,9},{7,8},{8,7},{9,6},... | collective-permute-start | bytes 24584 | tf_op jit(solution)/shard_map/ppermute | solution.py:248
  24.2 5.7 %collective-permute-start.15 = (bf16[64,256]{1,0:T(8,128)(2,1)S(1)}, bf16[64,256]{1,0:T(8,128)(2,1)S(1)}, u32[]{:S(2)}, u32[]{:S(2)}) collective-permute-start(bf16[64,256]{1,0:T(8,128)(2,1)S(1)} %get-tuple-element.40), channel_id=1, source_target_pairs={{0,1},{1,0},{2,3},{3,2},{4,5},{5,4},{6,7},{7,6},{8,9},{9,8},{10,11... | collective-permute-start | bytes 98312 | tf_op jit(solution)/shard_map/ppermute | solution.py:248
  24.5 7.1 %collective-permute-start.16 = (bf16[64,256]{1,0:T(8,128)(2,1)S(1)}, bf16[64,256]{1,0:T(8,128)(2,1)S(1)}, u32[]{:S(2)}, u32[]{:S(2)}) collective-permute-start(bf16[64,256]{1,0:T(8,128)(2,1)S(1)} %get-tuple-element.41), channel_id=1, source_target_pairs={{0,2},{1,3},{2,0},{3,1},{4,6},{5,7},{6,4},{7,5},{8,10},{9,11},{10,... | collective-permute-start | bytes 98312 | tf_op jit(solution)/shard_map/ppermute | solution.py:248
  26.0 6.2 %collective-permute-start.17 = (bf16[64,256]{1,0:T(8,128)(2,1)S(1)}, bf16[64,256]{1,0:T(8,128)(2,1)S(1)}, u32[]{:S(2)}, u32[]{:S(2)}) collective-permute-start(bf16[64,256]{1,0:T(8,128)(2,1)S(1)} %get-tuple-element.42), channel_id=1, source_target_pairs={{0,3},{1,2},{2,1},{3,0},{4,7},{5,6},{6,5},{7,4},{8,11},{9,10},{10,... | collective-permute-start | bytes 98312 | tf_op jit(solution)/shard_map/ppermute | solution.py:248
  26.1 7.1 %collective-permute-start.18 = (bf16[64,256]{1,0:T(8,128)(2,1)S(1)}, bf16[64,256]{1,0:T(8,128)(2,1)S(1)}, u32[]{:S(2)}, u32[]{:S(2)}) collective-permute-start(bf16[64,256]{1,0:T(8,128)(2,1)S(1)} %get-tuple-element.43), channel_id=1, source_target_pairs={{0,4},{1,5},{2,6},{3,7},{4,0},{5,1},{6,2},{7,3},{8,12},{9,13},{10,... | collective-permute-start | bytes 98312 | tf_op jit(solution)/shard_map/ppermute | solution.py:248
  29.8 5.3 %collective-permute-start.19 = (bf16[64,256]{1,0:T(8,128)(2,1)S(1)}, bf16[64,256]{1,0:T(8,128)(2,1)S(1)}, u32[]{:S(2)}, u32[]{:S(2)}) collective-permute-start(bf16[64,256]{1,0:T(8,128)(2,1)S(1)} %get-tuple-element.44), channel_id=1, source_target_pairs={{0,5},{1,4},{2,7},{3,6},{4,1},{5,0},{6,3},{7,2},{8,13},{9,12},{10,... | collective-permute-start | bytes 98312 | tf_op jit(solution)/shard_map/ppermute | solution.py:248
  29.8 6.8 %collective-permute-start.20 = (bf16[64,256]{1,0:T(8,128)(2,1)S(1)}, bf16[64,256]{1,0:T(8,128)(2,1)S(1)}, u32[]{:S(2)}, u32[]{:S(2)}) collective-permute-start(bf16[64,256]{1,0:T(8,128)(2,1)S(1)} %get-tuple-element.45), channel_id=1, source_target_pairs={{0,6},{1,7},{2,4},{3,5},{4,2},{5,3},{6,0},{7,1},{8,14},{9,15},{10,... | collective-permute-start | bytes 98312 | tf_op jit(solution)/shard_map/ppermute | solution.py:248
  31.6 6.9 %collective-permute-start.21 = (bf16[64,256]{1,0:T(8,128)(2,1)S(1)}, bf16[64,256]{1,0:T(8,128)(2,1)S(1)}, u32[]{:S(2)}, u32[]{:S(2)}) collective-permute-start(bf16[64,256]{1,0:T(8,128)(2,1)S(1)} %get-tuple-element.46), channel_id=1, source_target_pairs={{0,7},{1,6},{2,5},{3,4},{4,3},{5,2},{6,1},{7,0},{8,15},{9,14},{10,... | collective-permute-start | bytes 98312 | tf_op jit(solution)/shard_map/ppermute | solution.py:248
  32.2 7.9 %collective-permute-start.22 = (bf16[64,256]{1,0:T(8,128)(2,1)S(1)}, bf16[64,256]{1,0:T(8,128)(2,1)S(1)}, u32[]{:S(2)}, u32[]{:S(2)}) collective-permute-start(bf16[64,256]{1,0:T(8,128)(2,1)S(1)} %get-tuple-element.47), channel_id=1, source_target_pairs={{0,8},{1,9},{2,10},{3,11},{4,12},{5,13},{6,14},{7,15},{8,0},{9,1},... | collective-permute-start | bytes 98312 | tf_op jit(solution)/shard_map/ppermute | solution.py:248
  33.2 9.0 %collective-permute-start.23 = (bf16[64,256]{1,0:T(8,128)(2,1)S(1)}, bf16[64,256]{1,0:T(8,128)(2,1)S(1)}, u32[]{:S(2)}, u32[]{:S(2)}) collective-permute-start(bf16[64,256]{1,0:T(8,128)(2,1)S(1)} %get-tuple-element.48), channel_id=1, source_target_pairs={{0,9},{1,8},{2,11},{3,10},{4,13},{5,12},{6,15},{7,14},{8,1},{9,0},... | collective-permute-start | bytes 98312 | tf_op jit(solution)/shard_map/ppermute | solution.py:248
  35.1 9.7 %collective-permute-start.24 = (bf16[64,256]{1,0:T(8,128)(2,1)S(1)}, bf16[64,256]{1,0:T(8,128)(2,1)S(1)}, u32[]{:S(2)}, u32[]{:S(2)}) collective-permute-start(bf16[64,256]{1,0:T(8,128)(2,1)S(1)} %get-tuple-element.49), channel_id=1, source_target_pairs={{0,10},{1,11},{2,8},{3,9},{4,14},{5,15},{6,12},{7,13},{8,2},{9,3},... | collective-permute-start | bytes 98312 | tf_op jit(solution)/shard_map/ppermute | solution.py:248
  36.6 21.7 %collective-permute-start.25 = (bf16[64,256]{1,0:T(8,128)(2,1)S(1)}, bf16[64,256]{1,0:T(8,128)(2,1)S(1)}, u32[]{:S(2)}, u32[]{:S(2)}) collective-permute-start(bf16[64,256]{1,0:T(8,128)(2,1)S(1)} %get-tuple-element.50), channel_id=1, source_target_pairs={{0,11},{1,10},{2,9},{3,8},{4,15},{5,14},{6,13},{7,12},{8,3},{9,2},... | collective-permute-start | bytes 98312 | tf_op jit(solution)/shard_map/ppermute | solution.py:248
  38.4 19.9 %collective-permute-start.26 = (bf16[64,256]{1,0:T(8,128)(2,1)S(1)}, bf16[64,256]{1,0:T(8,128)(2,1)S(1)}, u32[]{:S(2)}, u32[]{:S(2)}) collective-permute-start(bf16[64,256]{1,0:T(8,128)(2,1)S(1)} %get-tuple-element.51), channel_id=1, source_target_pairs={{0,12},{1,13},{2,14},{3,15},{4,8},{5,9},{6,10},{7,11},{8,4},{9,5},... | collective-permute-start | bytes 98312 | tf_op jit(solution)/shard_map/ppermute | solution.py:248
  40.1 18.2 %collective-permute-start.27 = (bf16[64,256]{1,0:T(8,128)(2,1)S(1)}, bf16[64,256]{1,0:T(8,128)(2,1)S(1)}, u32[]{:S(2)}, u32[]{:S(2)}) collective-permute-start(bf16[64,256]{1,0:T(8,128)(2,1)S(1)} %get-tuple-element.52), channel_id=1, source_target_pairs={{0,13},{1,12},{2,15},{3,14},{4,9},{5,8},{6,11},{7,10},{8,5},{9,4},... | collective-permute-start | bytes 98312 | tf_op jit(solution)/shard_map/ppermute | solution.py:248
  42.2 16.1 %collective-permute-start.28 = (bf16[64,256]{1,0:T(8,128)(2,1)S(1)}, bf16[64,256]{1,0:T(8,128)(2,1)S(1)}, u32[]{:S(2)}, u32[]{:S(2)}) collective-permute-start(bf16[64,256]{1,0:T(8,128)(2,1)S(1)} %get-tuple-element.53), channel_id=1, source_target_pairs={{0,14},{1,15},{2,12},{3,13},{4,10},{5,11},{6,8},{7,9},{8,6},{9,7},... | collective-permute-start | bytes 98312 | tf_op jit(solution)/shard_map/ppermute | solution.py:248
  44.8 13.6 %collective-permute-start.29 = (bf16[64,256]{1,0:T(8,128)(2,1)S(1)}, bf16[64,256]{1,0:T(8,128)(2,1)S(1)}, u32[]{:S(2)}, u32[]{:S(2)}) collective-permute-start(bf16[64,256]{1,0:T(8,128)(2,1)S(1)} %get-tuple-element.54), channel_id=1, source_target_pairs={{0,15},{1,14},{2,13},{3,12},{4,11},{5,10},{6,9},{7,8},{8,7},{9,6},... | collective-permute-start | bytes 98312 | tf_op jit(solution)/shard_map/ppermute | solution.py:248
  46.4 11.9 %copy-start = (s32[4096]{0:T(1024)S(1)}, s32[4096]{0:T(1024)}, u32[]{:S(2)}) copy-start(s32[4096]{0:T(1024)} %param.8) | copy-start | bytes 49156
  58.4 25.0 %copy-start.1 = (s32[2048]{0:T(1024)S(1)}, s32[2048]{0:T(1024)}, u32[]{:S(2)}) copy-start(s32[2048]{0:T(1024)} %param.11) | copy-start | bytes 24580
  62.7 4.2 %collective-permute-start.30 = (bf16[64,256]{1,0:T(8,128)(2,1)S(1)}, bf16[64,256]{1,0:T(8,128)(2,1)S(1)}, u32[]{:S(2)}, u32[]{:S(2)}) collective-permute-start(bf16[64,256]{1,0:T(8,128)(2,1)S(1)} %get-tuple-element.57), channel_id=1, source_target_pairs={{0,1},{1,0},{2,3},{3,2},{4,5},{5,4},{6,7},{7,6},{8,9},{9,8},{10,11... | collective-permute-start | bytes 98312 | tf_op jit(solution)/shard_map/ppermute | solution.py:248
  63.4 4.2 %collective-permute-start.31 = (bf16[64,256]{1,0:T(8,128)(2,1)S(1)}, bf16[64,256]{1,0:T(8,128)(2,1)S(1)}, u32[]{:S(2)}, u32[]{:S(2)}) collective-permute-start(bf16[64,256]{1,0:T(8,128)(2,1)S(1)} %get-tuple-element.58), channel_id=1, source_target_pairs={{0,2},{1,3},{2,0},{3,1},{4,6},{5,7},{6,4},{7,5},{8,10},{9,11},{10,... | collective-permute-start | bytes 98312 | tf_op jit(solution)/shard_map/ppermute | solution.py:248
  64.0 5.2 %collective-permute-start.32 = (bf16[64,256]{1,0:T(8,128)(2,1)S(1)}, bf16[64,256]{1,0:T(8,128)(2,1)S(1)}, u32[]{:S(2)}, u32[]{:S(2)}) collective-permute-start(bf16[64,256]{1,0:T(8,128)(2,1)S(1)} %get-tuple-element.59), channel_id=1, source_target_pairs={{0,3},{1,2},{2,1},{3,0},{4,7},{5,6},{6,5},{7,4},{8,11},{9,10},{10,... | collective-permute-start | bytes 98312 | tf_op jit(solution)/shard_map/ppermute | solution.py:248
  64.8 5.3 %collective-permute-start.33 = (bf16[64,256]{1,0:T(8,128)(2,1)S(1)}, bf16[64,256]{1,0:T(8,128)(2,1)S(1)}, u32[]{:S(2)}, u32[]{:S(2)}) collective-permute-start(bf16[64,256]{1,0:T(8,128)(2,1)S(1)} %get-tuple-element.60), channel_id=1, source_target_pairs={{0,4},{1,5},{2,6},{3,7},{4,0},{5,1},{6,2},{7,3},{8,12},{9,13},{10,... | collective-permute-start | bytes 98312 | tf_op jit(solution)/shard_map/ppermute | solution.py:248
  64.8 7.4 %collective-permute-start.34 = (bf16[64,256]{1,0:T(8,128)(2,1)S(1)}, bf16[64,256]{1,0:T(8,128)(2,1)S(1)}, u32[]{:S(2)}, u32[]{:S(2)}) collective-permute-start(bf16[64,256]{1,0:T(8,128)(2,1)S(1)} %get-tuple-element.61), channel_id=1, source_target_pairs={{0,5},{1,4},{2,7},{3,6},{4,1},{5,0},{6,3},{7,2},{8,13},{9,12},{10,... | collective-permute-start | bytes 98312 | tf_op jit(solution)/shard_map/ppermute | solution.py:248
  66.9 6.7 %collective-permute-start.35 = (bf16[64,256]{1,0:T(8,128)(2,1)S(1)}, bf16[64,256]{1,0:T(8,128)(2,1)S(1)}, u32[]{:S(2)}, u32[]{:S(2)}) collective-permute-start(bf16[64,256]{1,0:T(8,128)(2,1)S(1)} %get-tuple-element.62), channel_id=1, source_target_pairs={{0,6},{1,7},{2,4},{3,5},{4,2},{5,3},{6,0},{7,1},{8,14},{9,15},{10,... | collective-permute-start | bytes 98312 | tf_op jit(solution)/shard_map/ppermute | solution.py:248
  67.5 7.8 %collective-permute-start.36 = (bf16[64,256]{1,0:T(8,128)(2,1)S(1)}, bf16[64,256]{1,0:T(8,128)(2,1)S(1)}, u32[]{:S(2)}, u32[]{:S(2)}) collective-permute-start(bf16[64,256]{1,0:T(8,128)(2,1)S(1)} %get-tuple-element.63), channel_id=1, source_target_pairs={{0,7},{1,6},{2,5},{3,4},{4,3},{5,2},{6,1},{7,0},{8,15},{9,14},{10,... | collective-permute-start | bytes 98312 | tf_op jit(solution)/shard_map/ppermute | solution.py:248
  69.2 7.9 %collective-permute-start.37 = (bf16[64,256]{1,0:T(8,128)(2,1)S(1)}, bf16[64,256]{1,0:T(8,128)(2,1)S(1)}, u32[]{:S(2)}, u32[]{:S(2)}) collective-permute-start(bf16[64,256]{1,0:T(8,128)(2,1)S(1)} %get-tuple-element.64), channel_id=1, source_target_pairs={{0,8},{1,9},{2,10},{3,11},{4,12},{5,13},{6,14},{7,15},{8,0},{9,1},... | collective-permute-start | bytes 98312 | tf_op jit(solution)/shard_map/ppermute | solution.py:248
  70.1 9.2 %collective-permute-start.38 = (bf16[64,256]{1,0:T(8,128)(2,1)S(1)}, bf16[64,256]{1,0:T(8,128)(2,1)S(1)}, u32[]{:S(2)}, u32[]{:S(2)}) collective-permute-start(bf16[64,256]{1,0:T(8,128)(2,1)S(1)} %get-tuple-element.65), channel_id=1, source_target_pairs={{0,9},{1,8},{2,11},{3,10},{4,13},{5,12},{6,15},{7,14},{8,1},{9,0},... | collective-permute-start | bytes 98312 | tf_op jit(solution)/shard_map/ppermute | solution.py:248
  72.2 9.7 %collective-permute-start.39 = (bf16[64,256]{1,0:T(8,128)(2,1)S(1)}, bf16[64,256]{1,0:T(8,128)(2,1)S(1)}, u32[]{:S(2)}, u32[]{:S(2)}) collective-permute-start(bf16[64,256]{1,0:T(8,128)(2,1)S(1)} %get-tuple-element.66), channel_id=1, source_target_pairs={{0,10},{1,11},{2,8},{3,9},{4,14},{5,15},{6,12},{7,13},{8,2},{9,3},... | collective-permute-start | bytes 98312 | tf_op jit(solution)/shard_map/ppermute | solution.py:248
  73.6 22.9 %collective-permute-start.40 = (bf16[64,256]{1,0:T(8,128)(2,1)S(1)}, bf16[64,256]{1,0:T(8,128)(2,1)S(1)}, u32[]{:S(2)}, u32[]{:S(2)}) collective-permute-start(bf16[64,256]{1,0:T(8,128)(2,1)S(1)} %get-tuple-element.67), channel_id=1, source_target_pairs={{0,11},{1,10},{2,9},{3,8},{4,15},{5,14},{6,13},{7,12},{8,3},{9,2},... | collective-permute-start | bytes 98312 | tf_op jit(solution)/shard_map/ppermute | solution.py:248
  75.4 21.2 %collective-permute-start.41 = (bf16[64,256]{1,0:T(8,128)(2,1)S(1)}, bf16[64,256]{1,0:T(8,128)(2,1)S(1)}, u32[]{:S(2)}, u32[]{:S(2)}) collective-permute-start(bf16[64,256]{1,0:T(8,128)(2,1)S(1)} %get-tuple-element.68), channel_id=1, source_target_pairs={{0,12},{1,13},{2,14},{3,15},{4,8},{5,9},{6,10},{7,11},{8,4},{9,5},... | collective-permute-start | bytes 98312 | tf_op jit(solution)/shard_map/ppermute | solution.py:248
  77.1 19.4 %collective-permute-start.42 = (bf16[64,256]{1,0:T(8,128)(2,1)S(1)}, bf16[64,256]{1,0:T(8,128)(2,1)S(1)}, u32[]{:S(2)}, u32[]{:S(2)}) collective-permute-start(bf16[64,256]{1,0:T(8,128)(2,1)S(1)} %get-tuple-element.69), channel_id=1, source_target_pairs={{0,13},{1,12},{2,15},{3,14},{4,9},{5,8},{6,11},{7,10},{8,5},{9,4},... | collective-permute-start | bytes 98312 | tf_op jit(solution)/shard_map/ppermute | solution.py:248
  79.3 17.3 %collective-permute-start.43 = (bf16[64,256]{1,0:T(8,128)(2,1)S(1)}, bf16[64,256]{1,0:T(8,128)(2,1)S(1)}, u32[]{:S(2)}, u32[]{:S(2)}) collective-permute-start(bf16[64,256]{1,0:T(8,128)(2,1)S(1)} %get-tuple-element.70), channel_id=1, source_target_pairs={{0,14},{1,15},{2,12},{3,13},{4,10},{5,11},{6,8},{7,9},{8,6},{9,7},... | collective-permute-start | bytes 98312 | tf_op jit(solution)/shard_map/ppermute | solution.py:248
  81.9 14.7 %collective-permute-start.44 = (bf16[64,256]{1,0:T(8,128)(2,1)S(1)}, bf16[64,256]{1,0:T(8,128)(2,1)S(1)}, u32[]{:S(2)}, u32[]{:S(2)}) collective-permute-start(bf16[64,256]{1,0:T(8,128)(2,1)S(1)} %get-tuple-element.71), channel_id=1, source_target_pairs={{0,15},{1,14},{2,13},{3,12},{4,11},{5,10},{6,9},{7,8},{8,7},{9,6},... | collective-permute-start | bytes 98312 | tf_op jit(solution)/shard_map/ppermute | solution.py:248

commit v5 on v2

--- a/solution.py
+++ b/solution.py
@@ -23,27 +23,31 @@
     return -(-value // multiple) * multiple
 
 
-def prepare_kernel(parts, corr_ref, points_ref, turned_ref, packets_ref):
+def split_in_two(values):
+    high = values.astype(jnp.bfloat16).astype(jnp.float32)
+    return [high, values - high]
+
+
+def prepare_kernel(corr_ref, points_ref, turned_ref, sent_ref):
     turned = corr_ref[...].astype(jnp.float32).T
-    turned_ref[...] = turned.astype(jnp.bfloat16)
     squares = jnp.sum(turned * turned, axis=0, keepdims=True)
-    rows = points_ref.shape[0] // parts
-    pieces = [
-        jnp.concatenate(
-            [points_ref[part * rows : (part + 1) * rows, :] for part in range(parts)],
-            axis=1,
-        )
-    ]
-    pieces += [
-        squares[:, part * LANES : (part + 1) * LANES]
-        for part in range(squares.shape[1] // LANES)
-    ]
-    used = rows + len(pieces) - 1
-    if packets_ref.shape[1] > used:
-        pieces.append(jnp.zeros((packets_ref.shape[1] - used, LANES), jnp.float32))
-    packet = jnp.concatenate(pieces, axis=0)
-    for i in range(packets_ref.shape[0]):
-        packets_ref[i] = packet
+    devices, sent_rows, terms = sent_ref.shape
+    count = turned.shape[0] // devices
+    dim, runs = points_ref.shape
+    rows = dim * runs // terms
+    points = jnp.concatenate(
+        [points_ref[start : start + rows, :] for start in range(0, dim, rows)], axis=1
+    )
+    pieces = split_in_two(points) + split_in_two(squares)
+    used = 2 * rows + 2
+    if sent_rows - count > used:
+        pieces.append(jnp.zeros((sent_rows - count - used, terms), jnp.float32))
+    packet = jnp.concatenate(pieces, axis=0).astype(jnp.bfloat16)
+    for i in range(devices):
+        block = turned[i * count : (i + 1) * count, :].astype(jnp.bfloat16)
+        turned_ref[i * count : (i + 1) * count, :] = block
+        sent_ref[i, 0:count, :] = block
+        sent_ref[i, count:sent_rows, :] = packet
 
 
 def hermite_columns(points):
@@ -60,29 +64,30 @@
     )
 
 
-def design_kernel(dim, run_count, packets_ref, codes_ref, design_ref, table, chosen):
-    devices = packets_ref.shape[0]
-    half = table.shape[1] // 2
-    parts = LANES // run_count
-    rows = dim // parts
+def design_kernel(
+    dim, run_count, count, blocks_ref, codes_ref, design_ref, exact, table, chosen
+):
+    devices = blocks_ref.shape[0]
+    half = exact.shape[1]
+    rows = dim * run_count // blocks_ref.shape[2]
 
     @pl.when(pl.program_id(0) == 0)
     def _():
-        for group in range(devices // parts):
+        per = LANES // run_count
+        for group in range(devices // per):
+            owned = []
+            for i in range(per):
+                packet = blocks_ref[
+                    group * per + i, count : blocks_ref.shape[1], :
+                ].astype(jnp.float32)
+                owned.append(packet[0:rows, :] + packet[rows : 2 * rows, :])
             points = jnp.concatenate(
                 [
                     jnp.concatenate(
-                        [
-                            packets_ref[
-                                group * parts + i,
-                                0:rows,
-                                part * run_count : (part + 1) * run_count,
-                            ]
-                            for i in range(parts)
-                        ],
+                        [inputs[:, start : start + run_count] for inputs in owned],
                         axis=1,
                     )
-                    for part in range(parts)
+                    for start in range(0, blocks_ref.shape[2], run_count)
                 ],
                 axis=0,
             )
@@ -97,6 +102,7 @@
             high = columns.astype(jnp.bfloat16)
             low = (columns - high.astype(jnp.float32)).astype(jnp.bfloat16)
             block = slice(group * LANES, (group + 1) * LANES)
+            exact[block, :] = columns
             table[block, 0:half] = high
             table[block, half : 2 * half] = low
 
@@ -104,7 +110,8 @@
     spots = (codes % DEGREES) * dim + codes // DEGREES
     slots, terms = codes.shape
     row = lax.broadcasted_iota(jnp.int32, (half, terms), 0)
-    for slot in range(slots):
+    matmuls = chosen.shape[0]
+    for slot in range(matmuls):
         picked = jnp.where(row == spots[slot : slot + 1, :], 1.0, 0.0).astype(
             jnp.bfloat16
         )
@@ -112,24 +119,28 @@
         chosen[slot, half : 2 * half, :] = picked
     for start in range(0, table.shape[0], LANES):
         block = slice(start, start + LANES)
+        rows = exact[block, :]
         product = None
-        for slot in range(slots):
+        for slot in range(matmuls):
             factor = jnp.dot(
                 table[block, :], chosen[slot], preferred_element_type=jnp.float32
             )
             product = factor if product is None else product * factor
-        design_ref[block, :] = product.astype(jnp.bfloat16)
-
-
-def penalty_rows(first_row, term_count, packets_ref, levels_ref):
-    squares = jnp.concatenate(
-        [
-            packets_ref[i, first_row + part : first_row + part + 1, :]
-            for i in range(packets_ref.shape[0])
-            for part in range(term_count // LANES)
-        ],
-        axis=1,
-    )
+        for part in range(0, terms, half):
+            lanes = slice(part, part + half)
+            factor = product[:, lanes]
+            for slot in range(matmuls, slots):
+                spot = jnp.broadcast_to(spots[slot : slot + 1, lanes], rows.shape)
+                factor = factor * jnp.take_along_axis(rows, spot, axis=1)
+            design_ref[block, lanes] = factor.astype(jnp.bfloat16)
+
+
+def penalty_rows(count, row, blocks_ref, levels_ref):
+    rows = []
+    for i in range(blocks_ref.shape[0]):
+        packet = blocks_ref[i, count : blocks_ref.shape[1], :].astype(jnp.float32)
+        rows.append(packet[row : row + 1, :] + packet[row + 1 : row + 2, :])
+    squares = jnp.concatenate(rows, axis=1)
     weights = jnp.exp2(levels_ref[...].astype(jnp.float32))
     ratio = jnp.max(jnp.sqrt(squares) / weights, axis=1, keepdims=True)
     return squares, weights, LAMBDA_FRACTION * ratio
@@ -140,27 +151,19 @@
 
 
 def fit_kernel(
-    first_row,
-    total_runs,
-    packets_ref,
-    levels_ref,
-    corr_ref,
-    design_ref,
-    summed_ref,
-    scale_ref,
-    first_ref,
-):
-    devices, _, term_count = corr_ref.shape
-    squares, weights, penalty = penalty_rows(
-        first_row, term_count, packets_ref, levels_ref
-    )
+    row, total_runs, levels_ref, blocks_ref, design_ref, summed_ref, scale_ref, first_ref
+):
+    devices, count, term_count = summed_ref.shape
+    squares, weights, penalty = penalty_rows(count, row, blocks_ref, levels_ref)
     limits = STEP * penalty * weights
     factor = shrink_factor(STEP * STEP * squares, limits)
     scale_ref[0:1, :] = factor
     scale_ref[1:2, :] = limits
     for i in range(devices):
         terms = slice(i * term_count, (i + 1) * term_count)
-        first = STEP * corr_ref[i].astype(jnp.float32) * factor[:, terms]
+        first = (
+            STEP * blocks_ref[i, 0:count, :].astype(jnp.float32) * factor[:, terms]
+        )
         first_ref[:, terms] = first.astype(jnp.bfloat16)
     fitted = lax.dot_general(
         first_ref[...],
@@ -203,9 +206,21 @@
     values,
     half,
     lifted,
+    held,
+    held_sem,
     out_sem,
     lifted_sem,
 ):
+    width = lifted.shape[2]
+    loads = []
+    for i in range(lifted.shape[0]):
+        block = slice(i * width, (i + 1) * width)
+        loads.append(
+            pltpu.make_async_copy(
+                modes_ref.at[:, block], held.at[:, block], held_sem.at[i]
+            )
+        )
+        loads[-1].start()
     modes, terms = corr_ref.shape
     squares = jnp.zeros((1, terms), jnp.float32)
     for start in range(0, modes, LANES):
@@ -224,11 +239,11 @@
         half[:, block] = turned.astype(jnp.bfloat16)
     copies = [pltpu.make_async_copy(values, out_ref, out_sem)]
     copies[0].start()
-    width = lifted.shape[2]
     for i in range(lifted.shape[0]):
         block = slice(i * width, (i + 1) * width)
+        loads[i].wait()
         lifted[i] = jnp.dot(
-            half[...], modes_ref[:, block], preferred_element_type=jnp.float32
+            half[...], held[:, block], preferred_element_type=jnp.float32
         ).astype(jnp.bfloat16)
         copies.append(
             pltpu.make_async_copy(
@@ -240,6 +255,10 @@
         copy.wait()
 
 
+def in_hbm(array):
+    return pltpu.with_memory_space_constraint(array, pltpu.HBM)
+
+
 def params(limit):
     return pltpu.CompilerParams(vmem_limit_bytes=limit * MIB)
 
@@ -256,53 +275,53 @@
     total_runs = run_count * devices
     own_modes = modes // devices
     offset = lax.axis_index("runs") * term_count
-    parts = LANES // run_count
-    first_row = dim // parts
-    packet_rows = round_up(first_row + term_count // LANES, 8)
-
-    turned, packets = pl.pallas_call(
-        functools.partial(prepare_kernel, parts),
+    rows = dim * run_count // term_count
+    sent_rows = round_up(own_modes + 2 * rows + 2, 16)
+    vmem = pl.BlockSpec(memory_space=pltpu.VMEM)
+    anywhere = pl.BlockSpec(memory_space=pl.ANY)
+
+    turned, sent = pl.pallas_call(
+        prepare_kernel,
         out_shape=(
             jax.ShapeDtypeStruct((modes, term_count), jnp.bfloat16),
-            jax.ShapeDtypeStruct((devices, packet_rows, LANES), jnp.float32),
+            jax.ShapeDtypeStruct((devices, sent_rows, term_count), jnp.bfloat16),
         ),
         compiler_params=params(16),
         name="prepare",
-    )(correlations, run_inputs.T)
-    packets = lax.all_to_all(packets, "runs", 0, 0, tiled=False)
-    blocks = lax.all_to_all(
-        turned.reshape(devices, own_modes, term_count), "runs", 0, 0, tiled=False
-    )
+    )(in_hbm(correlations), in_hbm(run_inputs.T))
+    blocks = lax.all_to_all(sent, "runs", 0, 0, tiled=False)
 
     tile = term_count
     half = round_up(DEGREES * dim, LANES)
     design = pl.pallas_call(
-        functools.partial(design_kernel, dim, run_count),
+        functools.partial(design_kernel, dim, run_count, own_modes),
         grid=(terms // tile,),
         in_specs=[
-            pl.BlockSpec((devices, packet_rows, LANES), lambda i: (0, 0, 0)),
+            pl.BlockSpec((devices, sent_rows, term_count), lambda i: (0, 0, 0)),
             pl.BlockSpec((slots, tile), lambda i: (0, i)),
         ],
         out_specs=pl.BlockSpec((total_runs, tile), lambda i: (0, i)),
         out_shape=jax.ShapeDtypeStruct((total_runs, terms), jnp.bfloat16),
         scratch_shapes=[
+            pltpu.VMEM((total_runs, half), jnp.float32),
             pltpu.VMEM((total_runs, 2 * half), jnp.bfloat16),
-            pltpu.VMEM((slots, 2 * half, tile), jnp.bfloat16),
+            pltpu.VMEM((slots - slots // 4, 2 * half, tile), jnp.bfloat16),
         ],
         compiler_params=params(16),
         name="design",
-    )(packets, term_codes.T)
+    )(blocks, in_hbm(term_codes.T))
 
     summed, scale = pl.pallas_call(
-        functools.partial(fit_kernel, first_row, float(total_runs)),
+        functools.partial(fit_kernel, 2 * rows, float(total_runs)),
+        in_specs=[vmem, vmem, vmem],
         out_shape=(
             jax.ShapeDtypeStruct((devices, own_modes, term_count), jnp.bfloat16),
             jax.ShapeDtypeStruct((8, terms), jnp.float32),
         ),
         scratch_shapes=[pltpu.VMEM((own_modes, terms), jnp.bfloat16)],
-        compiler_params=params(20),
+        compiler_params=params(24),
         name="fit",
-    )(packets, weight_levels[None, :], blocks, design)
+    )(weight_levels[None, :], blocks, design)
     own_scale = lax.dynamic_slice_in_dim(scale, offset, term_count, 1)
     returned = lax.all_to_all(summed, "runs", 0, 0, tiled=False).reshape(
         modes, term_count
@@ -317,17 +336,15 @@
             pl.BlockSpec((cells, modes), lambda i: (0, 0)),
         ],
         out_specs=pl.BlockSpec((modes, block), lambda i: (0, i)),
-        out_shape=jax.ShapeDtypeStruct((modes, slab_cells), jnp.bfloat16),
+        out_shape=pltpu.HBM((modes, slab_cells), jnp.bfloat16),
         scratch_shapes=[pltpu.VMEM((modes, cells), jnp.bfloat16)],
         compiler_params=params(24),
         name="reorder",
-    )(cell_map[None, :], slab_modes)
-
-    vmem = pl.BlockSpec(memory_space=pltpu.VMEM)
-    anywhere = pl.BlockSpec(memory_space=pl.ANY)
+    )(cell_map[None, :], in_hbm(slab_modes))
+
     return pl.pallas_call(
         finish_kernel,
-        in_specs=[vmem, vmem, vmem, vmem],
+        in_specs=[vmem, vmem, vmem, anywhere],
         out_specs=(anywhere, anywhere),
         out_shape=(
             jax.ShapeDtypeStruct((term_count, modes), jnp.float32),
@@ -338,12 +355,14 @@
             pltpu.VMEM((term_count, modes), jnp.float32),
             pltpu.VMEM((term_count, modes), jnp.bfloat16),
             pltpu.VMEM((slab_cells // block, term_count, block), jnp.bfloat16),
+            pltpu.VMEM((modes, slab_cells), jnp.bfloat16),
+            pltpu.SemaphoreType.DMA((slab_cells // block,)),
             pltpu.SemaphoreType.DMA,
             pltpu.SemaphoreType.DMA((slab_cells // block,)),
         ],
         compiler_params=params(20),
         name="finish",
-    )(returned, turned, own_scale, ordered)
+    )(returned, turned, own_scale, in_hbm(ordered))
 
 
 def hermite_table(points):
@@ -424,10 +443,12 @@
     term_count, modes = correlations.shape
     whole_tiles = (
         modes % (16 * devices) == 0
+        and DEGREES * run_inputs.shape[1] <= LANES
         and term_count % LANES == 0
         and LANES % run_count == 0
         and devices % (LANES // run_count) == 0
-        and run_inputs.shape[1] % (LANES // run_count) == 0
+        and term_count % run_count == 0
+        and run_inputs.shape[1] % (term_count // run_count) == 0
         and slab_modes.shape[0] % LANES == 0
         and cell_map.shape[0] % LANES == 0
     )

time: 75.9 us -> 67.5 us (0.89)
  local copies, waits for them, and re-layouts: 15.5 us -> 0.01 us
  blocking collectives: 15.1 us -> 25.4 us
  starting transfers between devices: 9.54 us -> 3.57 us
  Pallas kernels: 34.3 us -> 36.6 us
    unnamed x20 -> x4, local copies, waits for them, and re-layouts: 15.5 us -> 0.01 us
    all_to_all x1, blocking collectives: 15.1 us -> 25.4 us  [split_by_modes(): blocks = lax.all_to_all(sent, 'runs', 0, 0, tiled=False)]
    all_to_all x1 -> x0, starting transfers between devices: 3.57 us -> none  [split_by_modes(): lax.all_to_all(turned.reshape(devices, own_modes, term_count), 'runs', 0,...]
    pallas_call x1, Pallas kernels: 11 us -> 14 us  [split_by_modes(): pl.pallas_call(reorder_kernel, grid=(slab_cells // block,), in_specs=[pl....]
    all_to_all x1, starting transfers between devices: 5.97 us -> 3.57 us  [split_by_modes(): lax.all_to_all(summed, 'runs', 0, 0, tiled=False).reshape(modes, term_count)]
    pallas_call x4, Pallas kernels: 23.4 us -> 22.6 us  [the longest x1 11.8 us: split_by_modes(): pl.pallas_call(functools.partial(design_kernel, dim, run_count, own_modes...]
  transfers between devices with their start and end apart: 2 -> 1, of which waited for: 0 -> 1; matrix products, arithmetic and copies ran while one was open for 0% -> 0% of each run, Pallas kernels for 33% -> 21%
where the time goes in v5:
time: 67.5 us; the launch traced here: 66.7 us
  Pallas kernels  36.6 us (54%)
  blocking collectives  25.4 us (38%)
  starting transfers between devices  3.57 us (5%)
  between operations  0.68 us (1%)
    all_to_all x1, blocking collectives, split_by_modes(): blocks = lax.all_to_all(sent, 'runs', 0, 0, tiled=False)  25.4 us
    pallas_call x1, Pallas kernels, split_by_modes(): pl.pallas_call(reorder_kernel, grid=(slab_cells // block,), in_specs=[pl....  14 us
    pallas_call x1, Pallas kernels, split_by_modes(): pl.pallas_call(functools.partial(design_kernel, dim, run_count, own_modes...  11.8 us
    pallas_call x1, Pallas kernels, split_by_modes(): pl.pallas_call(functools.partial(fit_kernel, 2 * rows, float(total_runs))...  5.06 us
    pallas_call x1, Pallas kernels, split_by_modes(): pl.pallas_call(finish_kernel, in_specs=[vmem, vmem, vmem, anywhere], out_...  4.38 us
    all_to_all x1, starting transfers between devices, split_by_modes(): lax.all_to_all(summed, 'runs', 0, 0, tiled=False).reshape(modes, term_count)  3.57 us
  transfers between devices with their start and end apart: 1, of which 1 were waited for; matrix products, arithmetic and copies ran while one was open for 0% of the time, Pallas kernels for 21%

profile of v5, /device:TPU:0, one launch (start us, length us, event | category | flops | bytes accessed | tf_op | source)
XLA Modules:
  0.0 66.7 jit_solution(15562004121758098753)
XLA Ops:
  0.6 1.3 %prepare.1 = (bf16[1024,256]{1,0:T(8,128)(2,1)S(1)}, bf16[16,80,256]{2,1,0:T(8,128)(2,1)S(1)}) custom-call(bf16[256,1024]{1,0:T(8,128)(2,1)} %corr_ref.1, f32[24,64]{1,0:T(8,128)} %bitcast.9), custom_call_target="tpu_custom_call" | custom-call | tf_op jit(solution)/shard_map/prepare/pallas_call | solution.py:283
  2.0 25.4 %all_to_all.10.blocks_ref = bf16[16,80,256]{2,1,0:T(8,128)(2,1)S(1)} all-to-all(bf16[16,80,256]{2,1,0:T(8,128)(2,1)S(1)} %get-tuple-element.6), channel_id=1, replica_groups=mesh['cases'=2,'runs'=16] {'runs'}, dimensions={0} | all-to-all | bytes 1310720 | tf_op jit(solution)/shard_map/all_to_all | solution.py:292
  27.4 0.0 copy-start
  27.4 11.8 %design.1.design_ref = bf16[1024,4096]{1,0:T(8,128)(2,1)S(1)} custom-call(bf16[16,80,256]{2,1,0:T(8,128)(2,1)S(1)} %all_to_all.10.blocks_ref, s32[4,4096]{1,0:T(4,128)} %bitcast.8), custom_call_target="tpu_custom_call" | custom-call | tf_op jit(solution)/shard_map/design/pallas_call | solution.py:296
  39.2 0.0 copy-done
  39.2 0.0 copy-start.1
  39.2 5.1 %fit.1 = (bf16[16,64,256]{2,1,0:T(8,128)(2,1)}, f32[8,4096]{1,0:T(8,128)S(1)}) custom-call(s32[1,4096]{1,0:T(1,128)S(1)} %bitcast.6, bf16[16,80,256]{2,1,0:T(8,128)(2,1)S(1)} %all_to_all.10.blocks_ref, bf16[1024,4096]{1,0:T(8,128)(2,1)S(1)} %design.1.design_ref), custom_call_target="tpu_custom_call" | custom-call | tf_op jit(solution)/shard_map/fit/pallas_call | solution.py:314
  44.3 3.6 %all-to-all-start.1 = ((bf16[16,64,256]{2,1,0:T(8,128)(2,1)}), bf16[16,64,256]{2,1,0:T(8,128)(2,1)S(1)}, u32[]{:S(2)}, u32[]{:S(2)}) async-start(bf16[16,64,256]{2,1,0:T(8,128)(2,1)} %get-tuple-element.7), calls=%async_computation.1 | async-start | bytes 1048576 | tf_op jit(solution)/shard_map/all_to_all | solution.py:326
  47.8 0.0 copy-done.1
  47.9 14.0 %reorder.1.modes_ref = bf16[1024,2048]{1,0:T(8,128)(2,1)} custom-call(s32[1,2048]{1,0:T(1,128)S(1)} %bitcast.7, bf16[2048,1024]{1,0:T(8,128)(2,1)} %slab_ref.1), custom_call_target="tpu_custom_call" | custom-call | tf_op jit(solution)/shard_map/reorder/pallas_call | solution.py:331
  61.8 0.4 all-to-all-done.1
  62.3 4.4 %finish.1 = (f32[256,1024]{1,0:T(8,128)}, bf16[256,2048]{1,0:T(8,128)(2,1)}) custom-call(bf16[1024,256]{1,0:T(8,128)(2,1)S(1)} %bitcast.5, bf16[1024,256]{1,0:T(8,128)(2,1)S(1)} %get-tuple-element.8.corr_ref, f32[8,256]{1,0:T(8,128)S(1)} %constant_dynamic-slice_fusion.scale_ref, bf16[1024,2048]{1,0:T(8,128)(2,1)} %reorder.1.modes_ref), custom_call_target="tpu_custom_call" | custom-call | tf_op jit(solution)/shard_map/finish/pallas_call | solution.py:345
  (1 shorter events, 0.0 us)
Async XLA Ops:
  27.4 11.8 %copy-start = (s32[4096]{0:T(1024)S(1)}, s32[4096]{0:T(1024)}, u32[]{:S(2)}) copy-start(s32[4096]{0:T(1024)} %param.8) | copy-start | bytes 49156
  39.2 8.7 %copy-start.1 = (s32[2048]{0:T(1024)S(1)}, s32[2048]{0:T(1024)}, u32[]{:S(2)}) copy-start(s32[2048]{0:T(1024)} %param.11) | copy-start | bytes 24580
  44.3 18.0 %all-to-all-start.1 = ((bf16[16,64,256]{2,1,0:T(8,128)(2,1)}), bf16[16,64,256]{2,1,0:T(8,128)(2,1)S(1)}, u32[]{:S(2)}, u32[]{:S(2)}) async-start(bf16[16,64,256]{2,1,0:T(8,128)(2,1)} %get-tuple-element.7), calls=%async_computation.1 | async-start | bytes 1048576 | tf_op jit(solution)/shard_map/all_to_all | solution.py:326

commit v6 on v4

v6 whole, which is shorter than its diff:
```python
import functools
import math

import jax
import jax.numpy as jnp
from jax import lax
from jax.experimental import pallas as pl
from jax.experimental.pallas import tpu as pltpu
from jax.sharding import PartitionSpec as P

STEP = 0.5
LAMBDA_FRACTION = 0.05
EPSILON = 1e-06
DEGREES = 5
LANES = 128
CORES = 2
ROOT_TWO = math.sqrt(2.0)
ROOT_SIX = math.sqrt(6.0)
ROOT_TWENTYFOUR = math.sqrt(24.0)
MIB = 1 << 20


def round_up(value, multiple):
    return -(-value // multiple) * multiple


def split_in_two(values):
    high = values.astype(jnp.bfloat16).astype(jnp.float32)
    return [high, values - high]


def rows_of(index, count):
    return pl.ds(pl.multiple_of(index * count, count), count)


def prepare_kernel(me_ref, corr_ref, points_ref, turned_ref, *sent_refs):
    turned = corr_ref[...].astype(jnp.float32).T
    turned_ref[...] = turned.astype(jnp.bfloat16)
    squares = jnp.sum(turned * turned, axis=0, keepdims=True)
    sent_rows, terms = sent_refs[0].shape
    count = turned.shape[0] // len(sent_refs)
    dim, runs = points_ref.shape
    rows = dim * runs // terms
    points = jnp.concatenate(
        [points_ref[start : start + rows, :] for start in range(0, dim, rows)], axis=1
    )
    pieces = split_in_two(points) + split_in_two(squares)
    used = 2 * rows + 2
    if sent_rows - count > used:
        pieces.append(jnp.zeros((sent_rows - count - used, terms), jnp.float32))
    packet = jnp.concatenate(pieces, axis=0).astype(jnp.bfloat16)
    for k, sent_ref in enumerate(sent_refs):
        chip = (me_ref[0] // CORES) ^ k
        sent_ref[0:count, :] = turned_ref[rows_of(chip, count), :]
        sent_ref[count:sent_rows, :] = packet


def split_in_two(values):
    high = values.astype(jnp.bfloat16).astype(jnp.float32)
    return [high, values - high]


def hermite_columns(points):
    squared = points * points
    return jnp.concatenate(
        [
            jnp.ones_like(points),
            points,
            (squared - 1.0) / ROOT_TWO,
            points * (squared - 3.0) / ROOT_SIX,
            (squared * squared - 6.0 * squared + 3.0) / ROOT_TWENTYFOUR,
        ],
        axis=0,
    )


def design_kernel(dim, run_count, me_ref, codes_ref, own_ref, other_ref, *refs):
    design_ref, exact, table, chosen = refs[-4:]
    chips, _, terms = own_ref.shape
    half = exact.shape[1]
    rows = dim * run_count // terms
    core = me_ref[0] % CORES

    @pl.when(pl.program_id(0) == 0)
    def _():
        per = LANES // run_count
        sources = [
            (packets_ref, group, base)
            for packets_ref, base in ((own_ref, core), (other_ref, 1 - core))
            for group in range(chips // per)
        ]
        for packets_ref, group, base in sources:
            owned = []
            for i in range(per):
                packet = packets_ref[group * per + i].astype(jnp.float32)
                owned.append(packet[0:rows, :] + packet[rows : 2 * rows, :])
            points = jnp.concatenate(
                [
                    jnp.concatenate(
                        [inputs[:, start : start + run_count] for inputs in owned],
                        axis=1,
                    )
                    for start in range(0, terms, run_count)
                ],
                axis=0,
            )
            columns = hermite_columns(points)
            columns = jnp.concatenate(
                [
                    columns,
                    jnp.zeros((half - columns.shape[0], LANES), jnp.float32),
                ],
                axis=0,
            ).T
            high = columns.astype(jnp.bfloat16)
            low = (columns - high.astype(jnp.float32)).astype(jnp.bfloat16)
            block = rows_of(base * (chips // per) + group, LANES)
            exact[block, :] = columns
            table[block, 0:half] = high
            table[block, half : 2 * half] = low

    codes = codes_ref[...]
    spots = (codes % DEGREES) * dim + codes // DEGREES
    slots, terms = codes.shape
    row = lax.broadcasted_iota(jnp.int32, (half, terms), 0)
    matmuls = chosen.shape[0]
    for slot in range(matmuls):
        picked = jnp.where(row == spots[slot : slot + 1, :], 1.0, 0.0).astype(
            jnp.bfloat16
        )
        chosen[slot, 0:half, :] = picked
        chosen[slot, half : 2 * half, :] = picked
    for start in range(0, table.shape[0], LANES):
        block = slice(start, start + LANES)
        rows = exact[block, :]
        product = None
        for slot in range(matmuls):
            factor = jnp.dot(
                table[block, :], chosen[slot], preferred_element_type=jnp.float32
            )
            product = factor if product is None else product * factor
        for part in range(0, terms, half):
            lanes = slice(part, part + half)
            factor = product[:, lanes]
            for slot in range(matmuls, slots):
                spot = jnp.broadcast_to(spots[slot : slot + 1, lanes], rows.shape)
                factor = factor * jnp.take_along_axis(rows, spot, axis=1)
            design_ref[block, lanes] = factor.astype(jnp.bfloat16)


def shrink_factor(squares, limits):
    return jnp.maximum(0.0, 1.0 - limits / jnp.sqrt(squares + EPSILON))


def rows_and_weights(row, first, packets_ref, levels_ref):
    squares, levels = [], []
    for k in range(packets_ref.shape[0]):
        packet = packets_ref[k].astype(jnp.float32)
        squares.append(packet[row : row + 1, :] + packet[row + 1 : row + 2, :])
        device = first ^ (CORES * k)
        levels.append(levels_ref[:, rows_of(device, packets_ref.shape[2])])
    weights = jnp.exp2(jnp.concatenate(levels, axis=1).astype(jnp.float32))
    return jnp.concatenate(squares, axis=1), weights


def fit_kernel(row, me_ref, levels_ref, own_ref, other_ref, design_ref, *refs):
    *block_refs, fitted_ref, scale_ref, first_ref = refs
    count = fitted_ref.shape[0]
    term_count = own_ref.shape[2]
    me = me_ref[0]
    squares, weights = rows_and_weights(row, me, own_ref, levels_ref)
    others, other_weights = rows_and_weights(row, me ^ 1, other_ref, levels_ref)
    ratio = jnp.maximum(
        jnp.max(jnp.sqrt(squares) / weights, axis=1, keepdims=True),
        jnp.max(jnp.sqrt(others) / other_weights, axis=1, keepdims=True),
    )
    limits = STEP * (LAMBDA_FRACTION * ratio) * weights
    factor = shrink_factor(STEP * STEP * squares, limits)
    scale_ref[0:1, :] = factor[:, 0:term_count]
    scale_ref[1:2, :] = limits[:, 0:term_count]
    for k, block_ref in enumerate(block_refs):
        terms = slice(k * term_count, (k + 1) * term_count)
        first = STEP * block_ref[0:count, :].astype(jnp.float32) * factor[:, terms]
        first_ref[:, terms] = first.astype(jnp.bfloat16)
    fitted_ref[...] = lax.dot_general(
        first_ref[...],
        design_ref[...],
        (((1,), (1,)), ((), ())),
        preferred_element_type=jnp.float32,
    )


def sum_kernel(total_runs, own_ref, other_ref, design_ref, *summed_refs):
    fitted = (own_ref[...] + other_ref[...]).astype(jnp.bfloat16)
    term_count = summed_refs[0].shape[1]
    for k, summed_ref in enumerate(summed_refs):
        terms = slice(k * term_count, (k + 1) * term_count)
        summed = jnp.dot(
            fitted, design_ref[:, terms], preferred_element_type=jnp.float32
        )
        summed_ref[...] = (summed / total_runs).astype(jnp.bfloat16)


def reorder_kernel(map_ref, slab_ref, *refs):
    modes_ref = refs[-1]
    cells, block = slab_ref.shape[0], modes_ref.shape[0]
    row = lax.broadcasted_iota(jnp.int32, (cells, block), 0)
    chosen = jnp.where(row == map_ref[...], 1.0, 0.0).astype(jnp.bfloat16)
    modes_ref[...] = lax.dot_general(
        chosen,
        slab_ref[...],
        (((0,), (0,)), ((), ())),
        preferred_element_type=jnp.float32,
    ).astype(jnp.bfloat16)


def finish_kernel(pieces, me_ref, corr_ref, scale_ref, *refs):
    modes_refs, refs = refs[:pieces], refs[pieces:]
    *summed_refs, out_ref, lifted_ref, moved, values, half, lifted, out_sem, sems = refs
    modes, terms = corr_ref.shape
    count = summed_refs[0].shape[0]
    squares = jnp.zeros((1, terms), jnp.float32)
    for k, summed_ref in enumerate(summed_refs):
        rows = rows_of((me_ref[0] // CORES) ^ k, count)
        corr = corr_ref[rows, :].astype(jnp.float32)
        first = STEP * corr * scale_ref[0:1, :]
        gradient = summed_ref[...].astype(jnp.float32) - corr
        step = first - STEP * gradient
        moved[rows, :] = step
        squares = squares + jnp.sum(step * step, axis=0, keepdims=True)
    factor = shrink_factor(squares, scale_ref[1:2, :])
    for start in range(0, modes, LANES):
        block = slice(start, start + LANES)
        turned = (moved[block, :] * factor).T
        values[:, block] = turned
        half[:, block] = turned.astype(jnp.bfloat16)
    copies = [pltpu.make_async_copy(values, out_ref, out_sem)]
    copies[0].start()
    width = lifted.shape[2]
    for i, modes_ref in enumerate(modes_refs):
        block = slice(i * width, (i + 1) * width)
        lifted[i] = lax.dot_general(
            half[...],
            modes_ref[...],
            (((1,), (1,)), ((), ())),
            preferred_element_type=jnp.float32,
        ).astype(jnp.bfloat16)
        copies.append(
            pltpu.make_async_copy(lifted.at[i], lifted_ref.at[:, block], sems.at[i])
        )
        copies[-1].start()
    for copy in copies:
        copy.wait()


def in_hbm(array):
    return pltpu.with_memory_space_constraint(array, pltpu.HBM)


def params(limit):
    return pltpu.CompilerParams(vmem_limit_bytes=limit * MIB)


def cost(flops, moved):
    return pl.CostEstimate(flops=flops, bytes_accessed=moved, transcendentals=0)


def to_device(array, bits):
    devices = lax.axis_size("runs")
    return lax.ppermute(array, "runs", [(i, i ^ bits) for i in range(devices)])


def to_chips(arrays):
    moved = {0: arrays[0]}
    chips = len(arrays)
    for k in [*range(chips // 2, chips), *range(1, chips // 2)]:
        moved[k] = to_device(arrays[k], CORES * k)
    return [moved[k] for k in range(chips)]


def split_by_modes(
    run_inputs, term_codes, weight_levels, correlations, slab_modes, cell_map
):
    run_count, dim = run_inputs.shape
    term_count, modes = correlations.shape
    terms, slots = term_codes.shape
    cells = slab_modes.shape[0]
    slab_cells = cell_map.shape[0]
    chips = lax.axis_size("runs") // CORES
    total_runs = run_count * CORES * chips
    core_terms = terms // CORES
    own_modes = modes // chips
    rows = dim * run_count // term_count
    packet_rows = round_up(2 * rows + 2, 16)
    me = lax.axis_index("runs").astype(jnp.int32).reshape(1)
    smem = pl.BlockSpec(memory_space=pltpu.SMEM)
    vmem = pl.BlockSpec(memory_space=pltpu.VMEM)
    anywhere = pl.BlockSpec(memory_space=pl.ANY)

    turned, *sent = pl.pallas_call(
        prepare_kernel,
        in_specs=[smem, vmem, vmem],
        out_specs=[vmem] * (1 + chips),
        out_shape=[jax.ShapeDtypeStruct((modes, term_count), jnp.bfloat16)]
        + [jax.ShapeDtypeStruct((own_modes + packet_rows, term_count), jnp.bfloat16)]
        * chips,
        compiler_params=params(16),
        name="prepare",
    )(me, in_hbm(correlations), in_hbm(run_inputs.T))
    blocks = to_chips(sent)

    block = math.gcd(512, slab_cells)

    def reorder(start, *after):
        return pl.pallas_call(
            reorder_kernel,
            in_specs=[vmem, vmem] + [anywhere] * len(after),
            out_specs=vmem,
            out_shape=jax.ShapeDtypeStruct((block, modes), jnp.bfloat16),
            compiler_params=params(16),
            cost_estimate=cost(2 * cells * block * modes, 2 * cells * modes),
            name="reorder",
        )(cell_map[None, start : start + block], slab_modes, *after)

    starts = range(0, slab_cells, block)
    early = len(starts) // 2
    ordered = [reorder(start) for start in starts[:early]]
    packets = jnp.stack([block[own_modes:] for block in blocks])
    others = to_device(packets, 1)

    tile = term_count
    half = round_up(DEGREES * dim, LANES)
    packets_spec = pl.BlockSpec(
        (chips, packet_rows, term_count), lambda i, me: (0, 0, 0)
    )
    design = pl.pallas_call(
        functools.partial(design_kernel, dim, run_count),
        grid_spec=pltpu.PrefetchScalarGridSpec(
            num_scalar_prefetch=1,
            grid=(chips,),
            in_specs=[
                pl.BlockSpec((slots, tile), lambda i, me: (0, me[0] ^ (CORES * i))),
                packets_spec,
                packets_spec,
            ]
            + [anywhere] * early,
            out_specs=pl.BlockSpec((total_runs, tile), lambda i, me: (0, i)),
            scratch_shapes=[
                pltpu.VMEM((total_runs, half), jnp.float32),
                pltpu.VMEM((total_runs, 2 * half), jnp.bfloat16),
                pltpu.VMEM((slots - slots // 4, 2 * half, tile), jnp.bfloat16),
            ],
        ),
        out_shape=jax.ShapeDtypeStruct((total_runs, core_terms), jnp.bfloat16),
        compiler_params=params(16),
        cost_estimate=cost(
            4 * total_runs * core_terms * slots * half, 2 * total_runs * core_terms
        ),
        name="design",
    )(me, in_hbm(term_codes.T), packets, others, *ordered)

    fit_cost = cost(
        2 * total_runs * core_terms * own_modes, 2 * total_runs * core_terms
    )
    fitted, scale = pl.pallas_call(
        functools.partial(fit_kernel, 2 * rows),
        in_specs=[smem] + [vmem] * (4 + chips),
        out_specs=[vmem, vmem],
        out_shape=[
            jax.ShapeDtypeStruct((own_modes, total_runs), jnp.float32),
            jax.ShapeDtypeStruct((8, term_count), jnp.float32),
        ],
        scratch_shapes=[pltpu.VMEM((own_modes, core_terms), jnp.bfloat16)],
        compiler_params=params(16),
        cost_estimate=fit_cost,
        name="fit",
    )(me, weight_levels[None, :], packets, others, design, *blocks)
    summed = pl.pallas_call(
        functools.partial(sum_kernel, float(total_runs)),
        in_specs=[vmem] * 3,
        out_specs=[vmem] * chips,
        out_shape=[jax.ShapeDtypeStruct((own_modes, term_count), jnp.bfloat16)] * chips,
        compiler_params=params(16),
        cost_estimate=fit_cost,
        name="sum",
    )(fitted, to_device(fitted, 1), design)
    returned = to_chips(summed)
    ordered += [reorder(start, summed[0]) for start in starts[early:]]

    return pl.pallas_call(
        functools.partial(finish_kernel, len(ordered)),
        in_specs=[smem] + [vmem] * (2 + len(ordered) + chips),
        out_specs=(anywhere, anywhere),
        out_shape=(
            jax.ShapeDtypeStruct((term_count, modes), jnp.float32),
            jax.ShapeDtypeStruct((term_count, slab_cells), jnp.bfloat16),
        ),
        scratch_shapes=[
            pltpu.VMEM((modes, term_count), jnp.float32),
            pltpu.VMEM((term_count, modes), jnp.float32),
            pltpu.VMEM((term_count, modes), jnp.bfloat16),
            pltpu.VMEM((len(ordered), term_count, block), jnp.bfloat16),
            pltpu.SemaphoreType.DMA,
            pltpu.SemaphoreType.DMA((len(ordered),)),
        ],
        compiler_params=params(20),
        name="finish",
    )(me, turned, scale, *ordered, *returned)


def hermite_table(points):
    squared = points * points
    columns = [
        jnp.ones_like(points),
        points,
        (squared - 1.0) / ROOT_TWO,
        points * (squared - 3.0) / ROOT_SIX,
        (squared * squared - 6.0 * squared + 3.0) / ROOT_TWENTYFOUR,
    ]
    return jnp.stack(columns, axis=-1).reshape(points.shape[0], -1)


def basis(points, codes):
    hermite = hermite_table(points)
    product = jnp.take(hermite, codes[:, 0], axis=1)
    for column in range(1, codes.shape[1]):
        product = product * jnp.take(hermite, codes[:, column], axis=1)
    return product.astype(jnp.bfloat16)


def shrink(values, limits):
    length = jnp.sqrt(jnp.sum(values * values, axis=1, keepdims=True) + EPSILON)
    return values * jnp.maximum(0.0, 1.0 - limits[:, None] / length)


def transposed_product(left, right):
    return lax.dot_general(
        left, right, (((0,), (0,)), ((), ())), preferred_element_type=jnp.float32
    )


def split_by_runs(
    run_inputs, term_codes, weight_levels, correlations, slab_modes, cell_map
):
    run_count = run_inputs.shape[0]
    term_count = correlations.shape[0]
    devices = lax.axis_size("runs")
    offset = lax.axis_index("runs") * term_count
    total_runs = run_count * devices
    weights_all = jnp.exp2(weight_levels.astype(jnp.float32))
    own_weights = lax.dynamic_slice_in_dim(weights_all, offset, term_count)
    own_corr = correlations.astype(jnp.float32)
    ratio = jnp.max(jnp.sqrt(jnp.sum(own_corr * own_corr, axis=1)) / own_weights)
    penalty = LAMBDA_FRACTION * lax.pmax(ratio, "runs")
    first = shrink(STEP * own_corr, STEP * penalty * own_weights)
    design = basis(run_inputs, term_codes)
    fitted = jnp.dot(
        design,
        lax.all_gather(first.astype(jnp.bfloat16), "runs", axis=0, tiled=True),
        preferred_element_type=jnp.float32,
    )
    fitted_half = fitted.astype(jnp.bfloat16)
    all_points = lax.all_gather(run_inputs, "runs", axis=0, tiled=True)
    own_codes = lax.dynamic_slice_in_dim(term_codes, offset, term_count, 0)
    owned_design = basis(all_points, own_codes)
    summed = transposed_product(
        owned_design, lax.all_gather(fitted_half, "runs", axis=0, tiled=True)
    )
    gradient = summed / total_runs - own_corr
    coefficients = shrink(first - STEP * gradient, STEP * penalty * own_weights)
    modes = jnp.take(slab_modes, cell_map, axis=0)
    lifted = lax.dot_general(
        coefficients.astype(jnp.bfloat16),
        modes,
        (((1,), (1,)), ((), ())),
        preferred_element_type=jnp.float32,
    ).astype(jnp.bfloat16)
    return (coefficients, lifted)


def on_device(
    run_inputs, term_codes, weight_levels, correlations, slab_modes, cell_map
):
    devices = lax.axis_size("runs")
    run_count = run_inputs.shape[0]
    term_count, modes = correlations.shape
    chips = max(1, devices // CORES)
    whole_tiles = (
        devices >= CORES
        and devices & (devices - 1) == 0
        and modes % (LANES * chips) == 0
        and term_count % LANES == 0
        and DEGREES * run_inputs.shape[1] <= LANES
        and LANES % run_count == 0
        and chips % (LANES // run_count) == 0
        and term_count % run_count == 0
        and run_inputs.shape[1] % (term_count // run_count) == 0
        and slab_modes.shape[0] % LANES == 0
        and cell_map.shape[0] % LANES == 0
    )
    plan = split_by_modes if whole_tiles else split_by_runs
    return plan(
        run_inputs, term_codes, weight_levels, correlations, slab_modes, cell_map
    )


def solution(mesh):
    return jax.shard_map(
        on_device,
        mesh=mesh,
        in_specs=(
            P(("cases", "runs"), None),
            P(),
            P(),
            P(("cases", "runs"), None),
            P("cases", None),
            P(),
        ),
        out_specs=(P(("cases", "runs"), None), P(("cases", "runs"), None)),
        check_vma=False,
    )
```

time: 100 us -> 60.5 us (0.60)
  starting transfers between devices: 61 us -> 24.4 us
  Pallas kernels: 33.2 us -> 22.3 us
  waiting for transfers between devices: 4.1 us -> 9.28 us
  local copies, waits for them, and re-layouts: 0.01 us -> 2.98 us
    ppermute x45 -> x16, starting transfers between devices: 61 us -> 24.4 us  [to_device(): return lax.ppermute(array, 'runs', [(i, i ^ bits) for i in range(devices)])]
    pallas_call x4 -> x8, Pallas kernels: 21.4 us -> 15.7 us  [the longest x4 9.43 us: reorder(): pl.pallas_call(reorder_kernel, in_specs=[vmem, vmem] + [anywhere] * len(a...]
    pallas_call x1, Pallas kernels: 11.9 us -> 6.62 us  [split_by_modes(): pl.pallas_call(functools.partial(design_kernel, dim, run_count), grid_spe...]
    ppermute x45 -> x16, waiting for transfers between devices: 4.1 us -> 9.28 us  [to_device(): return lax.ppermute(array, 'runs', [(i, i ^ bits) for i in range(devices)])]
    unnamed x4 -> x13, local copies, waits for them, and re-layouts: 0.01 us -> 2.21 us
  transfers between devices with their start and end apart: 45 -> 16, of which waited for: 2 -> 4; matrix products, arithmetic and copies ran while one was open for 0% -> 1% of each run, Pallas kernels for 25% -> 16%
where the time goes in v6:
time: 60.5 us; the launch traced here: 60 us
  starting transfers between devices  24.4 us (40%)
  Pallas kernels  22.3 us (37%)
  waiting for transfers between devices  9.28 us (15%)
  local copies, waits for them, and re-layouts  2.98 us (5%)
  between operations  0.97 us (2%)
    ppermute x16, starting transfers between devices, to_device(): return lax.ppermute(array, 'runs', [(i, i ^ bits) for i in range(devices)])  24.4 us
    pallas_call x4, Pallas kernels, reorder(): pl.pallas_call(reorder_kernel, in_specs=[vmem, vmem] + [anywhere] * len(a...  9.43 us
    ppermute x16, waiting for transfers between devices, to_device(): return lax.ppermute(array, 'runs', [(i, i ^ bits) for i in range(devices)])  9.28 us
    pallas_call x1, Pallas kernels, split_by_modes(): pl.pallas_call(functools.partial(design_kernel, dim, run_count), grid_spe...  6.62 us
    pallas_call x1, Pallas kernels, split_by_modes(): pl.pallas_call(functools.partial(finish_kernel, len(ordered)), in_specs=[...  2.58 us
    unnamed x13, local copies, waits for them, and re-layouts  2.21 us
    pallas_call x1, Pallas kernels, split_by_modes(): pl.pallas_call(functools.partial(fit_kernel, 2 * rows), in_specs=[smem] +...  1.62 us
    pallas_call x1, Pallas kernels, split_by_modes(): pl.pallas_call(prepare_kernel, in_specs=[smem, vmem, vmem], out_specs=[vm...  1.35 us
  transfers between devices with their start and end apart: 16, of which 4 were waited for; matrix products, arithmetic and copies ran while one was open for 1% of the time, Pallas kernels for 16%

profile of v6, /device:TPU:0, one launch (start us, length us, event | category | flops | bytes accessed | tf_op | source)
XLA Modules:
  0.0 60.0 jit_solution(8524790548855753088)
XLA Ops:
  0.6 1.3 %prepare.1 = (bf16[1024,256]{1,0:T(8,128)(2,1)S(1)}, bf16[144,256]{1,0:T(8,128)(2,1)S(1)}, bf16[144,256]{1,0:T(8,128)(2,1)S(1)}, bf16[144,256]{1,0:T(8,128)(2,1)...) custom-call(s32[1]{0:T(128)} %bitcast.me_ref, ...), custom_call_target="tpu_custom_call" | custom-call | tf_op jit(solution)/shard_map/prepare/pallas_call | solution.py:300
  2.0 3.0 %collective-permute-start = (bf16[144,256]{1,0:T(8,128)(2,1)S(1)}, bf16[144,256]{1,0:T(8,128)(2,1)S(1)}, u32[]{:S(2)}, u32[]{:S(2)}) collective-permute-start(bf16[144,256]{1,0:T(8,128)(2,1)S(1)} %get-tuple-element.23), channel_id=1, source_target_pairs={{0,2},{1,3},{2,0},{3,1},{4,6},{5,7},{6,4},{7,5},{8,10},{9,11},{10,... | collective-permute-start | bytes 221192 | tf_op jit(solution)/shard_map/ppermute | solution.py:270
  5.0 1.6 %collective-permute-start.1 = (bf16[144,256]{1,0:T(8,128)(2,1)S(1)}, bf16[144,256]{1,0:T(8,128)(2,1)S(1)}, u32[]{:S(2)}, u32[]{:S(2)}) collective-permute-start(bf16[144,256]{1,0:T(8,128)(2,1)S(1)} %get-tuple-element.24), channel_id=1, source_target_pairs={{0,4},{1,5},{2,6},{3,7},{4,0},{5,1},{6,2},{7,3},{8,12},{9,13},{10,... | collective-permute-start | bytes 221192 | tf_op jit(solution)/shard_map/ppermute | solution.py:270
  6.6 0.0 collective-permute-start.2
  6.6 3.0 %collective-permute-start.3 = (bf16[144,256]{1,0:T(8,128)(2,1)S(1)}, bf16[144,256]{1,0:T(8,128)(2,1)S(1)}, u32[]{:S(2)}, u32[]{:S(2)}) collective-permute-start(bf16[144,256]{1,0:T(8,128)(2,1)S(1)} %get-tuple-element.26), channel_id=1, source_target_pairs={{0,8},{1,9},{2,10},{3,11},{4,12},{5,13},{6,14},{7,15},{8,0},{9,1},... | collective-permute-start | bytes 221192 | tf_op jit(solution)/shard_map/ppermute | solution.py:270
  9.6 1.3 %collective-permute-start.4 = (bf16[144,256]{1,0:T(8,128)(2,1)S(1)}, bf16[144,256]{1,0:T(8,128)(2,1)S(1)}, u32[]{:S(2)}, u32[]{:S(2)}) collective-permute-start(bf16[144,256]{1,0:T(8,128)(2,1)S(1)} %get-tuple-element.27), channel_id=1, source_target_pairs={{0,10},{1,11},{2,8},{3,9},{4,14},{5,15},{6,12},{7,13},{8,2},{9,3},... | collective-permute-start | bytes 221192 | tf_op jit(solution)/shard_map/ppermute | solution.py:270
  10.8 0.8 %fusion = (s32[512]{0:T(512)S(1)}, s32[512]{0:T(512)S(1)}, s32[512]{0:T(512)S(1)}, s32[512]{0:T(512)S(1)}) fusion(s32[2048]{0:T(1024)} %param.11), kind=kLoop, calls=%fused_computation.15 | loop fusion | bytes 16384 | tf_op jit(solution)/shard_map/slice | solution.py:323
  11.6 0.0 copy-start.1
  11.6 2.2 %copy-done.1 = bf16[2048,1024]{1,0:T(8,128)(2,1)S(1)} copy-done((bf16[2048,1024]{1,0:T(8,128)(2,1)S(1)}, bf16[2048,1024]{1,0:T(8,128)(2,1)}, u32[]{:S(2)}) %copy-start.1) | copy-done | bytes 4194328
  13.8 2.4 %reorder.5.refs_1_ = bf16[512,1024]{1,0:T(8,128)(2,1)S(1)} custom-call(s32[1,512]{1,0:T(1,128)S(1)} %bitcast.42, bf16[2048,1024]{1,0:T(8,128)(2,1)S(1)} %copy-done.1), custom_call_target="tpu_custom_call" | custom-call | flops 2147483648 | bytes 4194304 | tf_op jit(solution)/shard_map/reorder/pallas_call | solution.py:315
  16.2 0.0 collective-permute-done.refs_1_
  16.2 3.7 %collective-permute-start.5 = (bf16[144,256]{1,0:T(8,128)(2,1)S(1)}, bf16[144,256]{1,0:T(8,128)(2,1)S(1)}, u32[]{:S(2)}, u32[]{:S(2)}) collective-permute-start(bf16[144,256]{1,0:T(8,128)(2,1)S(1)} %get-tuple-element.28), channel_id=1, source_target_pairs={{0,12},{1,13},{2,14},{3,15},{4,8},{5,9},{6,10},{7,11},{8,4},{9,5},... | collective-permute-start | bytes 221192 | tf_op jit(solution)/shard_map/ppermute | solution.py:270
  19.8 0.0 collective-permute-done.1.refs_2_
  19.8 0.1 collective-permute-start.6
  19.9 0.0 collective-permute-done.2.refs_3_
  19.9 0.0 collective-permute-done.3.refs_4_
  19.9 0.0 collective-permute-done.4.refs_5_
  20.0 2.5 %collective-permute-done.5.refs_6_ = bf16[144,256]{1,0:T(8,128)(2,1)S(1)} collective-permute-done((bf16[144,256]{1,0:T(8,128)(2,1)S(1)}, bf16[144,256]{1,0:T(8,128)(2,1)S(1)}, u32[]{:S(2)}, u32[]{:S(2)}) %collective-permute-start.5) | collective-permute-done | bytes 73760 | tf_op jit(solution)/shard_map/ppermute | solution.py:270
  22.5 4.4 %collective-permute-done.6.refs_7_ = bf16[144,256]{1,0:T(8,128)(2,1)S(1)} collective-permute-done((bf16[144,256]{1,0:T(8,128)(2,1)S(1)}, bf16[144,256]{1,0:T(8,128)(2,1)S(1)}, u32[]{:S(2)}, u32[]{:S(2)}) %collective-permute-start.6) | collective-permute-done | bytes 73760 | tf_op jit(solution)/shard_map/ppermute | solution.py:270
  26.9 0.0 collective-permute-start.7
  26.9 2.4 %reorder.4.refs_0_ = bf16[512,1024]{1,0:T(8,128)(2,1)S(1)} custom-call(s32[1,512]{1,0:T(1,128)S(1)} %bitcast.41, bf16[2048,1024]{1,0:T(8,128)(2,1)S(1)} %copy-done.1), custom_call_target="tpu_custom_call" | custom-call | flops 2147483648 | bytes 4194304 | tf_op jit(solution)/shard_map/reorder/pallas_call | solution.py:315
  29.3 0.0 collective-permute-done.7.other_ref
  29.3 0.0 copy-start
  29.3 6.6 %design.1.design_ref = bf16[1024,2048]{1,0:T(8,128)(2,1)S(1)} custom-call(s32[1]{0:T(128)} %bitcast.me_ref, s32[4,4096]{1,0:T(4,128)} %bitcast.44, bf16[8,16,256]{2,1,0:T(8,128)(2,1)S(1)} %constant_dynamic-update-slice_fusion.own_ref, bf16[8,16,256]{2,1,0:T(8,128)(2,1)S(1)} %collective-permute-done.7.other_ref, bf16[512,1024]{1,0:T(8,128)(2,1)S(1)} %reorder.4.refs_0_, ...), custom_call_target="tpu_custom_call" | custom-call | flops 4294967296 | bytes 4194304 | tf_op jit(solution)/shard_map/design/pallas_call | solution.py:336
  35.9 0.0 copy-done
  35.9 0.0 copy-start.2
  35.9 1.6 %fit.1 = (f32[128,1024]{1,0:T(8,128)S(1)}, f32[8,256]{1,0:T(8,128)S(1)}) custom-call(s32[1]{0:T(128)} %bitcast.me_ref, s32[1,4096]{1,0:T(1,128)S(1)} %bitcast.38, bf16[8,16,256]{2,1,0:T(8,128)(2,1)S(1)} %constant_dynamic-update-slice_fusion.own_ref, bf16[8,16,256]{2,1,0:T(8,128)(2,1)S(1)} %collective-permute-done.7.other_ref, ...), custom_call_target="tpu_custom_call" | custom-call | flops 536870912 | bytes 4194304 | tf_op jit(solution)/shard_map/fit/pallas_call | solution.py:365
  37.6 0.6 collective-permute-start.8
  38.1 1.5 %collective-permute-done.8.other_ref = f32[128,1024]{1,0:T(8,128)S(1)} collective-permute-done((f32[128,1024]{1,0:T(8,128)S(1)}, f32[128,1024]{1,0:T(8,128)S(1)}, u32[]{:S(2)}, u32[]{:S(2)}) %collective-permute-start.8) | collective-permute-done | bytes 524320 | tf_op jit(solution)/shard_map/ppermute | solution.py:270
  39.7 0.7 %sum.1 = (bf16[128,256]{1,0:T(8,128)(2,1)S(1)}, bf16[128,256]{1,0:T(8,128)(2,1)S(1)}, bf16[128,256]{1,0:T(8,128)(2,1)S(1)}, bf16[128,256]{1,0:T(8,128)(2,1)S(1)}...) custom-call(f32[128,1024]{1,0:T(8,128)S(1)} %get-tuple-element.31.ow, ...), custom_call_target="tpu_custom_call" | custom-call | flops 536870912 | bytes 4194304 | tf_op jit(solution)/shard_map/sum/pallas_call | solution.py:378
  40.4 0.6 %collective-permute-start.9 = (bf16[128,256]{1,0:T(8,128)(2,1)S(1)}, bf16[128,256]{1,0:T(8,128)(2,1)S(1)}, u32[]{:S(2)}, u32[]{:S(2)}) collective-permute-start(bf16[128,256]{1,0:T(8,128)(2,1)S(1)} %get-tuple-element.33), channel_id=1, source_target_pairs={{0,2},{1,3},{2,0},{3,1},{4,6},{5,7},{6,4},{7,5},{8,10},{9,11},{10,... | collective-permute-start | bytes 196616 | tf_op jit(solution)/shard_map/ppermute | solution.py:270
  41.0 0.0 collective-permute-start.10
  41.0 3.0 %collective-permute-start.11 = (bf16[128,256]{1,0:T(8,128)(2,1)S(1)}, bf16[128,256]{1,0:T(8,128)(2,1)S(1)}, u32[]{:S(2)}, u32[]{:S(2)}) collective-permute-start(bf16[128,256]{1,0:T(8,128)(2,1)S(1)} %get-tuple-element.35), channel_id=1, source_target_pairs={{0,6},{1,7},{2,4},{3,5},{4,2},{5,3},{6,0},{7,1},{8,14},{9,15},{10,... | collective-permute-start | bytes 196616 | tf_op jit(solution)/shard_map/ppermute | solution.py:270
  44.0 0.0 collective-permute-start.12
  44.0 2.9 %collective-permute-start.13 = (bf16[128,256]{1,0:T(8,128)(2,1)S(1)}, bf16[128,256]{1,0:T(8,128)(2,1)S(1)}, u32[]{:S(2)}, u32[]{:S(2)}) collective-permute-start(bf16[128,256]{1,0:T(8,128)(2,1)S(1)} %get-tuple-element.37), channel_id=1, source_target_pairs={{0,10},{1,11},{2,8},{3,9},{4,14},{5,15},{6,12},{7,13},{8,2},{9,3},... | collective-permute-start | bytes 196616 | tf_op jit(solution)/shard_map/ppermute | solution.py:270
  46.9 0.0 copy-done.2
  46.9 2.4 %reorder.7.refs_3_ = bf16[512,1024]{1,0:T(8,128)(2,1)S(1)} custom-call(s32[1,512]{1,0:T(1,128)S(1)} %bitcast.40, bf16[2048,1024]{1,0:T(8,128)(2,1)S(1)} %copy-done.2, bf16[128,256]{1,0:T(8,128)(2,1)S(1)} %get-tuple-element.32.refs_0_.refs_4_), custom_call_target="tpu_custom_call" | custom-call | flops 2147483648 | bytes 4194304 | tf_op jit(solution)/shard_map/reorder/pallas_call | solution.py:315
  49.3 0.0 collective-permute-done.9.refs_5_
  49.3 1.0 %collective-permute-start.14 = (bf16[128,256]{1,0:T(8,128)(2,1)S(1)}, bf16[128,256]{1,0:T(8,128)(2,1)S(1)}, u32[]{:S(2)}, u32[]{:S(2)}) collective-permute-start(bf16[128,256]{1,0:T(8,128)(2,1)S(1)} %get-tuple-element.38), channel_id=1, source_target_pairs={{0,12},{1,13},{2,14},{3,15},{4,8},{5,9},{6,10},{7,11},{8,4},{9,5},... | collective-permute-start | bytes 196616 | tf_op jit(solution)/shard_map/ppermute | solution.py:270
  50.3 0.0 collective-permute-done.10.refs_6_
  50.3 3.8 %collective-permute-start.15 = (bf16[128,256]{1,0:T(8,128)(2,1)S(1)}, bf16[128,256]{1,0:T(8,128)(2,1)S(1)}, u32[]{:S(2)}, u32[]{:S(2)}) collective-permute-start(bf16[128,256]{1,0:T(8,128)(2,1)S(1)} %get-tuple-element.39), channel_id=1, source_target_pairs={{0,14},{1,15},{2,12},{3,13},{4,10},{5,11},{6,8},{7,9},{8,6},{9,7},... | collective-permute-start | bytes 196616 | tf_op jit(solution)/shard_map/ppermute | solution.py:270
  54.1 2.4 %reorder.6.refs_2_ = bf16[512,1024]{1,0:T(8,128)(2,1)S(1)} custom-call(s32[1,512]{1,0:T(1,128)S(1)} %bitcast.39, bf16[2048,1024]{1,0:T(8,128)(2,1)S(1)} %copy-done.2, bf16[128,256]{1,0:T(8,128)(2,1)S(1)} %get-tuple-element.32.refs_0_.refs_4_), custom_call_target="tpu_custom_call" | custom-call | flops 2147483648 | bytes 4194304 | tf_op jit(solution)/shard_map/reorder/pallas_call | solution.py:315
  56.5 0.0 collective-permute-done.11.refs_7_
  56.5 0.0 collective-permute-done.12.refs_8_
  56.5 0.0 collective-permute-done.13.refs_9_
  56.5 0.0 collective-permute-done.14.refs_10_
  56.5 0.8 %collective-permute-done.15.refs_11_ = bf16[128,256]{1,0:T(8,128)(2,1)S(1)} collective-permute-done((bf16[128,256]{1,0:T(8,128)(2,1)S(1)}, bf16[128,256]{1,0:T(8,128)(2,1)S(1)}, u32[]{:S(2)}, u32[]{:S(2)}) %collective-permute-start.15) | collective-permute-done | bytes 65568 | tf_op jit(solution)/shard_map/ppermute | solution.py:270
  57.3 2.6 %finish.1 = (f32[256,1024]{1,0:T(8,128)}, bf16[256,2048]{1,0:T(8,128)(2,1)}) custom-call(s32[1]{0:T(128)} %bitcast.me_ref, bf16[1024,256]{1,0:T(8,128)(2,1)S(1)} %get-tuple-element.21.corr_ref, f32[8,256]{1,0:T(8,128)S(1)} %get-tuple-element.30.scale_ref, bf16[512,1024]{1,0:T(8,128)(2,1)S(1)} %reorder.4.refs_0_, bf16[512,1024]{1,0:T(8,128)(2,1)S(1)} %reorder.5.refs_1_, ...), custom_call_target="tpu_custom_call" | custom-call | tf_op jit(solution)/shard_map/finish/pallas_call | solution.py:390
  (8 shorter events, 0.0 us)
Async XLA Ops:
  2.0 14.2 %collective-permute-start = (bf16[144,256]{1,0:T(8,128)(2,1)S(1)}, bf16[144,256]{1,0:T(8,128)(2,1)S(1)}, u32[]{:S(2)}, u32[]{:S(2)}) collective-permute-start(bf16[144,256]{1,0:T(8,128)(2,1)S(1)} %get-tuple-element.23), channel_id=1, source_target_pairs={{0,2},{1,3},{2,0},{3,1},{4,6},{5,7},{6,4},{7,5},{8,10},{9,11},{10,... | collective-permute-start | bytes 221192 | tf_op jit(solution)/shard_map/ppermute | solution.py:270
  5.0 14.9 %collective-permute-start.1 = (bf16[144,256]{1,0:T(8,128)(2,1)S(1)}, bf16[144,256]{1,0:T(8,128)(2,1)S(1)}, u32[]{:S(2)}, u32[]{:S(2)}) collective-permute-start(bf16[144,256]{1,0:T(8,128)(2,1)S(1)} %get-tuple-element.24), channel_id=1, source_target_pairs={{0,4},{1,5},{2,6},{3,7},{4,0},{5,1},{6,2},{7,3},{8,12},{9,13},{10,... | collective-permute-start | bytes 221192 | tf_op jit(solution)/shard_map/ppermute | solution.py:270
  6.6 13.3 %collective-permute-start.2 = (bf16[144,256]{1,0:T(8,128)(2,1)S(1)}, bf16[144,256]{1,0:T(8,128)(2,1)S(1)}, u32[]{:S(2)}, u32[]{:S(2)}) collective-permute-start(bf16[144,256]{1,0:T(8,128)(2,1)S(1)} %get-tuple-element.25), channel_id=1, source_target_pairs={{0,6},{1,7},{2,4},{3,5},{4,2},{5,3},{6,0},{7,1},{8,14},{9,15},{10,... | collective-permute-start | bytes 221192 | tf_op jit(solution)/shard_map/ppermute | solution.py:270
  6.6 13.4 %collective-permute-start.3 = (bf16[144,256]{1,0:T(8,128)(2,1)S(1)}, bf16[144,256]{1,0:T(8,128)(2,1)S(1)}, u32[]{:S(2)}, u32[]{:S(2)}) collective-permute-start(bf16[144,256]{1,0:T(8,128)(2,1)S(1)} %get-tuple-element.26), channel_id=1, source_target_pairs={{0,8},{1,9},{2,10},{3,11},{4,12},{5,13},{6,14},{7,15},{8,0},{9,1},... | collective-permute-start | bytes 221192 | tf_op jit(solution)/shard_map/ppermute | solution.py:270
  9.6 10.4 %collective-permute-start.4 = (bf16[144,256]{1,0:T(8,128)(2,1)S(1)}, bf16[144,256]{1,0:T(8,128)(2,1)S(1)}, u32[]{:S(2)}, u32[]{:S(2)}) collective-permute-start(bf16[144,256]{1,0:T(8,128)(2,1)S(1)} %get-tuple-element.27), channel_id=1, source_target_pairs={{0,10},{1,11},{2,8},{3,9},{4,14},{5,15},{6,12},{7,13},{8,2},{9,3},... | collective-permute-start | bytes 221192 | tf_op jit(solution)/shard_map/ppermute | solution.py:270
  11.6 2.2 %copy-start.1 = (bf16[2048,1024]{1,0:T(8,128)(2,1)S(1)}, bf16[2048,1024]{1,0:T(8,128)(2,1)}, u32[]{:S(2)}) copy-start(bf16[2048,1024]{1,0:T(8,128)(2,1)} %slab_ref.7) | copy-start | bytes 12582916
  16.2 6.3 %collective-permute-start.5 = (bf16[144,256]{1,0:T(8,128)(2,1)S(1)}, bf16[144,256]{1,0:T(8,128)(2,1)S(1)}, u32[]{:S(2)}, u32[]{:S(2)}) collective-permute-start(bf16[144,256]{1,0:T(8,128)(2,1)S(1)} %get-tuple-element.28), channel_id=1, source_target_pairs={{0,12},{1,13},{2,14},{3,15},{4,8},{5,9},{6,10},{7,11},{8,4},{9,5},... | collective-permute-start | bytes 221192 | tf_op jit(solution)/shard_map/ppermute | solution.py:270
  19.8 7.1 %collective-permute-start.6 = (bf16[144,256]{1,0:T(8,128)(2,1)S(1)}, bf16[144,256]{1,0:T(8,128)(2,1)S(1)}, u32[]{:S(2)}, u32[]{:S(2)}) collective-permute-start(bf16[144,256]{1,0:T(8,128)(2,1)S(1)} %get-tuple-element.29), channel_id=1, source_target_pairs={{0,14},{1,15},{2,12},{3,13},{4,10},{5,11},{6,8},{7,9},{8,6},{9,7},... | collective-permute-start | bytes 221192 | tf_op jit(solution)/shard_map/ppermute | solution.py:270
  26.9 2.4 %collective-permute-start.7 = (bf16[8,16,256]{2,1,0:T(8,128)(2,1)S(1)}, bf16[8,16,256]{2,1,0:T(8,128)(2,1)S(1)}, u32[]{:S(2)}, u32[]{:S(2)}) collective-permute-start(bf16[8,16,256]{2,1,0:T(8,128)(2,1)S(1)} %constant_dynamic-update-slice_fusion.own_ref), channel_id=1, source_target_pairs={{0,1},{1,0},{2,3},{3,2},{4,5},{5,4},{6,7},{7,6},{8,9},{9,8},{10,11... | collective-permute-start | bytes 196616 | tf_op jit(solution)/shard_map/ppermute | solution.py:270
  29.3 6.6 %copy-start = (s32[4096]{0:T(1024)S(1)}, s32[4096]{0:T(1024)}, u32[]{:S(2)}) copy-start(s32[4096]{0:T(1024)} %param.8) | copy-start | bytes 49156
  35.9 11.0 %copy-start.2 = (bf16[2048,1024]{1,0:T(8,128)(2,1)S(1)}, bf16[2048,1024]{1,0:T(8,128)(2,1)}, u32[]{:S(2)}) copy-start(bf16[2048,1024]{1,0:T(8,128)(2,1)} %slab_ref.7) | copy-start | bytes 12582916
  37.6 2.1 %collective-permute-start.8 = (f32[128,1024]{1,0:T(8,128)S(1)}, f32[128,1024]{1,0:T(8,128)S(1)}, u32[]{:S(2)}, u32[]{:S(2)}) collective-permute-start(f32[128,1024]{1,0:T(8,128)S(1)} %get-tuple-element.31.own_ref), channel_id=1, source_target_pairs={{0,1},{1,0},{2,3},{3,2},{4,5},{5,4},{6,7},{7,6},{8,9},{9,8},{10,11... | collective-permute-start | bytes 1572872 | tf_op jit(solution)/shard_map/ppermute | solution.py:270
  40.4 8.8 %collective-permute-start.9 = (bf16[128,256]{1,0:T(8,128)(2,1)S(1)}, bf16[128,256]{1,0:T(8,128)(2,1)S(1)}, u32[]{:S(2)}, u32[]{:S(2)}) collective-permute-start(bf16[128,256]{1,0:T(8,128)(2,1)S(1)} %get-tuple-element.33), channel_id=1, source_target_pairs={{0,2},{1,3},{2,0},{3,1},{4,6},{5,7},{6,4},{7,5},{8,10},{9,11},{10,... | collective-permute-start | bytes 196616 | tf_op jit(solution)/shard_map/ppermute | solution.py:270
  41.0 9.2 %collective-permute-start.10 = (bf16[128,256]{1,0:T(8,128)(2,1)S(1)}, bf16[128,256]{1,0:T(8,128)(2,1)S(1)}, u32[]{:S(2)}, u32[]{:S(2)}) collective-permute-start(bf16[128,256]{1,0:T(8,128)(2,1)S(1)} %get-tuple-element.34), channel_id=1, source_target_pairs={{0,4},{1,5},{2,6},{3,7},{4,0},{5,1},{6,2},{7,3},{8,12},{9,13},{10,... | collective-permute-start | bytes 196616 | tf_op jit(solution)/shard_map/ppermute | solution.py:270
  41.0 15.4 %collective-permute-start.11 = (bf16[128,256]{1,0:T(8,128)(2,1)S(1)}, bf16[128,256]{1,0:T(8,128)(2,1)S(1)}, u32[]{:S(2)}, u32[]{:S(2)}) collective-permute-start(bf16[128,256]{1,0:T(8,128)(2,1)S(1)} %get-tuple-element.35), channel_id=1, source_target_pairs={{0,6},{1,7},{2,4},{3,5},{4,2},{5,3},{6,0},{7,1},{8,14},{9,15},{10,... | collective-permute-start | bytes 196616 | tf_op jit(solution)/shard_map/ppermute | solution.py:270
  44.0 12.5 %collective-permute-start.12 = (bf16[128,256]{1,0:T(8,128)(2,1)S(1)}, bf16[128,256]{1,0:T(8,128)(2,1)S(1)}, u32[]{:S(2)}, u32[]{:S(2)}) collective-permute-start(bf16[128,256]{1,0:T(8,128)(2,1)S(1)} %get-tuple-element.36), channel_id=1, source_target_pairs={{0,8},{1,9},{2,10},{3,11},{4,12},{5,13},{6,14},{7,15},{8,0},{9,1},... | collective-permute-start | bytes 196616 | tf_op jit(solution)/shard_map/ppermute | solution.py:270
  44.0 12.5 %collective-permute-start.13 = (bf16[128,256]{1,0:T(8,128)(2,1)S(1)}, bf16[128,256]{1,0:T(8,128)(2,1)S(1)}, u32[]{:S(2)}, u32[]{:S(2)}) collective-permute-start(bf16[128,256]{1,0:T(8,128)(2,1)S(1)} %get-tuple-element.37), channel_id=1, source_target_pairs={{0,10},{1,11},{2,8},{3,9},{4,14},{5,15},{6,12},{7,13},{8,2},{9,3},... | collective-permute-start | bytes 196616 | tf_op jit(solution)/shard_map/ppermute | solution.py:270
  49.3 7.2 %collective-permute-start.14 = (bf16[128,256]{1,0:T(8,128)(2,1)S(1)}, bf16[128,256]{1,0:T(8,128)(2,1)S(1)}, u32[]{:S(2)}, u32[]{:S(2)}) collective-permute-start(bf16[128,256]{1,0:T(8,128)(2,1)S(1)} %get-tuple-element.38), channel_id=1, source_target_pairs={{0,12},{1,13},{2,14},{3,15},{4,8},{5,9},{6,10},{7,11},{8,4},{9,5},... | collective-permute-start | bytes 196616 | tf_op jit(solution)/shard_map/ppermute | solution.py:270
  50.3 7.0 %collective-permute-start.15 = (bf16[128,256]{1,0:T(8,128)(2,1)S(1)}, bf16[128,256]{1,0:T(8,128)(2,1)S(1)}, u32[]{:S(2)}, u32[]{:S(2)}) collective-permute-start(bf16[128,256]{1,0:T(8,128)(2,1)S(1)} %get-tuple-element.39), channel_id=1, source_target_pairs={{0,14},{1,15},{2,12},{3,13},{4,10},{5,11},{6,8},{7,9},{8,6},{9,7},... | collective-permute-start | bytes 196616 | tf_op jit(solution)/shard_map/ppermute | solution.py:270

commit v7 on v6

--- a/solution.py
+++ b/solution.py
@@ -74,22 +74,25 @@
     )
 
 
-def design_kernel(dim, run_count, me_ref, codes_ref, own_ref, other_ref, *refs):
-    design_ref, exact, table, chosen = refs[-4:]
-    chips, _, terms = own_ref.shape
+def collect_kernel(chips, *refs):
+    packets_ref = refs[-1]
+    rows = packets_ref.shape[1]
+    for k, block_ref in enumerate(refs[:chips]):
+        count = block_ref.shape[0]
+        packets_ref[k] = block_ref[count - rows : count, :]
+
+
+def design_kernel(
+    dim, run_count, me_ref, codes_ref, packets_ref, design_ref, exact, table, chosen
+):
+    chips, _, terms = packets_ref.shape
     half = exact.shape[1]
     rows = dim * run_count // terms
-    core = me_ref[0] % CORES
 
     @pl.when(pl.program_id(0) == 0)
     def _():
         per = LANES // run_count
-        sources = [
-            (packets_ref, group, base)
-            for packets_ref, base in ((own_ref, core), (other_ref, 1 - core))
-            for group in range(chips // per)
-        ]
-        for packets_ref, group, base in sources:
+        for group in range(chips // per):
             owned = []
             for i in range(per):
                 packet = packets_ref[group * per + i].astype(jnp.float32)
@@ -114,7 +117,7 @@
             ).T
             high = columns.astype(jnp.bfloat16)
             low = (columns - high.astype(jnp.float32)).astype(jnp.bfloat16)
-            block = rows_of(base * (chips // per) + group, LANES)
+            block = slice(group * LANES, (group + 1) * LANES)
             exact[block, :] = columns
             table[block, 0:half] = high
             table[block, half : 2 * half] = low
@@ -163,8 +166,9 @@
     return jnp.concatenate(squares, axis=1), weights
 
 
-def fit_kernel(row, me_ref, levels_ref, own_ref, other_ref, design_ref, *refs):
-    *block_refs, fitted_ref, scale_ref, first_ref = refs
+def fit_kernel(row, me_ref, levels_ref, own_ref, other_ref, *refs):
+    *refs, fitted_ref, scale_ref, first_ref = refs
+    block_refs, design_refs = refs[:-CORES], refs[-CORES:]
     count = fitted_ref.shape[0]
     term_count = own_ref.shape[2]
     me = me_ref[0]
@@ -182,22 +186,28 @@
         terms = slice(k * term_count, (k + 1) * term_count)
         first = STEP * block_ref[0:count, :].astype(jnp.float32) * factor[:, terms]
         first_ref[:, terms] = first.astype(jnp.bfloat16)
-    fitted_ref[...] = lax.dot_general(
-        first_ref[...],
-        design_ref[...],
-        (((1,), (1,)), ((), ())),
-        preferred_element_type=jnp.float32,
-    )
-
-
-def sum_kernel(total_runs, own_ref, other_ref, design_ref, *summed_refs):
-    fitted = (own_ref[...] + other_ref[...]).astype(jnp.bfloat16)
+    runs = design_refs[0].shape[0]
+    for i, design_ref in enumerate(design_refs):
+        fitted_ref[:, i * runs : (i + 1) * runs] = lax.dot_general(
+            first_ref[...],
+            design_ref[...],
+            (((1,), (1,)), ((), ())),
+            preferred_element_type=jnp.float32,
+        )
+
+
+def sum_kernel(total_runs, own_ref, other_ref, *refs):
+    design_refs, summed_refs = refs[:CORES], refs[CORES:]
+    runs = design_refs[0].shape[0]
+    near = own_ref[:, 0:runs] + other_ref[:, runs : 2 * runs]
+    far = own_ref[:, runs : 2 * runs] + other_ref[:, 0:runs]
+    near, far = near.astype(jnp.bfloat16), far.astype(jnp.bfloat16)
     term_count = summed_refs[0].shape[1]
     for k, summed_ref in enumerate(summed_refs):
         terms = slice(k * term_count, (k + 1) * term_count)
         summed = jnp.dot(
-            fitted, design_ref[:, terms], preferred_element_type=jnp.float32
-        )
+            near, design_refs[0][:, terms], preferred_element_type=jnp.float32
+        ) + jnp.dot(far, design_refs[1][:, terms], preferred_element_type=jnp.float32)
         summed_ref[...] = (summed / total_runs).astype(jnp.bfloat16)
 
 
@@ -271,11 +281,9 @@
 
 
 def to_chips(arrays):
-    moved = {0: arrays[0]}
-    chips = len(arrays)
-    for k in [*range(chips // 2, chips), *range(1, chips // 2)]:
-        moved[k] = to_device(arrays[k], CORES * k)
-    return [moved[k] for k in range(chips)]
+    return [arrays[0]] + [
+        to_device(arrays[k], CORES * k) for k in range(1, len(arrays))
+    ]
 
 
 def split_by_modes(
@@ -324,47 +332,54 @@
 
     starts = range(0, slab_cells, block)
     early = len(starts) // 2
-    ordered = [reorder(start) for start in starts[:early]]
-    packets = jnp.stack([block[own_modes:] for block in blocks])
+    ordered = [reorder(start, *blocks[1:3]) for start in starts[:early]]
+    packets = pl.pallas_call(
+        functools.partial(collect_kernel, chips),
+        in_specs=[vmem] * chips + [anywhere] * early,
+        out_specs=vmem,
+        out_shape=jax.ShapeDtypeStruct((chips, packet_rows, term_count), jnp.bfloat16),
+        compiler_params=params(8),
+        name="collect",
+    )(*blocks, *ordered)
     others = to_device(packets, 1)
 
     tile = term_count
     half = round_up(DEGREES * dim, LANES)
-    packets_spec = pl.BlockSpec(
-        (chips, packet_rows, term_count), lambda i, me: (0, 0, 0)
-    )
-    design = pl.pallas_call(
-        functools.partial(design_kernel, dim, run_count),
-        grid_spec=pltpu.PrefetchScalarGridSpec(
-            num_scalar_prefetch=1,
-            grid=(chips,),
-            in_specs=[
-                pl.BlockSpec((slots, tile), lambda i, me: (0, me[0] ^ (CORES * i))),
-                packets_spec,
-                packets_spec,
-            ]
-            + [anywhere] * early,
-            out_specs=pl.BlockSpec((total_runs, tile), lambda i, me: (0, i)),
-            scratch_shapes=[
-                pltpu.VMEM((total_runs, half), jnp.float32),
-                pltpu.VMEM((total_runs, 2 * half), jnp.bfloat16),
-                pltpu.VMEM((slots - slots // 4, 2 * half, tile), jnp.bfloat16),
-            ],
-        ),
-        out_shape=jax.ShapeDtypeStruct((total_runs, core_terms), jnp.bfloat16),
-        compiler_params=params(16),
-        cost_estimate=cost(
-            4 * total_runs * core_terms * slots * half, 2 * total_runs * core_terms
-        ),
-        name="design",
-    )(me, in_hbm(term_codes.T), packets, others, *ordered)
+    core_runs = run_count * chips
+
+    def design_of(packets):
+        return pl.pallas_call(
+            functools.partial(design_kernel, dim, run_count),
+            grid_spec=pltpu.PrefetchScalarGridSpec(
+                num_scalar_prefetch=1,
+                grid=(chips,),
+                in_specs=[
+                    pl.BlockSpec((slots, tile), lambda i, me: (0, me[0] ^ (CORES * i))),
+                    pl.BlockSpec(packets.shape, lambda i, me: (0, 0, 0)),
+                ],
+                out_specs=pl.BlockSpec((core_runs, tile), lambda i, me: (0, i)),
+                scratch_shapes=[
+                    pltpu.VMEM((core_runs, half), jnp.float32),
+                    pltpu.VMEM((core_runs, 2 * half), jnp.bfloat16),
+                    pltpu.VMEM((slots - slots // 4, 2 * half, tile), jnp.bfloat16),
+                ],
+            ),
+            out_shape=jax.ShapeDtypeStruct((core_runs, core_terms), jnp.bfloat16),
+            compiler_params=params(16),
+            cost_estimate=cost(
+                4 * core_runs * core_terms * slots * half, 2 * core_runs * core_terms
+            ),
+            name="design",
+        )(me, in_hbm(term_codes.T), packets)
+
+    designs = [design_of(packets), design_of(others)]
 
     fit_cost = cost(
         2 * total_runs * core_terms * own_modes, 2 * total_runs * core_terms
     )
     fitted, scale = pl.pallas_call(
         functools.partial(fit_kernel, 2 * rows),
-        in_specs=[smem] + [vmem] * (4 + chips),
+        in_specs=[smem] + [vmem] * (3 + chips + CORES),
         out_specs=[vmem, vmem],
         out_shape=[
             jax.ShapeDtypeStruct((own_modes, total_runs), jnp.float32),
@@ -374,18 +389,18 @@
         compiler_params=params(16),
         cost_estimate=fit_cost,
         name="fit",
-    )(me, weight_levels[None, :], packets, others, design, *blocks)
+    )(me, weight_levels[None, :], packets, others, *blocks, *designs)
     summed = pl.pallas_call(
         functools.partial(sum_kernel, float(total_runs)),
-        in_specs=[vmem] * 3,
+        in_specs=[vmem] * (2 + CORES),
         out_specs=[vmem] * chips,
         out_shape=[jax.ShapeDtypeStruct((own_modes, term_count), jnp.bfloat16)] * chips,
         compiler_params=params(16),
         cost_estimate=fit_cost,
         name="sum",
-    )(fitted, to_device(fitted, 1), design)
+    )(fitted, to_device(fitted, 1), *designs)
     returned = to_chips(summed)
-    ordered += [reorder(start, summed[0]) for start in starts[early:]]
+    ordered += [reorder(start, *returned[1:3]) for start in starts[early:]]
 
     return pl.pallas_call(
         functools.partial(finish_kernel, len(ordered)),

time: 60.5 us -> 58.8 us (0.972)
  waiting for transfers between devices: 9.28 us -> 3.63 us
  Pallas kernels: 22.3 us -> 26.1 us
    ppermute x16, waiting for transfers between devices: 9.28 us -> 3.63 us  [to_device(): return lax.ppermute(array, 'runs', [(i, i ^ bits) for i in range(devices)])]
    pallas_call x1 -> x3, Pallas kernels: 6.62 us -> 10.4 us  [the longest x2 10.4 us: design_of(): pl.pallas_call(functools.partial(design_kernel, dim, run_count), grid_spe...]
    unnamed x13 -> x6, local copies, waits for them, and re-layouts: 2.21 us -> 2.2 us
  transfers between devices with their start and end apart: 16 -> 16, of which waited for: 4 -> 3; matrix products, arithmetic and copies ran while one was open for 1% -> 1% of each run, Pallas kernels for 16% -> 25%
where the time goes in v7:
time: 58.8 us; the launch traced here: 58.2 us
  Pallas kernels  26.1 us (44%)
  starting transfers between devices  24.5 us (42%)
  waiting for transfers between devices  3.63 us (6%)
  local copies, waits for them, and re-layouts  2.97 us (5%)
  between operations  0.97 us (2%)
    ppermute x16, starting transfers between devices, to_device(): return lax.ppermute(array, 'runs', [(i, i ^ bits) for i in range(devices)])  24.5 us
    pallas_call x2, Pallas kernels, design_of(): pl.pallas_call(functools.partial(design_kernel, dim, run_count), grid_spe...  10.4 us
    pallas_call x4, Pallas kernels, reorder(): pl.pallas_call(reorder_kernel, in_specs=[vmem, vmem] + [anywhere] * len(a...  9.43 us
    ppermute x16, waiting for transfers between devices, to_device(): return lax.ppermute(array, 'runs', [(i, i ^ bits) for i in range(devices)])  3.63 us
    pallas_call x1, Pallas kernels, split_by_modes(): pl.pallas_call(functools.partial(finish_kernel, len(ordered)), in_specs=[...  2.58 us
    unnamed x6, local copies, waits for them, and re-layouts  2.2 us
    pallas_call x1, Pallas kernels, split_by_modes(): pl.pallas_call(functools.partial(fit_kernel, 2 * rows), in_specs=[smem] +...  1.61 us
    pallas_call x1, Pallas kernels, split_by_modes(): pl.pallas_call(prepare_kernel, in_specs=[smem, vmem, vmem], out_specs=[vm...  1.35 us
  transfers between devices with their start and end apart: 16, of which 3 were waited for; matrix products, arithmetic and copies ran while one was open for 1% of the time, Pallas kernels for 25%

profile of v7, /device:TPU:0, one launch (start us, length us, event | category | flops | bytes accessed | tf_op | source)
XLA Modules:
  0.0 58.2 jit_solution(12059513047712510169)
XLA Ops:
  0.6 1.3 %prepare.1 = (bf16[1024,256]{1,0:T(8,128)(2,1)S(1)}, bf16[144,256]{1,0:T(8,128)(2,1)S(1)}, bf16[144,256]{1,0:T(8,128)(2,1)S(1)}, bf16[144,256]{1,0:T(8,128)(2,1)...) custom-call(s32[1]{0:T(128)} %bitcast.me_ref, ...), custom_call_target="tpu_custom_call" | custom-call | tf_op jit(solution)/shard_map/prepare/pallas_call | solution.py:308
  2.0 3.0 %collective-permute-start = (bf16[144,256]{1,0:T(8,128)(2,1)S(1)}, bf16[144,256]{1,0:T(8,128)(2,1)S(1)}, u32[]{:S(2)}, u32[]{:S(2)}) collective-permute-start(bf16[144,256]{1,0:T(8,128)(2,1)S(1)} %get-tuple-element.23), channel_id=1, source_target_pairs={{0,2},{1,3},{2,0},{3,1},{4,6},{5,7},{6,4},{7,5},{8,10},{9,11},{10,... | collective-permute-start | bytes 221192 | tf_op jit(solution)/shard_map/ppermute | solution.py:280
  5.0 1.6 %collective-permute-start.1 = (bf16[144,256]{1,0:T(8,128)(2,1)S(1)}, bf16[144,256]{1,0:T(8,128)(2,1)S(1)}, u32[]{:S(2)}, u32[]{:S(2)}) collective-permute-start(bf16[144,256]{1,0:T(8,128)(2,1)S(1)} %get-tuple-element.24), channel_id=1, source_target_pairs={{0,4},{1,5},{2,6},{3,7},{4,0},{5,1},{6,2},{7,3},{8,12},{9,13},{10,... | collective-permute-start | bytes 221192 | tf_op jit(solution)/shard_map/ppermute | solution.py:280
  6.6 0.0 collective-permute-start.2
  6.6 3.0 %collective-permute-start.3 = (bf16[144,256]{1,0:T(8,128)(2,1)S(1)}, bf16[144,256]{1,0:T(8,128)(2,1)S(1)}, u32[]{:S(2)}, u32[]{:S(2)}) collective-permute-start(bf16[144,256]{1,0:T(8,128)(2,1)S(1)} %get-tuple-element.26), channel_id=1, source_target_pairs={{0,8},{1,9},{2,10},{3,11},{4,12},{5,13},{6,14},{7,15},{8,0},{9,1},... | collective-permute-start | bytes 221192 | tf_op jit(solution)/shard_map/ppermute | solution.py:280
  9.6 1.3 %collective-permute-start.4 = (bf16[144,256]{1,0:T(8,128)(2,1)S(1)}, bf16[144,256]{1,0:T(8,128)(2,1)S(1)}, u32[]{:S(2)}, u32[]{:S(2)}) collective-permute-start(bf16[144,256]{1,0:T(8,128)(2,1)S(1)} %get-tuple-element.27), channel_id=1, source_target_pairs={{0,10},{1,11},{2,8},{3,9},{4,14},{5,15},{6,12},{7,13},{8,2},{9,3},... | collective-permute-start | bytes 221192 | tf_op jit(solution)/shard_map/ppermute | solution.py:280
  10.8 0.8 %fusion = (s32[512]{0:T(512)S(1)}, s32[512]{0:T(512)S(1)}, s32[512]{0:T(512)S(1)}, s32[512]{0:T(512)S(1)}) fusion(s32[2048]{0:T(1024)} %param.11), kind=kLoop, calls=%fused_computation | loop fusion | bytes 16384 | tf_op jit(solution)/shard_map/slice | solution.py:331
  11.6 0.0 collective-permute-done.refs_0_.refs_1_
  11.6 3.6 %collective-permute-start.5 = (bf16[144,256]{1,0:T(8,128)(2,1)S(1)}, bf16[144,256]{1,0:T(8,128)(2,1)S(1)}, u32[]{:S(2)}, u32[]{:S(2)}) collective-permute-start(bf16[144,256]{1,0:T(8,128)(2,1)S(1)} %get-tuple-element.28), channel_id=1, source_target_pairs={{0,12},{1,13},{2,14},{3,15},{4,8},{5,9},{6,10},{7,11},{8,4},{9,5},... | collective-permute-start | bytes 221192 | tf_op jit(solution)/shard_map/ppermute | solution.py:280
  15.2 0.0 collective-permute-done.1.refs_1_.refs_2_
  15.2 0.1 collective-permute-start.6
  15.3 0.0 copy-start.1
  15.3 2.2 %copy-done.1 = bf16[2048,1024]{1,0:T(8,128)(2,1)S(1)} copy-done((bf16[2048,1024]{1,0:T(8,128)(2,1)S(1)}, bf16[2048,1024]{1,0:T(8,128)(2,1)}, u32[]{:S(2)}) %copy-start.1) | copy-done | bytes 4194328
  17.5 2.4 %reorder.5.refs_9_.refs_1_ = bf16[512,1024]{1,0:T(8,128)(2,1)S(1)} custom-call(s32[1,512]{1,0:T(1,128)S(1)} %bitcast.12, bf16[2048,1024]{1,0:T(8,128)(2,1)S(1)} %copy-done.1, bf16[144,256]{1,0:T(8,128)(2,1)S(1)} %collective-permute-done.refs_0_.refs_1_, bf16[144,256]{1,0:T(8,128)(2,1)S(1)} %collective-permute-done.1.refs_1_.refs_2_), custom_call_target="tpu_custom_call" | custom-call | flops 2147483648 | bytes 4194304 | tf_op jit(solution)/shard_map/reorder/pallas_call | solution.py:323
  19.9 2.4 %reorder.4.refs_8_.refs_0_ = bf16[512,1024]{1,0:T(8,128)(2,1)S(1)} custom-call(s32[1,512]{1,0:T(1,128)S(1)} %bitcast.11, bf16[2048,1024]{1,0:T(8,128)(2,1)S(1)} %copy-done.1, bf16[144,256]{1,0:T(8,128)(2,1)S(1)} %collective-permute-done.refs_0_.refs_1_, bf16[144,256]{1,0:T(8,128)(2,1)S(1)} %collective-permute-done.1.refs_1_.refs_2_), custom_call_target="tpu_custom_call" | custom-call | flops 2147483648 | bytes 4194304 | tf_op jit(solution)/shard_map/reorder/pallas_call | solution.py:323
  22.2 0.0 collective-permute-done.2.refs_3_
  22.2 0.0 collective-permute-done.3.refs_4_
  22.2 0.0 collective-permute-done.4.refs_5_
  22.2 0.0 collective-permute-done.5.refs_6_
  22.3 0.1 collective-permute-done.6.refs_7_
  22.4 0.0 collective-permute-start.7
  22.4 5.3 %design.2.refs_8_.refs_0_ = bf16[512,2048]{1,0:T(8,128)(2,1)S(1)} custom-call(s32[1]{0:T(128)} %bitcast.me_ref, s32[4,4096]{1,0:T(4,128)} %bitcast.14, bf16[8,16,256]{2,1,0:T(8,128)(2,1)S(1)} %collect.1.packets_ref.own_ref), custom_call_target="tpu_custom_call" | custom-call | flops 2147483648 | bytes 2097152 | tf_op jit(solution)/shard_map/design/pallas_call | solution.py:351
  27.7 0.0 copy-start
  27.7 0.0 collective-permute-done.7.packets_ref.other_ref
  27.7 5.1 %design.3.refs_9_.refs_1_ = bf16[512,2048]{1,0:T(8,128)(2,1)S(1)} custom-call(s32[1]{0:T(128)} %bitcast.me_ref, s32[4,4096]{1,0:T(4,128)} %bitcast.15, bf16[8,16,256]{2,1,0:T(8,128)(2,1)S(1)} %collective-permute-done.7.packets_ref.other_ref), custom_call_target="tpu_custom_call" | custom-call | flops 2147483648 | bytes 2097152 | tf_op jit(solution)/shard_map/design/pallas_call | solution.py:351
  32.9 0.0 copy-done
  32.9 1.6 %fit.1 = (f32[128,1024]{1,0:T(8,128)S(1)}, f32[8,256]{1,0:T(8,128)S(1)}) custom-call(s32[1]{0:T(128)} %bitcast.me_ref, s32[1,4096]{1,0:T(1,128)S(1)} %bitcast.8, bf16[8,16,256]{2,1,0:T(8,128)(2,1)S(1)} %collect.1.packets_ref.own_ref, bf16[8,16,256]{2,1,0:T(8,128)(2,1)S(1)} %collective-permute-done.7.packets_ref.other_ref, ...), custom_call_target="tpu_custom_call" | custom-call | flops 536870912 | bytes 4194304 | tf_op jit(solution)/shard_map/fit/pallas_call | solution.py:380
  34.5 0.0 copy-start.2
  34.5 0.4 collective-permute-start.8
  34.9 1.6 %collective-permute-done.8.other_ref = f32[128,1024]{1,0:T(8,128)S(1)} collective-permute-done((f32[128,1024]{1,0:T(8,128)S(1)}, f32[128,1024]{1,0:T(8,128)S(1)}, u32[]{:S(2)}, u32[]{:S(2)}) %collective-permute-start.8) | collective-permute-done | bytes 524320 | tf_op jit(solution)/shard_map/ppermute | solution.py:280
  36.5 0.7 %sum.1 = (bf16[128,256]{1,0:T(8,128)(2,1)S(1)}, bf16[128,256]{1,0:T(8,128)(2,1)S(1)}, bf16[128,256]{1,0:T(8,128)(2,1)S(1)}, bf16[128,256]{1,0:T(8,128)(2,1)S(1)}...) custom-call(f32[128,1024]{1,0:T(8,128)S(1)} %get-tuple-element.31.ow, ...), custom_call_target="tpu_custom_call" | custom-call | flops 536870912 | bytes 4194304 | tf_op jit(solution)/shard_map/sum/pallas_call | solution.py:393
  37.2 1.7 %collective-permute-start.9 = (bf16[128,256]{1,0:T(8,128)(2,1)S(1)}, bf16[128,256]{1,0:T(8,128)(2,1)S(1)}, u32[]{:S(2)}, u32[]{:S(2)}) collective-permute-start(bf16[128,256]{1,0:T(8,128)(2,1)S(1)} %get-tuple-element.32), channel_id=1, source_target_pairs={{0,2},{1,3},{2,0},{3,1},{4,6},{5,7},{6,4},{7,5},{8,10},{9,11},{10,... | collective-permute-start | bytes 196616 | tf_op jit(solution)/shard_map/ppermute | solution.py:280
  38.9 1.4 %collective-permute-start.10 = (bf16[128,256]{1,0:T(8,128)(2,1)S(1)}, bf16[128,256]{1,0:T(8,128)(2,1)S(1)}, u32[]{:S(2)}, u32[]{:S(2)}) collective-permute-start(bf16[128,256]{1,0:T(8,128)(2,1)S(1)} %get-tuple-element.33), channel_id=1, source_target_pairs={{0,4},{1,5},{2,6},{3,7},{4,0},{5,1},{6,2},{7,3},{8,12},{9,13},{10,... | collective-permute-start | bytes 196616 | tf_op jit(solution)/shard_map/ppermute | solution.py:280
  40.3 0.6 %collective-permute-start.11 = (bf16[128,256]{1,0:T(8,128)(2,1)S(1)}, bf16[128,256]{1,0:T(8,128)(2,1)S(1)}, u32[]{:S(2)}, u32[]{:S(2)}) collective-permute-start(bf16[128,256]{1,0:T(8,128)(2,1)S(1)} %get-tuple-element.35), channel_id=1, source_target_pairs={{0,6},{1,7},{2,4},{3,5},{4,2},{5,3},{6,0},{7,1},{8,14},{9,15},{10,... | collective-permute-start | bytes 196616 | tf_op jit(solution)/shard_map/ppermute | solution.py:280
  40.9 3.1 %collective-permute-start.12 = (bf16[128,256]{1,0:T(8,128)(2,1)S(1)}, bf16[128,256]{1,0:T(8,128)(2,1)S(1)}, u32[]{:S(2)}, u32[]{:S(2)}) collective-permute-start(bf16[128,256]{1,0:T(8,128)(2,1)S(1)} %get-tuple-element.36), channel_id=1, source_target_pairs={{0,8},{1,9},{2,10},{3,11},{4,12},{5,13},{6,14},{7,15},{8,0},{9,1},... | collective-permute-start | bytes 196616 | tf_op jit(solution)/shard_map/ppermute | solution.py:280
  44.1 0.7 %collective-permute-start.13 = (bf16[128,256]{1,0:T(8,128)(2,1)S(1)}, bf16[128,256]{1,0:T(8,128)(2,1)S(1)}, u32[]{:S(2)}, u32[]{:S(2)}) collective-permute-start(bf16[128,256]{1,0:T(8,128)(2,1)S(1)} %get-tuple-element.37), channel_id=1, source_target_pairs={{0,10},{1,11},{2,8},{3,9},{4,14},{5,15},{6,12},{7,13},{8,2},{9,3},... | collective-permute-start | bytes 196616 | tf_op jit(solution)/shard_map/ppermute | solution.py:280
  44.7 0.0 collective-permute-done.9.refs_0_.refs_5_
  44.7 3.6 %collective-permute-start.14 = (bf16[128,256]{1,0:T(8,128)(2,1)S(1)}, bf16[128,256]{1,0:T(8,128)(2,1)S(1)}, u32[]{:S(2)}, u32[]{:S(2)}) collective-permute-start(bf16[128,256]{1,0:T(8,128)(2,1)S(1)} %get-tuple-element.38), channel_id=1, source_target_pairs={{0,12},{1,13},{2,14},{3,15},{4,8},{5,9},{6,10},{7,11},{8,4},{9,5},... | collective-permute-start | bytes 196616 | tf_op jit(solution)/shard_map/ppermute | solution.py:280
  48.4 0.0 collective-permute-done.10.refs_1_.refs_6_
  48.4 0.4 collective-permute-start.15
  48.8 0.0 copy-done.2
  48.8 2.4 %reorder.7.refs_3_ = bf16[512,1024]{1,0:T(8,128)(2,1)S(1)} custom-call(s32[1,512]{1,0:T(1,128)S(1)} %bitcast.10, bf16[2048,1024]{1,0:T(8,128)(2,1)S(1)} %copy-done.2, bf16[128,256]{1,0:T(8,128)(2,1)S(1)} %collective-permute-done.9.refs_0_.refs_5_, bf16[128,256]{1,0:T(8,128)(2,1)S(1)} %collective-permute-done.10.refs_1_.refs_6_), custom_call_target="tpu_custom_call" | custom-call | flops 2147483648 | bytes 4194304 | tf_op jit(solution)/shard_map/reorder/pallas_call | solution.py:323
  51.2 2.4 %reorder.6.refs_2_ = bf16[512,1024]{1,0:T(8,128)(2,1)S(1)} custom-call(s32[1,512]{1,0:T(1,128)S(1)} %bitcast.9, bf16[2048,1024]{1,0:T(8,128)(2,1)S(1)} %copy-done.2, bf16[128,256]{1,0:T(8,128)(2,1)S(1)} %collective-permute-done.9.refs_0_.refs_5_, bf16[128,256]{1,0:T(8,128)(2,1)S(1)} %collective-permute-done.10.refs_1_.refs_6_), custom_call_target="tpu_custom_call" | custom-call | flops 2147483648 | bytes 4194304 | tf_op jit(solution)/shard_map/reorder/pallas_call | solution.py:323
  53.5 0.0 collective-permute-done.11.refs_7_
  53.5 0.0 collective-permute-done.12.refs_8_
  53.5 0.0 collective-permute-done.13.refs_9_
  53.6 0.0 collective-permute-done.14.refs_10_
  53.6 1.9 %collective-permute-done.15.refs_11_ = bf16[128,256]{1,0:T(8,128)(2,1)S(1)} collective-permute-done((bf16[128,256]{1,0:T(8,128)(2,1)S(1)}, bf16[128,256]{1,0:T(8,128)(2,1)S(1)}, u32[]{:S(2)}, u32[]{:S(2)}) %collective-permute-start.15) | collective-permute-done | bytes 65568 | tf_op jit(solution)/shard_map/ppermute | solution.py:280
  55.4 2.6 %finish.1 = (f32[256,1024]{1,0:T(8,128)}, bf16[256,2048]{1,0:T(8,128)(2,1)}) custom-call(s32[1]{0:T(128)} %bitcast.me_ref, bf16[1024,256]{1,0:T(8,128)(2,1)S(1)} %get-tuple-element.21.corr_ref, f32[8,256]{1,0:T(8,128)S(1)} %get-tuple-element.30.scale_ref, bf16[512,1024]{1,0:T(8,128)(2,1)S(1)} %reorder.4.refs_8_.refs_0_, ...), custom_call_target="tpu_custom_call" | custom-call | tf_op jit(solution)/shard_map/finish/pallas_call | solution.py:405
  (1 shorter events, 0.0 us)
Async XLA Ops:
  2.0 9.6 %collective-permute-start = (bf16[144,256]{1,0:T(8,128)(2,1)S(1)}, bf16[144,256]{1,0:T(8,128)(2,1)S(1)}, u32[]{:S(2)}, u32[]{:S(2)}) collective-permute-start(bf16[144,256]{1,0:T(8,128)(2,1)S(1)} %get-tuple-element.23), channel_id=1, source_target_pairs={{0,2},{1,3},{2,0},{3,1},{4,6},{5,7},{6,4},{7,5},{8,10},{9,11},{10,... | collective-permute-start | bytes 221192 | tf_op jit(solution)/shard_map/ppermute | solution.py:280
  5.0 10.3 %collective-permute-start.1 = (bf16[144,256]{1,0:T(8,128)(2,1)S(1)}, bf16[144,256]{1,0:T(8,128)(2,1)S(1)}, u32[]{:S(2)}, u32[]{:S(2)}) collective-permute-start(bf16[144,256]{1,0:T(8,128)(2,1)S(1)} %get-tuple-element.24), channel_id=1, source_target_pairs={{0,4},{1,5},{2,6},{3,7},{4,0},{5,1},{6,2},{7,3},{8,12},{9,13},{10,... | collective-permute-start | bytes 221192 | tf_op jit(solution)/shard_map/ppermute | solution.py:280
  6.6 15.7 %collective-permute-start.2 = (bf16[144,256]{1,0:T(8,128)(2,1)S(1)}, bf16[144,256]{1,0:T(8,128)(2,1)S(1)}, u32[]{:S(2)}, u32[]{:S(2)}) collective-permute-start(bf16[144,256]{1,0:T(8,128)(2,1)S(1)} %get-tuple-element.25), channel_id=1, source_target_pairs={{0,6},{1,7},{2,4},{3,5},{4,2},{5,3},{6,0},{7,1},{8,14},{9,15},{10,... | collective-permute-start | bytes 221192 | tf_op jit(solution)/shard_map/ppermute | solution.py:280
  6.6 15.7 %collective-permute-start.3 = (bf16[144,256]{1,0:T(8,128)(2,1)S(1)}, bf16[144,256]{1,0:T(8,128)(2,1)S(1)}, u32[]{:S(2)}, u32[]{:S(2)}) collective-permute-start(bf16[144,256]{1,0:T(8,128)(2,1)S(1)} %get-tuple-element.26), channel_id=1, source_target_pairs={{0,8},{1,9},{2,10},{3,11},{4,12},{5,13},{6,14},{7,15},{8,0},{9,1},... | collective-permute-start | bytes 221192 | tf_op jit(solution)/shard_map/ppermute | solution.py:280
  9.6 12.7 %collective-permute-start.4 = (bf16[144,256]{1,0:T(8,128)(2,1)S(1)}, bf16[144,256]{1,0:T(8,128)(2,1)S(1)}, u32[]{:S(2)}, u32[]{:S(2)}) collective-permute-start(bf16[144,256]{1,0:T(8,128)(2,1)S(1)} %get-tuple-element.27), channel_id=1, source_target_pairs={{0,10},{1,11},{2,8},{3,9},{4,14},{5,15},{6,12},{7,13},{8,2},{9,3},... | collective-permute-start | bytes 221192 | tf_op jit(solution)/shard_map/ppermute | solution.py:280
  11.6 10.6 %collective-permute-start.5 = (bf16[144,256]{1,0:T(8,128)(2,1)S(1)}, bf16[144,256]{1,0:T(8,128)(2,1)S(1)}, u32[]{:S(2)}, u32[]{:S(2)}) collective-permute-start(bf16[144,256]{1,0:T(8,128)(2,1)S(1)} %get-tuple-element.28), channel_id=1, source_target_pairs={{0,12},{1,13},{2,14},{3,15},{4,8},{5,9},{6,10},{7,11},{8,4},{9,5},... | collective-permute-start | bytes 221192 | tf_op jit(solution)/shard_map/ppermute | solution.py:280
  15.2 7.2 %collective-permute-start.6 = (bf16[144,256]{1,0:T(8,128)(2,1)S(1)}, bf16[144,256]{1,0:T(8,128)(2,1)S(1)}, u32[]{:S(2)}, u32[]{:S(2)}) collective-permute-start(bf16[144,256]{1,0:T(8,128)(2,1)S(1)} %get-tuple-element.29), channel_id=1, source_target_pairs={{0,14},{1,15},{2,12},{3,13},{4,10},{5,11},{6,8},{7,9},{8,6},{9,7},... | collective-permute-start | bytes 221192 | tf_op jit(solution)/shard_map/ppermute | solution.py:280
  15.3 2.2 %copy-start.1 = (bf16[2048,1024]{1,0:T(8,128)(2,1)S(1)}, bf16[2048,1024]{1,0:T(8,128)(2,1)}, u32[]{:S(2)}) copy-start(bf16[2048,1024]{1,0:T(8,128)(2,1)} %slab_ref.7) | copy-start | bytes 12582916
  22.4 5.3 %collective-permute-start.7 = (bf16[8,16,256]{2,1,0:T(8,128)(2,1)S(1)}, bf16[8,16,256]{2,1,0:T(8,128)(2,1)S(1)}, u32[]{:S(2)}, u32[]{:S(2)}) collective-permute-start(bf16[8,16,256]{2,1,0:T(8,128)(2,1)S(1)} %collect.1.packets_ref.own_ref), channel_id=1, source_target_pairs={{0,1},{1,0},{2,3},{3,2},{4,5},{5,4},{6,7},{7,6},{8,9},{9,8},{10,11... | collective-permute-start | bytes 196616 | tf_op jit(solution)/shard_map/ppermute | solution.py:280
  27.7 5.2 %copy-start = (s32[4096]{0:T(1024)S(1)}, s32[4096]{0:T(1024)}, u32[]{:S(2)}) copy-start(s32[4096]{0:T(1024)} %param.8) | copy-start | bytes 49156
  34.5 14.3 %copy-start.2 = (bf16[2048,1024]{1,0:T(8,128)(2,1)S(1)}, bf16[2048,1024]{1,0:T(8,128)(2,1)}, u32[]{:S(2)}) copy-start(bf16[2048,1024]{1,0:T(8,128)(2,1)} %slab_ref.7) | copy-start | bytes 12582916
  34.5 2.0 %collective-permute-start.8 = (f32[128,1024]{1,0:T(8,128)S(1)}, f32[128,1024]{1,0:T(8,128)S(1)}, u32[]{:S(2)}, u32[]{:S(2)}) collective-permute-start(f32[128,1024]{1,0:T(8,128)S(1)} %get-tuple-element.31.own_ref), channel_id=1, source_target_pairs={{0,1},{1,0},{2,3},{3,2},{4,5},{5,4},{6,7},{7,6},{8,9},{9,8},{10,11... | collective-permute-start | bytes 1572872 | tf_op jit(solution)/shard_map/ppermute | solution.py:280
  37.2 7.5 %collective-permute-start.9 = (bf16[128,256]{1,0:T(8,128)(2,1)S(1)}, bf16[128,256]{1,0:T(8,128)(2,1)S(1)}, u32[]{:S(2)}, u32[]{:S(2)}) collective-permute-start(bf16[128,256]{1,0:T(8,128)(2,1)S(1)} %get-tuple-element.32), channel_id=1, source_target_pairs={{0,2},{1,3},{2,0},{3,1},{4,6},{5,7},{6,4},{7,5},{8,10},{9,11},{10,... | collective-permute-start | bytes 196616 | tf_op jit(solution)/shard_map/ppermute | solution.py:280
  38.9 9.5 %collective-permute-start.10 = (bf16[128,256]{1,0:T(8,128)(2,1)S(1)}, bf16[128,256]{1,0:T(8,128)(2,1)S(1)}, u32[]{:S(2)}, u32[]{:S(2)}) collective-permute-start(bf16[128,256]{1,0:T(8,128)(2,1)S(1)} %get-tuple-element.33), channel_id=1, source_target_pairs={{0,4},{1,5},{2,6},{3,7},{4,0},{5,1},{6,2},{7,3},{8,12},{9,13},{10,... | collective-permute-start | bytes 196616 | tf_op jit(solution)/shard_map/ppermute | solution.py:280
  40.3 13.2 %collective-permute-start.11 = (bf16[128,256]{1,0:T(8,128)(2,1)S(1)}, bf16[128,256]{1,0:T(8,128)(2,1)S(1)}, u32[]{:S(2)}, u32[]{:S(2)}) collective-permute-start(bf16[128,256]{1,0:T(8,128)(2,1)S(1)} %get-tuple-element.35), channel_id=1, source_target_pairs={{0,6},{1,7},{2,4},{3,5},{4,2},{5,3},{6,0},{7,1},{8,14},{9,15},{10,... | collective-permute-start | bytes 196616 | tf_op jit(solution)/shard_map/ppermute | solution.py:280
  40.9 12.6 %collective-permute-start.12 = (bf16[128,256]{1,0:T(8,128)(2,1)S(1)}, bf16[128,256]{1,0:T(8,128)(2,1)S(1)}, u32[]{:S(2)}, u32[]{:S(2)}) collective-permute-start(bf16[128,256]{1,0:T(8,128)(2,1)S(1)} %get-tuple-element.36), channel_id=1, source_target_pairs={{0,8},{1,9},{2,10},{3,11},{4,12},{5,13},{6,14},{7,15},{8,0},{9,1},... | collective-permute-start | bytes 196616 | tf_op jit(solution)/shard_map/ppermute | solution.py:280
  44.1 9.5 %collective-permute-start.13 = (bf16[128,256]{1,0:T(8,128)(2,1)S(1)}, bf16[128,256]{1,0:T(8,128)(2,1)S(1)}, u32[]{:S(2)}, u32[]{:S(2)}) collective-permute-start(bf16[128,256]{1,0:T(8,128)(2,1)S(1)} %get-tuple-element.37), channel_id=1, source_target_pairs={{0,10},{1,11},{2,8},{3,9},{4,14},{5,15},{6,12},{7,13},{8,2},{9,3},... | collective-permute-start | bytes 196616 | tf_op jit(solution)/shard_map/ppermute | solution.py:280
  44.7 8.8 %collective-permute-start.14 = (bf16[128,256]{1,0:T(8,128)(2,1)S(1)}, bf16[128,256]{1,0:T(8,128)(2,1)S(1)}, u32[]{:S(2)}, u32[]{:S(2)}) collective-permute-start(bf16[128,256]{1,0:T(8,128)(2,1)S(1)} %get-tuple-element.38), channel_id=1, source_target_pairs={{0,12},{1,13},{2,14},{3,15},{4,8},{5,9},{6,10},{7,11},{8,4},{9,5},... | collective-permute-start | bytes 196616 | tf_op jit(solution)/shard_map/ppermute | solution.py:280
  48.4 7.1 %collective-permute-start.15 = (bf16[128,256]{1,0:T(8,128)(2,1)S(1)}, bf16[128,256]{1,0:T(8,128)(2,1)S(1)}, u32[]{:S(2)}, u32[]{:S(2)}) collective-permute-start(bf16[128,256]{1,0:T(8,128)(2,1)S(1)} %get-tuple-element.39), channel_id=1, source_target_pairs={{0,14},{1,15},{2,12},{3,13},{4,10},{5,11},{6,8},{7,9},{8,6},{9,7},... | collective-permute-start | bytes 196616 | tf_op jit(solution)/shard_map/ppermute | solution.py:280

commit v8 on v7

--- a/solution.py
+++ b/solution.py
@@ -29,6 +29,10 @@
     return [high, values - high]
 
 
+def partner(slot, chips):
+    return slot and (slot + chips // 2 - 2) % (chips - 1) + 1
+
+
 def rows_of(index, count):
     return pl.ds(pl.multiple_of(index * count, count), count)
 
@@ -50,7 +54,7 @@
         pieces.append(jnp.zeros((sent_rows - count - used, terms), jnp.float32))
     packet = jnp.concatenate(pieces, axis=0).astype(jnp.bfloat16)
     for k, sent_ref in enumerate(sent_refs):
-        chip = (me_ref[0] // CORES) ^ k
+        chip = (me_ref[0] // CORES) ^ partner(k, len(sent_refs))
         sent_ref[0:count, :] = turned_ref[rows_of(chip, count), :]
         sent_ref[count:sent_rows, :] = packet
 
@@ -82,73 +86,85 @@
         packets_ref[k] = block_ref[count - rows : count, :]
 
 
+def choose_kernel(dim, chips, me_ref, codes_ref, *refs):
+    chosen_ref, spots_ref = refs[-2:]
+    matmuls, rows, terms = chosen_ref.shape
+    half, tile = rows // 2, terms // chips
+    row = lax.broadcasted_iota(jnp.int32, (half, tile), 0)
+    for k in range(chips):
+        device = me_ref[0] ^ (CORES * partner(k, chips))
+        lanes = slice(k * tile, (k + 1) * tile)
+        codes = codes_ref[:, rows_of(device, tile)]
+        spots = (codes % DEGREES) * dim + codes // DEGREES
+        spots_ref[:, lanes] = spots[matmuls:, :]
+        for slot in range(matmuls):
+            picked = jnp.where(row == spots[slot : slot + 1, :], 1.0, 0.0).astype(
+                jnp.bfloat16
+            )
+            chosen_ref[slot, 0:half, lanes] = picked
+            chosen_ref[slot, half:rows, lanes] = picked
+
+
 def design_kernel(
-    dim, run_count, me_ref, codes_ref, packets_ref, design_ref, exact, table, chosen
+    dim, run_count, packets_ref, chosen_ref, spots_ref, design_ref, exact, table
 ):
-    chips, _, terms = packets_ref.shape
+    chips, _, tile = packets_ref.shape
     half = exact.shape[1]
-    rows = dim * run_count // terms
-
-    @pl.when(pl.program_id(0) == 0)
-    def _():
-        per = LANES // run_count
-        for group in range(chips // per):
-            owned = []
-            for i in range(per):
-                packet = packets_ref[group * per + i].astype(jnp.float32)
-                owned.append(packet[0:rows, :] + packet[rows : 2 * rows, :])
-            points = jnp.concatenate(
-                [
-                    jnp.concatenate(
-                        [inputs[:, start : start + run_count] for inputs in owned],
-                        axis=1,
-                    )
-                    for start in range(0, terms, run_count)
-                ],
-                axis=0,
-            )
-            columns = hermite_columns(points)
-            columns = jnp.concatenate(
-                [
-                    columns,
-                    jnp.zeros((half - columns.shape[0], LANES), jnp.float32),
-                ],
-                axis=0,
-            ).T
-            high = columns.astype(jnp.bfloat16)
-            low = (columns - high.astype(jnp.float32)).astype(jnp.bfloat16)
-            block = slice(group * LANES, (group + 1) * LANES)
-            exact[block, :] = columns
-            table[block, 0:half] = high
-            table[block, half : 2 * half] = low
-
-    codes = codes_ref[...]
-    spots = (codes % DEGREES) * dim + codes // DEGREES
-    slots, terms = codes.shape
-    row = lax.broadcasted_iota(jnp.int32, (half, terms), 0)
-    matmuls = chosen.shape[0]
-    for slot in range(matmuls):
-        picked = jnp.where(row == spots[slot : slot + 1, :], 1.0, 0.0).astype(
-            jnp.bfloat16
+    rows = dim * run_count // tile
+    terms = tile
+    per = LANES // run_count
+    for group in range(chips // per):
+        owned = []
+        for i in range(per):
+            packet = packets_ref[group * per + i].astype(jnp.float32)
+            owned.append(packet[0:rows, :] + packet[rows : 2 * rows, :])
+        points = jnp.concatenate(
+            [
+                jnp.concatenate(
+                    [inputs[:, start : start + run_count] for inputs in owned],
+                    axis=1,
+                )
+                for start in range(0, terms, run_count)
+            ],
+            axis=0,
         )
-        chosen[slot, 0:half, :] = picked
-        chosen[slot, half : 2 * half, :] = picked
+        columns = hermite_columns(points)
+        columns = jnp.concatenate(
+            [
+                columns,
+                jnp.zeros((half - columns.shape[0], LANES), jnp.float32),
+            ],
+            axis=0,
+        ).T
+        high = columns.astype(jnp.bfloat16)
+        low = (columns - high.astype(jnp.float32)).astype(jnp.bfloat16)
+        block = slice(group * LANES, (group + 1) * LANES)
+        exact[block, :] = columns
+        table[block, 0:half] = high
+        table[block, half : 2 * half] = low
+
     for start in range(0, table.shape[0], LANES):
         block = slice(start, start + LANES)
-        rows = exact[block, :]
-        product = None
-        for slot in range(matmuls):
-            factor = jnp.dot(
-                table[block, :], chosen[slot], preferred_element_type=jnp.float32
-            )
-            product = factor if product is None else product * factor
-        for part in range(0, terms, half):
-            lanes = slice(part, part + half)
-            factor = product[:, lanes]
-            for slot in range(matmuls, slots):
-                spot = jnp.broadcast_to(spots[slot : slot + 1, lanes], rows.shape)
-                factor = factor * jnp.take_along_axis(rows, spot, axis=1)
-            design_ref[block, lanes] = factor.astype(jnp.bfloat16)
+        values = exact[block, :]
+        for first in range(0, design_ref.shape[1], tile):
+            lanes = slice(first, first + tile)
+            product = None
+            for slot in range(chosen_ref.shape[0]):
+                factor = jnp.dot(
+                    table[block, :],
+                    chosen_ref[slot, :, lanes],
+                    preferred_element_type=jnp.float32,
+                )
+                product = factor if product is None else product * factor
+            for part in range(0, tile, half):
+                factor = product[:, part : part + half]
+                lanes = slice(first + part, first + part + half)
+                for slot in range(spots_ref.shape[0]):
+                    spot = jnp.broadcast_to(
+                        spots_ref[slot : slot + 1, lanes], values.shape
+                    )
+                    factor = factor * jnp.take_along_axis(values, spot, axis=1)
+                design_ref[block, lanes] = factor.astype(jnp.bfloat16)
 
 
 def shrink_factor(squares, limits):
@@ -160,7 +176,7 @@
     for k in range(packets_ref.shape[0]):
         packet = packets_ref[k].astype(jnp.float32)
         squares.append(packet[row : row + 1, :] + packet[row + 1 : row + 2, :])
-        device = first ^ (CORES * k)
+        device = first ^ (CORES * partner(k, packets_ref.shape[0]))
         levels.append(levels_ref[:, rows_of(device, packets_ref.shape[2])])
     weights = jnp.exp2(jnp.concatenate(levels, axis=1).astype(jnp.float32))
     return jnp.concatenate(squares, axis=1), weights
@@ -231,7 +247,7 @@
     count = summed_refs[0].shape[0]
     squares = jnp.zeros((1, terms), jnp.float32)
     for k, summed_ref in enumerate(summed_refs):
-        rows = rows_of((me_ref[0] // CORES) ^ k, count)
+        rows = rows_of((me_ref[0] // CORES) ^ partner(k, len(summed_refs)), count)
         corr = corr_ref[rows, :].astype(jnp.float32)
         first = STEP * corr * scale_ref[0:1, :]
         gradient = summed_ref[...].astype(jnp.float32) - corr
@@ -281,8 +297,9 @@
 
 
 def to_chips(arrays):
+    chips = len(arrays)
     return [arrays[0]] + [
-        to_device(arrays[k], CORES * k) for k in range(1, len(arrays))
+        to_device(arrays[k], CORES * partner(k, chips)) for k in range(1, chips)
     ]
 
 
@@ -333,44 +350,48 @@
     starts = range(0, slab_cells, block)
     early = len(starts) // 2
     ordered = [reorder(start, *blocks[1:3]) for start in starts[:early]]
+    half = round_up(DEGREES * dim, LANES)
+    gathers = slots // 4
+    chosen, spots = pl.pallas_call(
+        functools.partial(choose_kernel, dim, chips),
+        in_specs=[smem, vmem] + [anywhere] * 2,
+        out_specs=[vmem, vmem],
+        out_shape=[
+            jax.ShapeDtypeStruct((slots - gathers, 2 * half, core_terms), jnp.bfloat16),
+            jax.ShapeDtypeStruct((gathers, core_terms), jnp.int32),
+        ],
+        compiler_params=params(8),
+        cost_estimate=cost(0, 2 * slots * half * core_terms),
+        name="choose",
+    )(me, in_hbm(term_codes.T), *blocks[1:3])
     packets = pl.pallas_call(
         functools.partial(collect_kernel, chips),
-        in_specs=[vmem] * chips + [anywhere] * early,
+        in_specs=[vmem] * chips + [anywhere] * (early + 1),
         out_specs=vmem,
         out_shape=jax.ShapeDtypeStruct((chips, packet_rows, term_count), jnp.bfloat16),
         compiler_params=params(8),
         name="collect",
-    )(*blocks, *ordered)
+    )(*blocks, *ordered, spots)
     others = to_device(packets, 1)
 
-    tile = term_count
-    half = round_up(DEGREES * dim, LANES)
     core_runs = run_count * chips
 
     def design_of(packets):
         return pl.pallas_call(
             functools.partial(design_kernel, dim, run_count),
-            grid_spec=pltpu.PrefetchScalarGridSpec(
-                num_scalar_prefetch=1,
-                grid=(chips,),
-                in_specs=[
-                    pl.BlockSpec((slots, tile), lambda i, me: (0, me[0] ^ (CORES * i))),
-                    pl.BlockSpec(packets.shape, lambda i, me: (0, 0, 0)),
-                ],
-                out_specs=pl.BlockSpec((core_runs, tile), lambda i, me: (0, i)),
-                scratch_shapes=[
-                    pltpu.VMEM((core_runs, half), jnp.float32),
-                    pltpu.VMEM((core_runs, 2 * half), jnp.bfloat16),
-                    pltpu.VMEM((slots - slots // 4, 2 * half, tile), jnp.bfloat16),
-                ],
-            ),
+            in_specs=[vmem] * 3,
+            out_specs=vmem,
             out_shape=jax.ShapeDtypeStruct((core_runs, core_terms), jnp.bfloat16),
+            scratch_shapes=[
+                pltpu.VMEM((core_runs, half), jnp.float32),
+                pltpu.VMEM((core_runs, 2 * half), jnp.bfloat16),
+            ],
             compiler_params=params(16),
             cost_estimate=cost(
                 4 * core_runs * core_terms * slots * half, 2 * core_runs * core_terms
             ),
             name="design",
-        )(me, in_hbm(term_codes.T), packets)
+        )(packets, chosen, spots)
 
     designs = [design_of(packets), design_of(others)]
 

time: 58.8 us -> 57.2 us (0.973)
  Pallas kernels: 26.1 us -> 21.5 us
  waiting for transfers between devices: 3.63 us -> 8.07 us
  starting transfers between devices: 24.5 us -> 23.4 us
    pallas_call x2 -> x3, Pallas kernels: 10.4 us -> 5.6 us  [the longest x2 4.31 us: design_of(): pl.pallas_call(functools.partial(design_kernel, dim, run_count), in_specs...]
    ppermute x16, waiting for transfers between devices: 3.63 us -> 8.07 us  [to_device(): return lax.ppermute(array, 'runs', [(i, i ^ bits) for i in range(devices)])]
    ppermute x16, starting transfers between devices: 24.5 us -> 23.4 us  [to_device(): return lax.ppermute(array, 'runs', [(i, i ^ bits) for i in range(devices)])]
  transfers between devices with their start and end apart: 16 -> 16, of which waited for: 3 -> 5; matrix products, arithmetic and copies ran while one was open for 1% -> 1% of each run, Pallas kernels for 25% -> 23%
where the time goes in v8:
time: 57.2 us; the launch traced here: 57 us
  starting transfers between devices  23.4 us (41%)
  Pallas kernels  21.5 us (38%)
  waiting for transfers between devices  8.07 us (14%)
  local copies, waits for them, and re-layouts  2.97 us (5%)
  between operations  0.99 us (2%)
    ppermute x16, starting transfers between devices, to_device(): return lax.ppermute(array, 'runs', [(i, i ^ bits) for i in range(devices)])  23.4 us
    pallas_call x4, Pallas kernels, reorder(): pl.pallas_call(reorder_kernel, in_specs=[vmem, vmem] + [anywhere] * len(a...  9.64 us
    ppermute x16, waiting for transfers between devices, to_device(): return lax.ppermute(array, 'runs', [(i, i ^ bits) for i in range(devices)])  8.07 us
    pallas_call x2, Pallas kernels, design_of(): pl.pallas_call(functools.partial(design_kernel, dim, run_count), in_specs...  4.31 us
    pallas_call x1, Pallas kernels, split_by_modes(): pl.pallas_call(functools.partial(finish_kernel, len(ordered)), in_specs=[...  2.58 us
    unnamed x6, local copies, waits for them, and re-layouts  2.2 us
    pallas_call x1, Pallas kernels, split_by_modes(): pl.pallas_call(functools.partial(fit_kernel, 2 * rows), in_specs=[smem] +...  1.62 us
    pallas_call x1, Pallas kernels, split_by_modes(): pl.pallas_call(prepare_kernel, in_specs=[smem, vmem, vmem], out_specs=[vm...  1.35 us
  transfers between devices with their start and end apart: 16, of which 5 were waited for; matrix products, arithmetic and copies ran while one was open for 1% of the time, Pallas kernels for 23%

profile of v8, /device:TPU:0, one launch (start us, length us, event | category | flops | bytes accessed | tf_op | source)
XLA Modules:
  0.0 57.0 jit_solution(14444898138909015001)
XLA Ops:
  0.6 1.3 %prepare.1 = (bf16[1024,256]{1,0:T(8,128)(2,1)S(1)}, bf16[144,256]{1,0:T(8,128)(2,1)S(1)}, bf16[144,256]{1,0:T(8,128)(2,1)S(1)}, bf16[144,256]{1,0:T(8,128)(2,1)...) custom-call(s32[1]{0:T(128)} %bitcast.me_ref, ...), custom_call_target="tpu_custom_call" | custom-call | tf_op jit(solution)/shard_map/prepare/pallas_call | solution.py:325
  2.0 4.1 %collective-permute-start = (bf16[144,256]{1,0:T(8,128)(2,1)S(1)}, bf16[144,256]{1,0:T(8,128)(2,1)S(1)}, u32[]{:S(2)}, u32[]{:S(2)}) collective-permute-start(bf16[144,256]{1,0:T(8,128)(2,1)S(1)} %get-tuple-element.25), channel_id=1, source_target_pairs={{0,8},{1,9},{2,10},{3,11},{4,12},{5,13},{6,14},{7,15},{8,0},{9,1},... | collective-permute-start | bytes 221192 | tf_op jit(solution)/shard_map/ppermute | solution.py:296
  6.1 1.3 %collective-permute-start.1 = (bf16[144,256]{1,0:T(8,128)(2,1)S(1)}, bf16[144,256]{1,0:T(8,128)(2,1)S(1)}, u32[]{:S(2)}, u32[]{:S(2)}) collective-permute-start(bf16[144,256]{1,0:T(8,128)(2,1)S(1)} %get-tuple-element.26), channel_id=1, source_target_pairs={{0,10},{1,11},{2,8},{3,9},{4,14},{5,15},{6,12},{7,13},{8,2},{9,3},... | collective-permute-start | bytes 221192 | tf_op jit(solution)/shard_map/ppermute | solution.py:296
  7.3 3.6 %collective-permute-start.2 = (bf16[144,256]{1,0:T(8,128)(2,1)S(1)}, bf16[144,256]{1,0:T(8,128)(2,1)S(1)}, u32[]{:S(2)}, u32[]{:S(2)}) collective-permute-start(bf16[144,256]{1,0:T(8,128)(2,1)S(1)} %get-tuple-element.27), channel_id=1, source_target_pairs={{0,12},{1,13},{2,14},{3,15},{4,8},{5,9},{6,10},{7,11},{8,4},{9,5},... | collective-permute-start | bytes 221192 | tf_op jit(solution)/shard_map/ppermute | solution.py:296
  11.0 0.0 collective-permute-start.3
  11.0 1.7 %collective-permute-start.4 = (bf16[144,256]{1,0:T(8,128)(2,1)S(1)}, bf16[144,256]{1,0:T(8,128)(2,1)S(1)}, u32[]{:S(2)}, u32[]{:S(2)}) collective-permute-start(bf16[144,256]{1,0:T(8,128)(2,1)S(1)} %get-tuple-element.29), channel_id=1, source_target_pairs={{0,2},{1,3},{2,0},{3,1},{4,6},{5,7},{6,4},{7,5},{8,10},{9,11},{10,... | collective-permute-start | bytes 221192 | tf_op jit(solution)/shard_map/ppermute | solution.py:296
  12.6 0.8 %fusion = (s32[512]{0:T(512)S(1)}, s32[512]{0:T(512)S(1)}, s32[512]{0:T(512)S(1)}, s32[512]{0:T(512)S(1)}) fusion(s32[2048]{0:T(1024)} %param.11), kind=kLoop, calls=%fused_computation | loop fusion | bytes 16384 | tf_op jit(solution)/shard_map/slice | solution.py:348
  13.4 0.0 collective-permute-done.refs_0_.refs_1_
  13.4 1.0 %collective-permute-start.5 = (bf16[144,256]{1,0:T(8,128)(2,1)S(1)}, bf16[144,256]{1,0:T(8,128)(2,1)S(1)}, u32[]{:S(2)}, u32[]{:S(2)}) collective-permute-start(bf16[144,256]{1,0:T(8,128)(2,1)S(1)} %get-tuple-element.30), channel_id=1, source_target_pairs={{0,4},{1,5},{2,6},{3,7},{4,0},{5,1},{6,2},{7,3},{8,12},{9,13},{10,... | collective-permute-start | bytes 221192 | tf_op jit(solution)/shard_map/ppermute | solution.py:296
  14.4 2.7 %collective-permute-done.1.refs_1_.refs_2_ = bf16[144,256]{1,0:T(8,128)(2,1)S(1)} collective-permute-done((bf16[144,256]{1,0:T(8,128)(2,1)S(1)}, bf16[144,256]{1,0:T(8,128)(2,1)S(1)}, u32[]{:S(2)}, u32[]{:S(2)}) %collective-permute-start.1) | collective-permute-done | bytes 73760 | tf_op jit(solution)/shard_map/ppermute | solution.py:296
  17.1 0.9 %collective-permute-start.6 = (bf16[144,256]{1,0:T(8,128)(2,1)S(1)}, bf16[144,256]{1,0:T(8,128)(2,1)S(1)}, u32[]{:S(2)}, u32[]{:S(2)}) collective-permute-start(bf16[144,256]{1,0:T(8,128)(2,1)S(1)} %get-tuple-element.31), channel_id=1, source_target_pairs={{0,6},{1,7},{2,4},{3,5},{4,2},{5,3},{6,0},{7,1},{8,14},{9,15},{10,... | collective-permute-start | bytes 221192 | tf_op jit(solution)/shard_map/ppermute | solution.py:296
  18.0 0.0 copy-start.1
  18.0 2.2 %copy-done.1 = bf16[2048,1024]{1,0:T(8,128)(2,1)S(1)} copy-done((bf16[2048,1024]{1,0:T(8,128)(2,1)S(1)}, bf16[2048,1024]{1,0:T(8,128)(2,1)}, u32[]{:S(2)}) %copy-start.1) | copy-done | bytes 4194328
  20.2 2.4 %reorder.5.refs_9_.refs_1_ = bf16[512,1024]{1,0:T(8,128)(2,1)S(1)} custom-call(s32[1,512]{1,0:T(1,128)S(1)} %bitcast.12, bf16[2048,1024]{1,0:T(8,128)(2,1)S(1)} %copy-done.1, bf16[144,256]{1,0:T(8,128)(2,1)S(1)} %collective-permute-done.refs_0_.refs_1_, bf16[144,256]{1,0:T(8,128)(2,1)S(1)} %collective-permute-done.1.refs_1_.refs_2_), custom_call_target="tpu_custom_call" | custom-call | flops 2147483648 | bytes 4194304 | tf_op jit(solution)/shard_map/reorder/pallas_call | solution.py:340
  22.5 2.4 %reorder.4.refs_8_.refs_0_ = bf16[512,1024]{1,0:T(8,128)(2,1)S(1)} custom-call(s32[1,512]{1,0:T(1,128)S(1)} %bitcast.11, bf16[2048,1024]{1,0:T(8,128)(2,1)S(1)} %copy-done.1, bf16[144,256]{1,0:T(8,128)(2,1)S(1)} %collective-permute-done.refs_0_.refs_1_, bf16[144,256]{1,0:T(8,128)(2,1)S(1)} %collective-permute-done.1.refs_1_.refs_2_), custom_call_target="tpu_custom_call" | custom-call | flops 2147483648 | bytes 4194304 | tf_op jit(solution)/shard_map/reorder/pallas_call | solution.py:340
  24.9 1.3 %choose.1 = (bf16[3,256,2048]{2,1,0:T(8,128)(2,1)S(1)}, s32[1,2048]{1,0:T(1,128)S(1)}) custom-call(s32[1]{0:T(128)} %bitcast.me_ref, s32[4,4096]{1,0:T(4,128)} %bitcast.13, bf16[144,256]{1,0:T(8,128)(2,1)S(1)} %collective-permute-done.refs_0_.refs_1_, bf16[144,256]{1,0:T(8,128)(2,1)S(1)} %collective-permute-done.1.refs_1_.refs_2_), custom_call_target="tpu_custom_call" | custom-call | bytes 2097152 | tf_op jit(solution)/shard_map/choose/pallas_call | solution.py:355
  26.2 0.0 collective-permute-done.2.refs_3_
  26.2 0.0 collective-permute-done.3.refs_4_
  26.2 0.0 collective-permute-done.4.refs_5_
  26.2 0.0 collective-permute-done.5.refs_6_
  26.2 0.0 collective-permute-done.6.refs_7_
  26.3 0.1 collective-permute-start.7
  26.4 2.2 %design.2.refs_8_.refs_0_ = bf16[512,2048]{1,0:T(8,128)(2,1)S(1)} custom-call(bf16[8,16,256]{2,1,0:T(8,128)(2,1)S(1)} %collect.1.packets_ref.own_ref, bf16[3,256,2048]{2,1,0:T(8,128)(2,1)S(1)} %get-tuple-element.33.chosen_ref, s32[1,2048]{1,0:T(1,128)S(1)} %get-tuple-element.32.refs_10_.spots_ref), custom_call_target="tpu_custom_call" | custom-call | flops 2147483648 | bytes 2097152 | tf_op jit(solution)/shard_map/design/pallas_call | solution.py:380
  28.5 0.0 copy-start
  28.5 0.0 collective-permute-done.7.packets_ref.other_ref
  28.5 2.2 %design.3.refs_9_.refs_1_ = bf16[512,2048]{1,0:T(8,128)(2,1)S(1)} custom-call(bf16[8,16,256]{2,1,0:T(8,128)(2,1)S(1)} %collective-permute-done.7.packets_ref.other_ref, bf16[3,256,2048]{2,1,0:T(8,128)(2,1)S(1)} %get-tuple-element.33.chosen_ref, s32[1,2048]{1,0:T(1,128)S(1)} %get-tuple-element.32.refs_10_.spots_ref), custom_call_target="tpu_custom_call" | custom-call | flops 2147483648 | bytes 2097152 | tf_op jit(solution)/shard_map/design/pallas_call | solution.py:380
  30.7 0.0 copy-done
  30.7 1.6 %fit.1 = (f32[128,1024]{1,0:T(8,128)S(1)}, f32[8,256]{1,0:T(8,128)S(1)}) custom-call(s32[1]{0:T(128)} %bitcast.me_ref, s32[1,4096]{1,0:T(1,128)S(1)} %bitcast.8, bf16[8,16,256]{2,1,0:T(8,128)(2,1)S(1)} %collect.1.packets_ref.own_ref, bf16[8,16,256]{2,1,0:T(8,128)(2,1)S(1)} %collective-permute-done.7.packets_ref.other_ref, ...), custom_call_target="tpu_custom_call" | custom-call | flops 536870912 | bytes 4194304 | tf_op jit(solution)/shard_map/fit/pallas_call | solution.py:401
  32.3 0.0 copy-start.2
  32.4 0.6 collective-permute-start.8
  32.9 1.5 %collective-permute-done.8.other_ref = f32[128,1024]{1,0:T(8,128)S(1)} collective-permute-done((f32[128,1024]{1,0:T(8,128)S(1)}, f32[128,1024]{1,0:T(8,128)S(1)}, u32[]{:S(2)}, u32[]{:S(2)}) %collective-permute-start.8) | collective-permute-done | bytes 524320 | tf_op jit(solution)/shard_map/ppermute | solution.py:296
  34.4 0.7 %sum.1 = (bf16[128,256]{1,0:T(8,128)(2,1)S(1)}, bf16[128,256]{1,0:T(8,128)(2,1)S(1)}, bf16[128,256]{1,0:T(8,128)(2,1)S(1)}, bf16[128,256]{1,0:T(8,128)(2,1)S(1)}...) custom-call(f32[128,1024]{1,0:T(8,128)S(1)} %get-tuple-element.35.ow, ...), custom_call_target="tpu_custom_call" | custom-call | flops 536870912 | bytes 4194304 | tf_op jit(solution)/shard_map/sum/pallas_call | solution.py:414
  35.2 3.6 %collective-permute-start.9 = (bf16[128,256]{1,0:T(8,128)(2,1)S(1)}, bf16[128,256]{1,0:T(8,128)(2,1)S(1)}, u32[]{:S(2)}, u32[]{:S(2)}) collective-permute-start(bf16[128,256]{1,0:T(8,128)(2,1)S(1)} %get-tuple-element.36), channel_id=1, source_target_pairs={{0,8},{1,9},{2,10},{3,11},{4,12},{5,13},{6,14},{7,15},{8,0},{9,1},... | collective-permute-start | bytes 196616 | tf_op jit(solution)/shard_map/ppermute | solution.py:296
  38.8 0.9 %collective-permute-start.10 = (bf16[128,256]{1,0:T(8,128)(2,1)S(1)}, bf16[128,256]{1,0:T(8,128)(2,1)S(1)}, u32[]{:S(2)}, u32[]{:S(2)}) collective-permute-start(bf16[128,256]{1,0:T(8,128)(2,1)S(1)} %get-tuple-element.37), channel_id=1, source_target_pairs={{0,10},{1,11},{2,8},{3,9},{4,14},{5,15},{6,12},{7,13},{8,2},{9,3},... | collective-permute-start | bytes 196616 | tf_op jit(solution)/shard_map/ppermute | solution.py:296
  39.6 1.5 %collective-permute-start.11 = (bf16[128,256]{1,0:T(8,128)(2,1)S(1)}, bf16[128,256]{1,0:T(8,128)(2,1)S(1)}, u32[]{:S(2)}, u32[]{:S(2)}) collective-permute-start(bf16[128,256]{1,0:T(8,128)(2,1)S(1)} %get-tuple-element.39), channel_id=1, source_target_pairs={{0,12},{1,13},{2,14},{3,15},{4,8},{5,9},{6,10},{7,11},{8,4},{9,5},... | collective-permute-start | bytes 196616 | tf_op jit(solution)/shard_map/ppermute | solution.py:296
  41.1 2.4 %collective-permute-start.12 = (bf16[128,256]{1,0:T(8,128)(2,1)S(1)}, bf16[128,256]{1,0:T(8,128)(2,1)S(1)}, u32[]{:S(2)}, u32[]{:S(2)}) collective-permute-start(bf16[128,256]{1,0:T(8,128)(2,1)S(1)} %get-tuple-element.40), channel_id=1, source_target_pairs={{0,14},{1,15},{2,12},{3,13},{4,10},{5,11},{6,8},{7,9},{8,6},{9,7},... | collective-permute-start | bytes 196616 | tf_op jit(solution)/shard_map/ppermute | solution.py:296
  43.6 1.4 %collective-permute-start.13 = (bf16[128,256]{1,0:T(8,128)(2,1)S(1)}, bf16[128,256]{1,0:T(8,128)(2,1)S(1)}, u32[]{:S(2)}, u32[]{:S(2)}) collective-permute-start(bf16[128,256]{1,0:T(8,128)(2,1)S(1)} %get-tuple-element.41), channel_id=1, source_target_pairs={{0,2},{1,3},{2,0},{3,1},{4,6},{5,7},{6,4},{7,5},{8,10},{9,11},{10,... | collective-permute-start | bytes 196616 | tf_op jit(solution)/shard_map/ppermute | solution.py:296
  44.9 0.8 %collective-permute-done.9.refs_0_.refs_5_ = bf16[128,256]{1,0:T(8,128)(2,1)S(1)} collective-permute-done((bf16[128,256]{1,0:T(8,128)(2,1)S(1)}, bf16[128,256]{1,0:T(8,128)(2,1)S(1)}, u32[]{:S(2)}, u32[]{:S(2)}) %collective-permute-start.9) | collective-permute-done | bytes 65568 | tf_op jit(solution)/shard_map/ppermute | solution.py:296
  45.7 0.6 %collective-permute-start.14 = (bf16[128,256]{1,0:T(8,128)(2,1)S(1)}, bf16[128,256]{1,0:T(8,128)(2,1)S(1)}, u32[]{:S(2)}, u32[]{:S(2)}) collective-permute-start(bf16[128,256]{1,0:T(8,128)(2,1)S(1)} %get-tuple-element.42), channel_id=1, source_target_pairs={{0,4},{1,5},{2,6},{3,7},{4,0},{5,1},{6,2},{7,3},{8,12},{9,13},{10,... | collective-permute-start | bytes 196616 | tf_op jit(solution)/shard_map/ppermute | solution.py:296
  46.3 2.8 %collective-permute-done.10.refs_1_.refs_6_ = bf16[128,256]{1,0:T(8,128)(2,1)S(1)} collective-permute-done((bf16[128,256]{1,0:T(8,128)(2,1)S(1)}, bf16[128,256]{1,0:T(8,128)(2,1)S(1)}, u32[]{:S(2)}, u32[]{:S(2)}) %collective-permute-start.10) | collective-permute-done | bytes 65568 | tf_op jit(solution)/shard_map/ppermute | solution.py:296
  49.1 0.0 collective-permute-start.15
  49.1 0.0 copy-done.2
  49.1 2.6 %reorder.7.refs_3_ = bf16[512,1024]{1,0:T(8,128)(2,1)S(1)} custom-call(s32[1,512]{1,0:T(1,128)S(1)} %bitcast.10, bf16[2048,1024]{1,0:T(8,128)(2,1)S(1)} %copy-done.2, bf16[128,256]{1,0:T(8,128)(2,1)S(1)} %collective-permute-done.9.refs_0_.refs_5_, bf16[128,256]{1,0:T(8,128)(2,1)S(1)} %collective-permute-done.10.refs_1_.refs_6_), custom_call_target="tpu_custom_call" | custom-call | flops 2147483648 | bytes 4194304 | tf_op jit(solution)/shard_map/reorder/pallas_call | solution.py:340
  51.7 2.4 %reorder.6.refs_2_ = bf16[512,1024]{1,0:T(8,128)(2,1)S(1)} custom-call(s32[1,512]{1,0:T(1,128)S(1)} %bitcast.9, bf16[2048,1024]{1,0:T(8,128)(2,1)S(1)} %copy-done.2, bf16[128,256]{1,0:T(8,128)(2,1)S(1)} %collective-permute-done.9.refs_0_.refs_5_, bf16[128,256]{1,0:T(8,128)(2,1)S(1)} %collective-permute-done.10.refs_1_.refs_6_), custom_call_target="tpu_custom_call" | custom-call | flops 2147483648 | bytes 4194304 | tf_op jit(solution)/shard_map/reorder/pallas_call | solution.py:340
  54.0 0.0 collective-permute-done.11.refs_7_
  54.0 0.0 collective-permute-done.12.refs_8_
  54.1 0.0 collective-permute-done.13.refs_9_
  54.1 0.0 collective-permute-done.14.refs_10_
  54.1 0.2 collective-permute-done.15.refs_11_
  54.3 2.6 %finish.1 = (f32[256,1024]{1,0:T(8,128)}, bf16[256,2048]{1,0:T(8,128)(2,1)}) custom-call(s32[1]{0:T(128)} %bitcast.me_ref, bf16[1024,256]{1,0:T(8,128)(2,1)S(1)} %get-tuple-element.23.corr_ref, f32[8,256]{1,0:T(8,128)S(1)} %get-tuple-element.34.scale_ref, bf16[512,1024]{1,0:T(8,128)(2,1)S(1)} %reorder.4.refs_8_.refs_0_, ...), custom_call_target="tpu_custom_call" | custom-call | tf_op jit(solution)/shard_map/finish/pallas_call | solution.py:426
  (1 shorter events, 0.0 us)
Async XLA Ops:
  2.0 11.4 %collective-permute-start = (bf16[144,256]{1,0:T(8,128)(2,1)S(1)}, bf16[144,256]{1,0:T(8,128)(2,1)S(1)}, u32[]{:S(2)}, u32[]{:S(2)}) collective-permute-start(bf16[144,256]{1,0:T(8,128)(2,1)S(1)} %get-tuple-element.25), channel_id=1, source_target_pairs={{0,8},{1,9},{2,10},{3,11},{4,12},{5,13},{6,14},{7,15},{8,0},{9,1},... | collective-permute-start | bytes 221192 | tf_op jit(solution)/shard_map/ppermute | solution.py:296
  6.1 11.0 %collective-permute-start.1 = (bf16[144,256]{1,0:T(8,128)(2,1)S(1)}, bf16[144,256]{1,0:T(8,128)(2,1)S(1)}, u32[]{:S(2)}, u32[]{:S(2)}) collective-permute-start(bf16[144,256]{1,0:T(8,128)(2,1)S(1)} %get-tuple-element.26), channel_id=1, source_target_pairs={{0,10},{1,11},{2,8},{3,9},{4,14},{5,15},{6,12},{7,13},{8,2},{9,3},... | collective-permute-start | bytes 221192 | tf_op jit(solution)/shard_map/ppermute | solution.py:296
  7.3 18.9 %collective-permute-start.2 = (bf16[144,256]{1,0:T(8,128)(2,1)S(1)}, bf16[144,256]{1,0:T(8,128)(2,1)S(1)}, u32[]{:S(2)}, u32[]{:S(2)}) collective-permute-start(bf16[144,256]{1,0:T(8,128)(2,1)S(1)} %get-tuple-element.27), channel_id=1, source_target_pairs={{0,12},{1,13},{2,14},{3,15},{4,8},{5,9},{6,10},{7,11},{8,4},{9,5},... | collective-permute-start | bytes 221192 | tf_op jit(solution)/shard_map/ppermute | solution.py:296
  11.0 15.3 %collective-permute-start.3 = (bf16[144,256]{1,0:T(8,128)(2,1)S(1)}, bf16[144,256]{1,0:T(8,128)(2,1)S(1)}, u32[]{:S(2)}, u32[]{:S(2)}) collective-permute-start(bf16[144,256]{1,0:T(8,128)(2,1)S(1)} %get-tuple-element.28), channel_id=1, source_target_pairs={{0,14},{1,15},{2,12},{3,13},{4,10},{5,11},{6,8},{7,9},{8,6},{9,7},... | collective-permute-start | bytes 221192 | tf_op jit(solution)/shard_map/ppermute | solution.py:296
  11.0 15.3 %collective-permute-start.4 = (bf16[144,256]{1,0:T(8,128)(2,1)S(1)}, bf16[144,256]{1,0:T(8,128)(2,1)S(1)}, u32[]{:S(2)}, u32[]{:S(2)}) collective-permute-start(bf16[144,256]{1,0:T(8,128)(2,1)S(1)} %get-tuple-element.29), channel_id=1, source_target_pairs={{0,2},{1,3},{2,0},{3,1},{4,6},{5,7},{6,4},{7,5},{8,10},{9,11},{10,... | collective-permute-start | bytes 221192 | tf_op jit(solution)/shard_map/ppermute | solution.py:296
  13.4 12.8 %collective-permute-start.5 = (bf16[144,256]{1,0:T(8,128)(2,1)S(1)}, bf16[144,256]{1,0:T(8,128)(2,1)S(1)}, u32[]{:S(2)}, u32[]{:S(2)}) collective-permute-start(bf16[144,256]{1,0:T(8,128)(2,1)S(1)} %get-tuple-element.30), channel_id=1, source_target_pairs={{0,4},{1,5},{2,6},{3,7},{4,0},{5,1},{6,2},{7,3},{8,12},{9,13},{10,... | collective-permute-start | bytes 221192 | tf_op jit(solution)/shard_map/ppermute | solution.py:296
  17.1 9.1 %collective-permute-start.6 = (bf16[144,256]{1,0:T(8,128)(2,1)S(1)}, bf16[144,256]{1,0:T(8,128)(2,1)S(1)}, u32[]{:S(2)}, u32[]{:S(2)}) collective-permute-start(bf16[144,256]{1,0:T(8,128)(2,1)S(1)} %get-tuple-element.31), channel_id=1, source_target_pairs={{0,6},{1,7},{2,4},{3,5},{4,2},{5,3},{6,0},{7,1},{8,14},{9,15},{10,... | collective-permute-start | bytes 221192 | tf_op jit(solution)/shard_map/ppermute | solution.py:296
  18.0 2.2 %copy-start.1 = (bf16[2048,1024]{1,0:T(8,128)(2,1)S(1)}, bf16[2048,1024]{1,0:T(8,128)(2,1)}, u32[]{:S(2)}) copy-start(bf16[2048,1024]{1,0:T(8,128)(2,1)} %slab_ref.7) | copy-start | bytes 12582916
  26.3 2.3 %collective-permute-start.7 = (bf16[8,16,256]{2,1,0:T(8,128)(2,1)S(1)}, bf16[8,16,256]{2,1,0:T(8,128)(2,1)S(1)}, u32[]{:S(2)}, u32[]{:S(2)}) collective-permute-start(bf16[8,16,256]{2,1,0:T(8,128)(2,1)S(1)} %collect.1.packets_ref.own_ref), channel_id=1, source_target_pairs={{0,1},{1,0},{2,3},{3,2},{4,5},{5,4},{6,7},{7,6},{8,9},{9,8},{10,11... | collective-permute-start | bytes 196616 | tf_op jit(solution)/shard_map/ppermute | solution.py:296
  28.5 2.2 %copy-start = (s32[4096]{0:T(1024)S(1)}, s32[4096]{0:T(1024)}, u32[]{:S(2)}) copy-start(s32[4096]{0:T(1024)} %param.8) | copy-start | bytes 49156
  32.3 16.8 %copy-start.2 = (bf16[2048,1024]{1,0:T(8,128)(2,1)S(1)}, bf16[2048,1024]{1,0:T(8,128)(2,1)}, u32[]{:S(2)}) copy-start(bf16[2048,1024]{1,0:T(8,128)(2,1)} %slab_ref.7) | copy-start | bytes 12582916
  32.4 2.1 %collective-permute-start.8 = (f32[128,1024]{1,0:T(8,128)S(1)}, f32[128,1024]{1,0:T(8,128)S(1)}, u32[]{:S(2)}, u32[]{:S(2)}) collective-permute-start(f32[128,1024]{1,0:T(8,128)S(1)} %get-tuple-element.35.own_ref), channel_id=1, source_target_pairs={{0,1},{1,0},{2,3},{3,2},{4,5},{5,4},{6,7},{7,6},{8,9},{9,8},{10,11... | collective-permute-start | bytes 1572872 | tf_op jit(solution)/shard_map/ppermute | solution.py:296
  35.2 10.6 %collective-permute-start.9 = (bf16[128,256]{1,0:T(8,128)(2,1)S(1)}, bf16[128,256]{1,0:T(8,128)(2,1)S(1)}, u32[]{:S(2)}, u32[]{:S(2)}) collective-permute-start(bf16[128,256]{1,0:T(8,128)(2,1)S(1)} %get-tuple-element.36), channel_id=1, source_target_pairs={{0,8},{1,9},{2,10},{3,11},{4,12},{5,13},{6,14},{7,15},{8,0},{9,1},... | collective-permute-start | bytes 196616 | tf_op jit(solution)/shard_map/ppermute | solution.py:296
  38.8 10.3 %collective-permute-start.10 = (bf16[128,256]{1,0:T(8,128)(2,1)S(1)}, bf16[128,256]{1,0:T(8,128)(2,1)S(1)}, u32[]{:S(2)}, u32[]{:S(2)}) collective-permute-start(bf16[128,256]{1,0:T(8,128)(2,1)S(1)} %get-tuple-element.37), channel_id=1, source_target_pairs={{0,10},{1,11},{2,8},{3,9},{4,14},{5,15},{6,12},{7,13},{8,2},{9,3},... | collective-permute-start | bytes 196616 | tf_op jit(solution)/shard_map/ppermute | solution.py:296
  39.6 14.4 %collective-permute-start.11 = (bf16[128,256]{1,0:T(8,128)(2,1)S(1)}, bf16[128,256]{1,0:T(8,128)(2,1)S(1)}, u32[]{:S(2)}, u32[]{:S(2)}) collective-permute-start(bf16[128,256]{1,0:T(8,128)(2,1)S(1)} %get-tuple-element.39), channel_id=1, source_target_pairs={{0,12},{1,13},{2,14},{3,15},{4,8},{5,9},{6,10},{7,11},{8,4},{9,5},... | collective-permute-start | bytes 196616 | tf_op jit(solution)/shard_map/ppermute | solution.py:296
  41.1 12.9 %collective-permute-start.12 = (bf16[128,256]{1,0:T(8,128)(2,1)S(1)}, bf16[128,256]{1,0:T(8,128)(2,1)S(1)}, u32[]{:S(2)}, u32[]{:S(2)}) collective-permute-start(bf16[128,256]{1,0:T(8,128)(2,1)S(1)} %get-tuple-element.40), channel_id=1, source_target_pairs={{0,14},{1,15},{2,12},{3,13},{4,10},{5,11},{6,8},{7,9},{8,6},{9,7},... | collective-permute-start | bytes 196616 | tf_op jit(solution)/shard_map/ppermute | solution.py:296
  43.6 10.5 %collective-permute-start.13 = (bf16[128,256]{1,0:T(8,128)(2,1)S(1)}, bf16[128,256]{1,0:T(8,128)(2,1)S(1)}, u32[]{:S(2)}, u32[]{:S(2)}) collective-permute-start(bf16[128,256]{1,0:T(8,128)(2,1)S(1)} %get-tuple-element.41), channel_id=1, source_target_pairs={{0,2},{1,3},{2,0},{3,1},{4,6},{5,7},{6,4},{7,5},{8,10},{9,11},{10,... | collective-permute-start | bytes 196616 | tf_op jit(solution)/shard_map/ppermute | solution.py:296
  45.7 8.3 %collective-permute-start.14 = (bf16[128,256]{1,0:T(8,128)(2,1)S(1)}, bf16[128,256]{1,0:T(8,128)(2,1)S(1)}, u32[]{:S(2)}, u32[]{:S(2)}) collective-permute-start(bf16[128,256]{1,0:T(8,128)(2,1)S(1)} %get-tuple-element.42), channel_id=1, source_target_pairs={{0,4},{1,5},{2,6},{3,7},{4,0},{5,1},{6,2},{7,3},{8,12},{9,13},{10,... | collective-permute-start | bytes 196616 | tf_op jit(solution)/shard_map/ppermute | solution.py:296
  49.1 5.2 %collective-permute-start.15 = (bf16[128,256]{1,0:T(8,128)(2,1)S(1)}, bf16[128,256]{1,0:T(8,128)(2,1)S(1)}, u32[]{:S(2)}, u32[]{:S(2)}) collective-permute-start(bf16[128,256]{1,0:T(8,128)(2,1)S(1)} %get-tuple-element.43), channel_id=1, source_target_pairs={{0,6},{1,7},{2,4},{3,5},{4,2},{5,3},{6,0},{7,1},{8,14},{9,15},{10,... | collective-permute-start | bytes 196616 | tf_op jit(solution)/shard_map/ppermute | solution.py:296

commit v9 on v8

--- a/solution.py
+++ b/solution.py
@@ -212,8 +212,9 @@
         )
 
 
-def sum_kernel(total_runs, own_ref, other_ref, *refs):
-    design_refs, summed_refs = refs[:CORES], refs[CORES:]
+def sum_kernel(total_runs, chips, own_ref, other_ref, *refs):
+    design_refs = refs[:CORES]
+    summed_refs = refs[len(refs) - chips :]
     runs = design_refs[0].shape[0]
     near = own_ref[:, 0:runs] + other_ref[:, runs : 2 * runs]
     far = own_ref[:, runs : 2 * runs] + other_ref[:, 0:runs]
@@ -348,8 +349,8 @@
         )(cell_map[None, start : start + block], slab_modes, *after)
 
     starts = range(0, slab_cells, block)
-    early = len(starts) // 2
-    ordered = [reorder(start, *blocks[1:3]) for start in starts[:early]]
+    quarters = [starts[i * len(starts) // 4 : (i + 1) * len(starts) // 4] for i in range(4)]
+    ordered = [reorder(start) for start in quarters[0]]
     half = round_up(DEGREES * dim, LANES)
     gathers = slots // 4
     chosen, spots = pl.pallas_call(
@@ -366,7 +367,7 @@
     )(me, in_hbm(term_codes.T), *blocks[1:3])
     packets = pl.pallas_call(
         functools.partial(collect_kernel, chips),
-        in_specs=[vmem] * chips + [anywhere] * (early + 1),
+        in_specs=[vmem] * chips + [anywhere] * (1 + len(ordered)),
         out_specs=vmem,
         out_shape=jax.ShapeDtypeStruct((chips, packet_rows, term_count), jnp.bfloat16),
         compiler_params=params(8),
@@ -411,17 +412,20 @@
         cost_estimate=fit_cost,
         name="fit",
     )(me, weight_levels[None, :], packets, others, *blocks, *designs)
+    beside = [reorder(start, fitted) for start in quarters[1]]
     summed = pl.pallas_call(
-        functools.partial(sum_kernel, float(total_runs)),
-        in_specs=[vmem] * (2 + CORES),
+        functools.partial(sum_kernel, float(total_runs), chips),
+        in_specs=[vmem] * (2 + CORES) + [anywhere] * len(beside),
         out_specs=[vmem] * chips,
         out_shape=[jax.ShapeDtypeStruct((own_modes, term_count), jnp.bfloat16)] * chips,
         compiler_params=params(16),
         cost_estimate=fit_cost,
         name="sum",
-    )(fitted, to_device(fitted, 1), *designs)
+    )(fitted, to_device(fitted, 1), *designs, *beside)
     returned = to_chips(summed)
-    ordered += [reorder(start, *returned[1:3]) for start in starts[early:]]
+    ordered += beside
+    ordered += [reorder(start, summed[0]) for start in quarters[2]]
+    ordered += [reorder(start, *returned[1:3]) for start in quarters[3]]
 
     return pl.pallas_call(
         functools.partial(finish_kernel, len(ordered)),

time: 57.2 us -> 56.3 us (0.984)
  waiting for transfers between devices: 8.07 us -> 6.74 us
    ppermute x16, waiting for transfers between devices: 8.07 us -> 6.74 us  [to_device(): return lax.ppermute(array, 'runs', [(i, i ^ bits) for i in range(devices)])]
  transfers between devices with their start and end apart: 16 -> 16, of which waited for: 5 -> 4; matrix products, arithmetic and copies ran while one was open for 1% -> 1% of each run, Pallas kernels for 23% -> 24%
where the time goes in v9:
time: 56.3 us; the launch traced here: 56 us
  starting transfers between devices  23.4 us (42%)
  Pallas kernels  21.9 us (39%)
  waiting for transfers between devices  6.74 us (12%)
  local copies, waits for them, and re-layouts  2.97 us (5%)
  between operations  1.01 us (2%)
    ppermute x16, starting transfers between devices, to_device(): return lax.ppermute(array, 'runs', [(i, i ^ bits) for i in range(devices)])  23.4 us
    pallas_call x4, Pallas kernels, reorder(): pl.pallas_call(reorder_kernel, in_specs=[vmem, vmem] + [anywhere] * len(a...  9.61 us
    ppermute x16, waiting for transfers between devices, to_device(): return lax.ppermute(array, 'runs', [(i, i ^ bits) for i in range(devices)])  6.74 us
    pallas_call x2, Pallas kernels, design_of(): pl.pallas_call(functools.partial(design_kernel, dim, run_count), in_specs...  4.73 us
    pallas_call x1, Pallas kernels, split_by_modes(): pl.pallas_call(functools.partial(finish_kernel, len(ordered)), in_specs=[...  2.56 us
    unnamed x6, local copies, waits for them, and re-layouts  2.2 us
    pallas_call x1, Pallas kernels, split_by_modes(): pl.pallas_call(functools.partial(fit_kernel, 2 * rows), in_specs=[smem] +...  1.62 us
    pallas_call x1, Pallas kernels, split_by_modes(): pl.pallas_call(prepare_kernel, in_specs=[smem, vmem, vmem], out_specs=[vm...  1.35 us
  transfers between devices with their start and end apart: 16, of which 4 were waited for; matrix products, arithmetic and copies ran while one was open for 1% of the time, Pallas kernels for 24%

profile of v9, /device:TPU:0, one launch (start us, length us, event | category | flops | bytes accessed | tf_op | source)
XLA Modules:
  0.0 56.0 jit_solution(2840342409359406714)
XLA Ops:
  0.6 1.3 %prepare.1 = (bf16[1024,256]{1,0:T(8,128)(2,1)S(1)}, bf16[144,256]{1,0:T(8,128)(2,1)S(1)}, bf16[144,256]{1,0:T(8,128)(2,1)S(1)}, bf16[144,256]{1,0:T(8,128)(2,1)...) custom-call(s32[1]{0:T(128)} %bitcast.me_ref, ...), custom_call_target="tpu_custom_call" | custom-call | tf_op jit(solution)/shard_map/prepare/pallas_call | solution.py:326
  2.0 4.1 %collective-permute-start = (bf16[144,256]{1,0:T(8,128)(2,1)S(1)}, bf16[144,256]{1,0:T(8,128)(2,1)S(1)}, u32[]{:S(2)}, u32[]{:S(2)}) collective-permute-start(bf16[144,256]{1,0:T(8,128)(2,1)S(1)} %get-tuple-element.25), channel_id=1, source_target_pairs={{0,8},{1,9},{2,10},{3,11},{4,12},{5,13},{6,14},{7,15},{8,0},{9,1},... | collective-permute-start | bytes 221192 | tf_op jit(solution)/shard_map/ppermute | solution.py:297
  6.1 1.3 %collective-permute-start.1 = (bf16[144,256]{1,0:T(8,128)(2,1)S(1)}, bf16[144,256]{1,0:T(8,128)(2,1)S(1)}, u32[]{:S(2)}, u32[]{:S(2)}) collective-permute-start(bf16[144,256]{1,0:T(8,128)(2,1)S(1)} %get-tuple-element.26), channel_id=1, source_target_pairs={{0,10},{1,11},{2,8},{3,9},{4,14},{5,15},{6,12},{7,13},{8,2},{9,3},... | collective-permute-start | bytes 221192 | tf_op jit(solution)/shard_map/ppermute | solution.py:297
  7.3 3.6 %collective-permute-start.2 = (bf16[144,256]{1,0:T(8,128)(2,1)S(1)}, bf16[144,256]{1,0:T(8,128)(2,1)S(1)}, u32[]{:S(2)}, u32[]{:S(2)}) collective-permute-start(bf16[144,256]{1,0:T(8,128)(2,1)S(1)} %get-tuple-element.27), channel_id=1, source_target_pairs={{0,12},{1,13},{2,14},{3,15},{4,8},{5,9},{6,10},{7,11},{8,4},{9,5},... | collective-permute-start | bytes 221192 | tf_op jit(solution)/shard_map/ppermute | solution.py:297
  10.9 0.0 collective-permute-start.3
  11.0 1.7 %collective-permute-start.4 = (bf16[144,256]{1,0:T(8,128)(2,1)S(1)}, bf16[144,256]{1,0:T(8,128)(2,1)S(1)}, u32[]{:S(2)}, u32[]{:S(2)}) collective-permute-start(bf16[144,256]{1,0:T(8,128)(2,1)S(1)} %get-tuple-element.29), channel_id=1, source_target_pairs={{0,2},{1,3},{2,0},{3,1},{4,6},{5,7},{6,4},{7,5},{8,10},{9,11},{10,... | collective-permute-start | bytes 221192 | tf_op jit(solution)/shard_map/ppermute | solution.py:297
  12.6 0.8 %fusion = (s32[512]{0:T(512)S(1)}, s32[512]{0:T(512)S(1)}, s32[512]{0:T(512)S(1)}, s32[512]{0:T(512)S(1)}) fusion(s32[2048]{0:T(1024)} %param.11), kind=kLoop, calls=%fused_computation | loop fusion | bytes 16384 | tf_op jit(solution)/shard_map/slice | solution.py:349
  13.4 0.0 collective-permute-done.refs_0_.refs_1_
  13.4 1.0 %collective-permute-start.5 = (bf16[144,256]{1,0:T(8,128)(2,1)S(1)}, bf16[144,256]{1,0:T(8,128)(2,1)S(1)}, u32[]{:S(2)}, u32[]{:S(2)}) collective-permute-start(bf16[144,256]{1,0:T(8,128)(2,1)S(1)} %get-tuple-element.30), channel_id=1, source_target_pairs={{0,4},{1,5},{2,6},{3,7},{4,0},{5,1},{6,2},{7,3},{8,12},{9,13},{10,... | collective-permute-start | bytes 221192 | tf_op jit(solution)/shard_map/ppermute | solution.py:297
  14.4 2.7 %collective-permute-done.1.refs_1_.refs_2_ = bf16[144,256]{1,0:T(8,128)(2,1)S(1)} collective-permute-done((bf16[144,256]{1,0:T(8,128)(2,1)S(1)}, bf16[144,256]{1,0:T(8,128)(2,1)S(1)}, u32[]{:S(2)}, u32[]{:S(2)}) %collective-permute-start.1) | collective-permute-done | bytes 73760 | tf_op jit(solution)/shard_map/ppermute | solution.py:297
  17.1 0.9 %collective-permute-start.6 = (bf16[144,256]{1,0:T(8,128)(2,1)S(1)}, bf16[144,256]{1,0:T(8,128)(2,1)S(1)}, u32[]{:S(2)}, u32[]{:S(2)}) collective-permute-start(bf16[144,256]{1,0:T(8,128)(2,1)S(1)} %get-tuple-element.31), channel_id=1, source_target_pairs={{0,6},{1,7},{2,4},{3,5},{4,2},{5,3},{6,0},{7,1},{8,14},{9,15},{10,... | collective-permute-start | bytes 221192 | tf_op jit(solution)/shard_map/ppermute | solution.py:297
  18.0 0.0 copy-start.1
  18.0 2.2 %copy-done.1 = bf16[2048,1024]{1,0:T(8,128)(2,1)S(1)} copy-done((bf16[2048,1024]{1,0:T(8,128)(2,1)S(1)}, bf16[2048,1024]{1,0:T(8,128)(2,1)}, u32[]{:S(2)}) %copy-start.1) | copy-done | bytes 4194328
  20.2 2.4 %reorder.4.refs_8_.refs_0_ = bf16[512,1024]{1,0:T(8,128)(2,1)S(1)} custom-call(s32[1,512]{1,0:T(1,128)S(1)} %bitcast.12, bf16[2048,1024]{1,0:T(8,128)(2,1)S(1)} %copy-done.1), custom_call_target="tpu_custom_call" | custom-call | flops 2147483648 | bytes 4194304 | tf_op jit(solution)/shard_map/reorder/pallas_call | solution.py:341
  22.5 1.3 %choose.1 = (bf16[3,256,2048]{2,1,0:T(8,128)(2,1)S(1)}, s32[1,2048]{1,0:T(1,128)S(1)}) custom-call(s32[1]{0:T(128)} %bitcast.me_ref, s32[4,4096]{1,0:T(4,128)} %bitcast.13, bf16[144,256]{1,0:T(8,128)(2,1)S(1)} %collective-permute-done.refs_0_.refs_1_, bf16[144,256]{1,0:T(8,128)(2,1)S(1)} %collective-permute-done.1.refs_1_.refs_2_), custom_call_target="tpu_custom_call" | custom-call | bytes 2097152 | tf_op jit(solution)/shard_map/choose/pallas_call | solution.py:356
  23.8 0.0 collective-permute-done.2.refs_3_
  23.9 0.0 collective-permute-done.3.refs_4_
  23.9 0.0 collective-permute-done.4.refs_5_
  23.9 0.0 collective-permute-done.5.refs_6_
  23.9 0.0 collective-permute-done.6.refs_7_
  23.9 0.1 collective-permute-start.7
  24.0 2.4 %design.2.refs_8_.refs_0_ = bf16[512,2048]{1,0:T(8,128)(2,1)S(1)} custom-call(bf16[8,16,256]{2,1,0:T(8,128)(2,1)S(1)} %collect.1.packets_ref.own_ref, bf16[3,256,2048]{2,1,0:T(8,128)(2,1)S(1)} %get-tuple-element.33.chosen_ref, s32[1,2048]{1,0:T(1,128)S(1)} %get-tuple-element.32.refs_9_.spots_ref), custom_call_target="tpu_custom_call" | custom-call | flops 2147483648 | bytes 2097152 | tf_op jit(solution)/shard_map/design/pallas_call | solution.py:381
  26.4 0.0 copy-start
  26.4 0.0 collective-permute-done.7.packets_ref.other_ref
  26.4 2.4 %design.3.refs_9_.refs_1_ = bf16[512,2048]{1,0:T(8,128)(2,1)S(1)} custom-call(bf16[8,16,256]{2,1,0:T(8,128)(2,1)S(1)} %collective-permute-done.7.packets_ref.other_ref, bf16[3,256,2048]{2,1,0:T(8,128)(2,1)S(1)} %get-tuple-element.33.chosen_ref, s32[1,2048]{1,0:T(1,128)S(1)} %get-tuple-element.32.refs_9_.spots_ref), custom_call_target="tpu_custom_call" | custom-call | flops 2147483648 | bytes 2097152 | tf_op jit(solution)/shard_map/design/pallas_call | solution.py:381
  28.8 0.0 copy-start.2
  28.8 0.0 copy-done
  28.8 1.6 %fit.1 = (f32[128,1024]{1,0:T(8,128)S(1)}, f32[8,256]{1,0:T(8,128)S(1)}) custom-call(s32[1]{0:T(128)} %bitcast.me_ref, s32[1,4096]{1,0:T(1,128)S(1)} %bitcast.8, bf16[8,16,256]{2,1,0:T(8,128)(2,1)S(1)} %collect.1.packets_ref.own_ref, bf16[8,16,256]{2,1,0:T(8,128)(2,1)S(1)} %collective-permute-done.7.packets_ref.other_ref, ...), custom_call_target="tpu_custom_call" | custom-call | flops 536870912 | bytes 4194304 | tf_op jit(solution)/shard_map/fit/pallas_call | solution.py:402
  30.4 0.6 collective-permute-start.8
  31.0 0.0 copy-done.2
  31.0 2.4 %reorder.5.refs_2_.refs_1_ = bf16[512,1024]{1,0:T(8,128)(2,1)S(1)} custom-call(s32[1,512]{1,0:T(1,128)S(1)} %bitcast.11, bf16[2048,1024]{1,0:T(8,128)(2,1)S(1)} %copy-done.2, f32[128,1024]{1,0:T(8,128)S(1)} %get-tuple-element.35.refs_0_.own_ref), custom_call_target="tpu_custom_call" | custom-call | flops 2147483648 | bytes 4194304 | tf_op jit(solution)/shard_map/reorder/pallas_call | solution.py:341
  33.3 0.0 collective-permute-done.8.other_ref
  33.4 0.7 %sum.1 = (bf16[128,256]{1,0:T(8,128)(2,1)S(1)}, bf16[128,256]{1,0:T(8,128)(2,1)S(1)}, bf16[128,256]{1,0:T(8,128)(2,1)S(1)}, bf16[128,256]{1,0:T(8,128)(2,1)S(1)}...) custom-call(f32[128,1024]{1,0:T(8,128)S(1)} %get-tuple-element.35.re, ...), custom_call_target="tpu_custom_call" | custom-call | flops 536870912 | bytes 4194304 | tf_op jit(solution)/shard_map/sum/pallas_call | solution.py:416
  34.1 3.5 %collective-permute-start.9 = (bf16[128,256]{1,0:T(8,128)(2,1)S(1)}, bf16[128,256]{1,0:T(8,128)(2,1)S(1)}, u32[]{:S(2)}, u32[]{:S(2)}) collective-permute-start(bf16[128,256]{1,0:T(8,128)(2,1)S(1)} %get-tuple-element.37), channel_id=1, source_target_pairs={{0,8},{1,9},{2,10},{3,11},{4,12},{5,13},{6,14},{7,15},{8,0},{9,1},... | collective-permute-start | bytes 196616 | tf_op jit(solution)/shard_map/ppermute | solution.py:297
  37.6 0.9 %collective-permute-start.10 = (bf16[128,256]{1,0:T(8,128)(2,1)S(1)}, bf16[128,256]{1,0:T(8,128)(2,1)S(1)}, u32[]{:S(2)}, u32[]{:S(2)}) collective-permute-start(bf16[128,256]{1,0:T(8,128)(2,1)S(1)} %get-tuple-element.38), channel_id=1, source_target_pairs={{0,10},{1,11},{2,8},{3,9},{4,14},{5,15},{6,12},{7,13},{8,2},{9,3},... | collective-permute-start | bytes 196616 | tf_op jit(solution)/shard_map/ppermute | solution.py:297
  38.5 1.5 %collective-permute-start.11 = (bf16[128,256]{1,0:T(8,128)(2,1)S(1)}, bf16[128,256]{1,0:T(8,128)(2,1)S(1)}, u32[]{:S(2)}, u32[]{:S(2)}) collective-permute-start(bf16[128,256]{1,0:T(8,128)(2,1)S(1)} %get-tuple-element.39), channel_id=1, source_target_pairs={{0,12},{1,13},{2,14},{3,15},{4,8},{5,9},{6,10},{7,11},{8,4},{9,5},... | collective-permute-start | bytes 196616 | tf_op jit(solution)/shard_map/ppermute | solution.py:297
  40.0 2.4 %collective-permute-start.12 = (bf16[128,256]{1,0:T(8,128)(2,1)S(1)}, bf16[128,256]{1,0:T(8,128)(2,1)S(1)}, u32[]{:S(2)}, u32[]{:S(2)}) collective-permute-start(bf16[128,256]{1,0:T(8,128)(2,1)S(1)} %get-tuple-element.40), channel_id=1, source_target_pairs={{0,14},{1,15},{2,12},{3,13},{4,10},{5,11},{6,8},{7,9},{8,6},{9,7},... | collective-permute-start | bytes 196616 | tf_op jit(solution)/shard_map/ppermute | solution.py:297
  42.4 1.4 %collective-permute-start.13 = (bf16[128,256]{1,0:T(8,128)(2,1)S(1)}, bf16[128,256]{1,0:T(8,128)(2,1)S(1)}, u32[]{:S(2)}, u32[]{:S(2)}) collective-permute-start(bf16[128,256]{1,0:T(8,128)(2,1)S(1)} %get-tuple-element.41), channel_id=1, source_target_pairs={{0,2},{1,3},{2,0},{3,1},{4,6},{5,7},{6,4},{7,5},{8,10},{9,11},{10,... | collective-permute-start | bytes 196616 | tf_op jit(solution)/shard_map/ppermute | solution.py:297
  43.8 2.5 %reorder.6.refs_2_ = bf16[512,1024]{1,0:T(8,128)(2,1)S(1)} custom-call(s32[1,512]{1,0:T(1,128)S(1)} %bitcast.10, bf16[2048,1024]{1,0:T(8,128)(2,1)S(1)} %copy-done.2, bf16[128,256]{1,0:T(8,128)(2,1)S(1)} %get-tuple-element.36.refs_0_.refs_4_), custom_call_target="tpu_custom_call" | custom-call | flops 2147483648 | bytes 4194304 | tf_op jit(solution)/shard_map/reorder/pallas_call | solution.py:341
  46.3 0.0 collective-permute-done.9.refs_0_.refs_5_
  46.4 0.1 collective-permute-start.14
  46.4 1.7 %collective-permute-done.10.refs_1_.refs_6_ = bf16[128,256]{1,0:T(8,128)(2,1)S(1)} collective-permute-done((bf16[128,256]{1,0:T(8,128)(2,1)S(1)}, bf16[128,256]{1,0:T(8,128)(2,1)S(1)}, u32[]{:S(2)}, u32[]{:S(2)}) %collective-permute-start.10) | collective-permute-done | bytes 65568 | tf_op jit(solution)/shard_map/ppermute | solution.py:297
  48.1 0.5 collective-permute-start.15
  48.6 2.4 %reorder.7.refs_3_ = bf16[512,1024]{1,0:T(8,128)(2,1)S(1)} custom-call(s32[1,512]{1,0:T(1,128)S(1)} %bitcast.9, bf16[2048,1024]{1,0:T(8,128)(2,1)S(1)} %copy-done.2, bf16[128,256]{1,0:T(8,128)(2,1)S(1)} %collective-permute-done.9.refs_0_.refs_5_, bf16[128,256]{1,0:T(8,128)(2,1)S(1)} %collective-permute-done.10.refs_1_.refs_6_), custom_call_target="tpu_custom_call" | custom-call | flops 2147483648 | bytes 4194304 | tf_op jit(solution)/shard_map/reorder/pallas_call | solution.py:341
  50.9 0.0 collective-permute-done.11.refs_7_
  50.9 0.0 collective-permute-done.12.refs_8_
  50.9 0.0 collective-permute-done.13.refs_9_
  50.9 0.3 collective-permute-done.14.refs_10_
  51.2 2.0 %collective-permute-done.15.refs_11_ = bf16[128,256]{1,0:T(8,128)(2,1)S(1)} collective-permute-done((bf16[128,256]{1,0:T(8,128)(2,1)S(1)}, bf16[128,256]{1,0:T(8,128)(2,1)S(1)}, u32[]{:S(2)}, u32[]{:S(2)}) %collective-permute-start.15) | collective-permute-done | bytes 65568 | tf_op jit(solution)/shard_map/ppermute | solution.py:297
  53.3 2.6 %finish.1 = (f32[256,1024]{1,0:T(8,128)}, bf16[256,2048]{1,0:T(8,128)(2,1)}) custom-call(s32[1]{0:T(128)} %bitcast.me_ref, bf16[1024,256]{1,0:T(8,128)(2,1)S(1)} %get-tuple-element.23.corr_ref, f32[8,256]{1,0:T(8,128)S(1)} %get-tuple-element.34.scale_ref, bf16[512,1024]{1,0:T(8,128)(2,1)S(1)} %reorder.4.refs_8_.refs_0_, ...), custom_call_target="tpu_custom_call" | custom-call | tf_op jit(solution)/shard_map/finish/pallas_call | solution.py:430
  (1 shorter events, 0.0 us)
Async XLA Ops:
  2.0 11.4 %collective-permute-start = (bf16[144,256]{1,0:T(8,128)(2,1)S(1)}, bf16[144,256]{1,0:T(8,128)(2,1)S(1)}, u32[]{:S(2)}, u32[]{:S(2)}) collective-permute-start(bf16[144,256]{1,0:T(8,128)(2,1)S(1)} %get-tuple-element.25), channel_id=1, source_target_pairs={{0,8},{1,9},{2,10},{3,11},{4,12},{5,13},{6,14},{7,15},{8,0},{9,1},... | collective-permute-start | bytes 221192 | tf_op jit(solution)/shard_map/ppermute | solution.py:297
  6.1 11.0 %collective-permute-start.1 = (bf16[144,256]{1,0:T(8,128)(2,1)S(1)}, bf16[144,256]{1,0:T(8,128)(2,1)S(1)}, u32[]{:S(2)}, u32[]{:S(2)}) collective-permute-start(bf16[144,256]{1,0:T(8,128)(2,1)S(1)} %get-tuple-element.26), channel_id=1, source_target_pairs={{0,10},{1,11},{2,8},{3,9},{4,14},{5,15},{6,12},{7,13},{8,2},{9,3},... | collective-permute-start | bytes 221192 | tf_op jit(solution)/shard_map/ppermute | solution.py:297
  7.3 16.5 %collective-permute-start.2 = (bf16[144,256]{1,0:T(8,128)(2,1)S(1)}, bf16[144,256]{1,0:T(8,128)(2,1)S(1)}, u32[]{:S(2)}, u32[]{:S(2)}) collective-permute-start(bf16[144,256]{1,0:T(8,128)(2,1)S(1)} %get-tuple-element.27), channel_id=1, source_target_pairs={{0,12},{1,13},{2,14},{3,15},{4,8},{5,9},{6,10},{7,11},{8,4},{9,5},... | collective-permute-start | bytes 221192 | tf_op jit(solution)/shard_map/ppermute | solution.py:297
  10.9 12.9 %collective-permute-start.3 = (bf16[144,256]{1,0:T(8,128)(2,1)S(1)}, bf16[144,256]{1,0:T(8,128)(2,1)S(1)}, u32[]{:S(2)}, u32[]{:S(2)}) collective-permute-start(bf16[144,256]{1,0:T(8,128)(2,1)S(1)} %get-tuple-element.28), channel_id=1, source_target_pairs={{0,14},{1,15},{2,12},{3,13},{4,10},{5,11},{6,8},{7,9},{8,6},{9,7},... | collective-permute-start | bytes 221192 | tf_op jit(solution)/shard_map/ppermute | solution.py:297
  11.0 12.9 %collective-permute-start.4 = (bf16[144,256]{1,0:T(8,128)(2,1)S(1)}, bf16[144,256]{1,0:T(8,128)(2,1)S(1)}, u32[]{:S(2)}, u32[]{:S(2)}) collective-permute-start(bf16[144,256]{1,0:T(8,128)(2,1)S(1)} %get-tuple-element.29), channel_id=1, source_target_pairs={{0,2},{1,3},{2,0},{3,1},{4,6},{5,7},{6,4},{7,5},{8,10},{9,11},{10,... | collective-permute-start | bytes 221192 | tf_op jit(solution)/shard_map/ppermute | solution.py:297
  13.4 10.5 %collective-permute-start.5 = (bf16[144,256]{1,0:T(8,128)(2,1)S(1)}, bf16[144,256]{1,0:T(8,128)(2,1)S(1)}, u32[]{:S(2)}, u32[]{:S(2)}) collective-permute-start(bf16[144,256]{1,0:T(8,128)(2,1)S(1)} %get-tuple-element.30), channel_id=1, source_target_pairs={{0,4},{1,5},{2,6},{3,7},{4,0},{5,1},{6,2},{7,3},{8,12},{9,13},{10,... | collective-permute-start | bytes 221192 | tf_op jit(solution)/shard_map/ppermute | solution.py:297
  17.1 6.8 %collective-permute-start.6 = (bf16[144,256]{1,0:T(8,128)(2,1)S(1)}, bf16[144,256]{1,0:T(8,128)(2,1)S(1)}, u32[]{:S(2)}, u32[]{:S(2)}) collective-permute-start(bf16[144,256]{1,0:T(8,128)(2,1)S(1)} %get-tuple-element.31), channel_id=1, source_target_pairs={{0,6},{1,7},{2,4},{3,5},{4,2},{5,3},{6,0},{7,1},{8,14},{9,15},{10,... | collective-permute-start | bytes 221192 | tf_op jit(solution)/shard_map/ppermute | solution.py:297
  18.0 2.2 %copy-start.1 = (bf16[2048,1024]{1,0:T(8,128)(2,1)S(1)}, bf16[2048,1024]{1,0:T(8,128)(2,1)}, u32[]{:S(2)}) copy-start(bf16[2048,1024]{1,0:T(8,128)(2,1)} %slab_ref.7) | copy-start | bytes 12582916
  23.9 2.5 %collective-permute-start.7 = (bf16[8,16,256]{2,1,0:T(8,128)(2,1)S(1)}, bf16[8,16,256]{2,1,0:T(8,128)(2,1)S(1)}, u32[]{:S(2)}, u32[]{:S(2)}) collective-permute-start(bf16[8,16,256]{2,1,0:T(8,128)(2,1)S(1)} %collect.1.packets_ref.own_ref), channel_id=1, source_target_pairs={{0,1},{1,0},{2,3},{3,2},{4,5},{5,4},{6,7},{7,6},{8,9},{9,8},{10,11... | collective-permute-start | bytes 196616 | tf_op jit(solution)/shard_map/ppermute | solution.py:297
  26.4 2.4 %copy-start = (s32[4096]{0:T(1024)S(1)}, s32[4096]{0:T(1024)}, u32[]{:S(2)}) copy-start(s32[4096]{0:T(1024)} %param.8) | copy-start | bytes 49156
  28.8 2.2 %copy-start.2 = (bf16[2048,1024]{1,0:T(8,128)(2,1)S(1)}, bf16[2048,1024]{1,0:T(8,128)(2,1)}, u32[]{:S(2)}) copy-start(bf16[2048,1024]{1,0:T(8,128)(2,1)} %slab_ref.7) | copy-start | bytes 12582916
  30.4 2.9 %collective-permute-start.8 = (f32[128,1024]{1,0:T(8,128)S(1)}, f32[128,1024]{1,0:T(8,128)S(1)}, u32[]{:S(2)}, u32[]{:S(2)}) collective-permute-start(f32[128,1024]{1,0:T(8,128)S(1)} %get-tuple-element.35.refs_0_.own_ref), channel_id=1, source_target_pairs={{0,1},{1,0},{2,3},{3,2},{4,5},{5,4},{6,7},{7,6},{8,9},{9,8},{10,11... | collective-permute-start | bytes 1572872 | tf_op jit(solution)/shard_map/ppermute | solution.py:297
  34.1 12.2 %collective-permute-start.9 = (bf16[128,256]{1,0:T(8,128)(2,1)S(1)}, bf16[128,256]{1,0:T(8,128)(2,1)S(1)}, u32[]{:S(2)}, u32[]{:S(2)}) collective-permute-start(bf16[128,256]{1,0:T(8,128)(2,1)S(1)} %get-tuple-element.37), channel_id=1, source_target_pairs={{0,8},{1,9},{2,10},{3,11},{4,12},{5,13},{6,14},{7,15},{8,0},{9,1},... | collective-permute-start | bytes 196616 | tf_op jit(solution)/shard_map/ppermute | solution.py:297
  37.6 10.4 %collective-permute-start.10 = (bf16[128,256]{1,0:T(8,128)(2,1)S(1)}, bf16[128,256]{1,0:T(8,128)(2,1)S(1)}, u32[]{:S(2)}, u32[]{:S(2)}) collective-permute-start(bf16[128,256]{1,0:T(8,128)(2,1)S(1)} %get-tuple-element.38), channel_id=1, source_target_pairs={{0,10},{1,11},{2,8},{3,9},{4,14},{5,15},{6,12},{7,13},{8,2},{9,3},... | collective-permute-start | bytes 196616 | tf_op jit(solution)/shard_map/ppermute | solution.py:297
  38.5 12.4 %collective-permute-start.11 = (bf16[128,256]{1,0:T(8,128)(2,1)S(1)}, bf16[128,256]{1,0:T(8,128)(2,1)S(1)}, u32[]{:S(2)}, u32[]{:S(2)}) collective-permute-start(bf16[128,256]{1,0:T(8,128)(2,1)S(1)} %get-tuple-element.39), channel_id=1, source_target_pairs={{0,12},{1,13},{2,14},{3,15},{4,8},{5,9},{6,10},{7,11},{8,4},{9,5},... | collective-permute-start | bytes 196616 | tf_op jit(solution)/shard_map/ppermute | solution.py:297
  40.0 10.9 %collective-permute-start.12 = (bf16[128,256]{1,0:T(8,128)(2,1)S(1)}, bf16[128,256]{1,0:T(8,128)(2,1)S(1)}, u32[]{:S(2)}, u32[]{:S(2)}) collective-permute-start(bf16[128,256]{1,0:T(8,128)(2,1)S(1)} %get-tuple-element.40), channel_id=1, source_target_pairs={{0,14},{1,15},{2,12},{3,13},{4,10},{5,11},{6,8},{7,9},{8,6},{9,7},... | collective-permute-start | bytes 196616 | tf_op jit(solution)/shard_map/ppermute | solution.py:297
  42.4 8.5 %collective-permute-start.13 = (bf16[128,256]{1,0:T(8,128)(2,1)S(1)}, bf16[128,256]{1,0:T(8,128)(2,1)S(1)}, u32[]{:S(2)}, u32[]{:S(2)}) collective-permute-start(bf16[128,256]{1,0:T(8,128)(2,1)S(1)} %get-tuple-element.41), channel_id=1, source_target_pairs={{0,2},{1,3},{2,0},{3,1},{4,6},{5,7},{6,4},{7,5},{8,10},{9,11},{10,... | collective-permute-start | bytes 196616 | tf_op jit(solution)/shard_map/ppermute | solution.py:297
  46.4 4.9 %collective-permute-start.14 = (bf16[128,256]{1,0:T(8,128)(2,1)S(1)}, bf16[128,256]{1,0:T(8,128)(2,1)S(1)}, u32[]{:S(2)}, u32[]{:S(2)}) collective-permute-start(bf16[128,256]{1,0:T(8,128)(2,1)S(1)} %get-tuple-element.42), channel_id=1, source_target_pairs={{0,4},{1,5},{2,6},{3,7},{4,0},{5,1},{6,2},{7,3},{8,12},{9,13},{10,... | collective-permute-start | bytes 196616 | tf_op jit(solution)/shard_map/ppermute | solution.py:297
  48.1 5.2 %collective-permute-start.15 = (bf16[128,256]{1,0:T(8,128)(2,1)S(1)}, bf16[128,256]{1,0:T(8,128)(2,1)S(1)}, u32[]{:S(2)}, u32[]{:S(2)}) collective-permute-start(bf16[128,256]{1,0:T(8,128)(2,1)S(1)} %get-tuple-element.43), channel_id=1, source_target_pairs={{0,6},{1,7},{2,4},{3,5},{4,2},{5,3},{6,0},{7,1},{8,14},{9,15},{10,... | collective-permute-start | bytes 196616 | tf_op jit(solution)/shard_map/ppermute | solution.py:297

commit v10 on v9

--- a/solution.py
+++ b/solution.py
@@ -14,6 +14,7 @@
 DEGREES = 5
 LANES = 128
 CORES = 2
+FIRST_SLOTS = 6
 ROOT_TWO = math.sqrt(2.0)
 ROOT_SIX = math.sqrt(6.0)
 ROOT_TWENTYFOUR = math.sqrt(24.0)
@@ -37,12 +38,11 @@
     return pl.ds(pl.multiple_of(index * count, count), count)
 
 
-def prepare_kernel(me_ref, corr_ref, points_ref, turned_ref, *sent_refs):
+def prepare_kernel(chips, me_ref, corr_ref, points_ref, turned_ref, packet_ref, *sent_refs):
     turned = corr_ref[...].astype(jnp.float32).T
     turned_ref[...] = turned.astype(jnp.bfloat16)
     squares = jnp.sum(turned * turned, axis=0, keepdims=True)
-    sent_rows, terms = sent_refs[0].shape
-    count = turned.shape[0] // len(sent_refs)
+    packet_rows, terms = packet_ref.shape
     dim, runs = points_ref.shape
     rows = dim * runs // terms
     points = jnp.concatenate(
@@ -50,13 +50,23 @@
     )
     pieces = split_in_two(points) + split_in_two(squares)
     used = 2 * rows + 2
-    if sent_rows - count > used:
-        pieces.append(jnp.zeros((sent_rows - count - used, terms), jnp.float32))
-    packet = jnp.concatenate(pieces, axis=0).astype(jnp.bfloat16)
-    for k, sent_ref in enumerate(sent_refs):
-        chip = (me_ref[0] // CORES) ^ partner(k, len(sent_refs))
+    if packet_rows > used:
+        pieces.append(jnp.zeros((packet_rows - used, terms), jnp.float32))
+    packet_ref[...] = jnp.concatenate(pieces, axis=0).astype(jnp.bfloat16)
+    fill_blocks(chips, 0, me_ref, turned_ref, packet_ref, sent_refs)
+
+
+def fill_blocks(chips, first, me_ref, turned_ref, packet_ref, sent_refs):
+    count = turned_ref.shape[0] // chips
+    for k, sent_ref in enumerate(sent_refs, first):
+        chip = (me_ref[0] // CORES) ^ partner(k, chips)
         sent_ref[0:count, :] = turned_ref[rows_of(chip, count), :]
-        sent_ref[count:sent_rows, :] = packet
+        sent_ref[count : sent_ref.shape[0], :] = packet_ref[...]
+
+
+def late_kernel(chips, me_ref, turned_ref, packet_ref, *refs):
+    sent_refs = refs[len(refs) - (chips - FIRST_SLOTS) :]
+    fill_blocks(chips, FIRST_SLOTS, me_ref, turned_ref, packet_ref, sent_refs)
 
 
 def split_in_two(values):
@@ -323,17 +333,20 @@
     vmem = pl.BlockSpec(memory_space=pltpu.VMEM)
     anywhere = pl.BlockSpec(memory_space=pl.ANY)
 
-    turned, *sent = pl.pallas_call(
-        prepare_kernel,
+    early = min(chips, FIRST_SLOTS)
+    block_type = jax.ShapeDtypeStruct((own_modes + packet_rows, term_count), jnp.bfloat16)
+    turned, packet, *sent = pl.pallas_call(
+        functools.partial(prepare_kernel, chips),
         in_specs=[smem, vmem, vmem],
-        out_specs=[vmem] * (1 + chips),
-        out_shape=[jax.ShapeDtypeStruct((modes, term_count), jnp.bfloat16)]
-        + [jax.ShapeDtypeStruct((own_modes + packet_rows, term_count), jnp.bfloat16)]
-        * chips,
+        out_specs=[vmem] * (2 + early),
+        out_shape=[
+            jax.ShapeDtypeStruct((modes, term_count), jnp.bfloat16),
+            jax.ShapeDtypeStruct((packet_rows, term_count), jnp.bfloat16),
+        ]
+        + [block_type] * early,
         compiler_params=params(16),
         name="prepare",
     )(me, in_hbm(correlations), in_hbm(run_inputs.T))
-    blocks = to_chips(sent)
 
     block = math.gcd(512, slab_cells)
 
@@ -355,7 +368,7 @@
     gathers = slots // 4
     chosen, spots = pl.pallas_call(
         functools.partial(choose_kernel, dim, chips),
-        in_specs=[smem, vmem] + [anywhere] * 2,
+        in_specs=[smem, vmem],
         out_specs=[vmem, vmem],
         out_shape=[
             jax.ShapeDtypeStruct((slots - gathers, 2 * half, core_terms), jnp.bfloat16),
@@ -364,15 +377,25 @@
         compiler_params=params(8),
         cost_estimate=cost(0, 2 * slots * half * core_terms),
         name="choose",
-    )(me, in_hbm(term_codes.T), *blocks[1:3])
+    )(me, in_hbm(term_codes.T))
+    if chips > early:
+        sent += pl.pallas_call(
+            functools.partial(late_kernel, chips),
+            in_specs=[smem, vmem, vmem] + [anywhere] * (1 + len(ordered)),
+            out_specs=[vmem] * (chips - early),
+            out_shape=[block_type] * (chips - early),
+            compiler_params=params(8),
+            name="late",
+        )(me, turned, packet, spots, *ordered)
+    blocks = to_chips(sent)
     packets = pl.pallas_call(
         functools.partial(collect_kernel, chips),
-        in_specs=[vmem] * chips + [anywhere] * (1 + len(ordered)),
+        in_specs=[vmem] * chips,
         out_specs=vmem,
         out_shape=jax.ShapeDtypeStruct((chips, packet_rows, term_count), jnp.bfloat16),
         compiler_params=params(8),
         name="collect",
-    )(*blocks, *ordered, spots)
+    )(*blocks)
     others = to_device(packets, 1)
 
     core_runs = run_count * chips

time: 56.3 us -> 56.1 us (level)
  starting transfers between devices: 23.4 us -> 24.4 us
  waiting for transfers between devices: 6.74 us -> 5.96 us
    ppermute x16, starting transfers between devices: 23.4 us -> 24.4 us  [to_device(): return lax.ppermute(array, 'runs', [(i, i ^ bits) for i in range(devices)])]
    ppermute x16, waiting for transfers between devices: 6.74 us -> 5.96 us  [to_device(): return lax.ppermute(array, 'runs', [(i, i ^ bits) for i in range(devices)])]
    pallas_call x1 -> x2, Pallas kernels: 1.35 us -> 1.36 us  [the longest x1 1.34 us: split_by_modes(): pl.pallas_call(functools.partial(prepare_kernel, chips), in_specs=[smem,...]
  transfers between devices with their start and end apart: 16 -> 16, of which waited for: 4 -> 4; matrix products, arithmetic and copies ran while one was open for 1% -> 1% of each run, Pallas kernels for 24% -> 23%
where the time goes in v10:
time: 56.1 us; the launch traced here: 55.8 us
  starting transfers between devices  24.4 us (43%)
  Pallas kernels  21.5 us (38%)
  waiting for transfers between devices  5.96 us (11%)
  local copies, waits for them, and re-layouts  2.97 us (5%)
  between operations  1 us (2%)
    ppermute x16, starting transfers between devices, to_device(): return lax.ppermute(array, 'runs', [(i, i ^ bits) for i in range(devices)])  24.4 us
    pallas_call x4, Pallas kernels, reorder(): pl.pallas_call(reorder_kernel, in_specs=[vmem, vmem] + [anywhere] * len(a...  9.59 us
    ppermute x16, waiting for transfers between devices, to_device(): return lax.ppermute(array, 'runs', [(i, i ^ bits) for i in range(devices)])  5.96 us
    pallas_call x2, Pallas kernels, design_of(): pl.pallas_call(functools.partial(design_kernel, dim, run_count), in_specs...  4.31 us
    pallas_call x1, Pallas kernels, split_by_modes(): pl.pallas_call(functools.partial(finish_kernel, len(ordered)), in_specs=[...  2.58 us
    unnamed x6, local copies, waits for them, and re-layouts  2.2 us
    pallas_call x1, Pallas kernels, split_by_modes(): pl.pallas_call(functools.partial(fit_kernel, 2 * rows), in_specs=[smem] +...  1.62 us
    pallas_call x1, Pallas kernels, split_by_modes(): pl.pallas_call(functools.partial(prepare_kernel, chips), in_specs=[smem,...  1.34 us
  transfers between devices with their start and end apart: 16, of which 4 were waited for; matrix products, arithmetic and copies ran while one was open for 1% of the time, Pallas kernels for 23%

profile of v10, /device:TPU:0, one launch (start us, length us, event | category | flops | bytes accessed | tf_op | source)
XLA Modules:
  0.0 55.8 jit_solution(11900423526564801875)
XLA Ops:
  0.6 1.3 %prepare.1 = (bf16[1024,256]{1,0:T(8,128)(2,1)S(1)}, bf16[16,256]{1,0:T(8,128)(2,1)S(1)}, bf16[144,256]{1,0:T(8,128)(2,1)S(1)}, bf16[144,256]{1,0:T(8,128)(2,1)S...) custom-call(s32[1]{0:T(128)} %bitcast.me_ref, ...), custom_call_target="tpu_custom_call" | custom-call | tf_op jit(solution)/shard_map/prepare/pallas_call | solution.py:338
  2.0 4.1 %collective-permute-start = (bf16[144,256]{1,0:T(8,128)(2,1)S(1)}, bf16[144,256]{1,0:T(8,128)(2,1)S(1)}, u32[]{:S(2)}, u32[]{:S(2)}) collective-permute-start(bf16[144,256]{1,0:T(8,128)(2,1)S(1)} %get-tuple-element.26), channel_id=1, source_target_pairs={{0,8},{1,9},{2,10},{3,11},{4,12},{5,13},{6,14},{7,15},{8,0},{9,1},... | collective-permute-start | bytes 221192 | tf_op jit(solution)/shard_map/ppermute | solution.py:307
  6.1 1.3 %collective-permute-start.1 = (bf16[144,256]{1,0:T(8,128)(2,1)S(1)}, bf16[144,256]{1,0:T(8,128)(2,1)S(1)}, u32[]{:S(2)}, u32[]{:S(2)}) collective-permute-start(bf16[144,256]{1,0:T(8,128)(2,1)S(1)} %get-tuple-element.27), channel_id=1, source_target_pairs={{0,10},{1,11},{2,8},{3,9},{4,14},{5,15},{6,12},{7,13},{8,2},{9,3},... | collective-permute-start | bytes 221192 | tf_op jit(solution)/shard_map/ppermute | solution.py:307
  7.3 3.6 %collective-permute-start.2 = (bf16[144,256]{1,0:T(8,128)(2,1)S(1)}, bf16[144,256]{1,0:T(8,128)(2,1)S(1)}, u32[]{:S(2)}, u32[]{:S(2)}) collective-permute-start(bf16[144,256]{1,0:T(8,128)(2,1)S(1)} %get-tuple-element.28), channel_id=1, source_target_pairs={{0,12},{1,13},{2,14},{3,15},{4,8},{5,9},{6,10},{7,11},{8,4},{9,5},... | collective-permute-start | bytes 221192 | tf_op jit(solution)/shard_map/ppermute | solution.py:307
  10.9 0.0 collective-permute-start.3
  10.9 1.7 %collective-permute-start.4 = (bf16[144,256]{1,0:T(8,128)(2,1)S(1)}, bf16[144,256]{1,0:T(8,128)(2,1)S(1)}, u32[]{:S(2)}, u32[]{:S(2)}) collective-permute-start(bf16[144,256]{1,0:T(8,128)(2,1)S(1)} %get-tuple-element.30), channel_id=1, source_target_pairs={{0,2},{1,3},{2,0},{3,1},{4,6},{5,7},{6,4},{7,5},{8,10},{9,11},{10,... | collective-permute-start | bytes 221192 | tf_op jit(solution)/shard_map/ppermute | solution.py:307
  12.6 0.8 %fusion = (s32[512]{0:T(512)S(1)}, s32[512]{0:T(512)S(1)}, s32[512]{0:T(512)S(1)}, s32[512]{0:T(512)S(1)}) fusion(s32[2048]{0:T(1024)} %param.11), kind=kLoop, calls=%fused_computation | loop fusion | bytes 16384 | tf_op jit(solution)/shard_map/slice | solution.py:362
  13.4 0.0 copy-start.1
  13.4 2.2 %copy-done.1 = bf16[2048,1024]{1,0:T(8,128)(2,1)S(1)} copy-done((bf16[2048,1024]{1,0:T(8,128)(2,1)S(1)}, bf16[2048,1024]{1,0:T(8,128)(2,1)}, u32[]{:S(2)}) %copy-start.1) | copy-done | bytes 4194328
  15.6 2.4 %reorder.4.refs_1_.refs_0_ = bf16[512,1024]{1,0:T(8,128)(2,1)S(1)} custom-call(s32[1,512]{1,0:T(1,128)S(1)} %bitcast.12, bf16[2048,1024]{1,0:T(8,128)(2,1)S(1)} %copy-done.1), custom_call_target="tpu_custom_call" | custom-call | flops 2147483648 | bytes 4194304 | tf_op jit(solution)/shard_map/reorder/pallas_call | solution.py:354
  17.9 1.3 %choose.1 = (bf16[3,256,2048]{2,1,0:T(8,128)(2,1)S(1)}, s32[1,2048]{1,0:T(1,128)S(1)}) custom-call(s32[1]{0:T(128)} %bitcast.me_ref, s32[4,4096]{1,0:T(4,128)} %bitcast.13), custom_call_target="tpu_custom_call" | custom-call | bytes 2097152 | tf_op jit(solution)/shard_map/choose/pallas_call | solution.py:369
  19.3 0.0 collective-permute-done.refs_1_
  19.3 0.1 collective-permute-start.5
  19.4 0.0 collective-permute-done.1.refs_2_
  19.4 1.8 %collective-permute-start.6 = (bf16[144,256]{1,0:T(8,128)(2,1)S(1)}, bf16[144,256]{1,0:T(8,128)(2,1)S(1)}, u32[]{:S(2)}, u32[]{:S(2)}) collective-permute-start(bf16[144,256]{1,0:T(8,128)(2,1)S(1)} %get-tuple-element.34), channel_id=1, source_target_pairs={{0,6},{1,7},{2,4},{3,5},{4,2},{5,3},{6,0},{7,1},{8,14},{9,15},{10,... | collective-permute-start | bytes 221192 | tf_op jit(solution)/shard_map/ppermute | solution.py:307
  21.2 0.0 collective-permute-done.2.refs_3_
  21.2 0.0 collective-permute-done.3.refs_4_
  21.2 0.0 collective-permute-done.4.refs_5_
  21.2 2.5 %collective-permute-done.5.refs_6_ = bf16[144,256]{1,0:T(8,128)(2,1)S(1)} collective-permute-done((bf16[144,256]{1,0:T(8,128)(2,1)S(1)}, bf16[144,256]{1,0:T(8,128)(2,1)S(1)}, u32[]{:S(2)}, u32[]{:S(2)}) %collective-permute-start.5) | collective-permute-done | bytes 73760 | tf_op jit(solution)/shard_map/ppermute | solution.py:307
  23.7 1.0 %collective-permute-done.6.refs_7_ = bf16[144,256]{1,0:T(8,128)(2,1)S(1)} collective-permute-done((bf16[144,256]{1,0:T(8,128)(2,1)S(1)}, bf16[144,256]{1,0:T(8,128)(2,1)S(1)}, u32[]{:S(2)}, u32[]{:S(2)}) %collective-permute-start.6) | collective-permute-done | bytes 73760 | tf_op jit(solution)/shard_map/ppermute | solution.py:307
  24.7 0.0 collective-permute-start.7
  24.7 2.2 %design.2.refs_8_.refs_0_ = bf16[512,2048]{1,0:T(8,128)(2,1)S(1)} custom-call(bf16[8,16,256]{2,1,0:T(8,128)(2,1)S(1)} %collect.1.packets_ref.own_ref, bf16[3,256,2048]{2,1,0:T(8,128)(2,1)S(1)} %get-tuple-element.35.chosen_ref, s32[1,2048]{1,0:T(1,128)S(1)} %get-tuple-element.32.refs_0_.spots_ref), custom_call_target="tpu_custom_call" | custom-call | flops 2147483648 | bytes 2097152 | tf_op jit(solution)/shard_map/design/pallas_call | solution.py:404
  26.9 0.0 copy-start
  26.9 0.0 collective-permute-done.7.packets_ref.other_ref
  26.9 2.2 %design.3.refs_9_.refs_1_ = bf16[512,2048]{1,0:T(8,128)(2,1)S(1)} custom-call(bf16[8,16,256]{2,1,0:T(8,128)(2,1)S(1)} %collective-permute-done.7.packets_ref.other_ref, bf16[3,256,2048]{2,1,0:T(8,128)(2,1)S(1)} %get-tuple-element.35.chosen_ref, s32[1,2048]{1,0:T(1,128)S(1)} %get-tuple-element.32.refs_0_.spots_ref), custom_call_target="tpu_custom_call" | custom-call | flops 2147483648 | bytes 2097152 | tf_op jit(solution)/shard_map/design/pallas_call | solution.py:404
  29.1 0.0 copy-start.2
  29.1 0.0 copy-done
  29.1 1.6 %fit.1 = (f32[128,1024]{1,0:T(8,128)S(1)}, f32[8,256]{1,0:T(8,128)S(1)}) custom-call(s32[1]{0:T(128)} %bitcast.me_ref, s32[1,4096]{1,0:T(1,128)S(1)} %bitcast.8, bf16[8,16,256]{2,1,0:T(8,128)(2,1)S(1)} %collect.1.packets_ref.own_ref, bf16[8,16,256]{2,1,0:T(8,128)(2,1)S(1)} %collective-permute-done.7.packets_ref.other_ref, ...), custom_call_target="tpu_custom_call" | custom-call | flops 536870912 | bytes 4194304 | tf_op jit(solution)/shard_map/fit/pallas_call | solution.py:425
  30.7 0.6 %collective-permute-start.8 = (f32[128,1024]{1,0:T(8,128)S(1)}, f32[128,1024]{1,0:T(8,128)S(1)}, u32[]{:S(2)}, u32[]{:S(2)}) collective-permute-start(f32[128,1024]{1,0:T(8,128)S(1)} %get-tuple-element.37.refs_0_.own_ref), channel_id=1, source_target_pairs={{0,1},{1,0},{2,3},{3,2},{4,5},{5,4},{6,7},{7,6},{8,9},{9,8},{10,11... | collective-permute-start | bytes 1572872 | tf_op jit(solution)/shard_map/ppermute | solution.py:307
  31.3 0.0 copy-done.2
  31.3 2.4 %reorder.5.refs_2_.refs_1_ = bf16[512,1024]{1,0:T(8,128)(2,1)S(1)} custom-call(s32[1,512]{1,0:T(1,128)S(1)} %bitcast.11, bf16[2048,1024]{1,0:T(8,128)(2,1)S(1)} %copy-done.2, f32[128,1024]{1,0:T(8,128)S(1)} %get-tuple-element.37.refs_0_.own_ref), custom_call_target="tpu_custom_call" | custom-call | flops 2147483648 | bytes 4194304 | tf_op jit(solution)/shard_map/reorder/pallas_call | solution.py:354
  33.6 0.0 collective-permute-done.8.other_ref
  33.6 0.7 %sum.1 = (bf16[128,256]{1,0:T(8,128)(2,1)S(1)}, bf16[128,256]{1,0:T(8,128)(2,1)S(1)}, bf16[128,256]{1,0:T(8,128)(2,1)S(1)}, bf16[128,256]{1,0:T(8,128)(2,1)S(1)}...) custom-call(f32[128,1024]{1,0:T(8,128)S(1)} %get-tuple-element.37.re, ...), custom_call_target="tpu_custom_call" | custom-call | flops 536870912 | bytes 4194304 | tf_op jit(solution)/shard_map/sum/pallas_call | solution.py:439
  34.4 4.2 %collective-permute-start.9 = (bf16[128,256]{1,0:T(8,128)(2,1)S(1)}, bf16[128,256]{1,0:T(8,128)(2,1)S(1)}, u32[]{:S(2)}, u32[]{:S(2)}) collective-permute-start(bf16[128,256]{1,0:T(8,128)(2,1)S(1)} %get-tuple-element.39), channel_id=1, source_target_pairs={{0,8},{1,9},{2,10},{3,11},{4,12},{5,13},{6,14},{7,15},{8,0},{9,1},... | collective-permute-start | bytes 196616 | tf_op jit(solution)/shard_map/ppermute | solution.py:307
  38.5 0.0 collective-permute-start.10
  38.6 3.1 %collective-permute-start.11 = (bf16[128,256]{1,0:T(8,128)(2,1)S(1)}, bf16[128,256]{1,0:T(8,128)(2,1)S(1)}, u32[]{:S(2)}, u32[]{:S(2)}) collective-permute-start(bf16[128,256]{1,0:T(8,128)(2,1)S(1)} %get-tuple-element.41), channel_id=1, source_target_pairs={{0,12},{1,13},{2,14},{3,15},{4,8},{5,9},{6,10},{7,11},{8,4},{9,5},... | collective-permute-start | bytes 196616 | tf_op jit(solution)/shard_map/ppermute | solution.py:307
  41.7 1.7 %collective-permute-start.12 = (bf16[128,256]{1,0:T(8,128)(2,1)S(1)}, bf16[128,256]{1,0:T(8,128)(2,1)S(1)}, u32[]{:S(2)}, u32[]{:S(2)}) collective-permute-start(bf16[128,256]{1,0:T(8,128)(2,1)S(1)} %get-tuple-element.42), channel_id=1, source_target_pairs={{0,14},{1,15},{2,12},{3,13},{4,10},{5,11},{6,8},{7,9},{8,6},{9,7},... | collective-permute-start | bytes 196616 | tf_op jit(solution)/shard_map/ppermute | solution.py:307
  43.4 0.5 collective-permute-start.13
  43.9 2.5 %reorder.6.refs_2_ = bf16[512,1024]{1,0:T(8,128)(2,1)S(1)} custom-call(s32[1,512]{1,0:T(1,128)S(1)} %bitcast.10, bf16[2048,1024]{1,0:T(8,128)(2,1)S(1)} %copy-done.2, bf16[128,256]{1,0:T(8,128)(2,1)S(1)} %get-tuple-element.38.refs_0_.refs_4_), custom_call_target="tpu_custom_call" | custom-call | flops 2147483648 | bytes 4194304 | tf_op jit(solution)/shard_map/reorder/pallas_call | solution.py:354
  46.4 0.0 collective-permute-done.9.refs_0_.refs_5_
  46.4 0.1 collective-permute-start.14
  46.5 1.2 %collective-permute-done.10.refs_1_.refs_6_ = bf16[128,256]{1,0:T(8,128)(2,1)S(1)} collective-permute-done((bf16[128,256]{1,0:T(8,128)(2,1)S(1)}, bf16[128,256]{1,0:T(8,128)(2,1)S(1)}, u32[]{:S(2)}, u32[]{:S(2)}) %collective-permute-start.10) | collective-permute-done | bytes 65568 | tf_op jit(solution)/shard_map/ppermute | solution.py:307
  47.7 1.8 %collective-permute-start.15 = (bf16[128,256]{1,0:T(8,128)(2,1)S(1)}, bf16[128,256]{1,0:T(8,128)(2,1)S(1)}, u32[]{:S(2)}, u32[]{:S(2)}) collective-permute-start(bf16[128,256]{1,0:T(8,128)(2,1)S(1)} %get-tuple-element.45), channel_id=1, source_target_pairs={{0,6},{1,7},{2,4},{3,5},{4,2},{5,3},{6,0},{7,1},{8,14},{9,15},{10,... | collective-permute-start | bytes 196616 | tf_op jit(solution)/shard_map/ppermute | solution.py:307
  49.4 2.4 %reorder.7.refs_3_ = bf16[512,1024]{1,0:T(8,128)(2,1)S(1)} custom-call(s32[1,512]{1,0:T(1,128)S(1)} %bitcast.9, bf16[2048,1024]{1,0:T(8,128)(2,1)S(1)} %copy-done.2, bf16[128,256]{1,0:T(8,128)(2,1)S(1)} %collective-permute-done.9.refs_0_.refs_5_, bf16[128,256]{1,0:T(8,128)(2,1)S(1)} %collective-permute-done.10.refs_1_.refs_6_), custom_call_target="tpu_custom_call" | custom-call | flops 2147483648 | bytes 4194304 | tf_op jit(solution)/shard_map/reorder/pallas_call | solution.py:354
  51.8 0.0 collective-permute-done.11.refs_7_
  51.8 0.0 collective-permute-done.12.refs_8_
  51.8 0.0 collective-permute-done.13.refs_9_
  51.8 0.0 collective-permute-done.14.refs_10_
  51.8 1.2 %collective-permute-done.15.refs_11_ = bf16[128,256]{1,0:T(8,128)(2,1)S(1)} collective-permute-done((bf16[128,256]{1,0:T(8,128)(2,1)S(1)}, bf16[128,256]{1,0:T(8,128)(2,1)S(1)}, u32[]{:S(2)}, u32[]{:S(2)}) %collective-permute-start.15) | collective-permute-done | bytes 65568 | tf_op jit(solution)/shard_map/ppermute | solution.py:307
  53.1 2.6 %finish.1 = (f32[256,1024]{1,0:T(8,128)}, bf16[256,2048]{1,0:T(8,128)(2,1)}) custom-call(s32[1]{0:T(128)} %bitcast.me_ref, bf16[1024,256]{1,0:T(8,128)(2,1)S(1)} %get-tuple-element.24.turned_ref.corr_ref, f32[8,256]{1,0:T(8,128)S(1)} %get-tuple-element.36.scale_ref, bf16[512,1024]{1,0:T(8,128)(2,1)S(1)} %reorder.4.refs_1_.refs_0_, ...), custom_call_target="tpu_custom_call" | custom-call | tf_op jit(solution)/shard_map/finish/pallas_call | solution.py:453
  (2 shorter events, 0.0 us)
Async XLA Ops:
  2.0 17.3 %collective-permute-start = (bf16[144,256]{1,0:T(8,128)(2,1)S(1)}, bf16[144,256]{1,0:T(8,128)(2,1)S(1)}, u32[]{:S(2)}, u32[]{:S(2)}) collective-permute-start(bf16[144,256]{1,0:T(8,128)(2,1)S(1)} %get-tuple-element.26), channel_id=1, source_target_pairs={{0,8},{1,9},{2,10},{3,11},{4,12},{5,13},{6,14},{7,15},{8,0},{9,1},... | collective-permute-start | bytes 221192 | tf_op jit(solution)/shard_map/ppermute | solution.py:307
  6.1 13.3 %collective-permute-start.1 = (bf16[144,256]{1,0:T(8,128)(2,1)S(1)}, bf16[144,256]{1,0:T(8,128)(2,1)S(1)}, u32[]{:S(2)}, u32[]{:S(2)}) collective-permute-start(bf16[144,256]{1,0:T(8,128)(2,1)S(1)} %get-tuple-element.27), channel_id=1, source_target_pairs={{0,10},{1,11},{2,8},{3,9},{4,14},{5,15},{6,12},{7,13},{8,2},{9,3},... | collective-permute-start | bytes 221192 | tf_op jit(solution)/shard_map/ppermute | solution.py:307
  7.3 13.8 %collective-permute-start.2 = (bf16[144,256]{1,0:T(8,128)(2,1)S(1)}, bf16[144,256]{1,0:T(8,128)(2,1)S(1)}, u32[]{:S(2)}, u32[]{:S(2)}) collective-permute-start(bf16[144,256]{1,0:T(8,128)(2,1)S(1)} %get-tuple-element.28), channel_id=1, source_target_pairs={{0,12},{1,13},{2,14},{3,15},{4,8},{5,9},{6,10},{7,11},{8,4},{9,5},... | collective-permute-start | bytes 221192 | tf_op jit(solution)/shard_map/ppermute | solution.py:307
  10.9 10.2 %collective-permute-start.3 = (bf16[144,256]{1,0:T(8,128)(2,1)S(1)}, bf16[144,256]{1,0:T(8,128)(2,1)S(1)}, u32[]{:S(2)}, u32[]{:S(2)}) collective-permute-start(bf16[144,256]{1,0:T(8,128)(2,1)S(1)} %get-tuple-element.29), channel_id=1, source_target_pairs={{0,14},{1,15},{2,12},{3,13},{4,10},{5,11},{6,8},{7,9},{8,6},{9,7},... | collective-permute-start | bytes 221192 | tf_op jit(solution)/shard_map/ppermute | solution.py:307
  10.9 10.2 %collective-permute-start.4 = (bf16[144,256]{1,0:T(8,128)(2,1)S(1)}, bf16[144,256]{1,0:T(8,128)(2,1)S(1)}, u32[]{:S(2)}, u32[]{:S(2)}) collective-permute-start(bf16[144,256]{1,0:T(8,128)(2,1)S(1)} %get-tuple-element.30), channel_id=1, source_target_pairs={{0,2},{1,3},{2,0},{3,1},{4,6},{5,7},{6,4},{7,5},{8,10},{9,11},{10,... | collective-permute-start | bytes 221192 | tf_op jit(solution)/shard_map/ppermute | solution.py:307
  13.4 2.2 %copy-start.1 = (bf16[2048,1024]{1,0:T(8,128)(2,1)S(1)}, bf16[2048,1024]{1,0:T(8,128)(2,1)}, u32[]{:S(2)}) copy-start(bf16[2048,1024]{1,0:T(8,128)(2,1)} %slab_ref.7) | copy-start | bytes 12582916
  19.3 4.4 %collective-permute-start.5 = (bf16[144,256]{1,0:T(8,128)(2,1)S(1)}, bf16[144,256]{1,0:T(8,128)(2,1)S(1)}, u32[]{:S(2)}, u32[]{:S(2)}) collective-permute-start(bf16[144,256]{1,0:T(8,128)(2,1)S(1)} %get-tuple-element.33), channel_id=1, source_target_pairs={{0,4},{1,5},{2,6},{3,7},{4,0},{5,1},{6,2},{7,3},{8,12},{9,13},{10,... | collective-permute-start | bytes 221192 | tf_op jit(solution)/shard_map/ppermute | solution.py:307
  19.4 5.3 %collective-permute-start.6 = (bf16[144,256]{1,0:T(8,128)(2,1)S(1)}, bf16[144,256]{1,0:T(8,128)(2,1)S(1)}, u32[]{:S(2)}, u32[]{:S(2)}) collective-permute-start(bf16[144,256]{1,0:T(8,128)(2,1)S(1)} %get-tuple-element.34), channel_id=1, source_target_pairs={{0,6},{1,7},{2,4},{3,5},{4,2},{5,3},{6,0},{7,1},{8,14},{9,15},{10,... | collective-permute-start | bytes 221192 | tf_op jit(solution)/shard_map/ppermute | solution.py:307
  24.7 2.2 %collective-permute-start.7 = (bf16[8,16,256]{2,1,0:T(8,128)(2,1)S(1)}, bf16[8,16,256]{2,1,0:T(8,128)(2,1)S(1)}, u32[]{:S(2)}, u32[]{:S(2)}) collective-permute-start(bf16[8,16,256]{2,1,0:T(8,128)(2,1)S(1)} %collect.1.packets_ref.own_ref), channel_id=1, source_target_pairs={{0,1},{1,0},{2,3},{3,2},{4,5},{5,4},{6,7},{7,6},{8,9},{9,8},{10,11... | collective-permute-start | bytes 196616 | tf_op jit(solution)/shard_map/ppermute | solution.py:307
  26.9 2.2 %copy-start = (s32[4096]{0:T(1024)S(1)}, s32[4096]{0:T(1024)}, u32[]{:S(2)}) copy-start(s32[4096]{0:T(1024)} %param.8) | copy-start | bytes 49156
  29.1 2.2 %copy-start.2 = (bf16[2048,1024]{1,0:T(8,128)(2,1)S(1)}, bf16[2048,1024]{1,0:T(8,128)(2,1)}, u32[]{:S(2)}) copy-start(bf16[2048,1024]{1,0:T(8,128)(2,1)} %slab_ref.7) | copy-start | bytes 12582916
  30.7 2.9 %collective-permute-start.8 = (f32[128,1024]{1,0:T(8,128)S(1)}, f32[128,1024]{1,0:T(8,128)S(1)}, u32[]{:S(2)}, u32[]{:S(2)}) collective-permute-start(f32[128,1024]{1,0:T(8,128)S(1)} %get-tuple-element.37.refs_0_.own_ref), channel_id=1, source_target_pairs={{0,1},{1,0},{2,3},{3,2},{4,5},{5,4},{6,7},{7,6},{8,9},{9,8},{10,11... | collective-permute-start | bytes 1572872 | tf_op jit(solution)/shard_map/ppermute | solution.py:307
  34.4 12.0 %collective-permute-start.9 = (bf16[128,256]{1,0:T(8,128)(2,1)S(1)}, bf16[128,256]{1,0:T(8,128)(2,1)S(1)}, u32[]{:S(2)}, u32[]{:S(2)}) collective-permute-start(bf16[128,256]{1,0:T(8,128)(2,1)S(1)} %get-tuple-element.39), channel_id=1, source_target_pairs={{0,8},{1,9},{2,10},{3,11},{4,12},{5,13},{6,14},{7,15},{8,0},{9,1},... | collective-permute-start | bytes 196616 | tf_op jit(solution)/shard_map/ppermute | solution.py:307
  38.5 9.1 %collective-permute-start.10 = (bf16[128,256]{1,0:T(8,128)(2,1)S(1)}, bf16[128,256]{1,0:T(8,128)(2,1)S(1)}, u32[]{:S(2)}, u32[]{:S(2)}) collective-permute-start(bf16[128,256]{1,0:T(8,128)(2,1)S(1)} %get-tuple-element.40), channel_id=1, source_target_pairs={{0,10},{1,11},{2,8},{3,9},{4,14},{5,15},{6,12},{7,13},{8,2},{9,3},... | collective-permute-start | bytes 196616 | tf_op jit(solution)/shard_map/ppermute | solution.py:307
  38.6 13.2 %collective-permute-start.11 = (bf16[128,256]{1,0:T(8,128)(2,1)S(1)}, bf16[128,256]{1,0:T(8,128)(2,1)S(1)}, u32[]{:S(2)}, u32[]{:S(2)}) collective-permute-start(bf16[128,256]{1,0:T(8,128)(2,1)S(1)} %get-tuple-element.41), channel_id=1, source_target_pairs={{0,12},{1,13},{2,14},{3,15},{4,8},{5,9},{6,10},{7,11},{8,4},{9,5},... | collective-permute-start | bytes 196616 | tf_op jit(solution)/shard_map/ppermute | solution.py:307
  41.7 10.1 %collective-permute-start.12 = (bf16[128,256]{1,0:T(8,128)(2,1)S(1)}, bf16[128,256]{1,0:T(8,128)(2,1)S(1)}, u32[]{:S(2)}, u32[]{:S(2)}) collective-permute-start(bf16[128,256]{1,0:T(8,128)(2,1)S(1)} %get-tuple-element.42), channel_id=1, source_target_pairs={{0,14},{1,15},{2,12},{3,13},{4,10},{5,11},{6,8},{7,9},{8,6},{9,7},... | collective-permute-start | bytes 196616 | tf_op jit(solution)/shard_map/ppermute | solution.py:307
  43.4 8.5 %collective-permute-start.13 = (bf16[128,256]{1,0:T(8,128)(2,1)S(1)}, bf16[128,256]{1,0:T(8,128)(2,1)S(1)}, u32[]{:S(2)}, u32[]{:S(2)}) collective-permute-start(bf16[128,256]{1,0:T(8,128)(2,1)S(1)} %get-tuple-element.43), channel_id=1, source_target_pairs={{0,2},{1,3},{2,0},{3,1},{4,6},{5,7},{6,4},{7,5},{8,10},{9,11},{10,... | collective-permute-start | bytes 196616 | tf_op jit(solution)/shard_map/ppermute | solution.py:307
  46.4 5.4 %collective-permute-start.14 = (bf16[128,256]{1,0:T(8,128)(2,1)S(1)}, bf16[128,256]{1,0:T(8,128)(2,1)S(1)}, u32[]{:S(2)}, u32[]{:S(2)}) collective-permute-start(bf16[128,256]{1,0:T(8,128)(2,1)S(1)} %get-tuple-element.44), channel_id=1, source_target_pairs={{0,4},{1,5},{2,6},{3,7},{4,0},{5,1},{6,2},{7,3},{8,12},{9,13},{10,... | collective-permute-start | bytes 196616 | tf_op jit(solution)/shard_map/ppermute | solution.py:307
  47.7 5.4 %collective-permute-start.15 = (bf16[128,256]{1,0:T(8,128)(2,1)S(1)}, bf16[128,256]{1,0:T(8,128)(2,1)S(1)}, u32[]{:S(2)}, u32[]{:S(2)}) collective-permute-start(bf16[128,256]{1,0:T(8,128)(2,1)S(1)} %get-tuple-element.45), channel_id=1, source_target_pairs={{0,6},{1,7},{2,4},{3,5},{4,2},{5,3},{6,0},{7,1},{8,14},{9,15},{10,... | collective-permute-start | bytes 196616 | tf_op jit(solution)/shard_map/ppermute | solution.py:307

commit v11 on v10

--- a/solution.py
+++ b/solution.py
@@ -388,14 +388,15 @@
             name="late",
         )(me, turned, packet, spots, *ordered)
     blocks = to_chips(sent)
+    tail = [reorder(start, *blocks[1:3]) for start in quarters[1]]
     packets = pl.pallas_call(
         functools.partial(collect_kernel, chips),
-        in_specs=[vmem] * chips,
+        in_specs=[vmem] * chips + [anywhere] * len(tail),
         out_specs=vmem,
         out_shape=jax.ShapeDtypeStruct((chips, packet_rows, term_count), jnp.bfloat16),
         compiler_params=params(8),
         name="collect",
-    )(*blocks)
+    )(*blocks, *tail)
     others = to_device(packets, 1)
 
     core_runs = run_count * chips
@@ -435,7 +436,7 @@
         cost_estimate=fit_cost,
         name="fit",
     )(me, weight_levels[None, :], packets, others, *blocks, *designs)
-    beside = [reorder(start, fitted) for start in quarters[1]]
+    beside = [reorder(start, fitted) for start in quarters[2]]
     summed = pl.pallas_call(
         functools.partial(sum_kernel, float(total_runs), chips),
         in_specs=[vmem] * (2 + CORES) + [anywhere] * len(beside),
@@ -446,9 +447,8 @@
         name="sum",
     )(fitted, to_device(fitted, 1), *designs, *beside)
     returned = to_chips(summed)
-    ordered += beside
-    ordered += [reorder(start, summed[0]) for start in quarters[2]]
-    ordered += [reorder(start, *returned[1:3]) for start in quarters[3]]
+    ordered += tail + beside
+    ordered += [reorder(start, summed[0]) for start in quarters[3]]
 
     return pl.pallas_call(
         functools.partial(finish_kernel, len(ordered)),

time: 56.1 us -> 56.1 us (level)
  waiting for transfers between devices: 5.96 us -> 6.78 us
  starting transfers between devices: 24.4 us -> 23.6 us
    ppermute x16, starting transfers between devices: 24.4 us -> 23.6 us  [to_device(): return lax.ppermute(array, 'runs', [(i, i ^ bits) for i in range(devices)])]
    ppermute x16, waiting for transfers between devices: 5.96 us -> 6.78 us  [to_device(): return lax.ppermute(array, 'runs', [(i, i ^ bits) for i in range(devices)])]
  transfers between devices with their start and end apart: 16 -> 16, of which waited for: 4 -> 5; matrix products, arithmetic and copies ran while one was open for 1% -> 1% of each run, Pallas kernels for 23% -> 23%
where the time goes in v11:
time: 56.1 us; the launch traced here: 55.8 us
  starting transfers between devices  23.6 us (42%)
  Pallas kernels  21.5 us (38%)
  waiting for transfers between devices  6.78 us (12%)
  local copies, waits for them, and re-layouts  2.97 us (5%)
  between operations  1.01 us (2%)
    ppermute x16, starting transfers between devices, to_device(): return lax.ppermute(array, 'runs', [(i, i ^ bits) for i in range(devices)])  23.6 us
    pallas_call x4, Pallas kernels, reorder(): pl.pallas_call(reorder_kernel, in_specs=[vmem, vmem] + [anywhere] * len(a...  9.43 us
    ppermute x16, waiting for transfers between devices, to_device(): return lax.ppermute(array, 'runs', [(i, i ^ bits) for i in range(devices)])  6.78 us
    pallas_call x2, Pallas kernels, design_of(): pl.pallas_call(functools.partial(design_kernel, dim, run_count), in_specs...  4.28 us
    pallas_call x1, Pallas kernels, split_by_modes(): pl.pallas_call(functools.partial(finish_kernel, len(ordered)), in_specs=[...  2.56 us
    unnamed x6, local copies, waits for them, and re-layouts  2.2 us
    pallas_call x1, Pallas kernels, split_by_modes(): pl.pallas_call(functools.partial(fit_kernel, 2 * rows), in_specs=[smem] +...  1.62 us
    pallas_call x1, Pallas kernels, split_by_modes(): pl.pallas_call(functools.partial(prepare_kernel, chips), in_specs=[smem,...  1.34 us
  transfers between devices with their start and end apart: 16, of which 5 were waited for; matrix products, arithmetic and copies ran while one was open for 1% of the time, Pallas kernels for 23%

profile of v11, /device:TPU:0, one launch (start us, length us, event | category | flops | bytes accessed | tf_op | source)
XLA Modules:
  0.0 55.8 jit_solution(698455228681224650)
XLA Ops:
  0.6 1.3 %prepare.1 = (bf16[1024,256]{1,0:T(8,128)(2,1)S(1)}, bf16[16,256]{1,0:T(8,128)(2,1)S(1)}, bf16[144,256]{1,0:T(8,128)(2,1)S(1)}, bf16[144,256]{1,0:T(8,128)(2,1)S...) custom-call(s32[1]{0:T(128)} %bitcast.me_ref, ...), custom_call_target="tpu_custom_call" | custom-call | tf_op jit(solution)/shard_map/prepare/pallas_call | solution.py:338
  2.0 4.1 %collective-permute-start = (bf16[144,256]{1,0:T(8,128)(2,1)S(1)}, bf16[144,256]{1,0:T(8,128)(2,1)S(1)}, u32[]{:S(2)}, u32[]{:S(2)}) collective-permute-start(bf16[144,256]{1,0:T(8,128)(2,1)S(1)} %get-tuple-element.26), channel_id=1, source_target_pairs={{0,8},{1,9},{2,10},{3,11},{4,12},{5,13},{6,14},{7,15},{8,0},{9,1},... | collective-permute-start | bytes 221192 | tf_op jit(solution)/shard_map/ppermute | solution.py:307
  6.1 1.3 %collective-permute-start.1 = (bf16[144,256]{1,0:T(8,128)(2,1)S(1)}, bf16[144,256]{1,0:T(8,128)(2,1)S(1)}, u32[]{:S(2)}, u32[]{:S(2)}) collective-permute-start(bf16[144,256]{1,0:T(8,128)(2,1)S(1)} %get-tuple-element.27), channel_id=1, source_target_pairs={{0,10},{1,11},{2,8},{3,9},{4,14},{5,15},{6,12},{7,13},{8,2},{9,3},... | collective-permute-start | bytes 221192 | tf_op jit(solution)/shard_map/ppermute | solution.py:307
  7.3 3.6 %collective-permute-start.2 = (bf16[144,256]{1,0:T(8,128)(2,1)S(1)}, bf16[144,256]{1,0:T(8,128)(2,1)S(1)}, u32[]{:S(2)}, u32[]{:S(2)}) collective-permute-start(bf16[144,256]{1,0:T(8,128)(2,1)S(1)} %get-tuple-element.28), channel_id=1, source_target_pairs={{0,12},{1,13},{2,14},{3,15},{4,8},{5,9},{6,10},{7,11},{8,4},{9,5},... | collective-permute-start | bytes 221192 | tf_op jit(solution)/shard_map/ppermute | solution.py:307
  10.9 0.0 collective-permute-start.3
  10.9 1.7 %collective-permute-start.4 = (bf16[144,256]{1,0:T(8,128)(2,1)S(1)}, bf16[144,256]{1,0:T(8,128)(2,1)S(1)}, u32[]{:S(2)}, u32[]{:S(2)}) collective-permute-start(bf16[144,256]{1,0:T(8,128)(2,1)S(1)} %get-tuple-element.30), channel_id=1, source_target_pairs={{0,2},{1,3},{2,0},{3,1},{4,6},{5,7},{6,4},{7,5},{8,10},{9,11},{10,... | collective-permute-start | bytes 221192 | tf_op jit(solution)/shard_map/ppermute | solution.py:307
  12.6 0.8 %fusion = (s32[512]{0:T(512)S(1)}, s32[512]{0:T(512)S(1)}, s32[512]{0:T(512)S(1)}, s32[512]{0:T(512)S(1)}) fusion(s32[2048]{0:T(1024)} %param.11), kind=kLoop, calls=%fused_computation | loop fusion | bytes 16384 | tf_op jit(solution)/shard_map/slice | solution.py:362
  13.4 0.0 copy-start.1
  13.4 2.2 %copy-done.1 = bf16[2048,1024]{1,0:T(8,128)(2,1)S(1)} copy-done((bf16[2048,1024]{1,0:T(8,128)(2,1)S(1)}, bf16[2048,1024]{1,0:T(8,128)(2,1)}, u32[]{:S(2)}) %copy-start.1) | copy-done | bytes 4194328
  15.6 2.4 %reorder.4.refs_1_.refs_0_ = bf16[512,1024]{1,0:T(8,128)(2,1)S(1)} custom-call(s32[1,512]{1,0:T(1,128)S(1)} %bitcast.12, bf16[2048,1024]{1,0:T(8,128)(2,1)S(1)} %copy-done.1), custom_call_target="tpu_custom_call" | custom-call | flops 2147483648 | bytes 4194304 | tf_op jit(solution)/shard_map/reorder/pallas_call | solution.py:354
  17.9 1.3 %choose.1 = (bf16[3,256,2048]{2,1,0:T(8,128)(2,1)S(1)}, s32[1,2048]{1,0:T(1,128)S(1)}) custom-call(s32[1]{0:T(128)} %bitcast.me_ref, s32[4,4096]{1,0:T(4,128)} %bitcast.13), custom_call_target="tpu_custom_call" | custom-call | bytes 2097152 | tf_op jit(solution)/shard_map/choose/pallas_call | solution.py:369
  19.3 0.0 collective-permute-done.refs_0_.refs_1_
  19.3 0.1 collective-permute-start.5
  19.4 0.0 collective-permute-done.1.refs_1_.refs_2_
  19.4 1.8 %collective-permute-start.6 = (bf16[144,256]{1,0:T(8,128)(2,1)S(1)}, bf16[144,256]{1,0:T(8,128)(2,1)S(1)}, u32[]{:S(2)}, u32[]{:S(2)}) collective-permute-start(bf16[144,256]{1,0:T(8,128)(2,1)S(1)} %get-tuple-element.34), channel_id=1, source_target_pairs={{0,6},{1,7},{2,4},{3,5},{4,2},{5,3},{6,0},{7,1},{8,14},{9,15},{10,... | collective-permute-start | bytes 221192 | tf_op jit(solution)/shard_map/ppermute | solution.py:307
  21.2 2.4 %reorder.5.refs_8_.refs_1_ = bf16[512,1024]{1,0:T(8,128)(2,1)S(1)} custom-call(s32[1,512]{1,0:T(1,128)S(1)} %bitcast.11, bf16[2048,1024]{1,0:T(8,128)(2,1)S(1)} %copy-done.1, bf16[144,256]{1,0:T(8,128)(2,1)S(1)} %collective-permute-done.refs_0_.refs_1_, bf16[144,256]{1,0:T(8,128)(2,1)S(1)} %collective-permute-done.1.refs_1_.refs_2_), custom_call_target="tpu_custom_call" | custom-call | flops 2147483648 | bytes 4194304 | tf_op jit(solution)/shard_map/reorder/pallas_call | solution.py:354
  23.5 0.0 collective-permute-done.2.refs_3_
  23.5 0.0 collective-permute-done.3.refs_4_
  23.6 0.0 collective-permute-done.4.refs_5_
  23.6 0.1 collective-permute-done.5.refs_6_
  23.7 1.0 %collective-permute-done.6.refs_7_ = bf16[144,256]{1,0:T(8,128)(2,1)S(1)} collective-permute-done((bf16[144,256]{1,0:T(8,128)(2,1)S(1)}, bf16[144,256]{1,0:T(8,128)(2,1)S(1)}, u32[]{:S(2)}, u32[]{:S(2)}) %collective-permute-start.6) | collective-permute-done | bytes 73760 | tf_op jit(solution)/shard_map/ppermute | solution.py:307
  24.7 0.0 collective-permute-start.7
  24.7 2.1 %design.2.refs_8_.refs_0_ = bf16[512,2048]{1,0:T(8,128)(2,1)S(1)} custom-call(bf16[8,16,256]{2,1,0:T(8,128)(2,1)S(1)} %collect.1.packets_ref.own_ref, bf16[3,256,2048]{2,1,0:T(8,128)(2,1)S(1)} %get-tuple-element.35.chosen_ref, s32[1,2048]{1,0:T(1,128)S(1)} %get-tuple-element.32.refs_0_.spots_ref), custom_call_target="tpu_custom_call" | custom-call | flops 2147483648 | bytes 2097152 | tf_op jit(solution)/shard_map/design/pallas_call | solution.py:405
  26.9 0.0 copy-start
  26.9 0.0 collective-permute-done.7.packets_ref.other_ref
  26.9 2.1 %design.3.refs_9_.refs_1_ = bf16[512,2048]{1,0:T(8,128)(2,1)S(1)} custom-call(bf16[8,16,256]{2,1,0:T(8,128)(2,1)S(1)} %collective-permute-done.7.packets_ref.other_ref, bf16[3,256,2048]{2,1,0:T(8,128)(2,1)S(1)} %get-tuple-element.35.chosen_ref, s32[1,2048]{1,0:T(1,128)S(1)} %get-tuple-element.32.refs_0_.spots_ref), custom_call_target="tpu_custom_call" | custom-call | flops 2147483648 | bytes 2097152 | tf_op jit(solution)/shard_map/design/pallas_call | solution.py:405
  29.0 0.0 copy-start.2
  29.0 0.0 copy-done
  29.1 1.6 %fit.1 = (f32[128,1024]{1,0:T(8,128)S(1)}, f32[8,256]{1,0:T(8,128)S(1)}) custom-call(s32[1]{0:T(128)} %bitcast.me_ref, s32[1,4096]{1,0:T(1,128)S(1)} %bitcast.8, bf16[8,16,256]{2,1,0:T(8,128)(2,1)S(1)} %collect.1.packets_ref.own_ref, bf16[8,16,256]{2,1,0:T(8,128)(2,1)S(1)} %collective-permute-done.7.packets_ref.other_ref, ...), custom_call_target="tpu_custom_call" | custom-call | flops 536870912 | bytes 4194304 | tf_op jit(solution)/shard_map/fit/pallas_call | solution.py:426
  30.7 0.6 %collective-permute-start.8 = (f32[128,1024]{1,0:T(8,128)S(1)}, f32[128,1024]{1,0:T(8,128)S(1)}, u32[]{:S(2)}, u32[]{:S(2)}) collective-permute-start(f32[128,1024]{1,0:T(8,128)S(1)} %get-tuple-element.37.refs_0_.own_ref), channel_id=1, source_target_pairs={{0,1},{1,0},{2,3},{3,2},{4,5},{5,4},{6,7},{7,6},{8,9},{9,8},{10,11... | collective-permute-start | bytes 1572872 | tf_op jit(solution)/shard_map/ppermute | solution.py:307
  31.2 0.0 copy-done.2
  31.2 2.4 %reorder.6.refs_2_ = bf16[512,1024]{1,0:T(8,128)(2,1)S(1)} custom-call(s32[1,512]{1,0:T(1,128)S(1)} %bitcast.10, bf16[2048,1024]{1,0:T(8,128)(2,1)S(1)} %copy-done.2, f32[128,1024]{1,0:T(8,128)S(1)} %get-tuple-element.37.refs_0_.own_ref), custom_call_target="tpu_custom_call" | custom-call | flops 2147483648 | bytes 4194304 | tf_op jit(solution)/shard_map/reorder/pallas_call | solution.py:354
  33.6 0.0 collective-permute-done.8.other_ref
  33.6 0.9 %sum.1 = (bf16[128,256]{1,0:T(8,128)(2,1)S(1)}, bf16[128,256]{1,0:T(8,128)(2,1)S(1)}, bf16[128,256]{1,0:T(8,128)(2,1)S(1)}, bf16[128,256]{1,0:T(8,128)(2,1)S(1)}...) custom-call(f32[128,1024]{1,0:T(8,128)S(1)} %get-tuple-element.37.re, ...), custom_call_target="tpu_custom_call" | custom-call | flops 536870912 | bytes 4194304 | tf_op jit(solution)/shard_map/sum/pallas_call | solution.py:440
  34.6 4.1 %collective-permute-start.9 = (bf16[128,256]{1,0:T(8,128)(2,1)S(1)}, bf16[128,256]{1,0:T(8,128)(2,1)S(1)}, u32[]{:S(2)}, u32[]{:S(2)}) collective-permute-start(bf16[128,256]{1,0:T(8,128)(2,1)S(1)} %get-tuple-element.39), channel_id=1, source_target_pairs={{0,8},{1,9},{2,10},{3,11},{4,12},{5,13},{6,14},{7,15},{8,0},{9,1},... | collective-permute-start | bytes 196616 | tf_op jit(solution)/shard_map/ppermute | solution.py:307
  38.7 0.1 collective-permute-start.10
  38.8 3.1 %collective-permute-start.11 = (bf16[128,256]{1,0:T(8,128)(2,1)S(1)}, bf16[128,256]{1,0:T(8,128)(2,1)S(1)}, u32[]{:S(2)}, u32[]{:S(2)}) collective-permute-start(bf16[128,256]{1,0:T(8,128)(2,1)S(1)} %get-tuple-element.41), channel_id=1, source_target_pairs={{0,12},{1,13},{2,14},{3,15},{4,8},{5,9},{6,10},{7,11},{8,4},{9,5},... | collective-permute-start | bytes 196616 | tf_op jit(solution)/shard_map/ppermute | solution.py:307
  41.9 1.6 %collective-permute-start.12 = (bf16[128,256]{1,0:T(8,128)(2,1)S(1)}, bf16[128,256]{1,0:T(8,128)(2,1)S(1)}, u32[]{:S(2)}, u32[]{:S(2)}) collective-permute-start(bf16[128,256]{1,0:T(8,128)(2,1)S(1)} %get-tuple-element.42), channel_id=1, source_target_pairs={{0,14},{1,15},{2,12},{3,13},{4,10},{5,11},{6,8},{7,9},{8,6},{9,7},... | collective-permute-start | bytes 196616 | tf_op jit(solution)/shard_map/ppermute | solution.py:307
  43.5 0.5 collective-permute-start.13
  44.0 1.6 %collective-permute-done.9.refs_5_ = bf16[128,256]{1,0:T(8,128)(2,1)S(1)} collective-permute-done((bf16[128,256]{1,0:T(8,128)(2,1)S(1)}, bf16[128,256]{1,0:T(8,128)(2,1)S(1)}, u32[]{:S(2)}, u32[]{:S(2)}) %collective-permute-start.9) | collective-permute-done | bytes 65568 | tf_op jit(solution)/shard_map/ppermute | solution.py:307
  45.6 0.0 collective-permute-start.14
  45.6 2.3 %collective-permute-done.10.refs_6_ = bf16[128,256]{1,0:T(8,128)(2,1)S(1)} collective-permute-done((bf16[128,256]{1,0:T(8,128)(2,1)S(1)}, bf16[128,256]{1,0:T(8,128)(2,1)S(1)}, u32[]{:S(2)}, u32[]{:S(2)}) %collective-permute-start.10) | collective-permute-done | bytes 65568 | tf_op jit(solution)/shard_map/ppermute | solution.py:307
  47.9 1.0 %collective-permute-start.15 = (bf16[128,256]{1,0:T(8,128)(2,1)S(1)}, bf16[128,256]{1,0:T(8,128)(2,1)S(1)}, u32[]{:S(2)}, u32[]{:S(2)}) collective-permute-start(bf16[128,256]{1,0:T(8,128)(2,1)S(1)} %get-tuple-element.45), channel_id=1, source_target_pairs={{0,6},{1,7},{2,4},{3,5},{4,2},{5,3},{6,0},{7,1},{8,14},{9,15},{10,... | collective-permute-start | bytes 196616 | tf_op jit(solution)/shard_map/ppermute | solution.py:307
  48.9 2.4 %reorder.7.refs_3_ = bf16[512,1024]{1,0:T(8,128)(2,1)S(1)} custom-call(s32[1,512]{1,0:T(1,128)S(1)} %bitcast.9, bf16[2048,1024]{1,0:T(8,128)(2,1)S(1)} %copy-done.2, bf16[128,256]{1,0:T(8,128)(2,1)S(1)} %get-tuple-element.38.refs_0_.refs_4_), custom_call_target="tpu_custom_call" | custom-call | flops 2147483648 | bytes 4194304 | tf_op jit(solution)/shard_map/reorder/pallas_call | solution.py:354
  51.3 0.0 collective-permute-done.11.refs_7_
  51.3 0.0 collective-permute-done.12.refs_8_
  51.3 0.0 collective-permute-done.13.refs_9_
  51.3 0.0 collective-permute-done.14.refs_10_
  51.3 1.7 %collective-permute-done.15.refs_11_ = bf16[128,256]{1,0:T(8,128)(2,1)S(1)} collective-permute-done((bf16[128,256]{1,0:T(8,128)(2,1)S(1)}, bf16[128,256]{1,0:T(8,128)(2,1)S(1)}, u32[]{:S(2)}, u32[]{:S(2)}) %collective-permute-start.15) | collective-permute-done | bytes 65568 | tf_op jit(solution)/shard_map/ppermute | solution.py:307
  53.1 2.6 %finish.1 = (f32[256,1024]{1,0:T(8,128)}, bf16[256,2048]{1,0:T(8,128)(2,1)}) custom-call(s32[1]{0:T(128)} %bitcast.me_ref, bf16[1024,256]{1,0:T(8,128)(2,1)S(1)} %get-tuple-element.24.turned_ref.corr_ref, f32[8,256]{1,0:T(8,128)S(1)} %get-tuple-element.36.scale_ref, bf16[512,1024]{1,0:T(8,128)(2,1)S(1)} %reorder.4.refs_1_.refs_0_, ...), custom_call_target="tpu_custom_call" | custom-call | tf_op jit(solution)/shard_map/finish/pallas_call | solution.py:453
  (2 shorter events, 0.0 us)
Async XLA Ops:
  2.0 17.3 %collective-permute-start = (bf16[144,256]{1,0:T(8,128)(2,1)S(1)}, bf16[144,256]{1,0:T(8,128)(2,1)S(1)}, u32[]{:S(2)}, u32[]{:S(2)}) collective-permute-start(bf16[144,256]{1,0:T(8,128)(2,1)S(1)} %get-tuple-element.26), channel_id=1, source_target_pairs={{0,8},{1,9},{2,10},{3,11},{4,12},{5,13},{6,14},{7,15},{8,0},{9,1},... | collective-permute-start | bytes 221192 | tf_op jit(solution)/shard_map/ppermute | solution.py:307
  6.1 13.3 %collective-permute-start.1 = (bf16[144,256]{1,0:T(8,128)(2,1)S(1)}, bf16[144,256]{1,0:T(8,128)(2,1)S(1)}, u32[]{:S(2)}, u32[]{:S(2)}) collective-permute-start(bf16[144,256]{1,0:T(8,128)(2,1)S(1)} %get-tuple-element.27), channel_id=1, source_target_pairs={{0,10},{1,11},{2,8},{3,9},{4,14},{5,15},{6,12},{7,13},{8,2},{9,3},... | collective-permute-start | bytes 221192 | tf_op jit(solution)/shard_map/ppermute | solution.py:307
  7.3 16.2 %collective-permute-start.2 = (bf16[144,256]{1,0:T(8,128)(2,1)S(1)}, bf16[144,256]{1,0:T(8,128)(2,1)S(1)}, u32[]{:S(2)}, u32[]{:S(2)}) collective-permute-start(bf16[144,256]{1,0:T(8,128)(2,1)S(1)} %get-tuple-element.28), channel_id=1, source_target_pairs={{0,12},{1,13},{2,14},{3,15},{4,8},{5,9},{6,10},{7,11},{8,4},{9,5},... | collective-permute-start | bytes 221192 | tf_op jit(solution)/shard_map/ppermute | solution.py:307
  10.9 12.6 %collective-permute-start.3 = (bf16[144,256]{1,0:T(8,128)(2,1)S(1)}, bf16[144,256]{1,0:T(8,128)(2,1)S(1)}, u32[]{:S(2)}, u32[]{:S(2)}) collective-permute-start(bf16[144,256]{1,0:T(8,128)(2,1)S(1)} %get-tuple-element.29), channel_id=1, source_target_pairs={{0,14},{1,15},{2,12},{3,13},{4,10},{5,11},{6,8},{7,9},{8,6},{9,7},... | collective-permute-start | bytes 221192 | tf_op jit(solution)/shard_map/ppermute | solution.py:307
  10.9 12.6 %collective-permute-start.4 = (bf16[144,256]{1,0:T(8,128)(2,1)S(1)}, bf16[144,256]{1,0:T(8,128)(2,1)S(1)}, u32[]{:S(2)}, u32[]{:S(2)}) collective-permute-start(bf16[144,256]{1,0:T(8,128)(2,1)S(1)} %get-tuple-element.30), channel_id=1, source_target_pairs={{0,2},{1,3},{2,0},{3,1},{4,6},{5,7},{6,4},{7,5},{8,10},{9,11},{10,... | collective-permute-start | bytes 221192 | tf_op jit(solution)/shard_map/ppermute | solution.py:307
  13.4 2.2 %copy-start.1 = (bf16[2048,1024]{1,0:T(8,128)(2,1)S(1)}, bf16[2048,1024]{1,0:T(8,128)(2,1)}, u32[]{:S(2)}) copy-start(bf16[2048,1024]{1,0:T(8,128)(2,1)} %slab_ref.7) | copy-start | bytes 12582916
  19.3 4.4 %collective-permute-start.5 = (bf16[144,256]{1,0:T(8,128)(2,1)S(1)}, bf16[144,256]{1,0:T(8,128)(2,1)S(1)}, u32[]{:S(2)}, u32[]{:S(2)}) collective-permute-start(bf16[144,256]{1,0:T(8,128)(2,1)S(1)} %get-tuple-element.33), channel_id=1, source_target_pairs={{0,4},{1,5},{2,6},{3,7},{4,0},{5,1},{6,2},{7,3},{8,12},{9,13},{10,... | collective-permute-start | bytes 221192 | tf_op jit(solution)/shard_map/ppermute | solution.py:307
  19.4 5.3 %collective-permute-start.6 = (bf16[144,256]{1,0:T(8,128)(2,1)S(1)}, bf16[144,256]{1,0:T(8,128)(2,1)S(1)}, u32[]{:S(2)}, u32[]{:S(2)}) collective-permute-start(bf16[144,256]{1,0:T(8,128)(2,1)S(1)} %get-tuple-element.34), channel_id=1, source_target_pairs={{0,6},{1,7},{2,4},{3,5},{4,2},{5,3},{6,0},{7,1},{8,14},{9,15},{10,... | collective-permute-start | bytes 221192 | tf_op jit(solution)/shard_map/ppermute | solution.py:307
  24.7 2.2 %collective-permute-start.7 = (bf16[8,16,256]{2,1,0:T(8,128)(2,1)S(1)}, bf16[8,16,256]{2,1,0:T(8,128)(2,1)S(1)}, u32[]{:S(2)}, u32[]{:S(2)}) collective-permute-start(bf16[8,16,256]{2,1,0:T(8,128)(2,1)S(1)} %collect.1.packets_ref.own_ref), channel_id=1, source_target_pairs={{0,1},{1,0},{2,3},{3,2},{4,5},{5,4},{6,7},{7,6},{8,9},{9,8},{10,11... | collective-permute-start | bytes 196616 | tf_op jit(solution)/shard_map/ppermute | solution.py:307
  26.9 2.2 %copy-start = (s32[4096]{0:T(1024)S(1)}, s32[4096]{0:T(1024)}, u32[]{:S(2)}) copy-start(s32[4096]{0:T(1024)} %param.8) | copy-start | bytes 49156
  29.0 2.2 %copy-start.2 = (bf16[2048,1024]{1,0:T(8,128)(2,1)S(1)}, bf16[2048,1024]{1,0:T(8,128)(2,1)}, u32[]{:S(2)}) copy-start(bf16[2048,1024]{1,0:T(8,128)(2,1)} %slab_ref.7) | copy-start | bytes 12582916
  30.7 2.9 %collective-permute-start.8 = (f32[128,1024]{1,0:T(8,128)S(1)}, f32[128,1024]{1,0:T(8,128)S(1)}, u32[]{:S(2)}, u32[]{:S(2)}) collective-permute-start(f32[128,1024]{1,0:T(8,128)S(1)} %get-tuple-element.37.refs_0_.own_ref), channel_id=1, source_target_pairs={{0,1},{1,0},{2,3},{3,2},{4,5},{5,4},{6,7},{7,6},{8,9},{9,8},{10,11... | collective-permute-start | bytes 1572872 | tf_op jit(solution)/shard_map/ppermute | solution.py:307
  34.6 11.0 %collective-permute-start.9 = (bf16[128,256]{1,0:T(8,128)(2,1)S(1)}, bf16[128,256]{1,0:T(8,128)(2,1)S(1)}, u32[]{:S(2)}, u32[]{:S(2)}) collective-permute-start(bf16[128,256]{1,0:T(8,128)(2,1)S(1)} %get-tuple-element.39), channel_id=1, source_target_pairs={{0,8},{1,9},{2,10},{3,11},{4,12},{5,13},{6,14},{7,15},{8,0},{9,1},... | collective-permute-start | bytes 196616 | tf_op jit(solution)/shard_map/ppermute | solution.py:307
  38.7 9.2 %collective-permute-start.10 = (bf16[128,256]{1,0:T(8,128)(2,1)S(1)}, bf16[128,256]{1,0:T(8,128)(2,1)S(1)}, u32[]{:S(2)}, u32[]{:S(2)}) collective-permute-start(bf16[128,256]{1,0:T(8,128)(2,1)S(1)} %get-tuple-element.40), channel_id=1, source_target_pairs={{0,10},{1,11},{2,8},{3,9},{4,14},{5,15},{6,12},{7,13},{8,2},{9,3},... | collective-permute-start | bytes 196616 | tf_op jit(solution)/shard_map/ppermute | solution.py:307
  38.8 12.5 %collective-permute-start.11 = (bf16[128,256]{1,0:T(8,128)(2,1)S(1)}, bf16[128,256]{1,0:T(8,128)(2,1)S(1)}, u32[]{:S(2)}, u32[]{:S(2)}) collective-permute-start(bf16[128,256]{1,0:T(8,128)(2,1)S(1)} %get-tuple-element.41), channel_id=1, source_target_pairs={{0,12},{1,13},{2,14},{3,15},{4,8},{5,9},{6,10},{7,11},{8,4},{9,5},... | collective-permute-start | bytes 196616 | tf_op jit(solution)/shard_map/ppermute | solution.py:307
  41.9 9.4 %collective-permute-start.12 = (bf16[128,256]{1,0:T(8,128)(2,1)S(1)}, bf16[128,256]{1,0:T(8,128)(2,1)S(1)}, u32[]{:S(2)}, u32[]{:S(2)}) collective-permute-start(bf16[128,256]{1,0:T(8,128)(2,1)S(1)} %get-tuple-element.42), channel_id=1, source_target_pairs={{0,14},{1,15},{2,12},{3,13},{4,10},{5,11},{6,8},{7,9},{8,6},{9,7},... | collective-permute-start | bytes 196616 | tf_op jit(solution)/shard_map/ppermute | solution.py:307
  43.5 7.8 %collective-permute-start.13 = (bf16[128,256]{1,0:T(8,128)(2,1)S(1)}, bf16[128,256]{1,0:T(8,128)(2,1)S(1)}, u32[]{:S(2)}, u32[]{:S(2)}) collective-permute-start(bf16[128,256]{1,0:T(8,128)(2,1)S(1)} %get-tuple-element.43), channel_id=1, source_target_pairs={{0,2},{1,3},{2,0},{3,1},{4,6},{5,7},{6,4},{7,5},{8,10},{9,11},{10,... | collective-permute-start | bytes 196616 | tf_op jit(solution)/shard_map/ppermute | solution.py:307
  45.6 5.7 %collective-permute-start.14 = (bf16[128,256]{1,0:T(8,128)(2,1)S(1)}, bf16[128,256]{1,0:T(8,128)(2,1)S(1)}, u32[]{:S(2)}, u32[]{:S(2)}) collective-permute-start(bf16[128,256]{1,0:T(8,128)(2,1)S(1)} %get-tuple-element.44), channel_id=1, source_target_pairs={{0,4},{1,5},{2,6},{3,7},{4,0},{5,1},{6,2},{7,3},{8,12},{9,13},{10,... | collective-permute-start | bytes 196616 | tf_op jit(solution)/shard_map/ppermute | solution.py:307
  47.9 5.2 %collective-permute-start.15 = (bf16[128,256]{1,0:T(8,128)(2,1)S(1)}, bf16[128,256]{1,0:T(8,128)(2,1)S(1)}, u32[]{:S(2)}, u32[]{:S(2)}) collective-permute-start(bf16[128,256]{1,0:T(8,128)(2,1)S(1)} %get-tuple-element.45), channel_id=1, source_target_pairs={{0,6},{1,7},{2,4},{3,5},{4,2},{5,3},{6,0},{7,1},{8,14},{9,15},{10,... | collective-permute-start | bytes 196616 | tf_op jit(solution)/shard_map/ppermute | solution.py:307

commit v12 on v11

--- a/solution.py
+++ b/solution.py
@@ -14,7 +14,7 @@
 DEGREES = 5
 LANES = 128
 CORES = 2
-FIRST_SLOTS = 6
+FIRST_SLOTS = 7
 ROOT_TWO = math.sqrt(2.0)
 ROOT_SIX = math.sqrt(6.0)
 ROOT_TWENTYFOUR = math.sqrt(24.0)
@@ -31,7 +31,7 @@
 
 
 def partner(slot, chips):
-    return slot and (slot + chips // 2 - 2) % (chips - 1) + 1
+    return slot and slot % (chips - 1) + 1
 
 
 def rows_of(index, count):

time: 56.1 us -> 55.5 us (0.989)
  waiting for transfers between devices: 6.78 us -> 5.35 us
  starting transfers between devices: 23.6 us -> 24.4 us
    ppermute x16, waiting for transfers between devices: 6.78 us -> 5.35 us  [to_device(): return lax.ppermute(array, 'runs', [(i, i ^ bits) for i in range(devices)])]
    ppermute x16, starting transfers between devices: 23.6 us -> 24.4 us  [to_device(): return lax.ppermute(array, 'runs', [(i, i ^ bits) for i in range(devices)])]
  transfers between devices with their start and end apart: 16 -> 16, of which waited for: 5 -> 3; matrix products, arithmetic and copies ran while one was open for 1% -> 1% of each run, Pallas kernels for 23% -> 23%
where the time goes in v12:
time: 55.5 us; the launch traced here: 55.2 us
  starting transfers between devices  24.4 us (44%)
  Pallas kernels  21.5 us (39%)
  waiting for transfers between devices  5.35 us (10%)
  local copies, waits for them, and re-layouts  2.97 us (5%)
  between operations  0.98 us (2%)
    ppermute x16, starting transfers between devices, to_device(): return lax.ppermute(array, 'runs', [(i, i ^ bits) for i in range(devices)])  24.4 us
    pallas_call x4, Pallas kernels, reorder(): pl.pallas_call(reorder_kernel, in_specs=[vmem, vmem] + [anywhere] * len(a...  9.43 us
    ppermute x16, waiting for transfers between devices, to_device(): return lax.ppermute(array, 'runs', [(i, i ^ bits) for i in range(devices)])  5.35 us
    pallas_call x2, Pallas kernels, design_of(): pl.pallas_call(functools.partial(design_kernel, dim, run_count), in_specs...  4.31 us
    pallas_call x1, Pallas kernels, split_by_modes(): pl.pallas_call(functools.partial(finish_kernel, len(ordered)), in_specs=[...  2.56 us
    unnamed x6, local copies, waits for them, and re-layouts  2.2 us
    pallas_call x1, Pallas kernels, split_by_modes(): pl.pallas_call(functools.partial(fit_kernel, 2 * rows), in_specs=[smem] +...  1.62 us
    pallas_call x1, Pallas kernels, split_by_modes(): pl.pallas_call(functools.partial(prepare_kernel, chips), in_specs=[smem,...  1.34 us
  transfers between devices with their start and end apart: 16, of which 3 were waited for; matrix products, arithmetic and copies ran while one was open for 1% of the time, Pallas kernels for 23%

profile of v12, /device:TPU:0, one launch (start us, length us, event | category | flops | bytes accessed | tf_op | source)
XLA Modules:
  0.0 55.2 jit_solution(3659647898592903266)
XLA Ops:
  0.6 1.3 %prepare.1 = (bf16[1024,256]{1,0:T(8,128)(2,1)S(1)}, bf16[16,256]{1,0:T(8,128)(2,1)S(1)}, bf16[144,256]{1,0:T(8,128)(2,1)S(1)}, bf16[144,256]{1,0:T(8,128)(2,1)S...) custom-call(s32[1]{0:T(128)} %bitcast.me_ref, ...), custom_call_target="tpu_custom_call" | custom-call | tf_op jit(solution)/shard_map/prepare/pallas_call | solution.py:338
  2.0 3.1 %collective-permute-start = (bf16[144,256]{1,0:T(8,128)(2,1)S(1)}, bf16[144,256]{1,0:T(8,128)(2,1)S(1)}, u32[]{:S(2)}, u32[]{:S(2)}) collective-permute-start(bf16[144,256]{1,0:T(8,128)(2,1)S(1)} %get-tuple-element.25), channel_id=1, source_target_pairs={{0,4},{1,5},{2,6},{3,7},{4,0},{5,1},{6,2},{7,3},{8,12},{9,13},{10,... | collective-permute-start | bytes 221192 | tf_op jit(solution)/shard_map/ppermute | solution.py:307
  5.1 1.4 %collective-permute-start.1 = (bf16[144,256]{1,0:T(8,128)(2,1)S(1)}, bf16[144,256]{1,0:T(8,128)(2,1)S(1)}, u32[]{:S(2)}, u32[]{:S(2)}) collective-permute-start(bf16[144,256]{1,0:T(8,128)(2,1)S(1)} %get-tuple-element.26), channel_id=1, source_target_pairs={{0,6},{1,7},{2,4},{3,5},{4,2},{5,3},{6,0},{7,1},{8,14},{9,15},{10,... | collective-permute-start | bytes 221192 | tf_op jit(solution)/shard_map/ppermute | solution.py:307
  6.4 2.6 %collective-permute-start.2 = (bf16[144,256]{1,0:T(8,128)(2,1)S(1)}, bf16[144,256]{1,0:T(8,128)(2,1)S(1)}, u32[]{:S(2)}, u32[]{:S(2)}) collective-permute-start(bf16[144,256]{1,0:T(8,128)(2,1)S(1)} %get-tuple-element.27), channel_id=1, source_target_pairs={{0,8},{1,9},{2,10},{3,11},{4,12},{5,13},{6,14},{7,15},{8,0},{9,1},... | collective-permute-start | bytes 221192 | tf_op jit(solution)/shard_map/ppermute | solution.py:307
  9.0 0.0 collective-permute-start.3
  9.0 3.9 %collective-permute-start.4 = (bf16[144,256]{1,0:T(8,128)(2,1)S(1)}, bf16[144,256]{1,0:T(8,128)(2,1)S(1)}, u32[]{:S(2)}, u32[]{:S(2)}) collective-permute-start(bf16[144,256]{1,0:T(8,128)(2,1)S(1)} %get-tuple-element.29), channel_id=1, source_target_pairs={{0,12},{1,13},{2,14},{3,15},{4,8},{5,9},{6,10},{7,11},{8,4},{9,5},... | collective-permute-start | bytes 221192 | tf_op jit(solution)/shard_map/ppermute | solution.py:307
  12.9 0.8 %fusion = (s32[512]{0:T(512)S(1)}, s32[512]{0:T(512)S(1)}, s32[512]{0:T(512)S(1)}, s32[512]{0:T(512)S(1)}) fusion(s32[2048]{0:T(1024)} %param.11), kind=kLoop, calls=%fused_computation | loop fusion | bytes 16384 | tf_op jit(solution)/shard_map/slice | solution.py:362
  13.7 0.0 copy-start.1
  13.7 2.2 %copy-done.1 = bf16[2048,1024]{1,0:T(8,128)(2,1)S(1)} copy-done((bf16[2048,1024]{1,0:T(8,128)(2,1)S(1)}, bf16[2048,1024]{1,0:T(8,128)(2,1)}, u32[]{:S(2)}) %copy-start.1) | copy-done | bytes 4194328
  15.9 2.4 %reorder.4.refs_1_.refs_0_ = bf16[512,1024]{1,0:T(8,128)(2,1)S(1)} custom-call(s32[1,512]{1,0:T(1,128)S(1)} %bitcast.12, bf16[2048,1024]{1,0:T(8,128)(2,1)S(1)} %copy-done.1), custom_call_target="tpu_custom_call" | custom-call | flops 2147483648 | bytes 4194304 | tf_op jit(solution)/shard_map/reorder/pallas_call | solution.py:354
  18.3 1.3 %choose.1 = (bf16[3,256,2048]{2,1,0:T(8,128)(2,1)S(1)}, s32[1,2048]{1,0:T(1,128)S(1)}) custom-call(s32[1]{0:T(128)} %bitcast.me_ref, s32[4,4096]{1,0:T(4,128)} %bitcast.13), custom_call_target="tpu_custom_call" | custom-call | bytes 2097152 | tf_op jit(solution)/shard_map/choose/pallas_call | solution.py:369
  19.6 0.0 collective-permute-done.refs_0_.refs_1_
  19.6 1.2 %collective-permute-start.5 = (bf16[144,256]{1,0:T(8,128)(2,1)S(1)}, bf16[144,256]{1,0:T(8,128)(2,1)S(1)}, u32[]{:S(2)}, u32[]{:S(2)}) collective-permute-start(bf16[144,256]{1,0:T(8,128)(2,1)S(1)} %get-tuple-element.30), channel_id=1, source_target_pairs={{0,14},{1,15},{2,12},{3,13},{4,10},{5,11},{6,8},{7,9},{8,6},{9,7},... | collective-permute-start | bytes 221192 | tf_op jit(solution)/shard_map/ppermute | solution.py:307
  20.8 0.0 collective-permute-done.1.refs_1_.refs_2_
  20.8 0.4 collective-permute-start.6
  21.2 2.4 %reorder.5.refs_8_.refs_1_ = bf16[512,1024]{1,0:T(8,128)(2,1)S(1)} custom-call(s32[1,512]{1,0:T(1,128)S(1)} %bitcast.11, bf16[2048,1024]{1,0:T(8,128)(2,1)S(1)} %copy-done.1, bf16[144,256]{1,0:T(8,128)(2,1)S(1)} %collective-permute-done.refs_0_.refs_1_, bf16[144,256]{1,0:T(8,128)(2,1)S(1)} %collective-permute-done.1.refs_1_.refs_2_), custom_call_target="tpu_custom_call" | custom-call | flops 2147483648 | bytes 4194304 | tf_op jit(solution)/shard_map/reorder/pallas_call | solution.py:354
  23.6 0.0 collective-permute-done.2.refs_3_
  23.6 0.0 collective-permute-done.3.refs_4_
  23.6 0.0 collective-permute-done.4.refs_5_
  23.6 3.1 %collective-permute-done.5.refs_6_ = bf16[144,256]{1,0:T(8,128)(2,1)S(1)} collective-permute-done((bf16[144,256]{1,0:T(8,128)(2,1)S(1)}, bf16[144,256]{1,0:T(8,128)(2,1)S(1)}, u32[]{:S(2)}, u32[]{:S(2)}) %collective-permute-start.5) | collective-permute-done | bytes 73760 | tf_op jit(solution)/shard_map/ppermute | solution.py:307
  26.7 0.0 collective-permute-done.6.refs_7_
  26.7 0.1 collective-permute-start.7
  26.8 2.2 %design.2.refs_8_.refs_0_ = bf16[512,2048]{1,0:T(8,128)(2,1)S(1)} custom-call(bf16[8,16,256]{2,1,0:T(8,128)(2,1)S(1)} %collect.1.packets_ref.own_ref, bf16[3,256,2048]{2,1,0:T(8,128)(2,1)S(1)} %get-tuple-element.33.chosen_ref, s32[1,2048]{1,0:T(1,128)S(1)} %get-tuple-element.32.refs_0_.spots_ref), custom_call_target="tpu_custom_call" | custom-call | flops 2147483648 | bytes 2097152 | tf_op jit(solution)/shard_map/design/pallas_call | solution.py:405
  29.0 0.0 copy-start
  29.0 0.0 collective-permute-done.7.packets_ref.other_ref
  29.0 2.2 %design.3.refs_9_.refs_1_ = bf16[512,2048]{1,0:T(8,128)(2,1)S(1)} custom-call(bf16[8,16,256]{2,1,0:T(8,128)(2,1)S(1)} %collective-permute-done.7.packets_ref.other_ref, bf16[3,256,2048]{2,1,0:T(8,128)(2,1)S(1)} %get-tuple-element.33.chosen_ref, s32[1,2048]{1,0:T(1,128)S(1)} %get-tuple-element.32.refs_0_.spots_ref), custom_call_target="tpu_custom_call" | custom-call | flops 2147483648 | bytes 2097152 | tf_op jit(solution)/shard_map/design/pallas_call | solution.py:405
  31.2 0.0 copy-start.2
  31.2 0.0 copy-done
  31.2 1.6 %fit.1 = (f32[128,1024]{1,0:T(8,128)S(1)}, f32[8,256]{1,0:T(8,128)S(1)}) custom-call(s32[1]{0:T(128)} %bitcast.me_ref, s32[1,4096]{1,0:T(1,128)S(1)} %bitcast.8, bf16[8,16,256]{2,1,0:T(8,128)(2,1)S(1)} %collect.1.packets_ref.own_ref, bf16[8,16,256]{2,1,0:T(8,128)(2,1)S(1)} %collective-permute-done.7.packets_ref.other_ref, ...), custom_call_target="tpu_custom_call" | custom-call | flops 536870912 | bytes 4194304 | tf_op jit(solution)/shard_map/fit/pallas_call | solution.py:426
  32.8 0.6 %collective-permute-start.8 = (f32[128,1024]{1,0:T(8,128)S(1)}, f32[128,1024]{1,0:T(8,128)S(1)}, u32[]{:S(2)}, u32[]{:S(2)}) collective-permute-start(f32[128,1024]{1,0:T(8,128)S(1)} %get-tuple-element.35.refs_0_.own_ref), channel_id=1, source_target_pairs={{0,1},{1,0},{2,3},{3,2},{4,5},{5,4},{6,7},{7,6},{8,9},{9,8},{10,11... | collective-permute-start | bytes 1572872 | tf_op jit(solution)/shard_map/ppermute | solution.py:307
  33.4 0.0 copy-done.2
  33.4 2.4 %reorder.6.refs_2_ = bf16[512,1024]{1,0:T(8,128)(2,1)S(1)} custom-call(s32[1,512]{1,0:T(1,128)S(1)} %bitcast.10, bf16[2048,1024]{1,0:T(8,128)(2,1)S(1)} %copy-done.2, f32[128,1024]{1,0:T(8,128)S(1)} %get-tuple-element.35.refs_0_.own_ref), custom_call_target="tpu_custom_call" | custom-call | flops 2147483648 | bytes 4194304 | tf_op jit(solution)/shard_map/reorder/pallas_call | solution.py:354
  35.7 0.0 collective-permute-done.8.other_ref
  35.7 0.9 %sum.1 = (bf16[128,256]{1,0:T(8,128)(2,1)S(1)}, bf16[128,256]{1,0:T(8,128)(2,1)S(1)}, bf16[128,256]{1,0:T(8,128)(2,1)S(1)}, bf16[128,256]{1,0:T(8,128)(2,1)S(1)}...) custom-call(f32[128,1024]{1,0:T(8,128)S(1)} %get-tuple-element.35.re, ...), custom_call_target="tpu_custom_call" | custom-call | flops 536870912 | bytes 4194304 | tf_op jit(solution)/shard_map/sum/pallas_call | solution.py:440
  36.7 0.1 collective-permute-start.9
  36.8 2.9 %collective-permute-start.10 = (bf16[128,256]{1,0:T(8,128)(2,1)S(1)}, bf16[128,256]{1,0:T(8,128)(2,1)S(1)}, u32[]{:S(2)}, u32[]{:S(2)}) collective-permute-start(bf16[128,256]{1,0:T(8,128)(2,1)S(1)} %get-tuple-element.38), channel_id=1, source_target_pairs={{0,6},{1,7},{2,4},{3,5},{4,2},{5,3},{6,0},{7,1},{8,14},{9,15},{10,... | collective-permute-start | bytes 196616 | tf_op jit(solution)/shard_map/ppermute | solution.py:307
  39.7 0.0 collective-permute-start.11
  39.7 2.9 %collective-permute-start.12 = (bf16[128,256]{1,0:T(8,128)(2,1)S(1)}, bf16[128,256]{1,0:T(8,128)(2,1)S(1)}, u32[]{:S(2)}, u32[]{:S(2)}) collective-permute-start(bf16[128,256]{1,0:T(8,128)(2,1)S(1)} %get-tuple-element.40), channel_id=1, source_target_pairs={{0,10},{1,11},{2,8},{3,9},{4,14},{5,15},{6,12},{7,13},{8,2},{9,3},... | collective-permute-start | bytes 196616 | tf_op jit(solution)/shard_map/ppermute | solution.py:307
  42.6 2.0 %collective-permute-start.13 = (bf16[128,256]{1,0:T(8,128)(2,1)S(1)}, bf16[128,256]{1,0:T(8,128)(2,1)S(1)}, u32[]{:S(2)}, u32[]{:S(2)}) collective-permute-start(bf16[128,256]{1,0:T(8,128)(2,1)S(1)} %get-tuple-element.41), channel_id=1, source_target_pairs={{0,12},{1,13},{2,14},{3,15},{4,8},{5,9},{6,10},{7,11},{8,4},{9,5},... | collective-permute-start | bytes 196616 | tf_op jit(solution)/shard_map/ppermute | solution.py:307
  44.6 0.0 collective-permute-done.9.refs_5_
  44.6 2.8 %collective-permute-start.14 = (bf16[128,256]{1,0:T(8,128)(2,1)S(1)}, bf16[128,256]{1,0:T(8,128)(2,1)S(1)}, u32[]{:S(2)}, u32[]{:S(2)}) collective-permute-start(bf16[128,256]{1,0:T(8,128)(2,1)S(1)} %get-tuple-element.42), channel_id=1, source_target_pairs={{0,14},{1,15},{2,12},{3,13},{4,10},{5,11},{6,8},{7,9},{8,6},{9,7},... | collective-permute-start | bytes 196616 | tf_op jit(solution)/shard_map/ppermute | solution.py:307
  47.3 0.0 collective-permute-done.10.refs_6_
  47.3 0.5 collective-permute-start.15
  47.9 2.4 %reorder.7.refs_3_ = bf16[512,1024]{1,0:T(8,128)(2,1)S(1)} custom-call(s32[1,512]{1,0:T(1,128)S(1)} %bitcast.9, bf16[2048,1024]{1,0:T(8,128)(2,1)S(1)} %copy-done.2, bf16[128,256]{1,0:T(8,128)(2,1)S(1)} %get-tuple-element.36.refs_0_.refs_4_), custom_call_target="tpu_custom_call" | custom-call | flops 2147483648 | bytes 4194304 | tf_op jit(solution)/shard_map/reorder/pallas_call | solution.py:354
  50.3 0.0 collective-permute-done.11.refs_7_
  50.3 1.8 %collective-permute-done.12.refs_8_ = bf16[128,256]{1,0:T(8,128)(2,1)S(1)} collective-permute-done((bf16[128,256]{1,0:T(8,128)(2,1)S(1)}, bf16[128,256]{1,0:T(8,128)(2,1)S(1)}, u32[]{:S(2)}, u32[]{:S(2)}) %collective-permute-start.12) | collective-permute-done | bytes 65568 | tf_op jit(solution)/shard_map/ppermute | solution.py:307
  52.0 0.0 collective-permute-done.13.refs_9_
  52.0 0.0 collective-permute-done.14.refs_10_
  52.0 0.5 collective-permute-done.15.refs_11_
  52.5 2.6 %finish.1 = (f32[256,1024]{1,0:T(8,128)}, bf16[256,2048]{1,0:T(8,128)(2,1)}) custom-call(s32[1]{0:T(128)} %bitcast.me_ref, bf16[1024,256]{1,0:T(8,128)(2,1)S(1)} %get-tuple-element.23.turned_ref.corr_ref, f32[8,256]{1,0:T(8,128)S(1)} %get-tuple-element.34.scale_ref, bf16[512,1024]{1,0:T(8,128)(2,1)S(1)} %reorder.4.refs_1_.refs_0_, ...), custom_call_target="tpu_custom_call" | custom-call | tf_op jit(solution)/shard_map/finish/pallas_call | solution.py:453
  (2 shorter events, 0.0 us)
Async XLA Ops:
  2.0 17.6 %collective-permute-start = (bf16[144,256]{1,0:T(8,128)(2,1)S(1)}, bf16[144,256]{1,0:T(8,128)(2,1)S(1)}, u32[]{:S(2)}, u32[]{:S(2)}) collective-permute-start(bf16[144,256]{1,0:T(8,128)(2,1)S(1)} %get-tuple-element.25), channel_id=1, source_target_pairs={{0,4},{1,5},{2,6},{3,7},{4,0},{5,1},{6,2},{7,3},{8,12},{9,13},{10,... | collective-permute-start | bytes 221192 | tf_op jit(solution)/shard_map/ppermute | solution.py:307
  5.1 15.7 %collective-permute-start.1 = (bf16[144,256]{1,0:T(8,128)(2,1)S(1)}, bf16[144,256]{1,0:T(8,128)(2,1)S(1)}, u32[]{:S(2)}, u32[]{:S(2)}) collective-permute-start(bf16[144,256]{1,0:T(8,128)(2,1)S(1)} %get-tuple-element.26), channel_id=1, source_target_pairs={{0,6},{1,7},{2,4},{3,5},{4,2},{5,3},{6,0},{7,1},{8,14},{9,15},{10,... | collective-permute-start | bytes 221192 | tf_op jit(solution)/shard_map/ppermute | solution.py:307
  6.4 17.2 %collective-permute-start.2 = (bf16[144,256]{1,0:T(8,128)(2,1)S(1)}, bf16[144,256]{1,0:T(8,128)(2,1)S(1)}, u32[]{:S(2)}, u32[]{:S(2)}) collective-permute-start(bf16[144,256]{1,0:T(8,128)(2,1)S(1)} %get-tuple-element.27), channel_id=1, source_target_pairs={{0,8},{1,9},{2,10},{3,11},{4,12},{5,13},{6,14},{7,15},{8,0},{9,1},... | collective-permute-start | bytes 221192 | tf_op jit(solution)/shard_map/ppermute | solution.py:307
  9.0 14.6 %collective-permute-start.3 = (bf16[144,256]{1,0:T(8,128)(2,1)S(1)}, bf16[144,256]{1,0:T(8,128)(2,1)S(1)}, u32[]{:S(2)}, u32[]{:S(2)}) collective-permute-start(bf16[144,256]{1,0:T(8,128)(2,1)S(1)} %get-tuple-element.28), channel_id=1, source_target_pairs={{0,10},{1,11},{2,8},{3,9},{4,14},{5,15},{6,12},{7,13},{8,2},{9,3},... | collective-permute-start | bytes 221192 | tf_op jit(solution)/shard_map/ppermute | solution.py:307
  9.0 14.6 %collective-permute-start.4 = (bf16[144,256]{1,0:T(8,128)(2,1)S(1)}, bf16[144,256]{1,0:T(8,128)(2,1)S(1)}, u32[]{:S(2)}, u32[]{:S(2)}) collective-permute-start(bf16[144,256]{1,0:T(8,128)(2,1)S(1)} %get-tuple-element.29), channel_id=1, source_target_pairs={{0,12},{1,13},{2,14},{3,15},{4,8},{5,9},{6,10},{7,11},{8,4},{9,5},... | collective-permute-start | bytes 221192 | tf_op jit(solution)/shard_map/ppermute | solution.py:307
  13.7 2.2 %copy-start.1 = (bf16[2048,1024]{1,0:T(8,128)(2,1)S(1)}, bf16[2048,1024]{1,0:T(8,128)(2,1)}, u32[]{:S(2)}) copy-start(bf16[2048,1024]{1,0:T(8,128)(2,1)} %slab_ref.7) | copy-start | bytes 12582916
  19.6 7.1 %collective-permute-start.5 = (bf16[144,256]{1,0:T(8,128)(2,1)S(1)}, bf16[144,256]{1,0:T(8,128)(2,1)S(1)}, u32[]{:S(2)}, u32[]{:S(2)}) collective-permute-start(bf16[144,256]{1,0:T(8,128)(2,1)S(1)} %get-tuple-element.30), channel_id=1, source_target_pairs={{0,14},{1,15},{2,12},{3,13},{4,10},{5,11},{6,8},{7,9},{8,6},{9,7},... | collective-permute-start | bytes 221192 | tf_op jit(solution)/shard_map/ppermute | solution.py:307
  20.8 5.9 %collective-permute-start.6 = (bf16[144,256]{1,0:T(8,128)(2,1)S(1)}, bf16[144,256]{1,0:T(8,128)(2,1)S(1)}, u32[]{:S(2)}, u32[]{:S(2)}) collective-permute-start(bf16[144,256]{1,0:T(8,128)(2,1)S(1)} %late.1), channel_id=1, source_target_pairs={{0,2},{1,3},{2,0},{3,1},{4,6},{5,7},{6,4},{7,5},{8,10},{9,11},{10,... | collective-permute-start | bytes 221192 | tf_op jit(solution)/shard_map/ppermute | solution.py:307
  26.7 2.3 %collective-permute-start.7 = (bf16[8,16,256]{2,1,0:T(8,128)(2,1)S(1)}, bf16[8,16,256]{2,1,0:T(8,128)(2,1)S(1)}, u32[]{:S(2)}, u32[]{:S(2)}) collective-permute-start(bf16[8,16,256]{2,1,0:T(8,128)(2,1)S(1)} %collect.1.packets_ref.own_ref), channel_id=1, source_target_pairs={{0,1},{1,0},{2,3},{3,2},{4,5},{5,4},{6,7},{7,6},{8,9},{9,8},{10,11... | collective-permute-start | bytes 196616 | tf_op jit(solution)/shard_map/ppermute | solution.py:307
  29.0 2.2 %copy-start = (s32[4096]{0:T(1024)S(1)}, s32[4096]{0:T(1024)}, u32[]{:S(2)}) copy-start(s32[4096]{0:T(1024)} %param.8) | copy-start | bytes 49156
  31.2 2.2 %copy-start.2 = (bf16[2048,1024]{1,0:T(8,128)(2,1)S(1)}, bf16[2048,1024]{1,0:T(8,128)(2,1)}, u32[]{:S(2)}) copy-start(bf16[2048,1024]{1,0:T(8,128)(2,1)} %slab_ref.7) | copy-start | bytes 12582916
  32.8 2.9 %collective-permute-start.8 = (f32[128,1024]{1,0:T(8,128)S(1)}, f32[128,1024]{1,0:T(8,128)S(1)}, u32[]{:S(2)}, u32[]{:S(2)}) collective-permute-start(f32[128,1024]{1,0:T(8,128)S(1)} %get-tuple-element.35.refs_0_.own_ref), channel_id=1, source_target_pairs={{0,1},{1,0},{2,3},{3,2},{4,5},{5,4},{6,7},{7,6},{8,9},{9,8},{10,11... | collective-permute-start | bytes 1572872 | tf_op jit(solution)/shard_map/ppermute | solution.py:307
  36.7 7.9 %collective-permute-start.9 = (bf16[128,256]{1,0:T(8,128)(2,1)S(1)}, bf16[128,256]{1,0:T(8,128)(2,1)S(1)}, u32[]{:S(2)}, u32[]{:S(2)}) collective-permute-start(bf16[128,256]{1,0:T(8,128)(2,1)S(1)} %get-tuple-element.37), channel_id=1, source_target_pairs={{0,4},{1,5},{2,6},{3,7},{4,0},{5,1},{6,2},{7,3},{8,12},{9,13},{10,... | collective-permute-start | bytes 196616 | tf_op jit(solution)/shard_map/ppermute | solution.py:307
  36.8 10.6 %collective-permute-start.10 = (bf16[128,256]{1,0:T(8,128)(2,1)S(1)}, bf16[128,256]{1,0:T(8,128)(2,1)S(1)}, u32[]{:S(2)}, u32[]{:S(2)}) collective-permute-start(bf16[128,256]{1,0:T(8,128)(2,1)S(1)} %get-tuple-element.38), channel_id=1, source_target_pairs={{0,6},{1,7},{2,4},{3,5},{4,2},{5,3},{6,0},{7,1},{8,14},{9,15},{10,... | collective-permute-start | bytes 196616 | tf_op jit(solution)/shard_map/ppermute | solution.py:307
  39.7 10.6 %collective-permute-start.11 = (bf16[128,256]{1,0:T(8,128)(2,1)S(1)}, bf16[128,256]{1,0:T(8,128)(2,1)S(1)}, u32[]{:S(2)}, u32[]{:S(2)}) collective-permute-start(bf16[128,256]{1,0:T(8,128)(2,1)S(1)} %get-tuple-element.39), channel_id=1, source_target_pairs={{0,8},{1,9},{2,10},{3,11},{4,12},{5,13},{6,14},{7,15},{8,0},{9,1},... | collective-permute-start | bytes 196616 | tf_op jit(solution)/shard_map/ppermute | solution.py:307
  39.7 12.3 %collective-permute-start.12 = (bf16[128,256]{1,0:T(8,128)(2,1)S(1)}, bf16[128,256]{1,0:T(8,128)(2,1)S(1)}, u32[]{:S(2)}, u32[]{:S(2)}) collective-permute-start(bf16[128,256]{1,0:T(8,128)(2,1)S(1)} %get-tuple-element.40), channel_id=1, source_target_pairs={{0,10},{1,11},{2,8},{3,9},{4,14},{5,15},{6,12},{7,13},{8,2},{9,3},... | collective-permute-start | bytes 196616 | tf_op jit(solution)/shard_map/ppermute | solution.py:307
  42.6 9.4 %collective-permute-start.13 = (bf16[128,256]{1,0:T(8,128)(2,1)S(1)}, bf16[128,256]{1,0:T(8,128)(2,1)S(1)}, u32[]{:S(2)}, u32[]{:S(2)}) collective-permute-start(bf16[128,256]{1,0:T(8,128)(2,1)S(1)} %get-tuple-element.41), channel_id=1, source_target_pairs={{0,12},{1,13},{2,14},{3,15},{4,8},{5,9},{6,10},{7,11},{8,4},{9,5},... | collective-permute-start | bytes 196616 | tf_op jit(solution)/shard_map/ppermute | solution.py:307
  44.6 7.5 %collective-permute-start.14 = (bf16[128,256]{1,0:T(8,128)(2,1)S(1)}, bf16[128,256]{1,0:T(8,128)(2,1)S(1)}, u32[]{:S(2)}, u32[]{:S(2)}) collective-permute-start(bf16[128,256]{1,0:T(8,128)(2,1)S(1)} %get-tuple-element.42), channel_id=1, source_target_pairs={{0,14},{1,15},{2,12},{3,13},{4,10},{5,11},{6,8},{7,9},{8,6},{9,7},... | collective-permute-start | bytes 196616 | tf_op jit(solution)/shard_map/ppermute | solution.py:307
  47.3 5.2 %collective-permute-start.15 = (bf16[128,256]{1,0:T(8,128)(2,1)S(1)}, bf16[128,256]{1,0:T(8,128)(2,1)S(1)}, u32[]{:S(2)}, u32[]{:S(2)}) collective-permute-start(bf16[128,256]{1,0:T(8,128)(2,1)S(1)} %get-tuple-element.43), channel_id=1, source_target_pairs={{0,2},{1,3},{2,0},{3,1},{4,6},{5,7},{6,4},{7,5},{8,10},{9,11},{10,... | collective-permute-start | bytes 196616 | tf_op jit(solution)/shard_map/ppermute | solution.py:307

commit v13 on v12

--- a/solution.py
+++ b/solution.py
@@ -14,7 +14,6 @@
 DEGREES = 5
 LANES = 128
 CORES = 2
-FIRST_SLOTS = 7
 ROOT_TWO = math.sqrt(2.0)
 ROOT_SIX = math.sqrt(6.0)
 ROOT_TWENTYFOUR = math.sqrt(24.0)
@@ -53,12 +52,51 @@
     if packet_rows > used:
         pieces.append(jnp.zeros((packet_rows - used, terms), jnp.float32))
     packet_ref[...] = jnp.concatenate(pieces, axis=0).astype(jnp.bfloat16)
-    fill_blocks(chips, 0, me_ref, turned_ref, packet_ref, sent_refs)
-
-
-def fill_blocks(chips, first, me_ref, turned_ref, packet_ref, sent_refs):
+    fill_blocks(chips, me_ref, turned_ref, packet_ref, sent_refs)
+
+
+def fill_blocks(chips, me_ref, turned_ref, packet_ref, sent_refs):
     count = turned_ref.shape[0] // chips
-    for k, sent_ref in enumerate(sent_refs, first):
+    for k, sent_ref in enumerate(sent_refs):
+        chip = (me_ref[0] // CORES) ^ partner(k, chips)
+        sent_ref[0:count, :] = turned_ref[rows_of(chip, count), :]
+        sent_ref[count : sent_ref.shape[0], :] = packet_ref[...]
+
+
+def split_in_two(values):
+    high = values.astype(jnp.bfloat16).astype(jnp.float32)
+    return [high, values - high]
+
+
+def partner(slot, chips):
+    return slot and slot % (chips - 1) + 1
+
+
+def rows_of(index, count):
+    return pl.ds(pl.multiple_of(index * count, count), count)
+
+
+def prepare_kernel(chips, me_ref, corr_ref, points_ref, turned_ref, packet_ref, *sent_refs):
+    turned = corr_ref[...].astype(jnp.float32).T
+    turned_ref[...] = turned.astype(jnp.bfloat16)
+    squares = jnp.sum(turned * turned, axis=0, keepdims=True)
+    packet_rows, terms = packet_ref.shape
+    dim, runs = points_ref.shape
+    rows = dim * runs // terms
+    points = jnp.concatenate(
+        [points_ref[start : start + rows, :] for start in range(0, dim, rows)], axis=1
+    )
+    pieces = split_in_two(points) + split_in_two(squares)
+    used = 2 * rows + 2
+    if packet_rows > used:
+        pieces.append(jnp.zeros((packet_rows - used, terms), jnp.float32))
+    packet_ref[...] = jnp.concatenate(pieces, axis=0).astype(jnp.bfloat16)
+    fill_blocks(chips, me_ref, turned_ref, packet_ref, sent_refs)
+
+
+def fill_blocks(chips, me_ref, turned_ref, packet_ref, sent_refs):
+    count = turned_ref.shape[0] // chips
+    for k, sent_ref in enumerate(sent_refs):
         chip = (me_ref[0] // CORES) ^ partner(k, chips)
         sent_ref[0:count, :] = turned_ref[rows_of(chip, count), :]
         sent_ref[count : sent_ref.shape[0], :] = packet_ref[...]
@@ -333,17 +371,16 @@
     vmem = pl.BlockSpec(memory_space=pltpu.VMEM)
     anywhere = pl.BlockSpec(memory_space=pl.ANY)
 
-    early = min(chips, FIRST_SLOTS)
     block_type = jax.ShapeDtypeStruct((own_modes + packet_rows, term_count), jnp.bfloat16)
     turned, packet, *sent = pl.pallas_call(
         functools.partial(prepare_kernel, chips),
         in_specs=[smem, vmem, vmem],
-        out_specs=[vmem] * (2 + early),
+        out_specs=[vmem] * (2 + chips),
         out_shape=[
             jax.ShapeDtypeStruct((modes, term_count), jnp.bfloat16),
             jax.ShapeDtypeStruct((packet_rows, term_count), jnp.bfloat16),
         ]
-        + [block_type] * early,
+        + [block_type] * chips,
         compiler_params=params(16),
         name="prepare",
     )(me, in_hbm(correlations), in_hbm(run_inputs.T))
@@ -363,12 +400,12 @@
 
     starts = range(0, slab_cells, block)
     quarters = [starts[i * len(starts) // 4 : (i + 1) * len(starts) // 4] for i in range(4)]
-    ordered = [reorder(start) for start in quarters[0]]
+    blocks = to_chips(sent)
     half = round_up(DEGREES * dim, LANES)
     gathers = slots // 4
     chosen, spots = pl.pallas_call(
         functools.partial(choose_kernel, dim, chips),
-        in_specs=[smem, vmem],
+        in_specs=[smem, vmem] + [anywhere] * len(blocks[1:3]),
         out_specs=[vmem, vmem],
         out_shape=[
             jax.ShapeDtypeStruct((slots - gathers, 2 * half, core_terms), jnp.bfloat16),
@@ -377,26 +414,18 @@
         compiler_params=params(8),
         cost_estimate=cost(0, 2 * slots * half * core_terms),
         name="choose",
-    )(me, in_hbm(term_codes.T))
-    if chips > early:
-        sent += pl.pallas_call(
-            functools.partial(late_kernel, chips),
-            in_specs=[smem, vmem, vmem] + [anywhere] * (1 + len(ordered)),
-            out_specs=[vmem] * (chips - early),
-            out_shape=[block_type] * (chips - early),
-            compiler_params=params(8),
-            name="late",
-        )(me, turned, packet, spots, *ordered)
-    blocks = to_chips(sent)
-    tail = [reorder(start, *blocks[1:3]) for start in quarters[1]]
+    )(me, in_hbm(term_codes.T), *blocks[1:3])
+    ordered = [
+        reorder(start, *blocks[1:3]) for start in [*quarters[0], *quarters[1]]
+    ]
     packets = pl.pallas_call(
         functools.partial(collect_kernel, chips),
-        in_specs=[vmem] * chips + [anywhere] * len(tail),
+        in_specs=[vmem] * chips + [anywhere] * (1 + len(ordered)),
         out_specs=vmem,
         out_shape=jax.ShapeDtypeStruct((chips, packet_rows, term_count), jnp.bfloat16),
         compiler_params=params(8),
         name="collect",
-    )(*blocks, *tail)
+    )(*blocks, spots, *ordered)
     others = to_device(packets, 1)
 
     core_runs = run_count * chips
@@ -447,7 +476,7 @@
         name="sum",
     )(fitted, to_device(fitted, 1), *designs, *beside)
     returned = to_chips(summed)
-    ordered += tail + beside
+    ordered += beside
     ordered += [reorder(start, summed[0]) for start in quarters[3]]
 
     return pl.pallas_call(

time: 55.5 us -> 53.8 us (0.969)
  waiting for transfers between devices: 5.35 us -> 3.14 us
  Pallas kernels: 21.5 us -> 22.1 us
    ppermute x16, waiting for transfers between devices: 5.35 us -> 3.14 us  [to_device(): return lax.ppermute(array, 'runs', [(i, i ^ bits) for i in range(devices)])]
    pallas_call x1, Pallas kernels: 1.34 us -> 1.95 us  [split_by_modes(): pl.pallas_call(functools.partial(prepare_kernel, chips), in_specs=[smem,...]
  transfers between devices with their start and end apart: 16 -> 16, of which waited for: 3 -> 2; matrix products, arithmetic and copies ran while one was open for 1% -> 1% of each run, Pallas kernels for 23% -> 24%
where the time goes in v13:
time: 53.8 us; the launch traced here: 53.5 us
  starting transfers between devices  24.3 us (45%)
  Pallas kernels  22.1 us (41%)
  waiting for transfers between devices  3.14 us (6%)
  local copies, waits for them, and re-layouts  2.97 us (6%)
  between operations  0.98 us (2%)
    ppermute x16, starting transfers between devices, to_device(): return lax.ppermute(array, 'runs', [(i, i ^ bits) for i in range(devices)])  24.3 us
    pallas_call x4, Pallas kernels, reorder(): pl.pallas_call(reorder_kernel, in_specs=[vmem, vmem] + [anywhere] * len(a...  9.43 us
    pallas_call x2, Pallas kernels, design_of(): pl.pallas_call(functools.partial(design_kernel, dim, run_count), in_specs...  4.32 us
    ppermute x16, waiting for transfers between devices, to_device(): return lax.ppermute(array, 'runs', [(i, i ^ bits) for i in range(devices)])  3.14 us
    pallas_call x1, Pallas kernels, split_by_modes(): pl.pallas_call(functools.partial(finish_kernel, len(ordered)), in_specs=[...  2.57 us
    unnamed x6, local copies, waits for them, and re-layouts  2.2 us
    pallas_call x1, Pallas kernels, split_by_modes(): pl.pallas_call(functools.partial(prepare_kernel, chips), in_specs=[smem,...  1.95 us
    pallas_call x1, Pallas kernels, split_by_modes(): pl.pallas_call(functools.partial(fit_kernel, 2 * rows), in_specs=[smem] +...  1.62 us
  transfers between devices with their start and end apart: 16, of which 2 were waited for; matrix products, arithmetic and copies ran while one was open for 1% of the time, Pallas kernels for 24%

profile of v13, /device:TPU:0, one launch (start us, length us, event | category | flops | bytes accessed | tf_op | source)
XLA Modules:
  0.0 53.5 jit_solution(7098912525171689985)
XLA Ops:
  0.6 1.9 %prepare.1 = (bf16[1024,256]{1,0:T(8,128)(2,1)S(1)}, bf16[16,256]{1,0:T(8,128)(2,1)}, bf16[144,256]{1,0:T(8,128)(2,1)S(1)}, bf16[144,256]{1,0:T(8,128)(2,1)S(1)}...) custom-call(s32[1]{0:T(128)} %bitcast.me_ref, ...), custom_call_target="tpu_custom_call" | custom-call | tf_op jit(solution)/shard_map/prepare/pallas_call | solution.py:375
  2.6 3.0 %collective-permute-start = (bf16[144,256]{1,0:T(8,128)(2,1)S(1)}, bf16[144,256]{1,0:T(8,128)(2,1)S(1)}, u32[]{:S(2)}, u32[]{:S(2)}) collective-permute-start(bf16[144,256]{1,0:T(8,128)(2,1)S(1)} %get-tuple-element.25), channel_id=1, source_target_pairs={{0,4},{1,5},{2,6},{3,7},{4,0},{5,1},{6,2},{7,3},{8,12},{9,13},{10,... | collective-permute-start | bytes 221192 | tf_op jit(solution)/shard_map/ppermute | solution.py:345
  5.6 1.4 %collective-permute-start.1 = (bf16[144,256]{1,0:T(8,128)(2,1)S(1)}, bf16[144,256]{1,0:T(8,128)(2,1)S(1)}, u32[]{:S(2)}, u32[]{:S(2)}) collective-permute-start(bf16[144,256]{1,0:T(8,128)(2,1)S(1)} %get-tuple-element.26), channel_id=1, source_target_pairs={{0,6},{1,7},{2,4},{3,5},{4,2},{5,3},{6,0},{7,1},{8,14},{9,15},{10,... | collective-permute-start | bytes 221192 | tf_op jit(solution)/shard_map/ppermute | solution.py:345
  7.0 2.6 %collective-permute-start.2 = (bf16[144,256]{1,0:T(8,128)(2,1)S(1)}, bf16[144,256]{1,0:T(8,128)(2,1)S(1)}, u32[]{:S(2)}, u32[]{:S(2)}) collective-permute-start(bf16[144,256]{1,0:T(8,128)(2,1)S(1)} %get-tuple-element.27), channel_id=1, source_target_pairs={{0,8},{1,9},{2,10},{3,11},{4,12},{5,13},{6,14},{7,15},{8,0},{9,1},... | collective-permute-start | bytes 221192 | tf_op jit(solution)/shard_map/ppermute | solution.py:345
  9.6 0.0 collective-permute-start.3
  9.6 3.9 %collective-permute-start.4 = (bf16[144,256]{1,0:T(8,128)(2,1)S(1)}, bf16[144,256]{1,0:T(8,128)(2,1)S(1)}, u32[]{:S(2)}, u32[]{:S(2)}) collective-permute-start(bf16[144,256]{1,0:T(8,128)(2,1)S(1)} %get-tuple-element.29), channel_id=1, source_target_pairs={{0,12},{1,13},{2,14},{3,15},{4,8},{5,9},{6,10},{7,11},{8,4},{9,5},... | collective-permute-start | bytes 221192 | tf_op jit(solution)/shard_map/ppermute | solution.py:345
  13.5 0.8 %fusion = (s32[512]{0:T(512)S(1)}, s32[512]{0:T(512)S(1)}, s32[512]{0:T(512)S(1)}, s32[512]{0:T(512)S(1)}) fusion(s32[2048]{0:T(1024)} %param.11), kind=kLoop, calls=%fused_computation | loop fusion | bytes 16384 | tf_op jit(solution)/shard_map/slice | solution.py:399
  14.3 0.0 collective-permute-done.refs_0_.refs_1_
  14.3 1.2 %collective-permute-start.5 = (bf16[144,256]{1,0:T(8,128)(2,1)S(1)}, bf16[144,256]{1,0:T(8,128)(2,1)S(1)}, u32[]{:S(2)}, u32[]{:S(2)}) collective-permute-start(bf16[144,256]{1,0:T(8,128)(2,1)S(1)} %get-tuple-element.30), channel_id=1, source_target_pairs={{0,14},{1,15},{2,12},{3,13},{4,10},{5,11},{6,8},{7,9},{8,6},{9,7},... | collective-permute-start | bytes 221192 | tf_op jit(solution)/shard_map/ppermute | solution.py:345
  15.4 0.0 collective-permute-done.1.refs_1_.refs_2_
  15.4 0.4 collective-permute-start.6
  15.9 0.0 copy-start.1
  15.9 2.2 %copy-done.1 = bf16[2048,1024]{1,0:T(8,128)(2,1)S(1)} copy-done((bf16[2048,1024]{1,0:T(8,128)(2,1)S(1)}, bf16[2048,1024]{1,0:T(8,128)(2,1)}, u32[]{:S(2)}) %copy-start.1) | copy-done | bytes 4194328
  18.1 2.4 %reorder.5.refs_10_.refs_1_ = bf16[512,1024]{1,0:T(8,128)(2,1)S(1)} custom-call(s32[1,512]{1,0:T(1,128)S(1)} %bitcast.12, bf16[2048,1024]{1,0:T(8,128)(2,1)S(1)} %copy-done.1, bf16[144,256]{1,0:T(8,128)(2,1)S(1)} %collective-permute-done.refs_0_.refs_1_, bf16[144,256]{1,0:T(8,128)(2,1)S(1)} %collective-permute-done.1.refs_1_.refs_2_), custom_call_target="tpu_custom_call" | custom-call | flops 2147483648 | bytes 4194304 | tf_op jit(solution)/shard_map/reorder/pallas_call | solution.py:391
  20.4 2.4 %reorder.4.refs_9_.refs_0_ = bf16[512,1024]{1,0:T(8,128)(2,1)S(1)} custom-call(s32[1,512]{1,0:T(1,128)S(1)} %bitcast.11, bf16[2048,1024]{1,0:T(8,128)(2,1)S(1)} %copy-done.1, bf16[144,256]{1,0:T(8,128)(2,1)S(1)} %collective-permute-done.refs_0_.refs_1_, bf16[144,256]{1,0:T(8,128)(2,1)S(1)} %collective-permute-done.1.refs_1_.refs_2_), custom_call_target="tpu_custom_call" | custom-call | flops 2147483648 | bytes 4194304 | tf_op jit(solution)/shard_map/reorder/pallas_call | solution.py:391
  22.8 1.3 %choose.1 = (bf16[3,256,2048]{2,1,0:T(8,128)(2,1)S(1)}, s32[1,2048]{1,0:T(1,128)S(1)}) custom-call(s32[1]{0:T(128)} %bitcast.me_ref, s32[4,4096]{1,0:T(4,128)} %bitcast.13, bf16[144,256]{1,0:T(8,128)(2,1)S(1)} %collective-permute-done.refs_0_.refs_1_, bf16[144,256]{1,0:T(8,128)(2,1)S(1)} %collective-permute-done.1.refs_1_.refs_2_), custom_call_target="tpu_custom_call" | custom-call | bytes 2097152 | tf_op jit(solution)/shard_map/choose/pallas_call | solution.py:406
  24.1 0.0 collective-permute-done.2.refs_3_
  24.1 0.0 collective-permute-done.3.refs_4_
  24.1 0.0 collective-permute-done.4.refs_5_
  24.1 0.0 collective-permute-done.5.refs_6_
  24.1 0.0 collective-permute-done.6.refs_7_
  24.1 0.1 collective-permute-start.7
  24.2 2.2 %design.2.refs_8_.refs_0_ = bf16[512,2048]{1,0:T(8,128)(2,1)S(1)} custom-call(bf16[8,16,256]{2,1,0:T(8,128)(2,1)S(1)} %collect.1.packets_ref.own_ref, bf16[3,256,2048]{2,1,0:T(8,128)(2,1)S(1)} %get-tuple-element.33.chosen_ref, s32[1,2048]{1,0:T(1,128)S(1)} %get-tuple-element.32.refs_8_.spots_ref), custom_call_target="tpu_custom_call" | custom-call | flops 2147483648 | bytes 2097152 | tf_op jit(solution)/shard_map/design/pallas_call | solution.py:434
  26.4 0.0 copy-start
  26.4 0.0 collective-permute-done.7.packets_ref.other_ref
  26.4 2.2 %design.3.refs_9_.refs_1_ = bf16[512,2048]{1,0:T(8,128)(2,1)S(1)} custom-call(bf16[8,16,256]{2,1,0:T(8,128)(2,1)S(1)} %collective-permute-done.7.packets_ref.other_ref, bf16[3,256,2048]{2,1,0:T(8,128)(2,1)S(1)} %get-tuple-element.33.chosen_ref, s32[1,2048]{1,0:T(1,128)S(1)} %get-tuple-element.32.refs_8_.spots_ref), custom_call_target="tpu_custom_call" | custom-call | flops 2147483648 | bytes 2097152 | tf_op jit(solution)/shard_map/design/pallas_call | solution.py:434
  28.6 0.0 copy-start.2
  28.6 0.0 copy-done
  28.6 1.6 %fit.1 = (f32[128,1024]{1,0:T(8,128)S(1)}, f32[8,256]{1,0:T(8,128)S(1)}) custom-call(s32[1]{0:T(128)} %bitcast.me_ref, s32[1,4096]{1,0:T(1,128)S(1)} %bitcast.8, bf16[8,16,256]{2,1,0:T(8,128)(2,1)S(1)} %collect.1.packets_ref.own_ref, bf16[8,16,256]{2,1,0:T(8,128)(2,1)S(1)} %collective-permute-done.7.packets_ref.other_ref, ...), custom_call_target="tpu_custom_call" | custom-call | flops 536870912 | bytes 4194304 | tf_op jit(solution)/shard_map/fit/pallas_call | solution.py:455
  30.2 0.6 %collective-permute-start.8 = (f32[128,1024]{1,0:T(8,128)S(1)}, f32[128,1024]{1,0:T(8,128)S(1)}, u32[]{:S(2)}, u32[]{:S(2)}) collective-permute-start(f32[128,1024]{1,0:T(8,128)S(1)} %get-tuple-element.35.refs_0_.own_ref), channel_id=1, source_target_pairs={{0,1},{1,0},{2,3},{3,2},{4,5},{5,4},{6,7},{7,6},{8,9},{9,8},{10,11... | collective-permute-start | bytes 1572872 | tf_op jit(solution)/shard_map/ppermute | solution.py:345
  30.8 0.0 copy-done.2
  30.8 2.4 %reorder.6.refs_2_ = bf16[512,1024]{1,0:T(8,128)(2,1)S(1)} custom-call(s32[1,512]{1,0:T(1,128)S(1)} %bitcast.10, bf16[2048,1024]{1,0:T(8,128)(2,1)S(1)} %copy-done.2, f32[128,1024]{1,0:T(8,128)S(1)} %get-tuple-element.35.refs_0_.own_ref), custom_call_target="tpu_custom_call" | custom-call | flops 2147483648 | bytes 4194304 | tf_op jit(solution)/shard_map/reorder/pallas_call | solution.py:391
  33.2 0.0 collective-permute-done.8.other_ref
  33.2 0.9 %sum.1 = (bf16[128,256]{1,0:T(8,128)(2,1)S(1)}, bf16[128,256]{1,0:T(8,128)(2,1)S(1)}, bf16[128,256]{1,0:T(8,128)(2,1)S(1)}, bf16[128,256]{1,0:T(8,128)(2,1)S(1)}...) custom-call(f32[128,1024]{1,0:T(8,128)S(1)} %get-tuple-element.35.re, ...), custom_call_target="tpu_custom_call" | custom-call | flops 536870912 | bytes 4194304 | tf_op jit(solution)/shard_map/sum/pallas_call | solution.py:469
  34.1 0.1 collective-permute-start.9
  34.2 3.0 %collective-permute-start.10 = (bf16[128,256]{1,0:T(8,128)(2,1)S(1)}, bf16[128,256]{1,0:T(8,128)(2,1)S(1)}, u32[]{:S(2)}, u32[]{:S(2)}) collective-permute-start(bf16[128,256]{1,0:T(8,128)(2,1)S(1)} %get-tuple-element.38), channel_id=1, source_target_pairs={{0,6},{1,7},{2,4},{3,5},{4,2},{5,3},{6,0},{7,1},{8,14},{9,15},{10,... | collective-permute-start | bytes 196616 | tf_op jit(solution)/shard_map/ppermute | solution.py:345
  37.2 2.2 %collective-permute-start.11 = (bf16[128,256]{1,0:T(8,128)(2,1)S(1)}, bf16[128,256]{1,0:T(8,128)(2,1)S(1)}, u32[]{:S(2)}, u32[]{:S(2)}) collective-permute-start(bf16[128,256]{1,0:T(8,128)(2,1)S(1)} %get-tuple-element.39), channel_id=1, source_target_pairs={{0,8},{1,9},{2,10},{3,11},{4,12},{5,13},{6,14},{7,15},{8,0},{9,1},... | collective-permute-start | bytes 196616 | tf_op jit(solution)/shard_map/ppermute | solution.py:345
  39.4 0.6 %collective-permute-start.12 = (bf16[128,256]{1,0:T(8,128)(2,1)S(1)}, bf16[128,256]{1,0:T(8,128)(2,1)S(1)}, u32[]{:S(2)}, u32[]{:S(2)}) collective-permute-start(bf16[128,256]{1,0:T(8,128)(2,1)S(1)} %get-tuple-element.40), channel_id=1, source_target_pairs={{0,10},{1,11},{2,8},{3,9},{4,14},{5,15},{6,12},{7,13},{8,2},{9,3},... | collective-permute-start | bytes 196616 | tf_op jit(solution)/shard_map/ppermute | solution.py:345
  40.0 3.7 %collective-permute-start.13 = (bf16[128,256]{1,0:T(8,128)(2,1)S(1)}, bf16[128,256]{1,0:T(8,128)(2,1)S(1)}, u32[]{:S(2)}, u32[]{:S(2)}) collective-permute-start(bf16[128,256]{1,0:T(8,128)(2,1)S(1)} %get-tuple-element.41), channel_id=1, source_target_pairs={{0,12},{1,13},{2,14},{3,15},{4,8},{5,9},{6,10},{7,11},{8,4},{9,5},... | collective-permute-start | bytes 196616 | tf_op jit(solution)/shard_map/ppermute | solution.py:345
  43.7 0.0 collective-permute-done.9.refs_5_
  43.7 1.1 %collective-permute-start.14 = (bf16[128,256]{1,0:T(8,128)(2,1)S(1)}, bf16[128,256]{1,0:T(8,128)(2,1)S(1)}, u32[]{:S(2)}, u32[]{:S(2)}) collective-permute-start(bf16[128,256]{1,0:T(8,128)(2,1)S(1)} %get-tuple-element.42), channel_id=1, source_target_pairs={{0,14},{1,15},{2,12},{3,13},{4,10},{5,11},{6,8},{7,9},{8,6},{9,7},... | collective-permute-start | bytes 196616 | tf_op jit(solution)/shard_map/ppermute | solution.py:345
  44.9 0.0 collective-permute-done.10.refs_6_
  44.9 0.4 collective-permute-start.15
  45.3 2.4 %reorder.7.refs_3_ = bf16[512,1024]{1,0:T(8,128)(2,1)S(1)} custom-call(s32[1,512]{1,0:T(1,128)S(1)} %bitcast.9, bf16[2048,1024]{1,0:T(8,128)(2,1)S(1)} %copy-done.2, bf16[128,256]{1,0:T(8,128)(2,1)S(1)} %get-tuple-element.36.refs_0_.refs_4_), custom_call_target="tpu_custom_call" | custom-call | flops 2147483648 | bytes 4194304 | tf_op jit(solution)/shard_map/reorder/pallas_call | solution.py:391
  47.7 0.0 collective-permute-done.11.refs_7_
  47.7 2.0 %collective-permute-done.12.refs_8_ = bf16[128,256]{1,0:T(8,128)(2,1)S(1)} collective-permute-done((bf16[128,256]{1,0:T(8,128)(2,1)S(1)}, bf16[128,256]{1,0:T(8,128)(2,1)S(1)}, u32[]{:S(2)}, u32[]{:S(2)}) %collective-permute-start.12) | collective-permute-done | bytes 65568 | tf_op jit(solution)/shard_map/ppermute | solution.py:345
  49.7 0.0 collective-permute-done.13.refs_9_
  49.7 1.1 %collective-permute-done.14.refs_10_ = bf16[128,256]{1,0:T(8,128)(2,1)S(1)} collective-permute-done((bf16[128,256]{1,0:T(8,128)(2,1)S(1)}, bf16[128,256]{1,0:T(8,128)(2,1)S(1)}, u32[]{:S(2)}, u32[]{:S(2)}) %collective-permute-start.14) | collective-permute-done | bytes 65568 | tf_op jit(solution)/shard_map/ppermute | solution.py:345
  50.8 0.0 collective-permute-done.15.refs_11_
  50.8 2.6 %finish.1 = (f32[256,1024]{1,0:T(8,128)}, bf16[256,2048]{1,0:T(8,128)(2,1)}) custom-call(s32[1]{0:T(128)} %bitcast.me_ref, bf16[1024,256]{1,0:T(8,128)(2,1)S(1)} %get-tuple-element.23.corr_ref, f32[8,256]{1,0:T(8,128)S(1)} %get-tuple-element.34.scale_ref, bf16[512,1024]{1,0:T(8,128)(2,1)S(1)} %reorder.4.refs_9_.refs_0_, ...), custom_call_target="tpu_custom_call" | custom-call | tf_op jit(solution)/shard_map/finish/pallas_call | solution.py:482
  (1 shorter events, 0.0 us)
Async XLA Ops:
  2.6 11.7 %collective-permute-start = (bf16[144,256]{1,0:T(8,128)(2,1)S(1)}, bf16[144,256]{1,0:T(8,128)(2,1)S(1)}, u32[]{:S(2)}, u32[]{:S(2)}) collective-permute-start(bf16[144,256]{1,0:T(8,128)(2,1)S(1)} %get-tuple-element.25), channel_id=1, source_target_pairs={{0,4},{1,5},{2,6},{3,7},{4,0},{5,1},{6,2},{7,3},{8,12},{9,13},{10,... | collective-permute-start | bytes 221192 | tf_op jit(solution)/shard_map/ppermute | solution.py:345
  5.6 9.8 %collective-permute-start.1 = (bf16[144,256]{1,0:T(8,128)(2,1)S(1)}, bf16[144,256]{1,0:T(8,128)(2,1)S(1)}, u32[]{:S(2)}, u32[]{:S(2)}) collective-permute-start(bf16[144,256]{1,0:T(8,128)(2,1)S(1)} %get-tuple-element.26), channel_id=1, source_target_pairs={{0,6},{1,7},{2,4},{3,5},{4,2},{5,3},{6,0},{7,1},{8,14},{9,15},{10,... | collective-permute-start | bytes 221192 | tf_op jit(solution)/shard_map/ppermute | solution.py:345
  7.0 17.1 %collective-permute-start.2 = (bf16[144,256]{1,0:T(8,128)(2,1)S(1)}, bf16[144,256]{1,0:T(8,128)(2,1)S(1)}, u32[]{:S(2)}, u32[]{:S(2)}) collective-permute-start(bf16[144,256]{1,0:T(8,128)(2,1)S(1)} %get-tuple-element.27), channel_id=1, source_target_pairs={{0,8},{1,9},{2,10},{3,11},{4,12},{5,13},{6,14},{7,15},{8,0},{9,1},... | collective-permute-start | bytes 221192 | tf_op jit(solution)/shard_map/ppermute | solution.py:345
  9.6 14.5 %collective-permute-start.3 = (bf16[144,256]{1,0:T(8,128)(2,1)S(1)}, bf16[144,256]{1,0:T(8,128)(2,1)S(1)}, u32[]{:S(2)}, u32[]{:S(2)}) collective-permute-start(bf16[144,256]{1,0:T(8,128)(2,1)S(1)} %get-tuple-element.28), channel_id=1, source_target_pairs={{0,10},{1,11},{2,8},{3,9},{4,14},{5,15},{6,12},{7,13},{8,2},{9,3},... | collective-permute-start | bytes 221192 | tf_op jit(solution)/shard_map/ppermute | solution.py:345
  9.6 14.5 %collective-permute-start.4 = (bf16[144,256]{1,0:T(8,128)(2,1)S(1)}, bf16[144,256]{1,0:T(8,128)(2,1)S(1)}, u32[]{:S(2)}, u32[]{:S(2)}) collective-permute-start(bf16[144,256]{1,0:T(8,128)(2,1)S(1)} %get-tuple-element.29), channel_id=1, source_target_pairs={{0,12},{1,13},{2,14},{3,15},{4,8},{5,9},{6,10},{7,11},{8,4},{9,5},... | collective-permute-start | bytes 221192 | tf_op jit(solution)/shard_map/ppermute | solution.py:345
  14.3 9.9 %collective-permute-start.5 = (bf16[144,256]{1,0:T(8,128)(2,1)S(1)}, bf16[144,256]{1,0:T(8,128)(2,1)S(1)}, u32[]{:S(2)}, u32[]{:S(2)}) collective-permute-start(bf16[144,256]{1,0:T(8,128)(2,1)S(1)} %get-tuple-element.30), channel_id=1, source_target_pairs={{0,14},{1,15},{2,12},{3,13},{4,10},{5,11},{6,8},{7,9},{8,6},{9,7},... | collective-permute-start | bytes 221192 | tf_op jit(solution)/shard_map/ppermute | solution.py:345
  15.4 8.7 %collective-permute-start.6 = (bf16[144,256]{1,0:T(8,128)(2,1)S(1)}, bf16[144,256]{1,0:T(8,128)(2,1)S(1)}, u32[]{:S(2)}, u32[]{:S(2)}) collective-permute-start(bf16[144,256]{1,0:T(8,128)(2,1)S(1)} %get-tuple-element.31), channel_id=1, source_target_pairs={{0,2},{1,3},{2,0},{3,1},{4,6},{5,7},{6,4},{7,5},{8,10},{9,11},{10,... | collective-permute-start | bytes 221192 | tf_op jit(solution)/shard_map/ppermute | solution.py:345
  15.9 2.2 %copy-start.1 = (bf16[2048,1024]{1,0:T(8,128)(2,1)S(1)}, bf16[2048,1024]{1,0:T(8,128)(2,1)}, u32[]{:S(2)}) copy-start(bf16[2048,1024]{1,0:T(8,128)(2,1)} %slab_ref.7) | copy-start | bytes 12582916
  24.1 2.3 %collective-permute-start.7 = (bf16[8,16,256]{2,1,0:T(8,128)(2,1)S(1)}, bf16[8,16,256]{2,1,0:T(8,128)(2,1)S(1)}, u32[]{:S(2)}, u32[]{:S(2)}) collective-permute-start(bf16[8,16,256]{2,1,0:T(8,128)(2,1)S(1)} %collect.1.packets_ref.own_ref), channel_id=1, source_target_pairs={{0,1},{1,0},{2,3},{3,2},{4,5},{5,4},{6,7},{7,6},{8,9},{9,8},{10,11... | collective-permute-start | bytes 196616 | tf_op jit(solution)/shard_map/ppermute | solution.py:345
  26.4 2.2 %copy-start = (s32[4096]{0:T(1024)S(1)}, s32[4096]{0:T(1024)}, u32[]{:S(2)}) copy-start(s32[4096]{0:T(1024)} %param.8) | copy-start | bytes 49156
  28.6 2.2 %copy-start.2 = (bf16[2048,1024]{1,0:T(8,128)(2,1)S(1)}, bf16[2048,1024]{1,0:T(8,128)(2,1)}, u32[]{:S(2)}) copy-start(bf16[2048,1024]{1,0:T(8,128)(2,1)} %slab_ref.7) | copy-start | bytes 12582916
  30.2 2.9 %collective-permute-start.8 = (f32[128,1024]{1,0:T(8,128)S(1)}, f32[128,1024]{1,0:T(8,128)S(1)}, u32[]{:S(2)}, u32[]{:S(2)}) collective-permute-start(f32[128,1024]{1,0:T(8,128)S(1)} %get-tuple-element.35.refs_0_.own_ref), channel_id=1, source_target_pairs={{0,1},{1,0},{2,3},{3,2},{4,5},{5,4},{6,7},{7,6},{8,9},{9,8},{10,11... | collective-permute-start | bytes 1572872 | tf_op jit(solution)/shard_map/ppermute | solution.py:345
  34.1 9.6 %collective-permute-start.9 = (bf16[128,256]{1,0:T(8,128)(2,1)S(1)}, bf16[128,256]{1,0:T(8,128)(2,1)S(1)}, u32[]{:S(2)}, u32[]{:S(2)}) collective-permute-start(bf16[128,256]{1,0:T(8,128)(2,1)S(1)} %get-tuple-element.37), channel_id=1, source_target_pairs={{0,4},{1,5},{2,6},{3,7},{4,0},{5,1},{6,2},{7,3},{8,12},{9,13},{10,... | collective-permute-start | bytes 196616 | tf_op jit(solution)/shard_map/ppermute | solution.py:345
  34.2 10.7 %collective-permute-start.10 = (bf16[128,256]{1,0:T(8,128)(2,1)S(1)}, bf16[128,256]{1,0:T(8,128)(2,1)S(1)}, u32[]{:S(2)}, u32[]{:S(2)}) collective-permute-start(bf16[128,256]{1,0:T(8,128)(2,1)S(1)} %get-tuple-element.38), channel_id=1, source_target_pairs={{0,6},{1,7},{2,4},{3,5},{4,2},{5,3},{6,0},{7,1},{8,14},{9,15},{10,... | collective-permute-start | bytes 196616 | tf_op jit(solution)/shard_map/ppermute | solution.py:345
  37.2 10.5 %collective-permute-start.11 = (bf16[128,256]{1,0:T(8,128)(2,1)S(1)}, bf16[128,256]{1,0:T(8,128)(2,1)S(1)}, u32[]{:S(2)}, u32[]{:S(2)}) collective-permute-start(bf16[128,256]{1,0:T(8,128)(2,1)S(1)} %get-tuple-element.39), channel_id=1, source_target_pairs={{0,8},{1,9},{2,10},{3,11},{4,12},{5,13},{6,14},{7,15},{8,0},{9,1},... | collective-permute-start | bytes 196616 | tf_op jit(solution)/shard_map/ppermute | solution.py:345
  39.4 10.3 %collective-permute-start.12 = (bf16[128,256]{1,0:T(8,128)(2,1)S(1)}, bf16[128,256]{1,0:T(8,128)(2,1)S(1)}, u32[]{:S(2)}, u32[]{:S(2)}) collective-permute-start(bf16[128,256]{1,0:T(8,128)(2,1)S(1)} %get-tuple-element.40), channel_id=1, source_target_pairs={{0,10},{1,11},{2,8},{3,9},{4,14},{5,15},{6,12},{7,13},{8,2},{9,3},... | collective-permute-start | bytes 196616 | tf_op jit(solution)/shard_map/ppermute | solution.py:345
  40.0 9.7 %collective-permute-start.13 = (bf16[128,256]{1,0:T(8,128)(2,1)S(1)}, bf16[128,256]{1,0:T(8,128)(2,1)S(1)}, u32[]{:S(2)}, u32[]{:S(2)}) collective-permute-start(bf16[128,256]{1,0:T(8,128)(2,1)S(1)} %get-tuple-element.41), channel_id=1, source_target_pairs={{0,12},{1,13},{2,14},{3,15},{4,8},{5,9},{6,10},{7,11},{8,4},{9,5},... | collective-permute-start | bytes 196616 | tf_op jit(solution)/shard_map/ppermute | solution.py:345
  43.7 7.1 %collective-permute-start.14 = (bf16[128,256]{1,0:T(8,128)(2,1)S(1)}, bf16[128,256]{1,0:T(8,128)(2,1)S(1)}, u32[]{:S(2)}, u32[]{:S(2)}) collective-permute-start(bf16[128,256]{1,0:T(8,128)(2,1)S(1)} %get-tuple-element.42), channel_id=1, source_target_pairs={{0,14},{1,15},{2,12},{3,13},{4,10},{5,11},{6,8},{7,9},{8,6},{9,7},... | collective-permute-start | bytes 196616 | tf_op jit(solution)/shard_map/ppermute | solution.py:345
  44.9 5.9 %collective-permute-start.15 = (bf16[128,256]{1,0:T(8,128)(2,1)S(1)}, bf16[128,256]{1,0:T(8,128)(2,1)S(1)}, u32[]{:S(2)}, u32[]{:S(2)}) collective-permute-start(bf16[128,256]{1,0:T(8,128)(2,1)S(1)} %get-tuple-element.43), channel_id=1, source_target_pairs={{0,2},{1,3},{2,0},{3,1},{4,6},{5,7},{6,4},{7,5},{8,10},{9,11},{10,... | collective-permute-start | bytes 196616 | tf_op jit(solution)/shard_map/ppermute | solution.py:345

commit v14 on v13

--- a/solution.py
+++ b/solution.py
@@ -37,10 +37,11 @@
     return pl.ds(pl.multiple_of(index * count, count), count)
 
 
-def prepare_kernel(chips, me_ref, corr_ref, points_ref, turned_ref, packet_ref, *sent_refs):
+def prepare_kernel(chips, me_ref, corr_ref, points_ref, turned_ref, *refs):
     turned = corr_ref[...].astype(jnp.float32).T
     turned_ref[...] = turned.astype(jnp.bfloat16)
     squares = jnp.sum(turned * turned, axis=0, keepdims=True)
+    *sent_refs, packet_ref = refs
     packet_rows, terms = packet_ref.shape
     dim, runs = points_ref.shape
     rows = dim * runs // terms
@@ -61,55 +62,6 @@
         chip = (me_ref[0] // CORES) ^ partner(k, chips)
         sent_ref[0:count, :] = turned_ref[rows_of(chip, count), :]
         sent_ref[count : sent_ref.shape[0], :] = packet_ref[...]
-
-
-def split_in_two(values):
-    high = values.astype(jnp.bfloat16).astype(jnp.float32)
-    return [high, values - high]
-
-
-def partner(slot, chips):
-    return slot and slot % (chips - 1) + 1
-
-
-def rows_of(index, count):
-    return pl.ds(pl.multiple_of(index * count, count), count)
-
-
-def prepare_kernel(chips, me_ref, corr_ref, points_ref, turned_ref, packet_ref, *sent_refs):
-    turned = corr_ref[...].astype(jnp.float32).T
-    turned_ref[...] = turned.astype(jnp.bfloat16)
-    squares = jnp.sum(turned * turned, axis=0, keepdims=True)
-    packet_rows, terms = packet_ref.shape
-    dim, runs = points_ref.shape
-    rows = dim * runs // terms
-    points = jnp.concatenate(
-        [points_ref[start : start + rows, :] for start in range(0, dim, rows)], axis=1
-    )
-    pieces = split_in_two(points) + split_in_two(squares)
-    used = 2 * rows + 2
-    if packet_rows > used:
-        pieces.append(jnp.zeros((packet_rows - used, terms), jnp.float32))
-    packet_ref[...] = jnp.concatenate(pieces, axis=0).astype(jnp.bfloat16)
-    fill_blocks(chips, me_ref, turned_ref, packet_ref, sent_refs)
-
-
-def fill_blocks(chips, me_ref, turned_ref, packet_ref, sent_refs):
-    count = turned_ref.shape[0] // chips
-    for k, sent_ref in enumerate(sent_refs):
-        chip = (me_ref[0] // CORES) ^ partner(k, chips)
-        sent_ref[0:count, :] = turned_ref[rows_of(chip, count), :]
-        sent_ref[count : sent_ref.shape[0], :] = packet_ref[...]
-
-
-def late_kernel(chips, me_ref, turned_ref, packet_ref, *refs):
-    sent_refs = refs[len(refs) - (chips - FIRST_SLOTS) :]
-    fill_blocks(chips, FIRST_SLOTS, me_ref, turned_ref, packet_ref, sent_refs)
-
-
-def split_in_two(values):
-    high = values.astype(jnp.bfloat16).astype(jnp.float32)
-    return [high, values - high]
 
 
 def hermite_columns(points):
@@ -372,15 +324,13 @@
     anywhere = pl.BlockSpec(memory_space=pl.ANY)
 
     block_type = jax.ShapeDtypeStruct((own_modes + packet_rows, term_count), jnp.bfloat16)
-    turned, packet, *sent = pl.pallas_call(
+    turned, *sent = pl.pallas_call(
         functools.partial(prepare_kernel, chips),
         in_specs=[smem, vmem, vmem],
-        out_specs=[vmem] * (2 + chips),
-        out_shape=[
-            jax.ShapeDtypeStruct((modes, term_count), jnp.bfloat16),
-            jax.ShapeDtypeStruct((packet_rows, term_count), jnp.bfloat16),
-        ]
+        out_specs=[vmem] * (1 + chips),
+        out_shape=[jax.ShapeDtypeStruct((modes, term_count), jnp.bfloat16)]
         + [block_type] * chips,
+        scratch_shapes=[pltpu.VMEM((packet_rows, term_count), jnp.bfloat16)],
         compiler_params=params(16),
         name="prepare",
     )(me, in_hbm(correlations), in_hbm(run_inputs.T))

time: 53.8 us -> 53.3 us (level)
  Pallas kernels: 22.1 us -> 21.5 us
    pallas_call x1, Pallas kernels: 1.95 us -> 1.35 us  [split_by_modes(): pl.pallas_call(functools.partial(prepare_kernel, chips), in_specs=[smem,...]
where the time goes in v14:
time: 53.3 us; the launch traced here: 53 us
  starting transfers between devices  24.4 us (46%)
  Pallas kernels  21.5 us (40%)
  waiting for transfers between devices  3.15 us (6%)
  local copies, waits for them, and re-layouts  2.97 us (6%)
  between operations  0.98 us (2%)
    ppermute x16, starting transfers between devices, to_device(): return lax.ppermute(array, 'runs', [(i, i ^ bits) for i in range(devices)])  24.4 us
    pallas_call x4, Pallas kernels, reorder(): pl.pallas_call(reorder_kernel, in_specs=[vmem, vmem] + [anywhere] * len(a...  9.43 us
    pallas_call x2, Pallas kernels, design_of(): pl.pallas_call(functools.partial(design_kernel, dim, run_count), in_specs...  4.3 us
    ppermute x16, waiting for transfers between devices, to_device(): return lax.ppermute(array, 'runs', [(i, i ^ bits) for i in range(devices)])  3.15 us
    pallas_call x1, Pallas kernels, split_by_modes(): pl.pallas_call(functools.partial(finish_kernel, len(ordered)), in_specs=[...  2.56 us
    unnamed x6, local copies, waits for them, and re-layouts  2.2 us
    pallas_call x1, Pallas kernels, split_by_modes(): pl.pallas_call(functools.partial(fit_kernel, 2 * rows), in_specs=[smem] +...  1.62 us
    pallas_call x1, Pallas kernels, split_by_modes(): pl.pallas_call(functools.partial(prepare_kernel, chips), in_specs=[smem,...  1.35 us
  transfers between devices with their start and end apart: 16, of which 2 were waited for; matrix products, arithmetic and copies ran while one was open for 1% of the time, Pallas kernels for 24%

profile of v14, /device:TPU:0, one launch (start us, length us, event | category | flops | bytes accessed | tf_op | source)
XLA Modules:
  0.0 53.0 jit_solution(10749926091869839002)
XLA Ops:
  0.6 1.3 %prepare.1 = (bf16[1024,256]{1,0:T(8,128)(2,1)S(1)}, bf16[144,256]{1,0:T(8,128)(2,1)S(1)}, bf16[144,256]{1,0:T(8,128)(2,1)S(1)}, bf16[144,256]{1,0:T(8,128)(2,1)...) custom-call(s32[1]{0:T(128)} %bitcast.me_ref, ...), custom_call_target="tpu_custom_call" | custom-call | tf_op jit(solution)/shard_map/prepare/pallas_call | solution.py:327
  2.0 3.1 %collective-permute-start = (bf16[144,256]{1,0:T(8,128)(2,1)S(1)}, bf16[144,256]{1,0:T(8,128)(2,1)S(1)}, u32[]{:S(2)}, u32[]{:S(2)}) collective-permute-start(bf16[144,256]{1,0:T(8,128)(2,1)S(1)} %get-tuple-element.25), channel_id=1, source_target_pairs={{0,4},{1,5},{2,6},{3,7},{4,0},{5,1},{6,2},{7,3},{8,12},{9,13},{10,... | collective-permute-start | bytes 221192 | tf_op jit(solution)/shard_map/ppermute | solution.py:297
  5.1 1.4 %collective-permute-start.1 = (bf16[144,256]{1,0:T(8,128)(2,1)S(1)}, bf16[144,256]{1,0:T(8,128)(2,1)S(1)}, u32[]{:S(2)}, u32[]{:S(2)}) collective-permute-start(bf16[144,256]{1,0:T(8,128)(2,1)S(1)} %get-tuple-element.26), channel_id=1, source_target_pairs={{0,6},{1,7},{2,4},{3,5},{4,2},{5,3},{6,0},{7,1},{8,14},{9,15},{10,... | collective-permute-start | bytes 221192 | tf_op jit(solution)/shard_map/ppermute | solution.py:297
  6.4 2.6 %collective-permute-start.2 = (bf16[144,256]{1,0:T(8,128)(2,1)S(1)}, bf16[144,256]{1,0:T(8,128)(2,1)S(1)}, u32[]{:S(2)}, u32[]{:S(2)}) collective-permute-start(bf16[144,256]{1,0:T(8,128)(2,1)S(1)} %get-tuple-element.27), channel_id=1, source_target_pairs={{0,8},{1,9},{2,10},{3,11},{4,12},{5,13},{6,14},{7,15},{8,0},{9,1},... | collective-permute-start | bytes 221192 | tf_op jit(solution)/shard_map/ppermute | solution.py:297
  9.0 0.0 collective-permute-start.3
  9.0 3.9 %collective-permute-start.4 = (bf16[144,256]{1,0:T(8,128)(2,1)S(1)}, bf16[144,256]{1,0:T(8,128)(2,1)S(1)}, u32[]{:S(2)}, u32[]{:S(2)}) collective-permute-start(bf16[144,256]{1,0:T(8,128)(2,1)S(1)} %get-tuple-element.29), channel_id=1, source_target_pairs={{0,12},{1,13},{2,14},{3,15},{4,8},{5,9},{6,10},{7,11},{8,4},{9,5},... | collective-permute-start | bytes 221192 | tf_op jit(solution)/shard_map/ppermute | solution.py:297
  12.9 0.8 %fusion = (s32[512]{0:T(512)S(1)}, s32[512]{0:T(512)S(1)}, s32[512]{0:T(512)S(1)}, s32[512]{0:T(512)S(1)}) fusion(s32[2048]{0:T(1024)} %param.11), kind=kLoop, calls=%fused_computation | loop fusion | bytes 16384 | tf_op jit(solution)/shard_map/slice | solution.py:349
  13.7 0.0 collective-permute-done.refs_0_.refs_1_
  13.7 1.2 %collective-permute-start.5 = (bf16[144,256]{1,0:T(8,128)(2,1)S(1)}, bf16[144,256]{1,0:T(8,128)(2,1)S(1)}, u32[]{:S(2)}, u32[]{:S(2)}) collective-permute-start(bf16[144,256]{1,0:T(8,128)(2,1)S(1)} %get-tuple-element.30), channel_id=1, source_target_pairs={{0,14},{1,15},{2,12},{3,13},{4,10},{5,11},{6,8},{7,9},{8,6},{9,7},... | collective-permute-start | bytes 221192 | tf_op jit(solution)/shard_map/ppermute | solution.py:297
  14.9 0.0 collective-permute-done.1.refs_1_.refs_2_
  14.9 0.4 collective-permute-start.6
  15.3 0.0 copy-start.1
  15.3 2.2 %copy-done.1 = bf16[2048,1024]{1,0:T(8,128)(2,1)S(1)} copy-done((bf16[2048,1024]{1,0:T(8,128)(2,1)S(1)}, bf16[2048,1024]{1,0:T(8,128)(2,1)}, u32[]{:S(2)}) %copy-start.1) | copy-done | bytes 4194328
  17.5 2.4 %reorder.5.refs_10_.refs_1_ = bf16[512,1024]{1,0:T(8,128)(2,1)S(1)} custom-call(s32[1,512]{1,0:T(1,128)S(1)} %bitcast.12, bf16[2048,1024]{1,0:T(8,128)(2,1)S(1)} %copy-done.1, bf16[144,256]{1,0:T(8,128)(2,1)S(1)} %collective-permute-done.refs_0_.refs_1_, bf16[144,256]{1,0:T(8,128)(2,1)S(1)} %collective-permute-done.1.refs_1_.refs_2_), custom_call_target="tpu_custom_call" | custom-call | flops 2147483648 | bytes 4194304 | tf_op jit(solution)/shard_map/reorder/pallas_call | solution.py:341
  19.9 2.4 %reorder.4.refs_9_.refs_0_ = bf16[512,1024]{1,0:T(8,128)(2,1)S(1)} custom-call(s32[1,512]{1,0:T(1,128)S(1)} %bitcast.11, bf16[2048,1024]{1,0:T(8,128)(2,1)S(1)} %copy-done.1, bf16[144,256]{1,0:T(8,128)(2,1)S(1)} %collective-permute-done.refs_0_.refs_1_, bf16[144,256]{1,0:T(8,128)(2,1)S(1)} %collective-permute-done.1.refs_1_.refs_2_), custom_call_target="tpu_custom_call" | custom-call | flops 2147483648 | bytes 4194304 | tf_op jit(solution)/shard_map/reorder/pallas_call | solution.py:341
  22.2 1.3 %choose.1 = (bf16[3,256,2048]{2,1,0:T(8,128)(2,1)S(1)}, s32[1,2048]{1,0:T(1,128)S(1)}) custom-call(s32[1]{0:T(128)} %bitcast.me_ref, s32[4,4096]{1,0:T(4,128)} %bitcast.13, bf16[144,256]{1,0:T(8,128)(2,1)S(1)} %collective-permute-done.refs_0_.refs_1_, bf16[144,256]{1,0:T(8,128)(2,1)S(1)} %collective-permute-done.1.refs_1_.refs_2_), custom_call_target="tpu_custom_call" | custom-call | bytes 2097152 | tf_op jit(solution)/shard_map/choose/pallas_call | solution.py:356
  23.5 0.0 collective-permute-done.2.refs_3_
  23.6 0.0 collective-permute-done.3.refs_4_
  23.6 0.0 collective-permute-done.4.refs_5_
  23.6 0.0 collective-permute-done.5.refs_6_
  23.6 0.0 collective-permute-done.6.refs_7_
  23.6 0.1 collective-permute-start.7
  23.7 2.1 %design.2.refs_8_.refs_0_ = bf16[512,2048]{1,0:T(8,128)(2,1)S(1)} custom-call(bf16[8,16,256]{2,1,0:T(8,128)(2,1)S(1)} %collect.1.packets_ref.own_ref, bf16[3,256,2048]{2,1,0:T(8,128)(2,1)S(1)} %get-tuple-element.33.chosen_ref, s32[1,2048]{1,0:T(1,128)S(1)} %get-tuple-element.32.refs_8_.spots_ref), custom_call_target="tpu_custom_call" | custom-call | flops 2147483648 | bytes 2097152 | tf_op jit(solution)/shard_map/design/pallas_call | solution.py:384
  25.8 0.0 copy-start
  25.9 0.0 collective-permute-done.7.packets_ref.other_ref
  25.9 2.2 %design.3.refs_9_.refs_1_ = bf16[512,2048]{1,0:T(8,128)(2,1)S(1)} custom-call(bf16[8,16,256]{2,1,0:T(8,128)(2,1)S(1)} %collective-permute-done.7.packets_ref.other_ref, bf16[3,256,2048]{2,1,0:T(8,128)(2,1)S(1)} %get-tuple-element.33.chosen_ref, s32[1,2048]{1,0:T(1,128)S(1)} %get-tuple-element.32.refs_8_.spots_ref), custom_call_target="tpu_custom_call" | custom-call | flops 2147483648 | bytes 2097152 | tf_op jit(solution)/shard_map/design/pallas_call | solution.py:384
  28.0 0.0 copy-start.2
  28.0 0.0 copy-done
  28.1 1.6 %fit.1 = (f32[128,1024]{1,0:T(8,128)S(1)}, f32[8,256]{1,0:T(8,128)S(1)}) custom-call(s32[1]{0:T(128)} %bitcast.me_ref, s32[1,4096]{1,0:T(1,128)S(1)} %bitcast.8, bf16[8,16,256]{2,1,0:T(8,128)(2,1)S(1)} %collect.1.packets_ref.own_ref, bf16[8,16,256]{2,1,0:T(8,128)(2,1)S(1)} %collective-permute-done.7.packets_ref.other_ref, ...), custom_call_target="tpu_custom_call" | custom-call | flops 536870912 | bytes 4194304 | tf_op jit(solution)/shard_map/fit/pallas_call | solution.py:405
  29.7 0.6 %collective-permute-start.8 = (f32[128,1024]{1,0:T(8,128)S(1)}, f32[128,1024]{1,0:T(8,128)S(1)}, u32[]{:S(2)}, u32[]{:S(2)}) collective-permute-start(f32[128,1024]{1,0:T(8,128)S(1)} %get-tuple-element.35.refs_0_.own_ref), channel_id=1, source_target_pairs={{0,1},{1,0},{2,3},{3,2},{4,5},{5,4},{6,7},{7,6},{8,9},{9,8},{10,11... | collective-permute-start | bytes 1572872 | tf_op jit(solution)/shard_map/ppermute | solution.py:297
  30.2 0.0 copy-done.2
  30.3 2.4 %reorder.6.refs_2_ = bf16[512,1024]{1,0:T(8,128)(2,1)S(1)} custom-call(s32[1,512]{1,0:T(1,128)S(1)} %bitcast.10, bf16[2048,1024]{1,0:T(8,128)(2,1)S(1)} %copy-done.2, f32[128,1024]{1,0:T(8,128)S(1)} %get-tuple-element.35.refs_0_.own_ref), custom_call_target="tpu_custom_call" | custom-call | flops 2147483648 | bytes 4194304 | tf_op jit(solution)/shard_map/reorder/pallas_call | solution.py:341
  32.6 0.0 collective-permute-done.8.other_ref
  32.6 0.9 %sum.1 = (bf16[128,256]{1,0:T(8,128)(2,1)S(1)}, bf16[128,256]{1,0:T(8,128)(2,1)S(1)}, bf16[128,256]{1,0:T(8,128)(2,1)S(1)}, bf16[128,256]{1,0:T(8,128)(2,1)S(1)}...) custom-call(f32[128,1024]{1,0:T(8,128)S(1)} %get-tuple-element.35.re, ...), custom_call_target="tpu_custom_call" | custom-call | flops 536870912 | bytes 4194304 | tf_op jit(solution)/shard_map/sum/pallas_call | solution.py:419
  33.6 0.1 collective-permute-start.9
  33.6 3.0 %collective-permute-start.10 = (bf16[128,256]{1,0:T(8,128)(2,1)S(1)}, bf16[128,256]{1,0:T(8,128)(2,1)S(1)}, u32[]{:S(2)}, u32[]{:S(2)}) collective-permute-start(bf16[128,256]{1,0:T(8,128)(2,1)S(1)} %get-tuple-element.38), channel_id=1, source_target_pairs={{0,6},{1,7},{2,4},{3,5},{4,2},{5,3},{6,0},{7,1},{8,14},{9,15},{10,... | collective-permute-start | bytes 196616 | tf_op jit(solution)/shard_map/ppermute | solution.py:297
  36.7 2.2 %collective-permute-start.11 = (bf16[128,256]{1,0:T(8,128)(2,1)S(1)}, bf16[128,256]{1,0:T(8,128)(2,1)S(1)}, u32[]{:S(2)}, u32[]{:S(2)}) collective-permute-start(bf16[128,256]{1,0:T(8,128)(2,1)S(1)} %get-tuple-element.39), channel_id=1, source_target_pairs={{0,8},{1,9},{2,10},{3,11},{4,12},{5,13},{6,14},{7,15},{8,0},{9,1},... | collective-permute-start | bytes 196616 | tf_op jit(solution)/shard_map/ppermute | solution.py:297
  38.9 0.6 %collective-permute-start.12 = (bf16[128,256]{1,0:T(8,128)(2,1)S(1)}, bf16[128,256]{1,0:T(8,128)(2,1)S(1)}, u32[]{:S(2)}, u32[]{:S(2)}) collective-permute-start(bf16[128,256]{1,0:T(8,128)(2,1)S(1)} %get-tuple-element.40), channel_id=1, source_target_pairs={{0,10},{1,11},{2,8},{3,9},{4,14},{5,15},{6,12},{7,13},{8,2},{9,3},... | collective-permute-start | bytes 196616 | tf_op jit(solution)/shard_map/ppermute | solution.py:297
  39.5 3.7 %collective-permute-start.13 = (bf16[128,256]{1,0:T(8,128)(2,1)S(1)}, bf16[128,256]{1,0:T(8,128)(2,1)S(1)}, u32[]{:S(2)}, u32[]{:S(2)}) collective-permute-start(bf16[128,256]{1,0:T(8,128)(2,1)S(1)} %get-tuple-element.41), channel_id=1, source_target_pairs={{0,12},{1,13},{2,14},{3,15},{4,8},{5,9},{6,10},{7,11},{8,4},{9,5},... | collective-permute-start | bytes 196616 | tf_op jit(solution)/shard_map/ppermute | solution.py:297
  43.2 0.0 collective-permute-done.9.refs_5_
  43.2 1.1 %collective-permute-start.14 = (bf16[128,256]{1,0:T(8,128)(2,1)S(1)}, bf16[128,256]{1,0:T(8,128)(2,1)S(1)}, u32[]{:S(2)}, u32[]{:S(2)}) collective-permute-start(bf16[128,256]{1,0:T(8,128)(2,1)S(1)} %get-tuple-element.42), channel_id=1, source_target_pairs={{0,14},{1,15},{2,12},{3,13},{4,10},{5,11},{6,8},{7,9},{8,6},{9,7},... | collective-permute-start | bytes 196616 | tf_op jit(solution)/shard_map/ppermute | solution.py:297
  44.3 0.0 collective-permute-done.10.refs_6_
  44.3 0.4 collective-permute-start.15
  44.8 2.4 %reorder.7.refs_3_ = bf16[512,1024]{1,0:T(8,128)(2,1)S(1)} custom-call(s32[1,512]{1,0:T(1,128)S(1)} %bitcast.9, bf16[2048,1024]{1,0:T(8,128)(2,1)S(1)} %copy-done.2, bf16[128,256]{1,0:T(8,128)(2,1)S(1)} %get-tuple-element.36.refs_0_.refs_4_), custom_call_target="tpu_custom_call" | custom-call | flops 2147483648 | bytes 4194304 | tf_op jit(solution)/shard_map/reorder/pallas_call | solution.py:341
  47.1 0.0 collective-permute-done.11.refs_7_
  47.1 2.1 %collective-permute-done.12.refs_8_ = bf16[128,256]{1,0:T(8,128)(2,1)S(1)} collective-permute-done((bf16[128,256]{1,0:T(8,128)(2,1)S(1)}, bf16[128,256]{1,0:T(8,128)(2,1)S(1)}, u32[]{:S(2)}, u32[]{:S(2)}) %collective-permute-start.12) | collective-permute-done | bytes 65568 | tf_op jit(solution)/shard_map/ppermute | solution.py:297
  49.2 0.0 collective-permute-done.13.refs_9_
  49.2 1.1 %collective-permute-done.14.refs_10_ = bf16[128,256]{1,0:T(8,128)(2,1)S(1)} collective-permute-done((bf16[128,256]{1,0:T(8,128)(2,1)S(1)}, bf16[128,256]{1,0:T(8,128)(2,1)S(1)}, u32[]{:S(2)}, u32[]{:S(2)}) %collective-permute-start.14) | collective-permute-done | bytes 65568 | tf_op jit(solution)/shard_map/ppermute | solution.py:297
  50.3 0.0 collective-permute-done.15.refs_11_
  50.3 2.6 %finish.1 = (f32[256,1024]{1,0:T(8,128)}, bf16[256,2048]{1,0:T(8,128)(2,1)}) custom-call(s32[1]{0:T(128)} %bitcast.me_ref, bf16[1024,256]{1,0:T(8,128)(2,1)S(1)} %get-tuple-element.23.corr_ref, f32[8,256]{1,0:T(8,128)S(1)} %get-tuple-element.34.scale_ref, bf16[512,1024]{1,0:T(8,128)(2,1)S(1)} %reorder.4.refs_9_.refs_0_, ...), custom_call_target="tpu_custom_call" | custom-call | tf_op jit(solution)/shard_map/finish/pallas_call | solution.py:432
  (1 shorter events, 0.0 us)
Async XLA Ops:
  2.0 11.7 %collective-permute-start = (bf16[144,256]{1,0:T(8,128)(2,1)S(1)}, bf16[144,256]{1,0:T(8,128)(2,1)S(1)}, u32[]{:S(2)}, u32[]{:S(2)}) collective-permute-start(bf16[144,256]{1,0:T(8,128)(2,1)S(1)} %get-tuple-element.25), channel_id=1, source_target_pairs={{0,4},{1,5},{2,6},{3,7},{4,0},{5,1},{6,2},{7,3},{8,12},{9,13},{10,... | collective-permute-start | bytes 221192 | tf_op jit(solution)/shard_map/ppermute | solution.py:297
  5.1 9.8 %collective-permute-start.1 = (bf16[144,256]{1,0:T(8,128)(2,1)S(1)}, bf16[144,256]{1,0:T(8,128)(2,1)S(1)}, u32[]{:S(2)}, u32[]{:S(2)}) collective-permute-start(bf16[144,256]{1,0:T(8,128)(2,1)S(1)} %get-tuple-element.26), channel_id=1, source_target_pairs={{0,6},{1,7},{2,4},{3,5},{4,2},{5,3},{6,0},{7,1},{8,14},{9,15},{10,... | collective-permute-start | bytes 221192 | tf_op jit(solution)/shard_map/ppermute | solution.py:297
  6.4 17.1 %collective-permute-start.2 = (bf16[144,256]{1,0:T(8,128)(2,1)S(1)}, bf16[144,256]{1,0:T(8,128)(2,1)S(1)}, u32[]{:S(2)}, u32[]{:S(2)}) collective-permute-start(bf16[144,256]{1,0:T(8,128)(2,1)S(1)} %get-tuple-element.27), channel_id=1, source_target_pairs={{0,8},{1,9},{2,10},{3,11},{4,12},{5,13},{6,14},{7,15},{8,0},{9,1},... | collective-permute-start | bytes 221192 | tf_op jit(solution)/shard_map/ppermute | solution.py:297
  9.0 14.5 %collective-permute-start.3 = (bf16[144,256]{1,0:T(8,128)(2,1)S(1)}, bf16[144,256]{1,0:T(8,128)(2,1)S(1)}, u32[]{:S(2)}, u32[]{:S(2)}) collective-permute-start(bf16[144,256]{1,0:T(8,128)(2,1)S(1)} %get-tuple-element.28), channel_id=1, source_target_pairs={{0,10},{1,11},{2,8},{3,9},{4,14},{5,15},{6,12},{7,13},{8,2},{9,3},... | collective-permute-start | bytes 221192 | tf_op jit(solution)/shard_map/ppermute | solution.py:297
  9.0 14.5 %collective-permute-start.4 = (bf16[144,256]{1,0:T(8,128)(2,1)S(1)}, bf16[144,256]{1,0:T(8,128)(2,1)S(1)}, u32[]{:S(2)}, u32[]{:S(2)}) collective-permute-start(bf16[144,256]{1,0:T(8,128)(2,1)S(1)} %get-tuple-element.29), channel_id=1, source_target_pairs={{0,12},{1,13},{2,14},{3,15},{4,8},{5,9},{6,10},{7,11},{8,4},{9,5},... | collective-permute-start | bytes 221192 | tf_op jit(solution)/shard_map/ppermute | solution.py:297
  13.7 9.9 %collective-permute-start.5 = (bf16[144,256]{1,0:T(8,128)(2,1)S(1)}, bf16[144,256]{1,0:T(8,128)(2,1)S(1)}, u32[]{:S(2)}, u32[]{:S(2)}) collective-permute-start(bf16[144,256]{1,0:T(8,128)(2,1)S(1)} %get-tuple-element.30), channel_id=1, source_target_pairs={{0,14},{1,15},{2,12},{3,13},{4,10},{5,11},{6,8},{7,9},{8,6},{9,7},... | collective-permute-start | bytes 221192 | tf_op jit(solution)/shard_map/ppermute | solution.py:297
  14.9 8.7 %collective-permute-start.6 = (bf16[144,256]{1,0:T(8,128)(2,1)S(1)}, bf16[144,256]{1,0:T(8,128)(2,1)S(1)}, u32[]{:S(2)}, u32[]{:S(2)}) collective-permute-start(bf16[144,256]{1,0:T(8,128)(2,1)S(1)} %get-tuple-element.31), channel_id=1, source_target_pairs={{0,2},{1,3},{2,0},{3,1},{4,6},{5,7},{6,4},{7,5},{8,10},{9,11},{10,... | collective-permute-start | bytes 221192 | tf_op jit(solution)/shard_map/ppermute | solution.py:297
  15.3 2.2 %copy-start.1 = (bf16[2048,1024]{1,0:T(8,128)(2,1)S(1)}, bf16[2048,1024]{1,0:T(8,128)(2,1)}, u32[]{:S(2)}) copy-start(bf16[2048,1024]{1,0:T(8,128)(2,1)} %slab_ref.7) | copy-start | bytes 12582916
  23.6 2.2 %collective-permute-start.7 = (bf16[8,16,256]{2,1,0:T(8,128)(2,1)S(1)}, bf16[8,16,256]{2,1,0:T(8,128)(2,1)S(1)}, u32[]{:S(2)}, u32[]{:S(2)}) collective-permute-start(bf16[8,16,256]{2,1,0:T(8,128)(2,1)S(1)} %collect.1.packets_ref.own_ref), channel_id=1, source_target_pairs={{0,1},{1,0},{2,3},{3,2},{4,5},{5,4},{6,7},{7,6},{8,9},{9,8},{10,11... | collective-permute-start | bytes 196616 | tf_op jit(solution)/shard_map/ppermute | solution.py:297
  25.8 2.2 %copy-start = (s32[4096]{0:T(1024)S(1)}, s32[4096]{0:T(1024)}, u32[]{:S(2)}) copy-start(s32[4096]{0:T(1024)} %param.8) | copy-start | bytes 49156
  28.0 2.2 %copy-start.2 = (bf16[2048,1024]{1,0:T(8,128)(2,1)S(1)}, bf16[2048,1024]{1,0:T(8,128)(2,1)}, u32[]{:S(2)}) copy-start(bf16[2048,1024]{1,0:T(8,128)(2,1)} %slab_ref.7) | copy-start | bytes 12582916
  29.7 2.9 %collective-permute-start.8 = (f32[128,1024]{1,0:T(8,128)S(1)}, f32[128,1024]{1,0:T(8,128)S(1)}, u32[]{:S(2)}, u32[]{:S(2)}) collective-permute-start(f32[128,1024]{1,0:T(8,128)S(1)} %get-tuple-element.35.refs_0_.own_ref), channel_id=1, source_target_pairs={{0,1},{1,0},{2,3},{3,2},{4,5},{5,4},{6,7},{7,6},{8,9},{9,8},{10,11... | collective-permute-start | bytes 1572872 | tf_op jit(solution)/shard_map/ppermute | solution.py:297
  33.6 9.6 %collective-permute-start.9 = (bf16[128,256]{1,0:T(8,128)(2,1)S(1)}, bf16[128,256]{1,0:T(8,128)(2,1)S(1)}, u32[]{:S(2)}, u32[]{:S(2)}) collective-permute-start(bf16[128,256]{1,0:T(8,128)(2,1)S(1)} %get-tuple-element.37), channel_id=1, source_target_pairs={{0,4},{1,5},{2,6},{3,7},{4,0},{5,1},{6,2},{7,3},{8,12},{9,13},{10,... | collective-permute-start | bytes 196616 | tf_op jit(solution)/shard_map/ppermute | solution.py:297
  33.6 10.7 %collective-permute-start.10 = (bf16[128,256]{1,0:T(8,128)(2,1)S(1)}, bf16[128,256]{1,0:T(8,128)(2,1)S(1)}, u32[]{:S(2)}, u32[]{:S(2)}) collective-permute-start(bf16[128,256]{1,0:T(8,128)(2,1)S(1)} %get-tuple-element.38), channel_id=1, source_target_pairs={{0,6},{1,7},{2,4},{3,5},{4,2},{5,3},{6,0},{7,1},{8,14},{9,15},{10,... | collective-permute-start | bytes 196616 | tf_op jit(solution)/shard_map/ppermute | solution.py:297
  36.7 10.5 %collective-permute-start.11 = (bf16[128,256]{1,0:T(8,128)(2,1)S(1)}, bf16[128,256]{1,0:T(8,128)(2,1)S(1)}, u32[]{:S(2)}, u32[]{:S(2)}) collective-permute-start(bf16[128,256]{1,0:T(8,128)(2,1)S(1)} %get-tuple-element.39), channel_id=1, source_target_pairs={{0,8},{1,9},{2,10},{3,11},{4,12},{5,13},{6,14},{7,15},{8,0},{9,1},... | collective-permute-start | bytes 196616 | tf_op jit(solution)/shard_map/ppermute | solution.py:297
  38.9 10.3 %collective-permute-start.12 = (bf16[128,256]{1,0:T(8,128)(2,1)S(1)}, bf16[128,256]{1,0:T(8,128)(2,1)S(1)}, u32[]{:S(2)}, u32[]{:S(2)}) collective-permute-start(bf16[128,256]{1,0:T(8,128)(2,1)S(1)} %get-tuple-element.40), channel_id=1, source_target_pairs={{0,10},{1,11},{2,8},{3,9},{4,14},{5,15},{6,12},{7,13},{8,2},{9,3},... | collective-permute-start | bytes 196616 | tf_op jit(solution)/shard_map/ppermute | solution.py:297
  39.5 9.7 %collective-permute-start.13 = (bf16[128,256]{1,0:T(8,128)(2,1)S(1)}, bf16[128,256]{1,0:T(8,128)(2,1)S(1)}, u32[]{:S(2)}, u32[]{:S(2)}) collective-permute-start(bf16[128,256]{1,0:T(8,128)(2,1)S(1)} %get-tuple-element.41), channel_id=1, source_target_pairs={{0,12},{1,13},{2,14},{3,15},{4,8},{5,9},{6,10},{7,11},{8,4},{9,5},... | collective-permute-start | bytes 196616 | tf_op jit(solution)/shard_map/ppermute | solution.py:297
  43.2 7.1 %collective-permute-start.14 = (bf16[128,256]{1,0:T(8,128)(2,1)S(1)}, bf16[128,256]{1,0:T(8,128)(2,1)S(1)}, u32[]{:S(2)}, u32[]{:S(2)}) collective-permute-start(bf16[128,256]{1,0:T(8,128)(2,1)S(1)} %get-tuple-element.42), channel_id=1, source_target_pairs={{0,14},{1,15},{2,12},{3,13},{4,10},{5,11},{6,8},{7,9},{8,6},{9,7},... | collective-permute-start | bytes 196616 | tf_op jit(solution)/shard_map/ppermute | solution.py:297
  44.3 5.9 %collective-permute-start.15 = (bf16[128,256]{1,0:T(8,128)(2,1)S(1)}, bf16[128,256]{1,0:T(8,128)(2,1)S(1)}, u32[]{:S(2)}, u32[]{:S(2)}) collective-permute-start(bf16[128,256]{1,0:T(8,128)(2,1)S(1)} %get-tuple-element.43), channel_id=1, source_target_pairs={{0,2},{1,3},{2,0},{3,1},{4,6},{5,7},{6,4},{7,5},{8,10},{9,11},{10,... | collective-permute-start | bytes 196616 | tf_op jit(solution)/shard_map/ppermute | solution.py:297

commit v15 on v14

--- a/solution.py
+++ b/solution.py
@@ -366,7 +366,7 @@
         name="choose",
     )(me, in_hbm(term_codes.T), *blocks[1:3])
     ordered = [
-        reorder(start, *blocks[1:3]) for start in [*quarters[0], *quarters[1]]
+        reorder(start, *blocks[1:3]) for start in quarters[0]
     ]
     packets = pl.pallas_call(
         functools.partial(collect_kernel, chips),
@@ -415,7 +415,7 @@
         cost_estimate=fit_cost,
         name="fit",
     )(me, weight_levels[None, :], packets, others, *blocks, *designs)
-    beside = [reorder(start, fitted) for start in quarters[2]]
+    beside = [reorder(start, fitted) for start in quarters[1]]
     summed = pl.pallas_call(
         functools.partial(sum_kernel, float(total_runs), chips),
         in_specs=[vmem] * (2 + CORES) + [anywhere] * len(beside),
@@ -427,7 +427,9 @@
     )(fitted, to_device(fitted, 1), *designs, *beside)
     returned = to_chips(summed)
     ordered += beside
-    ordered += [reorder(start, summed[0]) for start in quarters[3]]
+    ordered += [
+        reorder(start, *returned[1:3]) for start in [*quarters[2], *quarters[3]]
+    ]
 
     return pl.pallas_call(
         functools.partial(finish_kernel, len(ordered)),

time: 53.3 us -> 51.7 us (0.970)
  waiting for transfers between devices: 3.15 us -> 0.68 us
    ppermute x16, waiting for transfers between devices: 3.15 us -> 0.68 us  [to_device(): return lax.ppermute(array, 'runs', [(i, i ^ bits) for i in range(devices)])]
  transfers between devices with their start and end apart: 16 -> 16, of which waited for: 2 -> 2; matrix products, arithmetic and copies ran while one was open for 1% -> 1% of each run, Pallas kernels for 24% -> 26%
where the time goes in v15:
time: 51.7 us; the launch traced here: 51.4 us
  starting transfers between devices  24.8 us (48%)
  Pallas kernels  21.9 us (42%)
  local copies, waits for them, and re-layouts  2.97 us (6%)
  between operations  0.99 us (2%)
  waiting for transfers between devices  0.68 us (1%)
    ppermute x16, starting transfers between devices, to_device(): return lax.ppermute(array, 'runs', [(i, i ^ bits) for i in range(devices)])  24.8 us
    pallas_call x4, Pallas kernels, reorder(): pl.pallas_call(reorder_kernel, in_specs=[vmem, vmem] + [anywhere] * len(a...  9.64 us
    pallas_call x2, Pallas kernels, design_of(): pl.pallas_call(functools.partial(design_kernel, dim, run_count), in_specs...  4.73 us
    pallas_call x1, Pallas kernels, split_by_modes(): pl.pallas_call(functools.partial(finish_kernel, len(ordered)), in_specs=[...  2.57 us
    unnamed x6, local copies, waits for them, and re-layouts  2.2 us
    pallas_call x1, Pallas kernels, split_by_modes(): pl.pallas_call(functools.partial(fit_kernel, 2 * rows), in_specs=[smem] +...  1.62 us
    pallas_call x1, Pallas kernels, split_by_modes(): pl.pallas_call(functools.partial(prepare_kernel, chips), in_specs=[smem,...  1.35 us
    pallas_call x1, Pallas kernels, split_by_modes(): pl.pallas_call(functools.partial(choose_kernel, dim, chips), in_specs=[sm...  1.29 us
  transfers between devices with their start and end apart: 16, of which 2 were waited for; matrix products, arithmetic and copies ran while one was open for 1% of the time, Pallas kernels for 26%

profile of v15, /device:TPU:0, one launch (start us, length us, event | category | flops | bytes accessed | tf_op | source)
XLA Modules:
  0.0 51.4 jit_solution(5556810093802187949)
XLA Ops:
  0.6 1.3 %prepare.1 = (bf16[1024,256]{1,0:T(8,128)(2,1)S(1)}, bf16[144,256]{1,0:T(8,128)(2,1)S(1)}, bf16[144,256]{1,0:T(8,128)(2,1)S(1)}, bf16[144,256]{1,0:T(8,128)(2,1)...) custom-call(s32[1]{0:T(128)} %bitcast.me_ref, ...), custom_call_target="tpu_custom_call" | custom-call | tf_op jit(solution)/shard_map/prepare/pallas_call | solution.py:327
  2.0 3.1 %collective-permute-start = (bf16[144,256]{1,0:T(8,128)(2,1)S(1)}, bf16[144,256]{1,0:T(8,128)(2,1)S(1)}, u32[]{:S(2)}, u32[]{:S(2)}) collective-permute-start(bf16[144,256]{1,0:T(8,128)(2,1)S(1)} %get-tuple-element.25), channel_id=1, source_target_pairs={{0,4},{1,5},{2,6},{3,7},{4,0},{5,1},{6,2},{7,3},{8,12},{9,13},{10,... | collective-permute-start | bytes 221192 | tf_op jit(solution)/shard_map/ppermute | solution.py:297
  5.1 1.4 %collective-permute-start.1 = (bf16[144,256]{1,0:T(8,128)(2,1)S(1)}, bf16[144,256]{1,0:T(8,128)(2,1)S(1)}, u32[]{:S(2)}, u32[]{:S(2)}) collective-permute-start(bf16[144,256]{1,0:T(8,128)(2,1)S(1)} %get-tuple-element.26), channel_id=1, source_target_pairs={{0,6},{1,7},{2,4},{3,5},{4,2},{5,3},{6,0},{7,1},{8,14},{9,15},{10,... | collective-permute-start | bytes 221192 | tf_op jit(solution)/shard_map/ppermute | solution.py:297
  6.4 2.6 %collective-permute-start.2 = (bf16[144,256]{1,0:T(8,128)(2,1)S(1)}, bf16[144,256]{1,0:T(8,128)(2,1)S(1)}, u32[]{:S(2)}, u32[]{:S(2)}) collective-permute-start(bf16[144,256]{1,0:T(8,128)(2,1)S(1)} %get-tuple-element.27), channel_id=1, source_target_pairs={{0,8},{1,9},{2,10},{3,11},{4,12},{5,13},{6,14},{7,15},{8,0},{9,1},... | collective-permute-start | bytes 221192 | tf_op jit(solution)/shard_map/ppermute | solution.py:297
  9.0 0.0 collective-permute-start.3
  9.0 3.9 %collective-permute-start.4 = (bf16[144,256]{1,0:T(8,128)(2,1)S(1)}, bf16[144,256]{1,0:T(8,128)(2,1)S(1)}, u32[]{:S(2)}, u32[]{:S(2)}) collective-permute-start(bf16[144,256]{1,0:T(8,128)(2,1)S(1)} %get-tuple-element.29), channel_id=1, source_target_pairs={{0,12},{1,13},{2,14},{3,15},{4,8},{5,9},{6,10},{7,11},{8,4},{9,5},... | collective-permute-start | bytes 221192 | tf_op jit(solution)/shard_map/ppermute | solution.py:297
  12.9 0.8 %fusion = (s32[512]{0:T(512)S(1)}, s32[512]{0:T(512)S(1)}, s32[512]{0:T(512)S(1)}, s32[512]{0:T(512)S(1)}) fusion(s32[2048]{0:T(1024)} %param.11), kind=kLoop, calls=%fused_computation | loop fusion | bytes 16384 | tf_op jit(solution)/shard_map/slice | solution.py:349
  13.7 0.0 collective-permute-done.refs_0_.refs_1_
  13.7 1.2 %collective-permute-start.5 = (bf16[144,256]{1,0:T(8,128)(2,1)S(1)}, bf16[144,256]{1,0:T(8,128)(2,1)S(1)}, u32[]{:S(2)}, u32[]{:S(2)}) collective-permute-start(bf16[144,256]{1,0:T(8,128)(2,1)S(1)} %get-tuple-element.30), channel_id=1, source_target_pairs={{0,14},{1,15},{2,12},{3,13},{4,10},{5,11},{6,8},{7,9},{8,6},{9,7},... | collective-permute-start | bytes 221192 | tf_op jit(solution)/shard_map/ppermute | solution.py:297
  14.9 0.0 collective-permute-done.1.refs_1_.refs_2_
  14.9 0.4 collective-permute-start.6
  15.3 0.0 copy-start.1
  15.3 2.2 %copy-done.1 = bf16[2048,1024]{1,0:T(8,128)(2,1)S(1)} copy-done((bf16[2048,1024]{1,0:T(8,128)(2,1)S(1)}, bf16[2048,1024]{1,0:T(8,128)(2,1)}, u32[]{:S(2)}) %copy-start.1) | copy-done | bytes 4194328
  17.5 2.4 %reorder.4.refs_9_.refs_0_ = bf16[512,1024]{1,0:T(8,128)(2,1)S(1)} custom-call(s32[1,512]{1,0:T(1,128)S(1)} %bitcast.12, bf16[2048,1024]{1,0:T(8,128)(2,1)S(1)} %copy-done.1, bf16[144,256]{1,0:T(8,128)(2,1)S(1)} %collective-permute-done.refs_0_.refs_1_, bf16[144,256]{1,0:T(8,128)(2,1)S(1)} %collective-permute-done.1.refs_1_.refs_2_), custom_call_target="tpu_custom_call" | custom-call | flops 2147483648 | bytes 4194304 | tf_op jit(solution)/shard_map/reorder/pallas_call | solution.py:341
  19.9 1.3 %choose.1 = (bf16[3,256,2048]{2,1,0:T(8,128)(2,1)S(1)}, s32[1,2048]{1,0:T(1,128)S(1)}) custom-call(s32[1]{0:T(128)} %bitcast.me_ref, s32[4,4096]{1,0:T(4,128)} %bitcast.13, bf16[144,256]{1,0:T(8,128)(2,1)S(1)} %collective-permute-done.refs_0_.refs_1_, bf16[144,256]{1,0:T(8,128)(2,1)S(1)} %collective-permute-done.1.refs_1_.refs_2_), custom_call_target="tpu_custom_call" | custom-call | bytes 2097152 | tf_op jit(solution)/shard_map/choose/pallas_call | solution.py:356
  21.2 0.0 collective-permute-done.2.refs_3_
  21.2 0.0 collective-permute-done.3.refs_4_
  21.2 0.0 collective-permute-done.4.refs_5_
  21.2 0.0 collective-permute-done.5.refs_6_
  21.2 0.0 collective-permute-done.6.refs_7_
  21.2 0.1 collective-permute-start.7
  21.3 2.4 %design.2.refs_8_.refs_0_ = bf16[512,2048]{1,0:T(8,128)(2,1)S(1)} custom-call(bf16[8,16,256]{2,1,0:T(8,128)(2,1)S(1)} %collect.1.packets_ref.own_ref, bf16[3,256,2048]{2,1,0:T(8,128)(2,1)S(1)} %get-tuple-element.33.chosen_ref, s32[1,2048]{1,0:T(1,128)S(1)} %get-tuple-element.32.refs_8_.spots_ref), custom_call_target="tpu_custom_call" | custom-call | flops 2147483648 | bytes 2097152 | tf_op jit(solution)/shard_map/design/pallas_call | solution.py:384
  23.7 0.0 copy-start
  23.7 0.0 collective-permute-done.7.packets_ref.other_ref
  23.7 2.4 %design.3.refs_9_.refs_1_ = bf16[512,2048]{1,0:T(8,128)(2,1)S(1)} custom-call(bf16[8,16,256]{2,1,0:T(8,128)(2,1)S(1)} %collective-permute-done.7.packets_ref.other_ref, bf16[3,256,2048]{2,1,0:T(8,128)(2,1)S(1)} %get-tuple-element.33.chosen_ref, s32[1,2048]{1,0:T(1,128)S(1)} %get-tuple-element.32.refs_8_.spots_ref), custom_call_target="tpu_custom_call" | custom-call | flops 2147483648 | bytes 2097152 | tf_op jit(solution)/shard_map/design/pallas_call | solution.py:384
  26.1 0.0 copy-start.2
  26.1 0.0 copy-done
  26.1 1.6 %fit.1 = (f32[128,1024]{1,0:T(8,128)S(1)}, f32[8,256]{1,0:T(8,128)S(1)}) custom-call(s32[1]{0:T(128)} %bitcast.me_ref, s32[1,4096]{1,0:T(1,128)S(1)} %bitcast.8, bf16[8,16,256]{2,1,0:T(8,128)(2,1)S(1)} %collect.1.packets_ref.own_ref, bf16[8,16,256]{2,1,0:T(8,128)(2,1)S(1)} %collective-permute-done.7.packets_ref.other_ref, ...), custom_call_target="tpu_custom_call" | custom-call | flops 536870912 | bytes 4194304 | tf_op jit(solution)/shard_map/fit/pallas_call | solution.py:405
  27.7 0.6 %collective-permute-start.8 = (f32[128,1024]{1,0:T(8,128)S(1)}, f32[128,1024]{1,0:T(8,128)S(1)}, u32[]{:S(2)}, u32[]{:S(2)}) collective-permute-start(f32[128,1024]{1,0:T(8,128)S(1)} %get-tuple-element.35.refs_0_.own_ref), channel_id=1, source_target_pairs={{0,1},{1,0},{2,3},{3,2},{4,5},{5,4},{6,7},{7,6},{8,9},{9,8},{10,11... | collective-permute-start | bytes 1572872 | tf_op jit(solution)/shard_map/ppermute | solution.py:297
  28.3 0.0 copy-done.2
  28.3 2.4 %reorder.5.refs_2_.refs_1_ = bf16[512,1024]{1,0:T(8,128)(2,1)S(1)} custom-call(s32[1,512]{1,0:T(1,128)S(1)} %bitcast.11, bf16[2048,1024]{1,0:T(8,128)(2,1)S(1)} %copy-done.2, f32[128,1024]{1,0:T(8,128)S(1)} %get-tuple-element.35.refs_0_.own_ref), custom_call_target="tpu_custom_call" | custom-call | flops 2147483648 | bytes 4194304 | tf_op jit(solution)/shard_map/reorder/pallas_call | solution.py:341
  30.7 0.0 collective-permute-done.8.other_ref
  30.7 0.7 %sum.1 = (bf16[128,256]{1,0:T(8,128)(2,1)S(1)}, bf16[128,256]{1,0:T(8,128)(2,1)S(1)}, bf16[128,256]{1,0:T(8,128)(2,1)S(1)}, bf16[128,256]{1,0:T(8,128)(2,1)S(1)}...) custom-call(f32[128,1024]{1,0:T(8,128)S(1)} %get-tuple-element.35.re, ...), custom_call_target="tpu_custom_call" | custom-call | flops 536870912 | bytes 4194304 | tf_op jit(solution)/shard_map/sum/pallas_call | solution.py:419
  31.4 2.5 %collective-permute-start.9 = (bf16[128,256]{1,0:T(8,128)(2,1)S(1)}, bf16[128,256]{1,0:T(8,128)(2,1)S(1)}, u32[]{:S(2)}, u32[]{:S(2)}) collective-permute-start(bf16[128,256]{1,0:T(8,128)(2,1)S(1)} %get-tuple-element.36), channel_id=1, source_target_pairs={{0,4},{1,5},{2,6},{3,7},{4,0},{5,1},{6,2},{7,3},{8,12},{9,13},{10,... | collective-permute-start | bytes 196616 | tf_op jit(solution)/shard_map/ppermute | solution.py:297
  33.9 0.7 %collective-permute-start.10 = (bf16[128,256]{1,0:T(8,128)(2,1)S(1)}, bf16[128,256]{1,0:T(8,128)(2,1)S(1)}, u32[]{:S(2)}, u32[]{:S(2)}) collective-permute-start(bf16[128,256]{1,0:T(8,128)(2,1)S(1)} %get-tuple-element.37), channel_id=1, source_target_pairs={{0,6},{1,7},{2,4},{3,5},{4,2},{5,3},{6,0},{7,1},{8,14},{9,15},{10,... | collective-permute-start | bytes 196616 | tf_op jit(solution)/shard_map/ppermute | solution.py:297
  34.6 3.1 %collective-permute-start.11 = (bf16[128,256]{1,0:T(8,128)(2,1)S(1)}, bf16[128,256]{1,0:T(8,128)(2,1)S(1)}, u32[]{:S(2)}, u32[]{:S(2)}) collective-permute-start(bf16[128,256]{1,0:T(8,128)(2,1)S(1)} %get-tuple-element.39), channel_id=1, source_target_pairs={{0,8},{1,9},{2,10},{3,11},{4,12},{5,13},{6,14},{7,15},{8,0},{9,1},... | collective-permute-start | bytes 196616 | tf_op jit(solution)/shard_map/ppermute | solution.py:297
  37.7 0.1 collective-permute-start.12
  37.8 3.3 %collective-permute-start.13 = (bf16[128,256]{1,0:T(8,128)(2,1)S(1)}, bf16[128,256]{1,0:T(8,128)(2,1)S(1)}, u32[]{:S(2)}, u32[]{:S(2)}) collective-permute-start(bf16[128,256]{1,0:T(8,128)(2,1)S(1)} %get-tuple-element.41), channel_id=1, source_target_pairs={{0,12},{1,13},{2,14},{3,15},{4,8},{5,9},{6,10},{7,11},{8,4},{9,5},... | collective-permute-start | bytes 196616 | tf_op jit(solution)/shard_map/ppermute | solution.py:297
  41.1 0.0 collective-permute-done.9.refs_0_.refs_5_
  41.1 1.4 %collective-permute-start.14 = (bf16[128,256]{1,0:T(8,128)(2,1)S(1)}, bf16[128,256]{1,0:T(8,128)(2,1)S(1)}, u32[]{:S(2)}, u32[]{:S(2)}) collective-permute-start(bf16[128,256]{1,0:T(8,128)(2,1)S(1)} %get-tuple-element.42), channel_id=1, source_target_pairs={{0,14},{1,15},{2,12},{3,13},{4,10},{5,11},{6,8},{7,9},{8,6},{9,7},... | collective-permute-start | bytes 196616 | tf_op jit(solution)/shard_map/ppermute | solution.py:297
  42.4 0.0 collective-permute-done.10.refs_1_.refs_6_
  42.4 0.7 %collective-permute-start.15 = (bf16[128,256]{1,0:T(8,128)(2,1)S(1)}, bf16[128,256]{1,0:T(8,128)(2,1)S(1)}, u32[]{:S(2)}, u32[]{:S(2)}) collective-permute-start(bf16[128,256]{1,0:T(8,128)(2,1)S(1)} %get-tuple-element.43), channel_id=1, source_target_pairs={{0,2},{1,3},{2,0},{3,1},{4,6},{5,7},{6,4},{7,5},{8,10},{9,11},{10,... | collective-permute-start | bytes 196616 | tf_op jit(solution)/shard_map/ppermute | solution.py:297
  43.1 2.6 %reorder.7.refs_3_ = bf16[512,1024]{1,0:T(8,128)(2,1)S(1)} custom-call(s32[1,512]{1,0:T(1,128)S(1)} %bitcast.10, bf16[2048,1024]{1,0:T(8,128)(2,1)S(1)} %copy-done.2, bf16[128,256]{1,0:T(8,128)(2,1)S(1)} %collective-permute-done.9.refs_0_.refs_5_, bf16[128,256]{1,0:T(8,128)(2,1)S(1)} %collective-permute-done.10.refs_1_.refs_6_), custom_call_target="tpu_custom_call" | custom-call | flops 2147483648 | bytes 4194304 | tf_op jit(solution)/shard_map/reorder/pallas_call | solution.py:341
  45.7 2.4 %reorder.6.refs_2_ = bf16[512,1024]{1,0:T(8,128)(2,1)S(1)} custom-call(s32[1,512]{1,0:T(1,128)S(1)} %bitcast.9, bf16[2048,1024]{1,0:T(8,128)(2,1)S(1)} %copy-done.2, bf16[128,256]{1,0:T(8,128)(2,1)S(1)} %collective-permute-done.9.refs_0_.refs_5_, bf16[128,256]{1,0:T(8,128)(2,1)S(1)} %collective-permute-done.10.refs_1_.refs_6_), custom_call_target="tpu_custom_call" | custom-call | flops 2147483648 | bytes 4194304 | tf_op jit(solution)/shard_map/reorder/pallas_call | solution.py:341
  48.0 0.0 collective-permute-done.11.refs_7_
  48.0 0.0 collective-permute-done.12.refs_8_
  48.0 0.0 collective-permute-done.13.refs_9_
  48.1 0.1 collective-permute-done.14.refs_10_
  48.2 0.5 %collective-permute-done.15.refs_11_ = bf16[128,256]{1,0:T(8,128)(2,1)S(1)} collective-permute-done((bf16[128,256]{1,0:T(8,128)(2,1)S(1)}, bf16[128,256]{1,0:T(8,128)(2,1)S(1)}, u32[]{:S(2)}, u32[]{:S(2)}) %collective-permute-start.15) | collective-permute-done | bytes 65568 | tf_op jit(solution)/shard_map/ppermute | solution.py:297
  48.7 2.6 %finish.1 = (f32[256,1024]{1,0:T(8,128)}, bf16[256,2048]{1,0:T(8,128)(2,1)}) custom-call(s32[1]{0:T(128)} %bitcast.me_ref, bf16[1024,256]{1,0:T(8,128)(2,1)S(1)} %get-tuple-element.23.corr_ref, f32[8,256]{1,0:T(8,128)S(1)} %get-tuple-element.34.scale_ref, bf16[512,1024]{1,0:T(8,128)(2,1)S(1)} %reorder.4.refs_9_.refs_0_, ...), custom_call_target="tpu_custom_call" | custom-call | tf_op jit(solution)/shard_map/finish/pallas_call | solution.py:434
  (1 shorter events, 0.0 us)
Async XLA Ops:
  2.0 11.7 %collective-permute-start = (bf16[144,256]{1,0:T(8,128)(2,1)S(1)}, bf16[144,256]{1,0:T(8,128)(2,1)S(1)}, u32[]{:S(2)}, u32[]{:S(2)}) collective-permute-start(bf16[144,256]{1,0:T(8,128)(2,1)S(1)} %get-tuple-element.25), channel_id=1, source_target_pairs={{0,4},{1,5},{2,6},{3,7},{4,0},{5,1},{6,2},{7,3},{8,12},{9,13},{10,... | collective-permute-start | bytes 221192 | tf_op jit(solution)/shard_map/ppermute | solution.py:297
  5.1 9.8 %collective-permute-start.1 = (bf16[144,256]{1,0:T(8,128)(2,1)S(1)}, bf16[144,256]{1,0:T(8,128)(2,1)S(1)}, u32[]{:S(2)}, u32[]{:S(2)}) collective-permute-start(bf16[144,256]{1,0:T(8,128)(2,1)S(1)} %get-tuple-element.26), channel_id=1, source_target_pairs={{0,6},{1,7},{2,4},{3,5},{4,2},{5,3},{6,0},{7,1},{8,14},{9,15},{10,... | collective-permute-start | bytes 221192 | tf_op jit(solution)/shard_map/ppermute | solution.py:297
  6.4 14.7 %collective-permute-start.2 = (bf16[144,256]{1,0:T(8,128)(2,1)S(1)}, bf16[144,256]{1,0:T(8,128)(2,1)S(1)}, u32[]{:S(2)}, u32[]{:S(2)}) collective-permute-start(bf16[144,256]{1,0:T(8,128)(2,1)S(1)} %get-tuple-element.27), channel_id=1, source_target_pairs={{0,8},{1,9},{2,10},{3,11},{4,12},{5,13},{6,14},{7,15},{8,0},{9,1},... | collective-permute-start | bytes 221192 | tf_op jit(solution)/shard_map/ppermute | solution.py:297
  9.0 12.2 %collective-permute-start.3 = (bf16[144,256]{1,0:T(8,128)(2,1)S(1)}, bf16[144,256]{1,0:T(8,128)(2,1)S(1)}, u32[]{:S(2)}, u32[]{:S(2)}) collective-permute-start(bf16[144,256]{1,0:T(8,128)(2,1)S(1)} %get-tuple-element.28), channel_id=1, source_target_pairs={{0,10},{1,11},{2,8},{3,9},{4,14},{5,15},{6,12},{7,13},{8,2},{9,3},... | collective-permute-start | bytes 221192 | tf_op jit(solution)/shard_map/ppermute | solution.py:297
  9.0 12.2 %collective-permute-start.4 = (bf16[144,256]{1,0:T(8,128)(2,1)S(1)}, bf16[144,256]{1,0:T(8,128)(2,1)S(1)}, u32[]{:S(2)}, u32[]{:S(2)}) collective-permute-start(bf16[144,256]{1,0:T(8,128)(2,1)S(1)} %get-tuple-element.29), channel_id=1, source_target_pairs={{0,12},{1,13},{2,14},{3,15},{4,8},{5,9},{6,10},{7,11},{8,4},{9,5},... | collective-permute-start | bytes 221192 | tf_op jit(solution)/shard_map/ppermute | solution.py:297
  13.7 7.5 %collective-permute-start.5 = (bf16[144,256]{1,0:T(8,128)(2,1)S(1)}, bf16[144,256]{1,0:T(8,128)(2,1)S(1)}, u32[]{:S(2)}, u32[]{:S(2)}) collective-permute-start(bf16[144,256]{1,0:T(8,128)(2,1)S(1)} %get-tuple-element.30), channel_id=1, source_target_pairs={{0,14},{1,15},{2,12},{3,13},{4,10},{5,11},{6,8},{7,9},{8,6},{9,7},... | collective-permute-start | bytes 221192 | tf_op jit(solution)/shard_map/ppermute | solution.py:297
  14.9 6.3 %collective-permute-start.6 = (bf16[144,256]{1,0:T(8,128)(2,1)S(1)}, bf16[144,256]{1,0:T(8,128)(2,1)S(1)}, u32[]{:S(2)}, u32[]{:S(2)}) collective-permute-start(bf16[144,256]{1,0:T(8,128)(2,1)S(1)} %get-tuple-element.31), channel_id=1, source_target_pairs={{0,2},{1,3},{2,0},{3,1},{4,6},{5,7},{6,4},{7,5},{8,10},{9,11},{10,... | collective-permute-start | bytes 221192 | tf_op jit(solution)/shard_map/ppermute | solution.py:297
  15.3 2.2 %copy-start.1 = (bf16[2048,1024]{1,0:T(8,128)(2,1)S(1)}, bf16[2048,1024]{1,0:T(8,128)(2,1)}, u32[]{:S(2)}) copy-start(bf16[2048,1024]{1,0:T(8,128)(2,1)} %slab_ref.7) | copy-start | bytes 12582916
  21.2 2.5 %collective-permute-start.7 = (bf16[8,16,256]{2,1,0:T(8,128)(2,1)S(1)}, bf16[8,16,256]{2,1,0:T(8,128)(2,1)S(1)}, u32[]{:S(2)}, u32[]{:S(2)}) collective-permute-start(bf16[8,16,256]{2,1,0:T(8,128)(2,1)S(1)} %collect.1.packets_ref.own_ref), channel_id=1, source_target_pairs={{0,1},{1,0},{2,3},{3,2},{4,5},{5,4},{6,7},{7,6},{8,9},{9,8},{10,11... | collective-permute-start | bytes 196616 | tf_op jit(solution)/shard_map/ppermute | solution.py:297
  23.7 2.4 %copy-start = (s32[4096]{0:T(1024)S(1)}, s32[4096]{0:T(1024)}, u32[]{:S(2)}) copy-start(s32[4096]{0:T(1024)} %param.8) | copy-start | bytes 49156
  26.1 2.2 %copy-start.2 = (bf16[2048,1024]{1,0:T(8,128)(2,1)S(1)}, bf16[2048,1024]{1,0:T(8,128)(2,1)}, u32[]{:S(2)}) copy-start(bf16[2048,1024]{1,0:T(8,128)(2,1)} %slab_ref.7) | copy-start | bytes 12582916
  27.7 2.9 %collective-permute-start.8 = (f32[128,1024]{1,0:T(8,128)S(1)}, f32[128,1024]{1,0:T(8,128)S(1)}, u32[]{:S(2)}, u32[]{:S(2)}) collective-permute-start(f32[128,1024]{1,0:T(8,128)S(1)} %get-tuple-element.35.refs_0_.own_ref), channel_id=1, source_target_pairs={{0,1},{1,0},{2,3},{3,2},{4,5},{5,4},{6,7},{7,6},{8,9},{9,8},{10,11... | collective-permute-start | bytes 1572872 | tf_op jit(solution)/shard_map/ppermute | solution.py:297
  31.4 9.6 %collective-permute-start.9 = (bf16[128,256]{1,0:T(8,128)(2,1)S(1)}, bf16[128,256]{1,0:T(8,128)(2,1)S(1)}, u32[]{:S(2)}, u32[]{:S(2)}) collective-permute-start(bf16[128,256]{1,0:T(8,128)(2,1)S(1)} %get-tuple-element.36), channel_id=1, source_target_pairs={{0,4},{1,5},{2,6},{3,7},{4,0},{5,1},{6,2},{7,3},{8,12},{9,13},{10,... | collective-permute-start | bytes 196616 | tf_op jit(solution)/shard_map/ppermute | solution.py:297
  33.9 8.5 %collective-permute-start.10 = (bf16[128,256]{1,0:T(8,128)(2,1)S(1)}, bf16[128,256]{1,0:T(8,128)(2,1)S(1)}, u32[]{:S(2)}, u32[]{:S(2)}) collective-permute-start(bf16[128,256]{1,0:T(8,128)(2,1)S(1)} %get-tuple-element.37), channel_id=1, source_target_pairs={{0,6},{1,7},{2,4},{3,5},{4,2},{5,3},{6,0},{7,1},{8,14},{9,15},{10,... | collective-permute-start | bytes 196616 | tf_op jit(solution)/shard_map/ppermute | solution.py:297
  34.6 13.5 %collective-permute-start.11 = (bf16[128,256]{1,0:T(8,128)(2,1)S(1)}, bf16[128,256]{1,0:T(8,128)(2,1)S(1)}, u32[]{:S(2)}, u32[]{:S(2)}) collective-permute-start(bf16[128,256]{1,0:T(8,128)(2,1)S(1)} %get-tuple-element.39), channel_id=1, source_target_pairs={{0,8},{1,9},{2,10},{3,11},{4,12},{5,13},{6,14},{7,15},{8,0},{9,1},... | collective-permute-start | bytes 196616 | tf_op jit(solution)/shard_map/ppermute | solution.py:297
  37.7 10.3 %collective-permute-start.12 = (bf16[128,256]{1,0:T(8,128)(2,1)S(1)}, bf16[128,256]{1,0:T(8,128)(2,1)S(1)}, u32[]{:S(2)}, u32[]{:S(2)}) collective-permute-start(bf16[128,256]{1,0:T(8,128)(2,1)S(1)} %get-tuple-element.40), channel_id=1, source_target_pairs={{0,10},{1,11},{2,8},{3,9},{4,14},{5,15},{6,12},{7,13},{8,2},{9,3},... | collective-permute-start | bytes 196616 | tf_op jit(solution)/shard_map/ppermute | solution.py:297
  37.8 10.3 %collective-permute-start.13 = (bf16[128,256]{1,0:T(8,128)(2,1)S(1)}, bf16[128,256]{1,0:T(8,128)(2,1)S(1)}, u32[]{:S(2)}, u32[]{:S(2)}) collective-permute-start(bf16[128,256]{1,0:T(8,128)(2,1)S(1)} %get-tuple-element.41), channel_id=1, source_target_pairs={{0,12},{1,13},{2,14},{3,15},{4,8},{5,9},{6,10},{7,11},{8,4},{9,5},... | collective-permute-start | bytes 196616 | tf_op jit(solution)/shard_map/ppermute | solution.py:297
  41.1 7.1 %collective-permute-start.14 = (bf16[128,256]{1,0:T(8,128)(2,1)S(1)}, bf16[128,256]{1,0:T(8,128)(2,1)S(1)}, u32[]{:S(2)}, u32[]{:S(2)}) collective-permute-start(bf16[128,256]{1,0:T(8,128)(2,1)S(1)} %get-tuple-element.42), channel_id=1, source_target_pairs={{0,14},{1,15},{2,12},{3,13},{4,10},{5,11},{6,8},{7,9},{8,6},{9,7},... | collective-permute-start | bytes 196616 | tf_op jit(solution)/shard_map/ppermute | solution.py:297
  42.4 6.3 %collective-permute-start.15 = (bf16[128,256]{1,0:T(8,128)(2,1)S(1)}, bf16[128,256]{1,0:T(8,128)(2,1)S(1)}, u32[]{:S(2)}, u32[]{:S(2)}) collective-permute-start(bf16[128,256]{1,0:T(8,128)(2,1)S(1)} %get-tuple-element.43), channel_id=1, source_target_pairs={{0,2},{1,3},{2,0},{3,1},{4,6},{5,7},{6,4},{7,5},{8,10},{9,11},{10,... | collective-permute-start | bytes 196616 | tf_op jit(solution)/shard_map/ppermute | solution.py:297
